TPU v7x, 256 devices: a whole 4x4x8 slice. The times are simulated.
256 devices in a mesh: gx: 32 (over x, z), gz: 8 (over y, core).
Axes of the slice: x: 4, y: 4, z: 8, core: 2. Of those that a mesh axis runs over, the one named last changes fastest.
Arguments:
- atom_values: bfloat16 [160, 4, 1048576], P(None, None, ('gx', 'gz')), may hold values from -6 to 6
- atom_cell: int32 [1048576], P(('gx', 'gz')), may hold values from 0 to 511
- brick_column: int32 [2048], P(('gx', 'gz')), may hold values from 0 to 5, as said below
Outputs:
- denoised: bfloat16 [160, 4, 1048576], P(None, None, ('gx', 'gz'))
Inputs may be any that keep to these rules, and one draw needn't show every extreme that they name: `brick_column`: the 8 bricks of each device come in order: one or two bricks of column 0, then bricks of columns 1 to 4, then one or two bricks of column 5; the first device has two at each end.
All inputs are finite; a program needn't handle non-finite values.
Results may differ from a plain program's by a relative error of at most 0.00115.
Values may be sent and summed in bfloat16 or wider, within the bound.
No kernel may reach another device: no remote copies, remote signals or barrier semaphores. Data moves between devices by JAX's collectives and lax.ppermute only.
A program may use at most 128 MiB of HBM per device.

v0:
```python
import jax
import jax.numpy as jnp
from jax import lax
from jax.sharding import PartitionSpec as P

MODES = 8
SWEEPS = 3
CX = 4
CW = 512


def from_behind(block, axis, distance):
    devices = range(lax.axis_size(axis))
    route = [((i - distance) % len(devices), i) for i in devices]
    return lax.ppermute(block, axis, route)


def with_halo(cells, sides, width):
    for axis, dim in sides:
        count = lax.axis_size(axis)
        head = lax.slice_in_dim(cells, 0, width, axis=dim)
        tail = lax.slice_in_dim(cells, cells.shape[dim] - width, cells.shape[dim], axis=dim)
        cells = jnp.concatenate(
            [
                lax.ppermute(tail, axis, [(i, (i + 1) % count) for i in range(count)]),
                cells,
                lax.ppermute(head, axis, [((i + 1) % count, i) for i in range(count)]),
            ],
            axis=dim,
        )
    return cells


def normalize(basis):
    inner_gram = jnp.dot(basis.T, basis, precision=lax.Precision.HIGHEST)
    factor = jnp.linalg.cholesky(inner_gram)
    return lax.linalg.triangular_solve(factor, basis, left_side=False, lower=True, transpose_a=True)


def build_projector(gram):
    basis = gram[:, :MODES]
    for sweep in range(SWEEPS):
        basis = jnp.dot(gram, basis, precision=lax.Precision.HIGHEST)
        basis = normalize(basis)
    return (jnp.dot(basis, basis.T, precision=lax.Precision.HIGHEST), basis)


def local_gram(field_block, snaps):
    matrix = field_block.reshape(snaps, -1)
    return jnp.dot(matrix, matrix.T, precision=lax.Precision.HIGHEST)


def project_fields(projector, field_block, snaps):
    row_count, columns, width = field_block.shape
    matrix = field_block.reshape(snaps, -1)
    rebuilt = jnp.dot(projector, matrix, precision=lax.Precision.HIGHEST)
    return rebuilt.reshape(row_count, columns, width)


def on_device(atom_values, atom_cell, brick_column):
    snaps, fields, atom_count = atom_values.shape
    bricks = brick_column.shape[0]
    per_brick = atom_count // bricks
    row_count = snaps * fields
    values = atom_values.reshape(row_count, bricks, per_brick)
    cell_index = atom_cell.reshape(bricks, per_brick)
    onehot = (cell_index[:, :, None] == jnp.arange(CW, dtype=jnp.int32)[None, None, :]).astype(
        jnp.bfloat16
    )
    brick_sums = jnp.einsum("rba,bac->brc", values, onehot, preferred_element_type=jnp.float32)
    column_hot = (brick_column[:, None] == jnp.arange(CX + 2, dtype=jnp.int32)[None, :]).astype(
        jnp.float32
    )
    extended = jnp.einsum("brc,bk->rkc", brick_sums, column_hot, precision=lax.Precision.HIGHEST)
    from_above = from_behind(extended[:, 0, :], "gx", -1)
    from_below = from_behind(extended[:, CX + 1, :], "gx", 1)
    lead_column = extended[:, 1, :] + from_below
    tail_column = extended[:, CX, :] + from_above
    own_fields = jnp.concatenate(
        [lead_column[:, None, :], extended[:, 2:CX, :], tail_column[:, None, :]], axis=1
    )
    gram_part = local_gram(own_fields, snaps)
    summed = lax.psum(gram_part, ("gx", "gz"))
    projector, basis = build_projector(summed)
    rebuilt = project_fields(projector, own_fields, snaps).astype(jnp.bfloat16)
    rebuilt_ext = with_halo(rebuilt, (("gx", 1),), 1)
    flattened = rebuilt_ext.reshape(row_count, (CX + 2) * CW)
    atom_slot = jnp.repeat(brick_column, per_brick) * CW + atom_cell
    gathered = jnp.take(flattened, atom_slot, axis=1)
    return gathered.reshape(snaps, fields, atom_count)


def solution(mesh):
    in_specs = (P(None, None, ("gx", "gz")), P(("gx", "gz")), P(("gx", "gz")))
    out_specs = P(None, None, ("gx", "gz"))
    return jax.shard_map(
        on_device, mesh=mesh, in_specs=in_specs, out_specs=out_specs, check_vma=False
    )
```

profile of v0, /device:TPU:1, one launch (start us, length us, event | category | flops | bytes accessed | tf_op | source)
XLA Modules:
  0.0 474.5 jit_solution(992129393033600545)
XLA Ops:
  6.5 9.4 %reshape.40 = bf16[640,8,512]{2,1,0:T(8,128)(2,1)} reshape(bf16[160,4,4096]{2,1,0:T(4,128)(2,1)} %param.6) | data formatting | bytes 10485760 | tf_op jit(solution)/shard_map/reshape | solution.py:65
  15.9 12.4 %fusion.3 = f32[8,640,512]{1,2,0:T(8,128)} fusion(bf16[640,8,512]{2,1,0:T(8,128)(2,1)} %reshape.40, s32[8,512]{1,0:T(8,128)S(1)} %eq.31), kind=kOutput, calls=%fused_computation.10 | convolution fusion | flops 2686451712 | bytes 15745024 | tf_op jit(solution)/shard_map/rba,bac->brc/dot_general | solution.py:70
  28.4 11.5 %copy.29 = f32[8,640,512]{2,0,1:T(8,128)} copy(f32[8,640,512]{1,2,0:T(8,128)} %fusion.3) | data formatting | bytes 20971520 | tf_op jit(solution)/shard_map/rba,bac->brc/dot_general | solution.py:70
  39.8 8.5 %convolution_bitcast_fusion = f32[640,6,512]{2,1,0:T(8,128)S(1)} fusion(f32[8,640,512]{2,0,1:T(8,128)} %copy.29, s32[8]{0:T(128)S(1)} %copy-done.1), kind=kOutput, calls=%fused_computation.9 | convolution fusion | flops 188743728 | bytes 18350112 | tf_op jit(solution)/shard_map/brc,bk->rkc/dot_general | solution.py:74
  48.4 3.9 fusion.27
  52.4 2.5 collective-permute-start
  55.1 6.7 %collective-permute-start.1 = (f32[640,512]{1,0:T(8,128)S(1)}, f32[640,512]{1,0:T(8,128)}, u32[]{:S(2)}, u32[]{:S(2)}) collective-permute-start(f32[640,512]{1,0:T(8,128)S(1)} %bitcast.89), channel_id=1, source_target_pairs={{8,0},{16,8},{24,16},{32,24},{40,32},{48,40},{56,48},{64,56},{72,6... | collective-permute-start | bytes 3932168 | tf_op jit(solution)/shard_map/ppermute | solution.py:15
  61.8 1.4 slice.42
  63.1 26.6 %collective-permute-done = f32[640,512]{1,0:T(8,128)} collective-permute-done((f32[640,512]{1,0:T(8,128)S(1)}, f32[640,512]{1,0:T(8,128)}, u32[]{:S(2)}, u32[]{:S(2)}) %collective-permute-start) | collective-permute-done | bytes 1310752 | tf_op jit(solution)/shard_map/ppermute | solution.py:15
  89.7 1.6 fusion.8
  92.2 1.6 fusion.7
  93.8 1.3 copy.33
  95.2 4.8 %pad_maximum_fusion = f32[640,4,512]{2,1,0:T(4,128)} fusion(f32[640,1,512]{2,1,0:T(1,128)S(1)} %copy.33, f32[640,2,512]{2,1,0:T(2,128)S(1)} %slice.42, f32[640,1,512]{2,1,0:T(1,128)S(1)} %broadcast_in_dim.27), kind=kLoop, calls=%fused_computation.4 | loop fusion | flops 2621440 | bytes 10485760 | tf_op jit(solution)/shard_map/concatenate | solution.py:79
  100.0 7.7 %reshape.41 = f32[160,8192]{1,0:T(8,128)} reshape(f32[640,4,512]{2,1,0:T(4,128)} %pad_maximum_fusion) | data formatting | bytes 10485760 | tf_op jit(solution)/shard_map/reshape | solution.py:49
  107.7 9.0 %fusion.29 = f32[160,160]{1,0:T(8,128)} fusion(f32[160,8192]{1,0:T(8,128)} %reshape.41), kind=kOutput, calls=%fused_computation.58 | convolution fusion | flops 2516582400 | bytes 5345280 | tf_op jit(solution)/shard_map/dot_general | solution.py:50
  116.8 242.6 %all-reduce.2.cloned.1.call-done = f32[160,160]{1,0:T(8,128)} async-done(((f32[160,160]{1,0:T(8,128)}), f32[160,160]{1,0:T(8,128)}) %all-reduce.2.cloned.1.call-update) | async-done | bytes 102416 | tf_op jit(solution)/shard_map/psum | solution.py:83
  359.4 1.2 fusion.9
  363.8 1.1 fusion.31
  368.0 1.1 fusion.33
  372.7 8.8 %convolution_convert_fusion = bf16[160,8192]{1,0:T(8,128)(2,1)} fusion(f32[160,160]{1,0:T(8,128)S(1)} %fusion.35, f32[160,8192]{1,0:T(8,128)} %reshape.41), kind=kOutput, calls=%fused_computation.1 | convolution fusion | flops 2517893120 | bytes 7966720 | tf_op jit(solution)/shard_map/dot_general | solution.py:56
  381.5 4.5 convert_element_type.9
  386.0 1.8 fusion.28
  388.6 4.5 collective-permute-start.3
  393.3 14.1 %collective-permute-done.2 = bf16[640,1,512]{2,0,1:T(8,128)(2,1)S(1)} collective-permute-done((bf16[640,1,512]{2,0,1:T(8,128)(2,1)S(1)}, bf16[640,1,512]{2,0,1:T(8,128)(2,1)S(1)}, u32[]{:S(2)}, u32[]{:S(2)}) %collective-permute-start.2) | collective-permute-done | bytes 655392 | tf_op jit(solution)/shard_map/ppermute | solution.py:25
  407.3 1.0 copy.42
  408.4 1.0 copy.43
  409.4 5.6 %pad_maximum_fusion.1 = bf16[640,6,512]{2,1,0:T(8,128)(2,1)} fusion(bf16[640,1,512]{2,1,0:T(2,128)(2,1)S(1)} %copy.43, bf16[640,4,512]{2,1,0:T(4,128)(2,1)S(1)} %convert_element_type.9, bf16[640,1,512]{2,1,0:T(2,128)(2,1)S(1)} %copy.42), kind=kLoop, calls=%fused_computation.5 | loop fusion | flops 11796480 | bytes 7864320 | tf_op jit(solution)/shard_map/concatenate | solution.py:23
  415.0 8.1 %copy.44 = bf16[640,6,512]{0,2,1:T(8,128)(2,1)} copy(bf16[640,6,512]{2,1,0:T(8,128)(2,1)} %pad_maximum_fusion.1) | data formatting | bytes 7864320 | tf_op jit(solution)/shard_map/concatenate | solution.py:23
  423.1 20.6 %gather_fusion = bf16[4096,640]{1,0:T(8,128)(2,1)} fusion(bf16[640,3072]{0,1:T(8,128)(2,1)} %bitcast.87, s32[4096]{0:T(1024)S(1)} %broadcast_clamp_fusion), kind=kCustom, calls=%fused_computation | custom fusion | bytes 10502144 | tf_op jit(solution)/shard_map/jit(_take)/gather | solution.py:89
  443.7 8.0 %copy.45 = bf16[640,4096]{1,0:T(8,128)(2,1)} copy(bf16[640,4096]{0,1:T(8,128)(2,1)} %bitcast.88) | data formatting | bytes 10485760 | tf_op jit(solution)/shard_map/jit(_take)/gather | solution.py:89
  451.7 8.6 %gather.7 = bf16[160,4,4096]{2,1,0:T(4,128)(2,1)} reshape(bf16[640,4096]{1,0:T(8,128)(2,1)} %copy.45) | data formatting | bytes 10485760 | tf_op jit(solution)/shard_map/jit(_take)/gather | solution.py:89
  460.3 7.1 %broadcast_select_fusion = bf16[160,4,4096]{2,1,0:T(4,128)(2,1)} fusion(bf16[160,4,4096]{2,1,0:T(4,128)(2,1)} %gather.7, pred[4096]{0:T(1024)(128)(4,1)S(1)} %compare_and_fusion), kind=kLoop, calls=%fused_computation.7 | loop fusion | flops 2621440 | bytes 10489856 | tf_op jit(solution)/shard_map/jit(_take)/select_n | solution.py:89
  (48 shorter events, 11.8 us)
Async XLA Ops:
  6.5 9.4 %copy-start = (s32[4096]{0:T(1024)S(1)}, s32[4096]{0:T(1024)}, u32[]{:S(2)}) copy-start(s32[4096]{0:T(1024)} %param.7) | copy-start | bytes 49156
  6.5 352.9 %all-reduce.2.cloned.1.call-start = ((), (), s32[]{:S(2)}) async-start(), calls=%async_computation | async-start | bytes 327680 | tf_op jit(solution)/shard_map/psum | solution.py:83
  28.3 11.5 %copy-start.1 = (s32[8]{0:T(128)S(1)}, s32[8]{0:T(128)}, u32[]{:S(2)}) copy-start(s32[8]{0:T(128)} %param.8) | copy-start | bytes 100
  52.4 37.3 %collective-permute-start = (f32[640,512]{1,0:T(8,128)S(1)}, f32[640,512]{1,0:T(8,128)}, u32[]{:S(2)}, u32[]{:S(2)}) collective-permute-start(f32[640,512]{1,0:T(8,128)S(1)} %bitcast.90), channel_id=1, source_target_pairs={{248,0},{0,8},{8,16},{16,24},{24,32},{32,40},{40,48},{48,56},{56,6... | collective-permute-start | bytes 3932168 | tf_op jit(solution)/shard_map/ppermute | solution.py:15
  55.1 37.1 %collective-permute-start.1 = (f32[640,512]{1,0:T(8,128)S(1)}, f32[640,512]{1,0:T(8,128)}, u32[]{:S(2)}, u32[]{:S(2)}) collective-permute-start(f32[640,512]{1,0:T(8,128)S(1)} %bitcast.89), channel_id=1, source_target_pairs={{8,0},{16,8},{24,16},{32,24},{40,32},{48,40},{56,48},{64,56},{72,6... | collective-permute-start | bytes 3932168 | tf_op jit(solution)/shard_map/ppermute | solution.py:15
  388.0 19.3 %collective-permute-start.2 = (bf16[640,1,512]{2,0,1:T(8,128)(2,1)S(1)}, bf16[640,1,512]{2,0,1:T(8,128)(2,1)S(1)}, u32[]{:S(2)}, u32[]{:S(2)}) collective-permute-start(bf16[640,1,512]{2,0,1:T(8,128)(2,1)S(1)} %copy.50), channel_id=1, source_target_pairs={{0,8},{8,16},{16,24},{24,32},{32,40},{40,48},{48,56},{56,64},{64,7... | collective-permute-start | bytes 1966088 | tf_op jit(solution)/shard_map/ppermute | solution.py:25
  388.6 19.7 %collective-permute-start.3 = (bf16[640,1,512]{2,0,1:T(8,128)(2,1)S(1)}, bf16[640,1,512]{2,0,1:T(8,128)(2,1)S(1)}, u32[]{:S(2)}, u32[]{:S(2)}) collective-permute-start(bf16[640,1,512]{2,0,1:T(8,128)(2,1)S(1)} %copy.51), channel_id=1, source_target_pairs={{8,0},{16,8},{24,16},{32,24},{40,32},{48,40},{56,48},{64,56},{72,6... | collective-permute-start | bytes 1966088 | tf_op jit(solution)/shard_map/ppermute | solution.py:27
Sparse Core Ops, SparseCore 0:
  116.9 242.4 all-reduce.1
where the time goes:
time: 484 us; the launch traced here: 474 us
  waiting for transfers between devices  283 us (58%)
  local copies, waits for them, and re-layouts  90.7 us (19%)
  matrix products  43.7 us (9%)
  other arithmetic  28.8 us (6%)
  starting transfers between devices  14.2 us (3%)
  between operations  13.8 us (3%)
    psum x1, waiting for transfers between devices, on_device(): summed = lax.psum(gram_part, ('gx', 'gz'))  243 us
    gather x3, local copies, waits for them, and re-layouts, on_device(): gathered = jnp.take(flattened, atom_slot, axis=1)  37.2 us
    ppermute x2, waiting for transfers between devices, from_behind(): return lax.ppermute(block, axis, route)  26.6 us
    ppermute x1, waiting for transfers between devices, with_halo(): lax.ppermute(tail, axis, [(i, (i + 1) % count) for i in range(count)])  14.1 us
    dot_general x1, matrix products, on_device(): jnp.einsum('rba,bac->brc', values, onehot, preferred_element_type=jnp.flo...  12.4 us
    dot_general x1, local copies, waits for them, and re-layouts, on_device(): jnp.einsum('rba,bac->brc', values, onehot, preferred_element_type=jnp.flo...  11.5 us
  transfers between devices with their start and end apart: 5, of which 3 were waited for; matrix products, arithmetic and copies ran while one was open for 1% of the time, Pallas kernels for 0%

commit v1 on v0

v1 whole, which is shorter than its diff:
```python
import jax
import jax.numpy as jnp
from jax import lax
from jax.experimental import pallas as pl
from jax.experimental.pallas import tpu as pltpu
from jax.sharding import PartitionSpec as P

SNAPS = 160
FIELDS = 4
ROWS = SNAPS * FIELDS
MODES = 8
SWEEPS = 3
CX = 4
EXT = CX + 2
CW = 512
PER_BRICK = 512
BRICKS = 8
COEFS = MODES * FIELDS
SPLIT = 128
TAIL = SNAPS - SPLIT
LANES = CW // 128
F32 = jnp.float32
BF16 = jnp.bfloat16
NT = (((1,), (1,)), ((), ()))
TN = (((0,), (0,)), ((), ()))


def params(mib):
    return pltpu.CompilerParams(vmem_limit_bytes=mib * 1024 * 1024)


def dot_nt(a, b):
    return lax.dot_general(a, b, NT, preferred_element_type=F32)


def dot(a, b):
    return jnp.dot(a, b, preferred_element_type=F32)


def exact_dot(a, b):
    return jnp.dot(a, b, precision=lax.Precision.HIGHEST, preferred_element_type=F32)


def cell_hot(cell_ref, brick):
    cells = lax.broadcasted_iota(jnp.int32, (CW, PER_BRICK), 0)
    return (cells == cell_ref[pl.ds(brick, 1), :]).astype(F32).astype(BF16)


def brick_sums(values_ref, cell_ref, brick):
    values = values_ref[...].reshape(ROWS, PER_BRICK)
    return dot_nt(values, cell_hot(cell_ref, brick))


def halves(x):
    head = x.astype(BF16)
    return head, (x - head.astype(F32)).astype(BF16)


def add_lanes(total, sums):
    for t in range(LANES):
        total[t] += sums[:, t * 128 : (t + 1) * 128]


def one_field(total, field):
    rows = pl.ds(field, SNAPS, stride=FIELDS)
    return jnp.concatenate([total[t, rows, :] for t in range(LANES)], axis=1)


def face_brick(step):
    return jnp.where(step < 2, step, step + BRICKS - 4)


def faces_kernel(column_ref, values_ref, cell_ref, low_ref, high_ref, total):
    step = pl.program_id(0)
    brick = face_brick(step)
    column = column_ref[brick]

    @pl.when(step % 2 == 0)
    def _():
        total[...] = jnp.zeros_like(total)

    @pl.when((column == 0) | (column == EXT - 1))
    def _():
        add_lanes(total, brick_sums(values_ref, cell_ref, brick))

    def store(out_ref):
        for f in range(FIELDS):
            out_ref[f * SNAPS : (f + 1) * SNAPS, :] = one_field(total, f).astype(BF16)

    @pl.when(step == 1)
    def _():
        store(low_ref)

    @pl.when(step == 3)
    def _():
        store(high_ref)


def face_sums(values, cells, columns):
    shape = jax.ShapeDtypeStruct((ROWS, CW), BF16)
    whole = pl.BlockSpec((ROWS, CW), lambda i, c: (0, 0))
    return pl.pallas_call(
        faces_kernel,
        grid_spec=pltpu.PrefetchScalarGridSpec(
            num_scalar_prefetch=1,
            grid=(4,),
            in_specs=[
                pl.BlockSpec((SNAPS, FIELDS, PER_BRICK), lambda i, c: (0, 0, face_brick(i))),
                pl.BlockSpec((BRICKS, PER_BRICK), lambda i, c: (0, 0)),
            ],
            out_specs=[whole, whole],
            scratch_shapes=[pltpu.VMEM((LANES, ROWS, 128), F32)],
        ),
        out_shape=[shape, shape],
        compiler_params=params(32),
        name="faces",
    )(columns, values, cells)


def local_kernel(column_ref, values_ref, cell_ref, after_ref, head_ref, rest_ref, gram_ref, total):
    step = pl.program_id(0)

    @pl.when(step == 0)
    def _():
        total[...] = jnp.zeros_like(total)

    add_lanes(total.at[column_ref[step]], brick_sums(values_ref, cell_ref, step))

    @pl.when(step == BRICKS - 1)
    def _():
        same = jnp.zeros((SNAPS, SNAPS), F32)
        mixed = jnp.zeros((SNAPS, SNAPS), F32)
        for k in range(EXT):
            for f in range(FIELDS):
                head, rest = halves(one_field(total.at[k], f))
                head_ref[f * SNAPS : (f + 1) * SNAPS, k * CW : (k + 1) * CW] = head
                rest_ref[f * SNAPS : (f + 1) * SNAPS, k * CW : (k + 1) * CW] = rest
                same += dot_nt(head, head)
                mixed += dot_nt(head, rest)
        gram_ref[...] = same + mixed + mixed.T


def local_sums(values, cells, columns, after):
    half = jax.ShapeDtypeStruct((ROWS, EXT * CW), BF16)
    half_spec = pl.BlockSpec((ROWS, EXT * CW), lambda i, c: (0, 0))
    return pl.pallas_call(
        local_kernel,
        grid_spec=pltpu.PrefetchScalarGridSpec(
            num_scalar_prefetch=1,
            grid=(BRICKS,),
            in_specs=[
                pl.BlockSpec((SNAPS, FIELDS, PER_BRICK), lambda i, c: (0, 0, i)),
                pl.BlockSpec((BRICKS, PER_BRICK), lambda i, c: (0, 0)),
                pl.BlockSpec((16, 128), lambda i, c: (0, 0)),
            ],
            out_specs=[half_spec, half_spec, pl.BlockSpec((SNAPS, SNAPS), lambda i, c: (0, 0))],
            scratch_shapes=[pltpu.VMEM((EXT, LANES, ROWS, 128), F32)],
        ),
        out_shape=[half, half, jax.ShapeDtypeStruct((SNAPS, SNAPS), F32)],
        compiler_params=params(48),
        cost_estimate=pl.CostEstimate(flops=6_000_000_000, bytes_accessed=14_000_000, transcendentals=0),
        name="local",
    )(columns, values, cells, after)


def pack(gram):
    body = gram[:SPLIT, :SPLIT]
    side = gram[:SPLIT, SPLIT:]
    corner = gram[SPLIT:, SPLIT:]
    t = TAIL
    rows = [
        body[:t],
        jnp.concatenate([side[:t], body[t : 2 * t, t:]], axis=1),
        jnp.concatenate([side[t : 2 * t], side[2 * t : 3 * t], body[2 * t : 3 * t, 2 * t :]], axis=1),
        jnp.concatenate([side[3 * t :], corner, corner, body[3 * t :, 3 * t :]], axis=1),
    ]
    return jnp.concatenate(rows, axis=0)


def unpack(packed):
    t = TAIL
    row = lax.broadcasted_iota(jnp.int32, (SPLIT, SPLIT), 0) // t
    col = lax.broadcasted_iota(jnp.int32, (SPLIT, SPLIT), 1) // t
    above = jnp.where(col > row, packed, 0.0)
    body = jnp.where(col == row, packed, 0.0) + above + above.T
    side = jnp.concatenate(
        [packed[t : 2 * t, :t], packed[2 * t : 3 * t, :t], packed[2 * t : 3 * t, t : 2 * t], packed[3 * t :, :t]], axis=0
    )
    corner = packed[3 * t :, t : 2 * t]
    top = jnp.concatenate([body, side], axis=1)
    padded = jnp.concatenate([side, jnp.zeros((SPLIT, SPLIT - t), F32)], axis=1)
    bottom = jnp.concatenate([padded.T[:t], corner], axis=1)
    return jnp.concatenate([top, bottom], axis=0)


def cross_kernel(gram_ref, low_head, low_rest, high_head, high_rest, from_below, from_above, packed_ref):
    cross = jnp.zeros((SNAPS, SNAPS), F32)
    for f in range(FIELDS):
        rows = slice(f * SNAPS, (f + 1) * SNAPS)
        below, above = from_below[rows, :], from_above[rows, :]
        cross += dot_nt(low_head[rows, :], below) + dot_nt(low_rest[rows, :], below)
        cross += dot_nt(high_head[rows, :], above) + dot_nt(high_rest[rows, :], above)
    packed_ref[...] = pack(gram_ref[...] + cross + cross.T)


def packed_gram(gram, head, rest, from_below, from_above):
    first = pl.BlockSpec((ROWS, CW), lambda i: (0, 1))
    last = pl.BlockSpec((ROWS, CW), lambda i: (0, CX))
    face = pl.BlockSpec((ROWS, CW), lambda i: (0, 0))
    return pl.pallas_call(
        cross_kernel,
        grid=(1,),
        in_specs=[pl.BlockSpec((SNAPS, SNAPS), lambda i: (0, 0)), first, first, last, last, face, face],
        out_specs=pl.BlockSpec((SPLIT, SPLIT), lambda i: (0, 0)),
        out_shape=jax.ShapeDtypeStruct((SPLIT, SPLIT), F32),
        compiler_params=params(32),
        name="cross",
    )(gram, head, rest, head, rest, from_below, from_above)


def add_over_devices(x):
    def along(axis, pairs):
        return lambda y: lax.ppermute(y, axis, pairs)

    def y_pairs(move):
        return [(i, move(i // 2) * 2 + i % 2) for i in range(8)]

    def x_pairs(move):
        return [(i, move(i // 8) * 8 + i % 8) for i in range(32)]

    def z_pairs(move):
        return [(i, (i // 8) * 8 + move(i % 8)) for i in range(32)]

    x = x + along("gz", [(i, i ^ 1) for i in range(8)])(x)
    for axis, pairs in (("gz", y_pairs), ("gx", x_pairs)):
        x = x + along(axis, pairs(lambda i: i ^ 1))(x)
        x = x + along(axis, pairs(lambda i: 3 - i))(x)
    above = along("gx", z_pairs(lambda i: (i - 1) % 8))(x)
    below = along("gx", z_pairs(lambda i: (i + 1) % 8))(x)
    two = x + above
    three = two + below
    far_above = along("gx", z_pairs(lambda i: (i - 3) % 8))(three)
    far_below = along("gx", z_pairs(lambda i: (i + 3) % 8))(two)
    return three + far_above + far_below


def orthonormal(basis):
    inner = lax.dot_general(basis, basis, NT, precision=lax.Precision.HIGHEST, preferred_element_type=F32)
    row = lax.broadcasted_iota(jnp.int32, (MODES, 1), 0)
    square = lax.broadcasted_iota(jnp.int32, (MODES, MODES), 0) == lax.broadcasted_iota(jnp.int32, (MODES, MODES), 1)
    for j in range(MODES - 1):
        factor = jnp.where(row > j, inner[:, j : j + 1] / inner[j : j + 1, j : j + 1], 0.0)
        inner = inner - factor * inner[j : j + 1, :]
        basis = basis - factor * basis[j : j + 1, :]
    pivots = jnp.sum(jnp.where(square, inner, 0.0), axis=1, keepdims=True)
    return basis * lax.rsqrt(pivots)


def coefs_kernel(packed_ref, head_ref, rest_ref, basis_ref, own_ref, down_ref, up_ref):
    gram = unpack(packed_ref[...])
    basis = gram[:MODES, :]
    for _ in range(SWEEPS):
        basis = orthonormal(exact_dot(basis, gram))
    basis_ref[...] = basis
    wide = jnp.concatenate([basis] * FIELDS, axis=1)
    tall = jnp.concatenate([wide] * FIELDS, axis=0)
    row_field = lax.broadcasted_iota(jnp.int32, (COEFS, ROWS), 0) // MODES
    col_field = lax.broadcasted_iota(jnp.int32, (COEFS, ROWS), 1) // SNAPS
    head, rest = halves(jnp.where(row_field == col_field, tall, 0.0))
    both = jnp.concatenate([head, rest], axis=0)
    for k in range(EXT):
        columns = slice(k * CW, (k + 1) * CW)
        pair = dot(both, head_ref[:, columns])
        own_ref[:, columns] = pair[:COEFS] + pair[COEFS:] + dot(head, rest_ref[:, columns])
    down_ref[...] = own_ref[:, : 2 * CW]
    up_ref[...] = own_ref[:, CX * CW :]


def coefficients(packed, head, rest):
    side = jax.ShapeDtypeStruct((COEFS, 2 * CW), F32)
    return pl.pallas_call(
        coefs_kernel,
        out_shape=[
            jax.ShapeDtypeStruct((MODES, SNAPS), F32),
            jax.ShapeDtypeStruct((COEFS, EXT * CW), F32),
            side,
            side,
        ],
        compiler_params=params(48),
        name="coefs",
    )(packed, head, rest)


def spread_kernel(basis_ref, spread_ref):
    head, rest = halves(basis_ref[...])
    snap = lax.broadcasted_iota(jnp.int32, (SNAPS, ROWS), 0)
    column = lax.broadcasted_iota(jnp.int32, (SNAPS, ROWS), 1)
    repeat = (snap == column // FIELDS).astype(F32).astype(BF16)
    both = dot(jnp.concatenate([head, rest], axis=0), repeat)
    field = lax.broadcasted_iota(jnp.int32, (COEFS, ROWS), 0) // MODES
    mine = field == lax.broadcasted_iota(jnp.int32, (COEFS, ROWS), 1) % FIELDS
    head = jnp.where(mine, jnp.concatenate([both[:MODES]] * FIELDS, axis=0), 0.0)
    rest = jnp.where(mine, jnp.concatenate([both[MODES:]] * FIELDS, axis=0), 0.0)
    stacked = jnp.concatenate([head, head, rest, jnp.zeros_like(rest)], axis=0)
    spread_ref[...] = stacked.T.astype(BF16)


def spread_matrix(basis):
    return pl.pallas_call(
        spread_kernel,
        out_shape=jax.ShapeDtypeStruct((ROWS, 4 * COEFS), BF16),
        name="spread",
    )(basis)


def atoms_kernel(column_ref, own_ref, below_ref, above_ref, spread_ref, cell_ref, out_ref, whole):
    step = pl.program_id(0)

    @pl.when(step == 0)
    def _():
        for k in range(EXT):
            value = own_ref[:, k * CW : (k + 1) * CW]
            if k < 2:
                value = value + below_ref[:, k * CW : (k + 1) * CW]
            if k >= CX:
                value = value + above_ref[:, (k - CX) * CW : (k - CX + 1) * CW]
            head, rest = halves(value)
            whole[k] = jnp.concatenate([head, rest], axis=0)

    picked = dot(whole[column_ref[step]], cell_hot(cell_ref, step)).astype(BF16)
    stacked = jnp.concatenate([picked, picked[:COEFS], jnp.zeros((COEFS, PER_BRICK), BF16)], axis=0)
    out_ref[...] = dot(spread_ref[...], stacked).astype(BF16).reshape(SNAPS, FIELDS, PER_BRICK)


def atom_fields(columns, own, below, above, spread, cells):
    side = pl.BlockSpec((COEFS, 2 * CW), lambda i, c: (0, 0))
    return pl.pallas_call(
        atoms_kernel,
        grid_spec=pltpu.PrefetchScalarGridSpec(
            num_scalar_prefetch=1,
            grid=(BRICKS,),
            in_specs=[
                pl.BlockSpec((COEFS, EXT * CW), lambda i, c: (0, 0)),
                side,
                side,
                pl.BlockSpec((ROWS, 4 * COEFS), lambda i, c: (0, 0)),
                pl.BlockSpec((BRICKS, PER_BRICK), lambda i, c: (0, 0)),
            ],
            out_specs=pl.BlockSpec((SNAPS, FIELDS, PER_BRICK), lambda i, c: (0, 0, i)),
            scratch_shapes=[pltpu.VMEM((EXT, 2 * COEFS, CW), BF16)],
        ),
        out_shape=jax.ShapeDtypeStruct((SNAPS, FIELDS, BRICKS * PER_BRICK), BF16),
        compiler_params=params(32),
        name="atoms",
    )(columns, own, below, above, spread, cells)


def on_device(atom_values, atom_cell, brick_column):
    cells = atom_cell.reshape(BRICKS, PER_BRICK)
    count = lax.axis_size("gx")
    to_lower = [((i + 1) % count, i) for i in range(count)]
    to_upper = [(i, (i + 1) % count) for i in range(count)]
    low, high = face_sums(atom_values, cells, brick_column)
    from_above = lax.ppermute(low, "gx", to_lower)
    from_below = lax.ppermute(high, "gx", to_upper)
    head, rest, gram = local_sums(atom_values, cells, brick_column, low)
    packed = add_over_devices(packed_gram(gram, head, rest, from_below, from_above))
    basis, own, down, up = coefficients(packed, head, rest)
    above = lax.ppermute(down, "gx", to_lower)
    below = lax.ppermute(up, "gx", to_upper)
    spread = spread_matrix(basis)
    return atom_fields(brick_column, own, below, above, spread, cells)


def solution(mesh):
    in_specs = (P(None, None, ("gx", "gz")), P(("gx", "gz")), P(("gx", "gz")))
    out_specs = P(None, None, ("gx", "gz"))
    return jax.shard_map(on_device, mesh=mesh, in_specs=in_specs, out_specs=out_specs, check_vma=False)
```

time: 484 us -> 94.1 us (0.19)
  the two profiles are of different devices: /device:TPU:1 before, /device:TPU:24 now
where the time goes in v1:
time: 94.1 us; the launch traced here: 93.5 us
  Pallas kernels  31.4 us (33%)
  waiting for transfers between devices  29.1 us (31%)
  starting transfers between devices  25.4 us (27%)
  local copies, waits for them, and re-layouts  7.52 us (8%)
    ppermute x9, waiting for transfers between devices, along(): return lambda y: lax.ppermute(y, axis, pairs)  25.7 us
    pallas_call x1, Pallas kernels, local_sums(): pl.pallas_call(local_kernel, grid_spec=pltpu.PrefetchScalarGridSpec(num_s...  12.6 us
    ppermute x9, starting transfers between devices, along(): return lambda y: lax.ppermute(y, axis, pairs)  11.8 us
    unnamed x12, local copies, waits for them, and re-layouts  6.79 us
    ppermute x1, starting transfers between devices, on_device(): from_above = lax.ppermute(low, 'gx', to_lower)  6.75 us
    pallas_call x1, Pallas kernels, atom_fields(): pl.pallas_call(atoms_kernel, grid_spec=pltpu.PrefetchScalarGridSpec(num_s...  6.58 us
    pallas_call x1, Pallas kernels, coefficients(): pl.pallas_call(coefs_kernel, out_shape=[jax.ShapeDtypeStruct((MODES, SNAP...  6.5 us
    ppermute x1, starting transfers between devices, on_device(): above = lax.ppermute(down, 'gx', to_lower)  4.8 us
  transfers between devices with their start and end apart: 13, of which 10 were waited for; matrix products, arithmetic and copies ran while one was open for 0% of the time, Pallas kernels for 15%

profile of v1, /device:TPU:24, one launch (start us, length us, event | category | flops | bytes accessed | tf_op | source)
XLA Modules:
  0.0 93.5 jit_solution(11700044964044176478)
XLA Ops:
  0.0 0.7 reshape.3.cell_ref
  0.7 2.5 %copy-done.1 = bf16[160,4,4096]{2,1,0:T(4,128)(2,1)S(1)} copy-done((bf16[160,4,4096]{2,1,0:T(4,128)(2,1)S(1)}, bf16[160,4,4096]{2,1,0:T(4,128)(2,1)}, u32[]{:S(2)}) %copy-start.1) | copy-done | bytes 5242904
  3.2 0.7 copy-done.4
  3.9 3.1 %faces.1 = (bf16[640,512]{1,0:T(8,128)(2,1)S(1)}, bf16[640,512]{1,0:T(8,128)(2,1)S(1)}) custom-call(s32[8]{0:T(128)S(1)} %copy-done.4, bf16[160,4,4096]{2,1,0:T(4,128)(2,1)S(1)} %copy-done.1, s32[8,512]{1,0:T(8,128)S(1)} %reshape.3.cell_ref), custom_call_target="tpu_custom_call" | custom-call | tf_op jit(solution)/shard_map/faces/pallas_call | solution.py:102
  7.0 1.5 %collective-permute-start = (bf16[640,512]{1,0:T(8,128)(2,1)S(1)}, bf16[640,512]{1,0:T(8,128)(2,1)S(1)}, u32[]{:S(2)}, u32[]{:S(2)}) collective-permute-start(bf16[640,512]{1,0:T(8,128)(2,1)S(1)} %get-tuple-element.18), channel_id=1, source_target_pairs={{0,8},{8,16},{16,24},{24,32},{32,40},{40,48},{48,56},{56,64},{64,7... | collective-permute-start | bytes 1966088 | tf_op jit(solution)/shard_map/ppermute | solution.py:365
  8.4 6.7 %collective-permute-start.1 = (bf16[640,512]{1,0:T(8,128)(2,1)S(1)}, bf16[640,512]{1,0:T(8,128)(2,1)S(1)}, u32[]{:S(2)}, u32[]{:S(2)}) collective-permute-start(bf16[640,512]{1,0:T(8,128)(2,1)S(1)} %get-tuple-element.14.after_ref), channel_id=1, source_target_pairs={{8,0},{16,8},{24,16},{32,24},{40,32},{48,40},{56,48},{64,56},{72,6... | collective-permute-start | bytes 1966088 | tf_op jit(solution)/shard_map/ppermute | solution.py:364
  15.2 12.6 %local.1 = (bf16[640,3072]{1,0:T(8,128)(2,1)S(1)}, bf16[640,3072]{1,0:T(8,128)(2,1)}, f32[160,160]{1,0:T(8,128)S(1)}) custom-call(s32[8]{0:T(128)S(1)} %copy-done.5, bf16[160,4,4096]{2,1,0:T(4,128)(2,1)} %values_ref.3, s32[8,512]{1,0:T(8,128)S(1)} %reshape.3.cell_ref, bf16[640,512]{1,0:T(8,128)(2,1)S(1)} %get-tuple-element.14.after_ref), custom_call_target="tpu_custom_call" | custom-call | flops 6000000000 | bytes 14000000 | tf_op jit(solution)/shard_map/local/pallas_call | solution.py:146
  27.8 2.1 %collective-permute-done.from_below = bf16[640,512]{1,0:T(8,128)(2,1)S(1)} collective-permute-done((bf16[640,512]{1,0:T(8,128)(2,1)S(1)}, bf16[640,512]{1,0:T(8,128)(2,1)S(1)}, u32[]{:S(2)}, u32[]{:S(2)}) %collective-permute-start) | collective-permute-done | bytes 655392 | tf_op jit(solution)/shard_map/ppermute | solution.py:365
  29.8 2.1 %copy-done = bf16[640,3072]{1,0:T(8,128)(2,1)S(1)} copy-done((bf16[640,3072]{1,0:T(8,128)(2,1)S(1)}, bf16[640,3072]{1,0:T(8,128)(2,1)}, u32[]{:S(2)}) %copy-start) | copy-done | bytes 3932184
  31.9 1.0 %cross.1 = f32[128,128]{1,0:T(8,128)S(1)} custom-call(f32[160,160]{1,0:T(8,128)S(1)} %get-tuple-element.15.gram_ref, bf16[640,3072]{1,0:T(8,128)(2,1)S(1)} %get-tuple-element.16.low_head.high_head.head_ref, bf16[640,3072]{1,0:T(8,128)(2,1)S(1)} %copy-done, bf16[640,3072]{1,0:T(8,128)(2,1)S(1)} %get-tuple-element.16.low_head.high_head.head_ref, ...), custom_call_target="tpu_custom_call" | custom-call | tf_op jit(solution)/shard_map/cross/pallas_call | solution.py:210
  33.1 1.2 %collective-permute-done.2 = f32[128,128]{1,0:T(8,128)S(1)} collective-permute-done((f32[128,128]{1,0:T(8,128)S(1)}, f32[128,128]{1,0:T(8,128)S(1)}, u32[]{:S(2)}, u32[]{:S(2)}) %collective-permute-start.2) | collective-permute-done | bytes 65568 | tf_op jit(solution)/shard_map/ppermute | solution.py:223
  34.3 1.4 %collective-permute-start.3 = (f32[128,128]{1,0:T(8,128)S(1)}, f32[128,128]{1,0:T(8,128)S(1)}, u32[]{:S(2)}, u32[]{:S(2)}) collective-permute-start(f32[128,128]{1,0:T(8,128)S(1)} %add.27), channel_id=1, source_target_pairs={{0,2},{1,3},{2,0},{3,1},{4,6},{5,7},{6,4},{7,5},{8,10},{9,11},{10,... | collective-permute-start | bytes 196616 | tf_op jit(solution)/shard_map/ppermute | solution.py:223
  35.7 3.0 %collective-permute-done.3 = f32[128,128]{1,0:T(8,128)S(1)} collective-permute-done((f32[128,128]{1,0:T(8,128)S(1)}, f32[128,128]{1,0:T(8,128)S(1)}, u32[]{:S(2)}, u32[]{:S(2)}) %collective-permute-start.3) | collective-permute-done | bytes 65568 | tf_op jit(solution)/shard_map/ppermute | solution.py:223
  38.7 0.8 collective-permute-start.4
  39.5 4.7 %collective-permute-done.4 = f32[128,128]{1,0:T(8,128)S(1)} collective-permute-done((f32[128,128]{1,0:T(8,128)S(1)}, f32[128,128]{1,0:T(8,128)S(1)}, u32[]{:S(2)}, u32[]{:S(2)}) %collective-permute-start.4) | collective-permute-done | bytes 65568 | tf_op jit(solution)/shard_map/ppermute | solution.py:223
  44.4 4.3 %collective-permute-done.5 = f32[128,128]{1,0:T(8,128)S(1)} collective-permute-done((f32[128,128]{1,0:T(8,128)S(1)}, f32[128,128]{1,0:T(8,128)S(1)}, u32[]{:S(2)}, u32[]{:S(2)}) %collective-permute-start.5) | collective-permute-done | bytes 65568 | tf_op jit(solution)/shard_map/ppermute | solution.py:223
  48.6 1.0 %collective-permute-start.6 = (f32[128,128]{1,0:T(8,128)S(1)}, f32[128,128]{1,0:T(8,128)S(1)}, u32[]{:S(2)}, u32[]{:S(2)}) collective-permute-start(f32[128,128]{1,0:T(8,128)S(1)} %add.30), channel_id=1, source_target_pairs={{0,192},{8,200},{16,208},{24,216},{32,224},{40,232},{48,240},{56,2... | collective-permute-start | bytes 196616 | tf_op jit(solution)/shard_map/ppermute | solution.py:223
  49.6 4.6 %collective-permute-done.6 = f32[128,128]{1,0:T(8,128)S(1)} collective-permute-done((f32[128,128]{1,0:T(8,128)S(1)}, f32[128,128]{1,0:T(8,128)S(1)}, u32[]{:S(2)}, u32[]{:S(2)}) %collective-permute-start.6) | collective-permute-done | bytes 65568 | tf_op jit(solution)/shard_map/ppermute | solution.py:223
  54.3 3.2 %collective-permute-start.7 = (f32[128,128]{1,0:T(8,128)S(1)}, f32[128,128]{1,0:T(8,128)S(1)}, u32[]{:S(2)}, u32[]{:S(2)}) collective-permute-start(f32[128,128]{1,0:T(8,128)S(1)} %add.31), channel_id=1, source_target_pairs={{0,56},{8,0},{16,8},{24,16},{32,24},{40,32},{48,40},{56,48},{64,12... | collective-permute-start | bytes 196616 | tf_op jit(solution)/shard_map/ppermute | solution.py:223
  57.5 4.1 %collective-permute-done.8 = f32[128,128]{1,0:T(8,128)S(1)} collective-permute-done((f32[128,128]{1,0:T(8,128)S(1)}, f32[128,128]{1,0:T(8,128)S(1)}, u32[]{:S(2)}, u32[]{:S(2)}) %collective-permute-start.8) | collective-permute-done | bytes 65568 | tf_op jit(solution)/shard_map/ppermute | solution.py:223
  61.7 1.5 %collective-permute-start.10 = (f32[128,128]{1,0:T(8,128)S(1)}, f32[128,128]{1,0:T(8,128)S(1)}, u32[]{:S(2)}, u32[]{:S(2)}) collective-permute-start(f32[128,128]{1,0:T(8,128)S(1)} %get-tuple-element.24), channel_id=1, source_target_pairs={{0,24},{8,32},{16,40},{24,48},{32,56},{40,0},{48,8},{56,16},{64,88... | collective-permute-start | bytes 196616 | tf_op jit(solution)/shard_map/ppermute | solution.py:223
  63.1 3.6 %collective-permute-start.9 = (f32[128,128]{1,0:T(8,128)S(1)}, f32[128,128]{1,0:T(8,128)S(1)}, u32[]{:S(2)}, u32[]{:S(2)}) collective-permute-start(f32[128,128]{1,0:T(8,128)S(1)} %get-tuple-element.23), channel_id=1, source_target_pairs={{0,40},{8,48},{16,56},{24,0},{32,8},{40,16},{48,24},{56,32},{64,10... | collective-permute-start | bytes 196616 | tf_op jit(solution)/shard_map/ppermute | solution.py:223
  66.8 3.5 %collective-permute-done.10 = f32[128,128]{1,0:T(8,128)S(1)} collective-permute-done((f32[128,128]{1,0:T(8,128)S(1)}, f32[128,128]{1,0:T(8,128)S(1)}, u32[]{:S(2)}, u32[]{:S(2)}) %collective-permute-start.10) | collective-permute-done | bytes 65568 | tf_op jit(solution)/shard_map/ppermute | solution.py:223
  70.3 0.3 collective-permute-done.9
  70.6 6.5 %coefs.1 = (f32[8,160]{1,0:T(8,128)S(1)}, f32[32,3072]{1,0:T(8,128)S(1)}, f32[32,1024]{1,0:T(8,128)S(1)}, f32[32,1024]{1,0:T(8,128)S(1)}) custom-call(f32[128,128]{1,0:T(8,128)S(1)} %add_add_fusion.packed_ref, bf16[640,3072]{1,0:T(8,128)(2,1)S(1)} %get-tuple-element.16.low_head.high_head.head_ref, bf16[640,3072]{1,0:T(8,128)(2,1)} %get-tuple-element.17.low_rest.high_rest.rest_ref), custom_call_target="tpu_custom_call" | custom-call | tf_op jit(solution)/shard_map/coefs/pallas_call | solution.py:281
  77.1 0.6 copy-done.3
  77.7 0.6 collective-permute-start.11
  78.3 4.8 %collective-permute-start.12 = (f32[32,1024]{1,0:T(8,128)S(1)}, f32[32,1024]{1,0:T(8,128)S(1)}, u32[]{:S(2)}, u32[]{:S(2)}) collective-permute-start(f32[32,1024]{1,0:T(8,128)S(1)} %get-tuple-element.21), channel_id=1, source_target_pairs={{8,0},{16,8},{24,16},{32,24},{40,32},{48,40},{56,48},{64,56},{72,6... | collective-permute-start | bytes 393224 | tf_op jit(solution)/shard_map/ppermute | solution.py:369
  83.1 1.6 %spread.1.spread_ref = bf16[640,128]{1,0:T(8,128)(2,1)} custom-call(f32[8,160]{1,0:T(8,128)} %copy-done.3), custom_call_target="tpu_custom_call" | custom-call | tf_op jit(solution)/shard_map/spread/pallas_call | solution.py:309
  84.7 1.3 %collective-permute-done.11.below_ref = f32[32,1024]{1,0:T(8,128)S(1)} collective-permute-done((f32[32,1024]{1,0:T(8,128)S(1)}, f32[32,1024]{1,0:T(8,128)S(1)}, u32[]{:S(2)}, u32[]{:S(2)}) %collective-permute-start.11) | collective-permute-done | bytes 131104 | tf_op jit(solution)/shard_map/ppermute | solution.py:370
  86.0 0.9 copy-done.2
  86.9 6.6 %atoms.1 = bf16[160,4,4096]{2,1,0:T(4,128)(2,1)} custom-call(s32[8]{0:T(128)S(1)} %copy-done.5, f32[32,3072]{1,0:T(8,128)S(1)} %get-tuple-element.19.own_ref, f32[32,1024]{1,0:T(8,128)S(1)} %collective-permute-done.11.below_ref, f32[32,1024]{1,0:T(8,128)S(1)} %collective-permute-done.12.above_ref, bf16[640,128]{1,0:T(8,128)(2,1)S(1)} %copy-done.2, ...), custom_call_target="tpu_custom_call" | custom-call | tf_op jit(solution)/shard_map/atoms/pallas_call | solution.py:337
  (20 shorter events, 0.4 us)
Async XLA Ops:
  0.0 15.2 %copy-start.5 = (s32[8]{0:T(128)S(1)}, s32[8]{0:T(128)}, u32[]{:S(2)}) copy-start(s32[8]{0:T(128)} %column_ref.5) | copy-start | bytes 100
  0.7 2.5 %copy-start.1 = (bf16[160,4,4096]{2,1,0:T(4,128)(2,1)S(1)}, bf16[160,4,4096]{2,1,0:T(4,128)(2,1)}, u32[]{:S(2)}) copy-start(bf16[160,4,4096]{2,1,0:T(4,128)(2,1)} %values_ref.3) | copy-start | bytes 15728644
  3.2 0.7 copy-start.4
  7.0 22.9 %collective-permute-start = (bf16[640,512]{1,0:T(8,128)(2,1)S(1)}, bf16[640,512]{1,0:T(8,128)(2,1)S(1)}, u32[]{:S(2)}, u32[]{:S(2)}) collective-permute-start(bf16[640,512]{1,0:T(8,128)(2,1)S(1)} %get-tuple-element.18), channel_id=1, source_target_pairs={{0,8},{8,16},{16,24},{24,32},{32,40},{40,48},{48,56},{56,64},{64,7... | collective-permute-start | bytes 1966088 | tf_op jit(solution)/shard_map/ppermute | solution.py:365
  8.4 21.4 %collective-permute-start.1 = (bf16[640,512]{1,0:T(8,128)(2,1)S(1)}, bf16[640,512]{1,0:T(8,128)(2,1)S(1)}, u32[]{:S(2)}, u32[]{:S(2)}) collective-permute-start(bf16[640,512]{1,0:T(8,128)(2,1)S(1)} %get-tuple-element.14.after_ref), channel_id=1, source_target_pairs={{8,0},{16,8},{24,16},{32,24},{40,32},{48,40},{56,48},{64,56},{72,6... | collective-permute-start | bytes 1966088 | tf_op jit(solution)/shard_map/ppermute | solution.py:364
  29.8 2.1 %copy-start = (bf16[640,3072]{1,0:T(8,128)(2,1)S(1)}, bf16[640,3072]{1,0:T(8,128)(2,1)}, u32[]{:S(2)}) copy-start(bf16[640,3072]{1,0:T(8,128)(2,1)} %get-tuple-element.17.low_rest.high_rest.rest_ref) | copy-start | bytes 11796484
  33.0 1.3 %collective-permute-start.2 = (f32[128,128]{1,0:T(8,128)S(1)}, f32[128,128]{1,0:T(8,128)S(1)}, u32[]{:S(2)}, u32[]{:S(2)}) collective-permute-start(f32[128,128]{1,0:T(8,128)S(1)} %cross.1), channel_id=1, source_target_pairs={{0,1},{1,0},{2,3},{3,2},{4,5},{5,4},{6,7},{7,6},{8,9},{9,8},{10,11... | collective-permute-start | bytes 196616 | tf_op jit(solution)/shard_map/ppermute | solution.py:223
  34.3 4.4 %collective-permute-start.3 = (f32[128,128]{1,0:T(8,128)S(1)}, f32[128,128]{1,0:T(8,128)S(1)}, u32[]{:S(2)}, u32[]{:S(2)}) collective-permute-start(f32[128,128]{1,0:T(8,128)S(1)} %add.27), channel_id=1, source_target_pairs={{0,2},{1,3},{2,0},{3,1},{4,6},{5,7},{6,4},{7,5},{8,10},{9,11},{10,... | collective-permute-start | bytes 196616 | tf_op jit(solution)/shard_map/ppermute | solution.py:223
  38.7 5.6 %collective-permute-start.4 = (f32[128,128]{1,0:T(8,128)S(1)}, f32[128,128]{1,0:T(8,128)S(1)}, u32[]{:S(2)}, u32[]{:S(2)}) collective-permute-start(f32[128,128]{1,0:T(8,128)S(1)} %add.28), channel_id=1, source_target_pairs={{0,6},{1,7},{2,4},{3,5},{4,2},{5,3},{6,0},{7,1},{8,14},{9,15},{10,... | collective-permute-start | bytes 196616 | tf_op jit(solution)/shard_map/ppermute | solution.py:223
  44.3 4.4 %collective-permute-start.5 = (f32[128,128]{1,0:T(8,128)S(1)}, f32[128,128]{1,0:T(8,128)S(1)}, u32[]{:S(2)}, u32[]{:S(2)}) collective-permute-start(f32[128,128]{1,0:T(8,128)S(1)} %add.29), channel_id=1, source_target_pairs={{0,64},{8,72},{16,80},{24,88},{32,96},{40,104},{48,112},{56,120},{... | collective-permute-start | bytes 196616 | tf_op jit(solution)/shard_map/ppermute | solution.py:223
  48.6 5.6 %collective-permute-start.6 = (f32[128,128]{1,0:T(8,128)S(1)}, f32[128,128]{1,0:T(8,128)S(1)}, u32[]{:S(2)}, u32[]{:S(2)}) collective-permute-start(f32[128,128]{1,0:T(8,128)S(1)} %add.30), channel_id=1, source_target_pairs={{0,192},{8,200},{16,208},{24,216},{32,224},{40,232},{48,240},{56,2... | collective-permute-start | bytes 196616 | tf_op jit(solution)/shard_map/ppermute | solution.py:223
  54.2 7.4 %collective-permute-start.8 = (f32[128,128]{1,0:T(8,128)S(1)}, f32[128,128]{1,0:T(8,128)S(1)}, u32[]{:S(2)}, u32[]{:S(2)}) collective-permute-start(f32[128,128]{1,0:T(8,128)S(1)} %add.31), channel_id=1, source_target_pairs={{0,8},{8,16},{16,24},{24,32},{32,40},{40,48},{48,56},{56,0},{64,72... | collective-permute-start | bytes 196616 | tf_op jit(solution)/shard_map/ppermute | solution.py:223
  54.3 7.3 %collective-permute-start.7 = (f32[128,128]{1,0:T(8,128)S(1)}, f32[128,128]{1,0:T(8,128)S(1)}, u32[]{:S(2)}, u32[]{:S(2)}) collective-permute-start(f32[128,128]{1,0:T(8,128)S(1)} %add.31), channel_id=1, source_target_pairs={{0,56},{8,0},{16,8},{24,16},{32,24},{40,32},{48,40},{56,48},{64,12... | collective-permute-start | bytes 196616 | tf_op jit(solution)/shard_map/ppermute | solution.py:223
  61.7 8.6 %collective-permute-start.10 = (f32[128,128]{1,0:T(8,128)S(1)}, f32[128,128]{1,0:T(8,128)S(1)}, u32[]{:S(2)}, u32[]{:S(2)}) collective-permute-start(f32[128,128]{1,0:T(8,128)S(1)} %get-tuple-element.24), channel_id=1, source_target_pairs={{0,24},{8,32},{16,40},{24,48},{32,56},{40,0},{48,8},{56,16},{64,88... | collective-permute-start | bytes 196616 | tf_op jit(solution)/shard_map/ppermute | solution.py:223
  63.1 7.5 %collective-permute-start.9 = (f32[128,128]{1,0:T(8,128)S(1)}, f32[128,128]{1,0:T(8,128)S(1)}, u32[]{:S(2)}, u32[]{:S(2)}) collective-permute-start(f32[128,128]{1,0:T(8,128)S(1)} %get-tuple-element.23), channel_id=1, source_target_pairs={{0,40},{8,48},{16,56},{24,0},{32,8},{40,16},{48,24},{56,32},{64,10... | collective-permute-start | bytes 196616 | tf_op jit(solution)/shard_map/ppermute | solution.py:223
  77.1 0.6 copy-start.3
  77.7 8.3 %collective-permute-start.11 = (f32[32,1024]{1,0:T(8,128)S(1)}, f32[32,1024]{1,0:T(8,128)S(1)}, u32[]{:S(2)}, u32[]{:S(2)}) collective-permute-start(f32[32,1024]{1,0:T(8,128)S(1)} %get-tuple-element.20), channel_id=1, source_target_pairs={{0,8},{8,16},{16,24},{24,32},{32,40},{40,48},{48,56},{56,64},{64,7... | collective-permute-start | bytes 393224 | tf_op jit(solution)/shard_map/ppermute | solution.py:370
  78.3 7.7 %collective-permute-start.12 = (f32[32,1024]{1,0:T(8,128)S(1)}, f32[32,1024]{1,0:T(8,128)S(1)}, u32[]{:S(2)}, u32[]{:S(2)}) collective-permute-start(f32[32,1024]{1,0:T(8,128)S(1)} %get-tuple-element.21), channel_id=1, source_target_pairs={{8,0},{16,8},{24,16},{32,24},{40,32},{48,40},{56,48},{64,56},{72,6... | collective-permute-start | bytes 393224 | tf_op jit(solution)/shard_map/ppermute | solution.py:369
  86.0 0.9 copy-start.2

commit v2 on v1

v2 whole, which is shorter than its diff:
```python
import jax
import jax.numpy as jnp
from jax import lax
from jax.experimental import pallas as pl
from jax.experimental.pallas import tpu as pltpu
from jax.sharding import PartitionSpec as P

SNAPS = 160
FIELDS = 4
ROWS = SNAPS * FIELDS
MODES = 8
SWEEPS = 3
CX = 4
EXT = CX + 2
CW = 512
PER_BRICK = 512
BRICKS = 8
COEFS = MODES * FIELDS
SPLIT = 128
TAIL = SNAPS - SPLIT
LANES = CW // 128
F32 = jnp.float32
BF16 = jnp.bfloat16
NT = (((1,), (1,)), ((), ()))
TN = (((0,), (0,)), ((), ()))


def params(mib):
    return pltpu.CompilerParams(vmem_limit_bytes=mib * 1024 * 1024)


def dot_nt(a, b):
    return lax.dot_general(a, b, NT, preferred_element_type=F32)


def dot(a, b):
    return jnp.dot(a, b, preferred_element_type=F32)


def exact_dot(a, b):
    return jnp.dot(a, b, precision=lax.Precision.HIGHEST, preferred_element_type=F32)


def cell_hot(cells, brick, keep=None):
    ids = lax.broadcasted_iota(jnp.int32, (CW, 128), 0)
    tiles = []
    for t in range(LANES):
        row = cells[brick * LANES + t : brick * LANES + t + 1, :]
        if keep is not None:
            row = jnp.where(keep, row, -1)
        tiles.append((ids == row).astype(F32).astype(BF16))
    return jnp.concatenate(tiles, axis=1)


def halves(x):
    head = x.astype(BF16)
    return head, (x - head.astype(F32)).astype(BF16)


def one_field(total, field):
    rows = pl.ds(field, SNAPS, stride=FIELDS)
    return jnp.concatenate([total[t, rows, :] for t in range(LANES)], axis=1)


def brick_copy(values_hbm, held, sems, brick, slot):
    source = values_hbm.at[:, :, pl.ds(brick * PER_BRICK, PER_BRICK)]
    return pltpu.make_async_copy(source, held.at[slot], sems.at[slot])


HBM = pl.BlockSpec(memory_space=pltpu.HBM)
VMEM = pl.BlockSpec(memory_space=pltpu.VMEM)
SMEM = pl.BlockSpec(memory_space=pltpu.SMEM)


def faces_kernel(values_hbm, cells_hbm, column_hbm, low_ref, high_ref, cells_ref, column_ref, held, total, sems, small):
    bricks = (0, 1, BRICKS - 2, BRICKS - 1)
    ids = pltpu.make_async_copy(cells_hbm, cells_ref, small.at[0])
    columns = pltpu.make_async_copy(column_hbm, column_ref, small.at[1])
    ids.start()
    columns.start()
    copies = [brick_copy(values_hbm, held, sems, brick, slot) for slot, brick in enumerate(bricks)]
    for copy in copies:
        copy.start()
    ids.wait()
    columns.wait()
    for face, (first, out_ref, column) in enumerate(((0, low_ref, 0), (2, high_ref, EXT - 1))):
        sums = None
        for slot in (first, first + 1):
            brick = bricks[slot]
            hot = cell_hot(cells_ref, brick, column_ref[:, brick : brick + 1] == column)
            copies[slot].wait()
            part = dot_nt(held[slot].reshape(ROWS, PER_BRICK), hot)
            sums = part if sums is None else sums + part
        for t in range(LANES):
            total[face, t] = sums[:, t * 128 : (t + 1) * 128]
        for f in range(FIELDS):
            out_ref[f * SNAPS : (f + 1) * SNAPS, :] = one_field(total.at[face], f).astype(BF16)


def face_sums(values, cells, columns):
    shape = jax.ShapeDtypeStruct((ROWS, CW), BF16)
    return pl.pallas_call(
        faces_kernel,
        in_specs=[HBM, HBM, HBM],
        out_specs=[VMEM] * 4,
        scratch_shapes=[
            pltpu.VMEM((4, SNAPS, FIELDS, PER_BRICK), BF16),
            pltpu.VMEM((2, LANES, ROWS, 128), F32),
            pltpu.SemaphoreType.DMA((4,)),
            pltpu.SemaphoreType.DMA((2,)),
        ],
        out_shape=[
            shape,
            shape,
            jax.ShapeDtypeStruct((BRICKS * LANES, 128), jnp.int32),
            jax.ShapeDtypeStruct((1, BRICKS), jnp.int32),
        ],
        compiler_params=params(63),
        name="faces",
    )(values, cells, columns)


def local_kernel(column_ref, values_hbm, cells, head_ref, rest_ref, gram_ref, held, total, sems):
    copies = [brick_copy(values_hbm, held, sems, brick, brick) for brick in range(BRICKS)]
    for copy in copies:
        copy.start()
    total[...] = jnp.zeros_like(total)
    for brick in range(BRICKS):
        hot = cell_hot(cells, brick)
        copies[brick].wait()
        sums = dot_nt(held[brick].reshape(ROWS, PER_BRICK), hot)
        column = column_ref[brick]
        for t in range(LANES):
            total[column, t] += sums[:, t * 128 : (t + 1) * 128]
    same = jnp.zeros((SNAPS, SNAPS), F32)
    mixed = jnp.zeros((SNAPS, SNAPS), F32)
    for k in range(EXT):
        for f in range(FIELDS):
            head, rest = halves(one_field(total.at[k], f))
            head_ref[f * SNAPS : (f + 1) * SNAPS, k * CW : (k + 1) * CW] = head
            rest_ref[f * SNAPS : (f + 1) * SNAPS, k * CW : (k + 1) * CW] = rest
            same += dot_nt(head, head)
            mixed += dot_nt(head, rest)
    gram_ref[...] = same + mixed + mixed.T


def local_sums(values, cells, columns):
    half = jax.ShapeDtypeStruct((ROWS, EXT * CW), BF16)
    return pl.pallas_call(
        local_kernel,
        in_specs=[SMEM, HBM, VMEM],
        out_specs=[VMEM, VMEM, VMEM],
        scratch_shapes=[
            pltpu.VMEM((BRICKS, SNAPS, FIELDS, PER_BRICK), BF16),
            pltpu.VMEM((EXT, LANES, ROWS, 128), F32),
            pltpu.SemaphoreType.DMA((BRICKS,)),
        ],
        out_shape=[half, half, jax.ShapeDtypeStruct((SNAPS, SNAPS), F32)],
        compiler_params=params(44),
        cost_estimate=pl.CostEstimate(flops=6_000_000_000, bytes_accessed=14_000_000, transcendentals=0),
        name="local",
    )(columns, values, cells)


def pack(gram):
    body = gram[:SPLIT, :SPLIT]
    side = gram[:SPLIT, SPLIT:]
    corner = gram[SPLIT:, SPLIT:]
    t = TAIL
    rows = [
        body[:t],
        jnp.concatenate([side[:t], body[t : 2 * t, t:]], axis=1),
        jnp.concatenate([side[t : 2 * t], side[2 * t : 3 * t], body[2 * t : 3 * t, 2 * t :]], axis=1),
        jnp.concatenate([side[3 * t :], corner, corner, body[3 * t :, 3 * t :]], axis=1),
    ]
    return jnp.concatenate(rows, axis=0)


def unpack(packed):
    t = TAIL
    row = lax.broadcasted_iota(jnp.int32, (SPLIT, SPLIT), 0) // t
    col = lax.broadcasted_iota(jnp.int32, (SPLIT, SPLIT), 1) // t
    above = jnp.where(col > row, packed, 0.0)
    body = jnp.where(col == row, packed, 0.0) + above + above.T
    side = jnp.concatenate(
        [packed[t : 2 * t, :t], packed[2 * t : 3 * t, :t], packed[2 * t : 3 * t, t : 2 * t], packed[3 * t :, :t]], axis=0
    )
    corner = packed[3 * t :, t : 2 * t]
    top = jnp.concatenate([body, side], axis=1)
    padded = jnp.concatenate([side, jnp.zeros((SPLIT, SPLIT - t), F32)], axis=1)
    bottom = jnp.concatenate([padded.T[:t], corner], axis=1)
    return jnp.concatenate([top, bottom], axis=0)


def cross_kernel(gram_ref, head_ref, rest_ref, from_below, from_above, packed_ref):
    cross = jnp.zeros((SNAPS, SNAPS), F32)
    for f in range(FIELDS):
        rows = slice(f * SNAPS, (f + 1) * SNAPS)
        for column, received in ((1, from_below), (CX, from_above)):
            lanes = slice(column * CW, (column + 1) * CW)
            other = received[rows, :]
            cross += dot_nt(head_ref[rows, lanes], other) + dot_nt(rest_ref[rows, lanes], other)
    packed_ref[...] = pack(gram_ref[...] + cross + cross.T)


def packed_gram(gram, head, rest, from_below, from_above):
    return pl.pallas_call(
        cross_kernel,
        in_specs=[VMEM] * 5,
        out_specs=VMEM,
        out_shape=jax.ShapeDtypeStruct((SPLIT, SPLIT), F32),
        compiler_params=params(16),
        name="cross",
    )(gram, head, rest, from_below, from_above)


def add_over_devices(x):
    places = [(a, z, y, c) for a in range(4) for z in range(8) for y in range(4) for c in range(2)]
    number = {place: i for i, place in enumerate(places)}

    def move(y, target):
        return lax.ppermute(y, ("gx", "gz"), [(number[place], number[target(*place)]) for place in places])

    def pair(i, step):
        return i ^ 1 if step == 0 else 3 - i

    for turn in range(4):
        step = turn % 2

        def target(a, z, y, c):
            return (a, z, pair(y, step), c) if c == turn // 2 else (pair(a, step), z, y, c)

        x = x + move(x, target)

    def swap(y):
        return move(y, lambda a, z, y, c: (a, z, y, 1 - c))

    first = lax.axis_index("gz") % 2 == 0
    x = x + swap(x)
    near = move(x, lambda a, z, y, c: (a, (z + 2 * c - 1) % 8, y, c))
    other = swap(near)
    two = x + other
    three = two + near
    far = move(jnp.where(first, three, two), lambda a, z, y, c: (a, (z + 6 * c - 3) % 8, y, c))
    return three + far + swap(far)


def orthonormal(basis):
    inner = lax.dot_general(basis, basis, NT, precision=lax.Precision.HIGHEST, preferred_element_type=F32)
    row = lax.broadcasted_iota(jnp.int32, (MODES, 1), 0)
    square = lax.broadcasted_iota(jnp.int32, (MODES, MODES), 0) == lax.broadcasted_iota(jnp.int32, (MODES, MODES), 1)
    for j in range(MODES - 1):
        factor = jnp.where(row > j, inner[:, j : j + 1] / inner[j : j + 1, j : j + 1], 0.0)
        inner = inner - factor * inner[j : j + 1, :]
        basis = basis - factor * basis[j : j + 1, :]
    pivots = jnp.sum(jnp.where(square, inner, 0.0), axis=1, keepdims=True)
    return basis * lax.rsqrt(pivots)


def coefs_kernel(packed_ref, head_ref, rest_ref, basis_ref, own_ref, down_ref, up_ref):
    gram = unpack(packed_ref[...])
    basis = gram[:MODES, :]
    for _ in range(SWEEPS):
        basis = orthonormal(exact_dot(basis, gram))
    basis_ref[...] = basis
    wide = jnp.concatenate([basis] * FIELDS, axis=1)
    tall = jnp.concatenate([wide] * FIELDS, axis=0)
    row_field = lax.broadcasted_iota(jnp.int32, (COEFS, ROWS), 0) // MODES
    col_field = lax.broadcasted_iota(jnp.int32, (COEFS, ROWS), 1) // SNAPS
    head, rest = halves(jnp.where(row_field == col_field, tall, 0.0))
    both = jnp.concatenate([head, rest], axis=0)
    for k in range(EXT):
        columns = slice(k * CW, (k + 1) * CW)
        pair = dot(both, head_ref[:, columns])
        own_ref[:, columns] = pair[:COEFS] + pair[COEFS:] + dot(head, rest_ref[:, columns])
    down_ref[...] = own_ref[:, : 2 * CW]
    up_ref[...] = own_ref[:, CX * CW :]


def coefficients(packed, head, rest):
    side = jax.ShapeDtypeStruct((COEFS, 2 * CW), F32)
    return pl.pallas_call(
        coefs_kernel,
        out_shape=[
            jax.ShapeDtypeStruct((MODES, SNAPS), F32),
            jax.ShapeDtypeStruct((COEFS, EXT * CW), F32),
            side,
            side,
        ],
        in_specs=[VMEM] * 3,
        out_specs=[VMEM] * 4,
        compiler_params=params(16),
        name="coefs",
    )(packed, head, rest)


def spread_kernel(basis_ref, spread_ref):
    head, rest = halves(basis_ref[...])
    snap = lax.broadcasted_iota(jnp.int32, (SNAPS, ROWS), 0)
    column = lax.broadcasted_iota(jnp.int32, (SNAPS, ROWS), 1)
    repeat = (snap == column // FIELDS).astype(F32).astype(BF16)
    both = dot(jnp.concatenate([head, rest], axis=0), repeat)
    field = lax.broadcasted_iota(jnp.int32, (COEFS, ROWS), 0) // MODES
    mine = field == lax.broadcasted_iota(jnp.int32, (COEFS, ROWS), 1) % FIELDS
    head = jnp.where(mine, jnp.concatenate([both[:MODES]] * FIELDS, axis=0), 0.0)
    rest = jnp.where(mine, jnp.concatenate([both[MODES:]] * FIELDS, axis=0), 0.0)
    stacked = jnp.concatenate([head, head, rest, jnp.zeros_like(rest)], axis=0)
    spread_ref[...] = stacked.T.astype(BF16)


def spread_matrix(basis):
    return pl.pallas_call(
        spread_kernel,
        in_specs=[VMEM],
        out_specs=VMEM,
        out_shape=jax.ShapeDtypeStruct((ROWS, 4 * COEFS), BF16),
        compiler_params=params(16),
        name="spread",
    )(basis)


def atoms_kernel(own_ref, below_ref, above_ref, spread_ref, cells, column_ref, out_hbm, held, sems):
    whole = []
    for k in range(EXT):
        value = own_ref[:, k * CW : (k + 1) * CW]
        if k < 2:
            value = value + below_ref[:, k * CW : (k + 1) * CW]
        if k >= CX:
            value = value + above_ref[:, (k - CX) * CW : (k - CX + 1) * CW]
        whole.append(jnp.concatenate(halves(value), axis=0))
    blank = jnp.zeros((COEFS, PER_BRICK), BF16)
    copies = []
    for brick in range(BRICKS):
        column = column_ref[:, brick : brick + 1]
        mine = whole[0]
        for k in range(1, EXT):
            mine = jnp.where(column == k, whole[k], mine)
        picked = dot(mine, cell_hot(cells, brick)).astype(BF16)
        stacked = jnp.concatenate([picked, picked[:COEFS], blank], axis=0)
        fields = dot(spread_ref[...], stacked).astype(BF16)
        held[brick] = fields.reshape(SNAPS, FIELDS, PER_BRICK)
        target = out_hbm.at[:, :, pl.ds(brick * PER_BRICK, PER_BRICK)]
        copy = pltpu.make_async_copy(held.at[brick], target, sems.at[brick])
        copy.start()
        copies.append(copy)
    for copy in copies:
        copy.wait()


def atom_fields(columns, own, below, above, spread, cells):
    return pl.pallas_call(
        atoms_kernel,
        in_specs=[VMEM] * 6,
        out_specs=HBM,
        scratch_shapes=[
            pltpu.VMEM((BRICKS, SNAPS, FIELDS, PER_BRICK), BF16),
            pltpu.SemaphoreType.DMA((BRICKS,)),
        ],
        out_shape=jax.ShapeDtypeStruct((SNAPS, FIELDS, BRICKS * PER_BRICK), BF16),
        compiler_params=params(32),
        name="atoms",
    )(own, below, above, spread, cells, columns)


def on_device(atom_values, atom_cell, brick_column):
    count = lax.axis_size("gx")
    to_lower = [((i + 1) % count, i) for i in range(count)]
    to_upper = [(i, (i + 1) % count) for i in range(count)]
    low, high, cells, columns = face_sums(
        atom_values, atom_cell.reshape(BRICKS * LANES, 128), brick_column.reshape(1, BRICKS)
    )
    from_above = lax.ppermute(low, "gx", to_lower)
    from_below = lax.ppermute(high, "gx", to_upper)
    head, rest, gram = local_sums(atom_values, cells, brick_column)
    packed = add_over_devices(packed_gram(gram, head, rest, from_below, from_above))
    basis, own, down, up = coefficients(packed, head, rest)
    above = lax.ppermute(down, "gx", to_lower)
    below = lax.ppermute(up, "gx", to_upper)
    spread = spread_matrix(basis)
    return atom_fields(columns, own, below, above, spread, cells)


def solution(mesh):
    in_specs = (P(None, None, ("gx", "gz")), P(("gx", "gz")), P(("gx", "gz")))
    out_specs = P(None, None, ("gx", "gz"))
    return jax.shard_map(on_device, mesh=mesh, in_specs=in_specs, out_specs=out_specs, check_vma=False)
```

time: 94.1 us -> 90.7 us (0.964)
  the two profiles are of different devices: /device:TPU:24 before, /device:TPU:1 now
where the time goes in v2:
time: 90.7 us; the launch traced here: 90.5 us
  starting transfers between devices  31 us (34%)
  waiting for transfers between devices  27.8 us (31%)
  Pallas kernels  24.6 us (27%)
  local copies, waits for them, and re-layouts  6.87 us (8%)
    ppermute x9, waiting for transfers between devices, move(): lax.ppermute(y, ('gx', 'gz'), [(number[place], number[target(*place)]) fo...  20.3 us
    ppermute x9, starting transfers between devices, move(): lax.ppermute(y, ('gx', 'gz'), [(number[place], number[target(*place)]) fo...  15.6 us
    pallas_call x1, Pallas kernels, local_sums(): pl.pallas_call(local_kernel, in_specs=[SMEM, HBM, VMEM], out_specs=[VMEM,...  9.64 us
    unnamed x16, local copies, waits for them, and re-layouts  6.87 us
    ppermute x1, starting transfers between devices, on_device(): above = lax.ppermute(down, 'gx', to_lower)  6.54 us
    ppermute x1, starting transfers between devices, on_device(): from_above = lax.ppermute(low, 'gx', to_lower)  6.22 us
    pallas_call x1, Pallas kernels, face_sums(): pl.pallas_call(faces_kernel, in_specs=[HBM, HBM, HBM], out_specs=[VMEM] *...  4.82 us
    pallas_call x1, Pallas kernels, atom_fields(): pl.pallas_call(atoms_kernel, in_specs=[VMEM] * 6, out_specs=HBM, scratch_...  4.45 us
  transfers between devices with their start and end apart: 13, of which 11 were waited for; matrix products, arithmetic and copies ran while one was open for 0% of the time, Pallas kernels for 11%

profile of v2, /device:TPU:1, one launch (start us, length us, event | category | flops | bytes accessed | tf_op | source)
XLA Modules:
  0.0 90.5 jit_solution(4532287133702218416)
XLA Ops:
  0.0 4.8 %faces.1 = (bf16[640,512]{1,0:T(8,128)(2,1)}, bf16[640,512]{1,0:T(8,128)(2,1)}, s32[32,128]{1,0:T(8,128)}, s32[1,8]{1,0:T(1,128)}) custom-call(bf16[160,4,4096]{2,1,0:T(4,128)(2,1)} %values_hbm.3, s32[32,128]{1,0:T(8,128)} %bitcast.3, s32[1,8]{1,0:T(1,128)} %bitcast.2), custom_call_target="tpu_custom_call" | custom-call | tf_op jit(solution)/shard_map/faces/pallas_call | solution.py:102
  4.8 2.5 %collective-permute-start = (bf16[640,512]{1,0:T(8,128)(2,1)}, bf16[640,512]{1,0:T(8,128)(2,1)S(1)}, u32[]{:S(2)}, u32[]{:S(2)}) collective-permute-start(bf16[640,512]{1,0:T(8,128)(2,1)} %get-tuple-element.20), channel_id=1, source_target_pairs={{0,8},{8,16},{16,24},{24,32},{32,40},{40,48},{48,56},{56,64},{64,7... | collective-permute-start | bytes 1966088 | tf_op jit(solution)/shard_map/ppermute | solution.py:373
  7.4 6.2 %collective-permute-start.1 = (bf16[640,512]{1,0:T(8,128)(2,1)}, bf16[640,512]{1,0:T(8,128)(2,1)S(1)}, u32[]{:S(2)}, u32[]{:S(2)}) collective-permute-start(bf16[640,512]{1,0:T(8,128)(2,1)} %get-tuple-element.21), channel_id=1, source_target_pairs={{8,0},{16,8},{24,16},{32,24},{40,32},{48,40},{56,48},{64,56},{72,6... | collective-permute-start | bytes 1966088 | tf_op jit(solution)/shard_map/ppermute | solution.py:372
  13.6 0.7 copy-done.4
  14.3 9.6 %local.1 = (bf16[640,3072]{1,0:T(8,128)(2,1)S(1)}, bf16[640,3072]{1,0:T(8,128)(2,1)S(1)}, f32[160,160]{1,0:T(8,128)S(1)}) custom-call(s32[8]{0:T(128)S(1)} %copy-done.7, bf16[160,4,4096]{2,1,0:T(4,128)(2,1)} %values_hbm.3, s32[32,128]{1,0:T(8,128)S(1)} %copy-done.4), custom_call_target="tpu_custom_call" | custom-call | flops 6000000000 | bytes 14000000 | tf_op jit(solution)/shard_map/local/pallas_call | solution.py:149
  24.0 4.2 %collective-permute-done.from_below = bf16[640,512]{1,0:T(8,128)(2,1)S(1)} collective-permute-done((bf16[640,512]{1,0:T(8,128)(2,1)}, bf16[640,512]{1,0:T(8,128)(2,1)S(1)}, u32[]{:S(2)}, u32[]{:S(2)}) %collective-permute-start) | collective-permute-done | bytes 655392 | tf_op jit(solution)/shard_map/ppermute | solution.py:373
  28.2 1.0 %cross.1 = f32[128,128]{1,0:T(8,128)S(1)} custom-call(f32[160,160]{1,0:T(8,128)S(1)} %get-tuple-element.17.gram_ref, bf16[640,3072]{1,0:T(8,128)(2,1)S(1)} %get-tuple-element.18.head_ref, bf16[640,3072]{1,0:T(8,128)(2,1)S(1)} %get-tuple-element.19.rest_ref, bf16[640,512]{1,0:T(8,128)(2,1)S(1)} %collective-permute-done.from_below, ...), custom_call_target="tpu_custom_call" | custom-call | tf_op jit(solution)/shard_map/cross/pallas_call | solution.py:207
  29.2 1.9 %copy-done = bf16[640,3072]{1,0:T(8,128)(2,1)} copy-done((bf16[640,3072]{1,0:T(8,128)(2,1)}, bf16[640,3072]{1,0:T(8,128)(2,1)S(1)}, u32[]{:S(2)}) %copy-start) | copy-done | bytes 3932184
  31.1 3.1 %collective-permute-done.2 = f32[128,128]{1,0:T(8,128)S(1)} collective-permute-done((f32[128,128]{1,0:T(8,128)S(1)}, f32[128,128]{1,0:T(8,128)S(1)}, u32[]{:S(2)}, u32[]{:S(2)}) %collective-permute-start.2) | collective-permute-done | bytes 65568 | tf_op jit(solution)/shard_map/ppermute | solution.py:222
  34.3 0.8 collective-permute-start.3
  35.1 3.8 %collective-permute-done.3 = f32[128,128]{1,0:T(8,128)S(1)} collective-permute-done((f32[128,128]{1,0:T(8,128)S(1)}, f32[128,128]{1,0:T(8,128)S(1)}, u32[]{:S(2)}, u32[]{:S(2)}) %collective-permute-start.3) | collective-permute-done | bytes 65568 | tf_op jit(solution)/shard_map/ppermute | solution.py:222
  38.9 1.4 %collective-permute-start.4 = (f32[128,128]{1,0:T(8,128)S(1)}, f32[128,128]{1,0:T(8,128)S(1)}, u32[]{:S(2)}, u32[]{:S(2)}) collective-permute-start(f32[128,128]{1,0:T(8,128)S(1)} %add.32), channel_id=1, source_target_pairs={{0,64},{1,3},{2,66},{3,1},{4,68},{5,7},{6,70},{7,5},{8,72},{9,11},... | collective-permute-start | bytes 196616 | tf_op jit(solution)/shard_map/ppermute | solution.py:222
  40.2 1.8 %collective-permute-done.4 = f32[128,128]{1,0:T(8,128)S(1)} collective-permute-done((f32[128,128]{1,0:T(8,128)S(1)}, f32[128,128]{1,0:T(8,128)S(1)}, u32[]{:S(2)}, u32[]{:S(2)}) %collective-permute-start.4) | collective-permute-done | bytes 65568 | tf_op jit(solution)/shard_map/ppermute | solution.py:222
  42.1 2.8 %collective-permute-start.5 = (f32[128,128]{1,0:T(8,128)S(1)}, f32[128,128]{1,0:T(8,128)S(1)}, u32[]{:S(2)}, u32[]{:S(2)}) collective-permute-start(f32[128,128]{1,0:T(8,128)S(1)} %add.33), channel_id=1, source_target_pairs={{0,192},{1,7},{2,194},{3,5},{4,196},{5,3},{6,198},{7,1},{8,200},{9... | collective-permute-start | bytes 196616 | tf_op jit(solution)/shard_map/ppermute | solution.py:222
  44.9 1.7 %collective-permute-done.5 = f32[128,128]{1,0:T(8,128)S(1)} collective-permute-done((f32[128,128]{1,0:T(8,128)S(1)}, f32[128,128]{1,0:T(8,128)S(1)}, u32[]{:S(2)}, u32[]{:S(2)}) %collective-permute-start.5) | collective-permute-done | bytes 65568 | tf_op jit(solution)/shard_map/ppermute | solution.py:222
  46.6 5.8 %collective-permute-start.6 = (f32[128,128]{1,0:T(8,128)S(1)}, f32[128,128]{1,0:T(8,128)S(1)}, u32[]{:S(2)}, u32[]{:S(2)}) collective-permute-start(f32[128,128]{1,0:T(8,128)S(1)} %add.34), channel_id=1, source_target_pairs={{0,1},{1,0},{2,3},{3,2},{4,5},{5,4},{6,7},{7,6},{8,9},{9,8},{10,11... | collective-permute-start | bytes 196616 | tf_op jit(solution)/shard_map/ppermute | solution.py:222
  52.4 0.9 collective-permute-done.6
  53.3 0.1 collective-permute-start.7
  53.4 4.3 %collective-permute-done.7 = f32[128,128]{1,0:T(8,128)S(1)} collective-permute-done((f32[128,128]{1,0:T(8,128)S(1)}, f32[128,128]{1,0:T(8,128)S(1)}, u32[]{:S(2)}, u32[]{:S(2)}) %collective-permute-start.7) | collective-permute-done | bytes 65568 | tf_op jit(solution)/shard_map/ppermute | solution.py:222
  57.7 0.4 collective-permute-start.8
  58.2 0.9 collective-permute-done.8
  59.1 3.3 %collective-permute-start.9 = (f32[128,128]{1,0:T(8,128)S(1)}, f32[128,128]{1,0:T(8,128)S(1)}, u32[]{:S(2)}, u32[]{:S(2)}) collective-permute-start(f32[128,128]{1,0:T(8,128)S(1)} %get-tuple-element.27), channel_id=1, source_target_pairs={{0,40},{1,25},{2,42},{3,27},{4,44},{5,29},{6,46},{7,31},{8,48},{9,... | collective-permute-start | bytes 196616 | tf_op jit(solution)/shard_map/ppermute | solution.py:222
  62.3 2.9 %collective-permute-done.9 = f32[128,128]{1,0:T(8,128)S(1)} collective-permute-done((f32[128,128]{1,0:T(8,128)S(1)}, f32[128,128]{1,0:T(8,128)S(1)}, u32[]{:S(2)}, u32[]{:S(2)}) %collective-permute-start.9) | collective-permute-done | bytes 65568 | tf_op jit(solution)/shard_map/ppermute | solution.py:222
  65.3 1.0 %collective-permute-start.10 = (f32[128,128]{1,0:T(8,128)S(1)}, f32[128,128]{1,0:T(8,128)S(1)}, u32[]{:S(2)}, u32[]{:S(2)}) collective-permute-start(f32[128,128]{1,0:T(8,128)S(1)} %collective-permute-done.9), channel_id=1, source_target_pairs={{0,1},{1,0},{2,3},{3,2},{4,5},{5,4},{6,7},{7,6},{8,9},{9,8},{10,11... | collective-permute-start | bytes 196616 | tf_op jit(solution)/shard_map/ppermute | solution.py:222
  66.3 0.9 collective-permute-done.10
  67.2 2.1 %copy-done.1 = bf16[640,3072]{1,0:T(8,128)(2,1)S(1)} copy-done((bf16[640,3072]{1,0:T(8,128)(2,1)S(1)}, bf16[640,3072]{1,0:T(8,128)(2,1)}, u32[]{:S(2)}) %copy-start.1) | copy-done | bytes 3932184
  69.3 2.1 %copy-done.3 = bf16[640,3072]{1,0:T(8,128)(2,1)S(1)} copy-done((bf16[640,3072]{1,0:T(8,128)(2,1)S(1)}, bf16[640,3072]{1,0:T(8,128)(2,1)}, u32[]{:S(2)}) %copy-start.3) | copy-done | bytes 3932184
  71.4 4.4 %coefs.1 = (f32[8,160]{1,0:T(8,128)S(1)}, f32[32,3072]{1,0:T(8,128)S(1)}, f32[32,1024]{1,0:T(8,128)S(1)}, f32[32,1024]{1,0:T(8,128)S(1)}) custom-call(f32[128,128]{1,0:T(8,128)S(1)} %add_add_fusion.packed_ref, bf16[640,3072]{1,0:T(8,128)(2,1)S(1)} %copy-done.1, bf16[640,3072]{1,0:T(8,128)(2,1)S(1)} %copy-done.3), custom_call_target="tpu_custom_call" | custom-call | tf_op jit(solution)/shard_map/coefs/pallas_call | solution.py:282
  75.8 6.5 %collective-permute-start.12 = (f32[32,1024]{1,0:T(8,128)S(1)}, f32[32,1024]{1,0:T(8,128)S(1)}, u32[]{:S(2)}, u32[]{:S(2)}) collective-permute-start(f32[32,1024]{1,0:T(8,128)S(1)} %get-tuple-element.24), channel_id=1, source_target_pairs={{8,0},{16,8},{24,16},{32,24},{40,32},{48,40},{56,48},{64,56},{72,6... | collective-permute-start | bytes 393224 | tf_op jit(solution)/shard_map/ppermute | solution.py:377
  82.4 0.3 spread.1.spread_ref
  82.7 3.2 %collective-permute-done.11.below_ref = f32[32,1024]{1,0:T(8,128)S(1)} collective-permute-done((f32[32,1024]{1,0:T(8,128)S(1)}, f32[32,1024]{1,0:T(8,128)S(1)}, u32[]{:S(2)}, u32[]{:S(2)}) %collective-permute-start.11) | collective-permute-done | bytes 131104 | tf_op jit(solution)/shard_map/ppermute | solution.py:378
  85.9 4.4 %atoms.1 = bf16[160,4,4096]{2,1,0:T(4,128)(2,1)} custom-call(f32[32,3072]{1,0:T(8,128)S(1)} %get-tuple-element.22.own_ref, f32[32,1024]{1,0:T(8,128)S(1)} %collective-permute-done.11.below_ref, f32[32,1024]{1,0:T(8,128)S(1)} %collective-permute-done.12.above_ref, bf16[640,128]{1,0:T(8,128)(2,1)S(1)} %spread.1.spread_ref, s32[32,128]{1,0:T(8,128)S(1)} %copy-done.5, ...), custom_call_target="tpu_custom_call" | custom-call | tf_op jit(solution)/shard_map/atoms/pallas_call | solution.py:351
  (23 shorter events, 0.2 us)
Async XLA Ops:
  0.0 13.6 %copy-start.7 = (s32[8]{0:T(128)S(1)}, s32[8]{0:T(128)}, u32[]{:S(2)}) copy-start(s32[8]{0:T(128)} %column_ref.1) | copy-start | bytes 100
  4.8 23.3 %collective-permute-start = (bf16[640,512]{1,0:T(8,128)(2,1)}, bf16[640,512]{1,0:T(8,128)(2,1)S(1)}, u32[]{:S(2)}, u32[]{:S(2)}) collective-permute-start(bf16[640,512]{1,0:T(8,128)(2,1)} %get-tuple-element.20), channel_id=1, source_target_pairs={{0,8},{8,16},{16,24},{24,32},{32,40},{40,48},{48,56},{56,64},{64,7... | collective-permute-start | bytes 1966088 | tf_op jit(solution)/shard_map/ppermute | solution.py:373
  7.4 20.8 %collective-permute-start.1 = (bf16[640,512]{1,0:T(8,128)(2,1)}, bf16[640,512]{1,0:T(8,128)(2,1)S(1)}, u32[]{:S(2)}, u32[]{:S(2)}) collective-permute-start(bf16[640,512]{1,0:T(8,128)(2,1)} %get-tuple-element.21), channel_id=1, source_target_pairs={{8,0},{16,8},{24,16},{32,24},{40,32},{48,40},{56,48},{64,56},{72,6... | collective-permute-start | bytes 1966088 | tf_op jit(solution)/shard_map/ppermute | solution.py:372
  13.6 0.7 copy-start.4
  24.0 5.2 %copy-start.2 = (bf16[640,3072]{1,0:T(8,128)(2,1)}, bf16[640,3072]{1,0:T(8,128)(2,1)S(1)}, u32[]{:S(2)}) copy-start(bf16[640,3072]{1,0:T(8,128)(2,1)S(1)} %get-tuple-element.19.rest_ref) | copy-start | bytes 11796484
  29.2 1.9 %copy-start = (bf16[640,3072]{1,0:T(8,128)(2,1)}, bf16[640,3072]{1,0:T(8,128)(2,1)S(1)}, u32[]{:S(2)}) copy-start(bf16[640,3072]{1,0:T(8,128)(2,1)S(1)} %get-tuple-element.18.head_ref) | copy-start | bytes 11796484
  31.1 54.8 %copy-start.5 = (s32[32,128]{1,0:T(8,128)S(1)}, s32[32,128]{1,0:T(8,128)}, u32[]{:S(2)}) copy-start(s32[32,128]{1,0:T(8,128)} %get-tuple-element.16.cells) | copy-start | bytes 49156
  31.1 54.8 %copy-start.6 = (s32[1,8]{1,0:T(1,128)S(1)}, s32[1,8]{1,0:T(1,128)}, u32[]{:S(2)}) copy-start(s32[1,8]{1,0:T(1,128)} %get-tuple-element.26.column_ref) | copy-start | bytes 100
  31.1 3.1 %collective-permute-start.2 = (f32[128,128]{1,0:T(8,128)S(1)}, f32[128,128]{1,0:T(8,128)S(1)}, u32[]{:S(2)}, u32[]{:S(2)}) collective-permute-start(f32[128,128]{1,0:T(8,128)S(1)} %cross.1), channel_id=1, source_target_pairs={{0,2},{1,65},{2,0},{3,67},{4,6},{5,69},{6,4},{7,71},{8,10},{9,73},... | collective-permute-start | bytes 196616 | tf_op jit(solution)/shard_map/ppermute | solution.py:222
  34.3 4.6 %collective-permute-start.3 = (f32[128,128]{1,0:T(8,128)S(1)}, f32[128,128]{1,0:T(8,128)S(1)}, u32[]{:S(2)}, u32[]{:S(2)}) collective-permute-start(f32[128,128]{1,0:T(8,128)S(1)} %add.31), channel_id=1, source_target_pairs={{0,6},{1,193},{2,4},{3,195},{4,2},{5,197},{6,0},{7,199},{8,14},{9,... | collective-permute-start | bytes 196616 | tf_op jit(solution)/shard_map/ppermute | solution.py:222
  38.9 3.2 %collective-permute-start.4 = (f32[128,128]{1,0:T(8,128)S(1)}, f32[128,128]{1,0:T(8,128)S(1)}, u32[]{:S(2)}, u32[]{:S(2)}) collective-permute-start(f32[128,128]{1,0:T(8,128)S(1)} %add.32), channel_id=1, source_target_pairs={{0,64},{1,3},{2,66},{3,1},{4,68},{5,7},{6,70},{7,5},{8,72},{9,11},... | collective-permute-start | bytes 196616 | tf_op jit(solution)/shard_map/ppermute | solution.py:222
  42.1 4.5 %collective-permute-start.5 = (f32[128,128]{1,0:T(8,128)S(1)}, f32[128,128]{1,0:T(8,128)S(1)}, u32[]{:S(2)}, u32[]{:S(2)}) collective-permute-start(f32[128,128]{1,0:T(8,128)S(1)} %add.33), channel_id=1, source_target_pairs={{0,192},{1,7},{2,194},{3,5},{4,196},{5,3},{6,198},{7,1},{8,200},{9... | collective-permute-start | bytes 196616 | tf_op jit(solution)/shard_map/ppermute | solution.py:222
  46.6 6.7 %collective-permute-start.6 = (f32[128,128]{1,0:T(8,128)S(1)}, f32[128,128]{1,0:T(8,128)S(1)}, u32[]{:S(2)}, u32[]{:S(2)}) collective-permute-start(f32[128,128]{1,0:T(8,128)S(1)} %add.34), channel_id=1, source_target_pairs={{0,1},{1,0},{2,3},{3,2},{4,5},{5,4},{6,7},{7,6},{8,9},{9,8},{10,11... | collective-permute-start | bytes 196616 | tf_op jit(solution)/shard_map/ppermute | solution.py:222
  53.3 4.4 %collective-permute-start.7 = (f32[128,128]{1,0:T(8,128)S(1)}, f32[128,128]{1,0:T(8,128)S(1)}, u32[]{:S(2)}, u32[]{:S(2)}) collective-permute-start(f32[128,128]{1,0:T(8,128)S(1)} %add.35), channel_id=1, source_target_pairs={{0,56},{1,9},{2,58},{3,11},{4,60},{5,13},{6,62},{7,15},{8,0},{9,17... | collective-permute-start | bytes 196616 | tf_op jit(solution)/shard_map/ppermute | solution.py:222
  57.7 1.3 %collective-permute-start.8 = (f32[128,128]{1,0:T(8,128)S(1)}, f32[128,128]{1,0:T(8,128)S(1)}, u32[]{:S(2)}, u32[]{:S(2)}) collective-permute-start(f32[128,128]{1,0:T(8,128)S(1)} %collective-permute-done.7), channel_id=1, source_target_pairs={{0,1},{1,0},{2,3},{3,2},{4,5},{5,4},{6,7},{7,6},{8,9},{9,8},{10,11... | collective-permute-start | bytes 196616 | tf_op jit(solution)/shard_map/ppermute | solution.py:222
  59.1 6.2 %collective-permute-start.9 = (f32[128,128]{1,0:T(8,128)S(1)}, f32[128,128]{1,0:T(8,128)S(1)}, u32[]{:S(2)}, u32[]{:S(2)}) collective-permute-start(f32[128,128]{1,0:T(8,128)S(1)} %get-tuple-element.27), channel_id=1, source_target_pairs={{0,40},{1,25},{2,42},{3,27},{4,44},{5,29},{6,46},{7,31},{8,48},{9,... | collective-permute-start | bytes 196616 | tf_op jit(solution)/shard_map/ppermute | solution.py:222
  65.3 1.9 %collective-permute-start.10 = (f32[128,128]{1,0:T(8,128)S(1)}, f32[128,128]{1,0:T(8,128)S(1)}, u32[]{:S(2)}, u32[]{:S(2)}) collective-permute-start(f32[128,128]{1,0:T(8,128)S(1)} %collective-permute-done.9), channel_id=1, source_target_pairs={{0,1},{1,0},{2,3},{3,2},{4,5},{5,4},{6,7},{7,6},{8,9},{9,8},{10,11... | collective-permute-start | bytes 196616 | tf_op jit(solution)/shard_map/ppermute | solution.py:222
  67.2 2.1 %copy-start.1 = (bf16[640,3072]{1,0:T(8,128)(2,1)S(1)}, bf16[640,3072]{1,0:T(8,128)(2,1)}, u32[]{:S(2)}) copy-start(bf16[640,3072]{1,0:T(8,128)(2,1)} %copy-done) | copy-start | bytes 11796484
  69.3 2.1 %copy-start.3 = (bf16[640,3072]{1,0:T(8,128)(2,1)S(1)}, bf16[640,3072]{1,0:T(8,128)(2,1)}, u32[]{:S(2)}) copy-start(bf16[640,3072]{1,0:T(8,128)(2,1)} %copy-done.2) | copy-start | bytes 11796484
  75.8 10.1 %collective-permute-start.11 = (f32[32,1024]{1,0:T(8,128)S(1)}, f32[32,1024]{1,0:T(8,128)S(1)}, u32[]{:S(2)}, u32[]{:S(2)}) collective-permute-start(f32[32,1024]{1,0:T(8,128)S(1)} %get-tuple-element.23), channel_id=1, source_target_pairs={{0,8},{8,16},{16,24},{24,32},{32,40},{40,48},{48,56},{56,64},{64,7... | collective-permute-start | bytes 393224 | tf_op jit(solution)/shard_map/ppermute | solution.py:378
  75.8 10.0 %collective-permute-start.12 = (f32[32,1024]{1,0:T(8,128)S(1)}, f32[32,1024]{1,0:T(8,128)S(1)}, u32[]{:S(2)}, u32[]{:S(2)}) collective-permute-start(f32[32,1024]{1,0:T(8,128)S(1)} %get-tuple-element.24), channel_id=1, source_target_pairs={{8,0},{16,8},{24,16},{32,24},{40,32},{48,40},{56,48},{64,56},{72,6... | collective-permute-start | bytes 393224 | tf_op jit(solution)/shard_map/ppermute | solution.py:377

commit v3 on v2

v3 whole, which is shorter than its diff:
```python
import jax
import jax.numpy as jnp
from jax import lax
from jax.experimental import pallas as pl
from jax.experimental.pallas import tpu as pltpu
from jax.sharding import PartitionSpec as P

SNAPS = 160
FIELDS = 4
ROWS = SNAPS * FIELDS
MODES = 8
SWEEPS = 3
CX = 4
EXT = CX + 2
CW = 512
PER_BRICK = 512
BRICKS = 8
COEFS = MODES * FIELDS
SPLIT = 128
TAIL = SNAPS - SPLIT
LANES = CW // 128
F32 = jnp.float32
BF16 = jnp.bfloat16
NT = (((1,), (1,)), ((), ()))
TN = (((0,), (0,)), ((), ()))


def params(mib):
    return pltpu.CompilerParams(vmem_limit_bytes=mib * 1024 * 1024)


def dot_nt(a, b):
    return lax.dot_general(a, b, NT, preferred_element_type=F32)


def dot(a, b):
    return jnp.dot(a, b, preferred_element_type=F32)


def exact_dot(a, b):
    return jnp.dot(a, b, precision=lax.Precision.HIGHEST, preferred_element_type=F32)


def cell_hot(cells, brick, keep=None):
    ids = lax.broadcasted_iota(jnp.int32, (CW, 128), 0)
    tiles = []
    for t in range(LANES):
        row = cells[brick * LANES + t : brick * LANES + t + 1, :]
        if keep is not None:
            row = jnp.where(keep, row, -1)
        tiles.append((ids == row).astype(F32).astype(BF16))
    return jnp.concatenate(tiles, axis=1)


def halves(x):
    head = x.astype(BF16)
    return head, (x - head.astype(F32)).astype(BF16)


def one_field(total, field):
    rows = pl.ds(field, SNAPS, stride=FIELDS)
    return jnp.concatenate([total[t, rows, :] for t in range(LANES)], axis=1)


def brick_copy(values_hbm, held, sems, brick, slot):
    source = values_hbm.at[:, :, pl.ds(brick * PER_BRICK, PER_BRICK)]
    return pltpu.make_async_copy(source, held.at[slot], sems.at[slot])


HBM = pl.BlockSpec(memory_space=pltpu.HBM)
VMEM = pl.BlockSpec(memory_space=pltpu.VMEM)
SMEM = pl.BlockSpec(memory_space=pltpu.SMEM)


def faces_kernel(values_hbm, cells_hbm, column_hbm, low_hbm, high_hbm, held, total, face, cells, columns, sems, small, out_sems):
    bricks = (0, 1, BRICKS - 2, BRICKS - 1)
    targets = ((0, low_hbm), (EXT - 1, high_hbm))
    inputs = [
        pltpu.make_async_copy(cells_hbm, cells, small.at[0]),
        pltpu.make_async_copy(column_hbm, columns, small.at[1]),
    ]
    copies = [brick_copy(values_hbm, held, sems, brick, slot) for slot, brick in enumerate(bricks)]
    outputs = [pltpu.make_async_copy(face.at[i], out, out_sems.at[i]) for i, (_, out) in enumerate(targets)]
    for copy in inputs + copies:
        copy.start()
    for copy in inputs:
        copy.wait()
    hots = [
        cell_hot(cells, brick, columns[:, brick : brick + 1] == targets[slot // 2][0]) for slot, brick in enumerate(bricks)
    ]
    for i in range(2):
        sums = None
        for slot in (2 * i, 2 * i + 1):
            copies[slot].wait()
            part = dot_nt(held[slot].reshape(ROWS, PER_BRICK), hots[slot])
            sums = part if sums is None else sums + part
        for t in range(LANES):
            total[i, t] = sums[:, t * 128 : (t + 1) * 128]
        for f in range(FIELDS):
            face[i, f * SNAPS : (f + 1) * SNAPS, :] = one_field(total.at[i], f).astype(BF16)
        outputs[i].start()
    for copy in outputs:
        copy.wait()


def face_sums(values, cells, columns):
    shape = jax.ShapeDtypeStruct((ROWS, CW), BF16)
    return pl.pallas_call(
        faces_kernel,
        in_specs=[HBM] * 3,
        out_specs=[HBM] * 2,
        scratch_shapes=[
            pltpu.VMEM((4, SNAPS, FIELDS, PER_BRICK), BF16),
            pltpu.VMEM((2, LANES, ROWS, 128), F32),
            pltpu.VMEM((2, ROWS, CW), BF16),
            pltpu.VMEM((BRICKS * LANES, 128), jnp.int32),
            pltpu.VMEM((1, BRICKS), jnp.int32),
            pltpu.SemaphoreType.DMA((4,)),
            pltpu.SemaphoreType.DMA((2,)),
            pltpu.SemaphoreType.DMA((2,)),
        ],
        out_shape=[shape, shape],
        compiler_params=params(63),
        name="faces",
    )(values, cells, columns)


def local_kernel(column_ref, values_hbm, cells, after, head_hbm, rest_hbm, face_ref, gram_ref, held, total, heads, rests, sems, out_sems):
    copies = [brick_copy(values_hbm, held, sems, brick, brick) for brick in range(BRICKS)]
    for copy in copies:
        copy.start()
    total[...] = jnp.zeros_like(total)
    for brick in range(BRICKS):
        hot = cell_hot(cells, brick)
        copies[brick].wait()
        sums = dot_nt(held[brick].reshape(ROWS, PER_BRICK), hot)
        column = column_ref[brick]
        for t in range(LANES):
            total[column, t] += sums[:, t * 128 : (t + 1) * 128]
    same = jnp.zeros((SNAPS, SNAPS), F32)
    mixed = jnp.zeros((SNAPS, SNAPS), F32)
    outputs = []
    for k in range(EXT):
        for f in range(FIELDS):
            rows = slice(f * SNAPS, (f + 1) * SNAPS)
            head, rest = halves(one_field(total.at[k], f))
            heads[k, rows, :] = head
            rests[k, rows, :] = rest
            if k in (1, CX):
                face_ref[2 * (k // CX), rows, :] = head
                face_ref[2 * (k // CX) + 1, rows, :] = rest
            same += dot_nt(head, head)
            mixed += dot_nt(head, rest)
        for i, (source, target) in enumerate(((heads, head_hbm), (rests, rest_hbm))):
            outputs.append(pltpu.make_async_copy(source.at[k], target.at[k], out_sems.at[i, k]))
            outputs[-1].start()
    gram_ref[...] = same + mixed + mixed.T
    for copy in outputs:
        copy.wait()


def local_sums(values, cells, columns, after):
    half = jax.ShapeDtypeStruct((EXT, ROWS, CW), BF16)
    return pl.pallas_call(
        local_kernel,
        in_specs=[SMEM, HBM, VMEM, HBM],
        out_specs=[HBM, HBM, VMEM, VMEM],
        scratch_shapes=[
            pltpu.VMEM((BRICKS, SNAPS, FIELDS, PER_BRICK), BF16),
            pltpu.VMEM((EXT, LANES, ROWS, 128), F32),
            pltpu.VMEM((EXT, ROWS, CW), BF16),
            pltpu.VMEM((EXT, ROWS, CW), BF16),
            pltpu.SemaphoreType.DMA((BRICKS,)),
            pltpu.SemaphoreType.DMA((2, EXT)),
        ],
        out_shape=[
            half,
            half,
            jax.ShapeDtypeStruct((4, ROWS, CW), BF16),
            jax.ShapeDtypeStruct((SNAPS, SNAPS), F32),
        ],
        compiler_params=params(50),
        cost_estimate=pl.CostEstimate(flops=6_000_000_000, bytes_accessed=14_000_000, transcendentals=0),
        name="local",
    )(columns, values, cells, after)


def pack(gram):
    body = gram[:SPLIT, :SPLIT]
    side = gram[:SPLIT, SPLIT:]
    corner = gram[SPLIT:, SPLIT:]
    t = TAIL
    rows = [
        body[:t],
        jnp.concatenate([side[:t], body[t : 2 * t, t:]], axis=1),
        jnp.concatenate([side[t : 2 * t], side[2 * t : 3 * t], body[2 * t : 3 * t, 2 * t :]], axis=1),
        jnp.concatenate([side[3 * t :], corner, corner, body[3 * t :, 3 * t :]], axis=1),
    ]
    return jnp.concatenate(rows, axis=0)


def unpack(packed):
    t = TAIL
    row = lax.broadcasted_iota(jnp.int32, (SPLIT, SPLIT), 0) // t
    col = lax.broadcasted_iota(jnp.int32, (SPLIT, SPLIT), 1) // t
    above = jnp.where(col > row, packed, 0.0)
    body = jnp.where(col == row, packed, 0.0) + above + above.T
    side = jnp.concatenate(
        [packed[t : 2 * t, :t], packed[2 * t : 3 * t, :t], packed[2 * t : 3 * t, t : 2 * t], packed[3 * t :, :t]], axis=0
    )
    corner = packed[3 * t :, t : 2 * t]
    top = jnp.concatenate([body, side], axis=1)
    padded = jnp.concatenate([side, jnp.zeros((SPLIT, SPLIT - t), F32)], axis=1)
    bottom = jnp.concatenate([padded.T[:t], corner], axis=1)
    return jnp.concatenate([top, bottom], axis=0)


def cross_kernel(gram_ref, face_ref, from_below, from_above, packed_ref):
    cross = jnp.zeros((SNAPS, SNAPS), F32)
    for f in range(FIELDS):
        rows = slice(f * SNAPS, (f + 1) * SNAPS)
        for i, received in enumerate((from_below, from_above)):
            other = received[rows, :]
            cross += dot_nt(face_ref[2 * i, rows, :], other) + dot_nt(face_ref[2 * i + 1, rows, :], other)
    packed_ref[...] = pack(gram_ref[...] + cross + cross.T)


def packed_gram(gram, faces, from_below, from_above):
    return pl.pallas_call(
        cross_kernel,
        in_specs=[VMEM] * 4,
        out_specs=VMEM,
        out_shape=jax.ShapeDtypeStruct((SPLIT, SPLIT), F32),
        compiler_params=params(16),
        name="cross",
    )(gram, faces, from_below, from_above)


def add_over_devices(x):
    axes = ("gx", "gz")
    depth = 8
    planes = [[i * 8 + j for i in range(z, 32, depth) for j in range(8)] for z in range(depth)]
    lines = [list(line) for line in zip(*planes)]
    size = len(planes[0])

    def trade(parts, groups):
        return lax.all_to_all(parts, axes, 0, 0, axis_index_groups=groups, tiled=True)

    shape = (SPLIT // size, SPLIT)
    mine = trade(x.reshape((size,) + shape), planes).sum(0)
    mine = trade(jnp.broadcast_to(mine, (depth,) + shape), lines).sum(0)
    return trade(jnp.broadcast_to(mine, (size,) + shape), planes).reshape(SPLIT, SPLIT)


def orthonormal(basis):
    inner = lax.dot_general(basis, basis, NT, precision=lax.Precision.HIGHEST, preferred_element_type=F32)
    row = lax.broadcasted_iota(jnp.int32, (MODES, 1), 0)
    columns = [jnp.broadcast_to(inner[:, j : j + 1], (MODES, 128)) for j in range(MODES)]
    wide = jnp.concatenate([basis, jnp.zeros((MODES, 256 - SNAPS), F32)], axis=1)
    parts = [wide[:, :128], wide[:, 128:]]
    scale = jnp.zeros((MODES, 128), F32)
    for j in range(MODES):
        pivot = columns[j][j : j + 1, :]
        scale = jnp.where(row == j, lax.rsqrt(pivot), scale)
        factor = jnp.where(row > j, columns[j] * (1.0 / pivot), 0.0)
        for k in range(j + 1, MODES):
            columns[k] = columns[k] - factor * columns[k][j : j + 1, :]
        parts = [part - factor * part[j : j + 1, :] for part in parts]
    return jnp.concatenate([part * scale for part in parts], axis=1)[:, :SNAPS]


def coefs_kernel(packed_ref, head_hbm, rest_hbm, basis_ref, own_ref, down_ref, up_ref, heads, rests, sems):
    copies = [
        pltpu.make_async_copy(head_hbm, heads, sems.at[0]),
        pltpu.make_async_copy(rest_hbm, rests, sems.at[1]),
    ]
    for copy in copies:
        copy.start()
    gram = unpack(packed_ref[...])
    basis = gram[:MODES, :]
    for _ in range(SWEEPS):
        basis = orthonormal(exact_dot(basis, gram))
    basis_ref[...] = basis
    wide = jnp.concatenate([basis] * FIELDS, axis=1)
    tall = jnp.concatenate([wide] * FIELDS, axis=0)
    row_field = lax.broadcasted_iota(jnp.int32, (COEFS, ROWS), 0) // MODES
    col_field = lax.broadcasted_iota(jnp.int32, (COEFS, ROWS), 1) // SNAPS
    head, rest = halves(jnp.where(row_field == col_field, tall, 0.0))
    both = jnp.concatenate([head, rest], axis=0)
    for copy in copies:
        copy.wait()
    for k in range(EXT):
        pair = dot(both, heads[k])
        own = pair[:COEFS] + pair[COEFS:] + dot(head, rests[k])
        own_ref[:, k * CW : (k + 1) * CW] = own
        if k < 2:
            down_ref[:, k * CW : (k + 1) * CW] = own
        if k >= CX:
            up_ref[:, (k - CX) * CW : (k - CX + 1) * CW] = own


def coefficients(packed, head, rest):
    side = jax.ShapeDtypeStruct((COEFS, 2 * CW), F32)
    return pl.pallas_call(
        coefs_kernel,
        in_specs=[VMEM, HBM, HBM],
        out_specs=[VMEM] * 4,
        scratch_shapes=[
            pltpu.VMEM((EXT, ROWS, CW), BF16),
            pltpu.VMEM((EXT, ROWS, CW), BF16),
            pltpu.SemaphoreType.DMA((2,)),
        ],
        out_shape=[
            jax.ShapeDtypeStruct((MODES, SNAPS), F32),
            jax.ShapeDtypeStruct((COEFS, EXT * CW), F32),
            side,
            side,
        ],
        compiler_params=params(52),
        name="coefs",
    )(packed, head, rest)


def prepare_kernel(basis_ref, cells, spread_ref, hots_ref):
    head, rest = halves(basis_ref[...])
    snap = lax.broadcasted_iota(jnp.int32, (SNAPS, ROWS), 0)
    column = lax.broadcasted_iota(jnp.int32, (SNAPS, ROWS), 1)
    repeat = (snap == column // FIELDS).astype(F32).astype(BF16)
    both = dot(jnp.concatenate([head, rest], axis=0), repeat)
    field = lax.broadcasted_iota(jnp.int32, (COEFS, ROWS), 0) // MODES
    mine = field == lax.broadcasted_iota(jnp.int32, (COEFS, ROWS), 1) % FIELDS
    head = jnp.where(mine, jnp.concatenate([both[:MODES]] * FIELDS, axis=0), 0.0)
    rest = jnp.where(mine, jnp.concatenate([both[MODES:]] * FIELDS, axis=0), 0.0)
    stacked = jnp.concatenate([head, head, rest, jnp.zeros_like(rest)], axis=0)
    spread_ref[...] = stacked.T.astype(BF16)
    for brick in range(BRICKS):
        hots_ref[brick] = cell_hot(cells, brick)


def prepare(basis, cells):
    return pl.pallas_call(
        prepare_kernel,
        in_specs=[VMEM, VMEM],
        out_specs=[VMEM, VMEM],
        out_shape=[
            jax.ShapeDtypeStruct((ROWS, 4 * COEFS), BF16),
            jax.ShapeDtypeStruct((BRICKS, CW, PER_BRICK), BF16),
        ],
        compiler_params=params(16),
        name="prepare",
    )(basis, cells)


def atoms_kernel(own_ref, below_ref, above_ref, spread_ref, hots_ref, column_ref, out_hbm, held, sems):
    whole = []
    for k in range(EXT):
        value = own_ref[:, k * CW : (k + 1) * CW]
        if k < 2:
            value = value + below_ref[:, k * CW : (k + 1) * CW]
        if k >= CX:
            value = value + above_ref[:, (k - CX) * CW : (k - CX + 1) * CW]
        whole.append(jnp.concatenate(halves(value), axis=0))
    blank = jnp.zeros((COEFS, PER_BRICK), BF16)
    copies = []
    for brick in range(BRICKS):
        column = column_ref[:, brick : brick + 1]
        mine = whole[0]
        for k in range(1, EXT):
            mine = jnp.where(column == k, whole[k], mine)
        picked = dot(mine, hots_ref[brick]).astype(BF16)
        stacked = jnp.concatenate([picked, picked[:COEFS], blank], axis=0)
        fields = dot(spread_ref[...], stacked).astype(BF16)
        held[brick] = fields.reshape(SNAPS, FIELDS, PER_BRICK)
        target = out_hbm.at[:, :, pl.ds(brick * PER_BRICK, PER_BRICK)]
        copy = pltpu.make_async_copy(held.at[brick], target, sems.at[brick])
        copy.start()
        copies.append(copy)
    for copy in copies:
        copy.wait()


def atom_fields(columns, own, below, above, spread, hots):
    return pl.pallas_call(
        atoms_kernel,
        in_specs=[VMEM] * 6,
        out_specs=HBM,
        scratch_shapes=[
            pltpu.VMEM((BRICKS, SNAPS, FIELDS, PER_BRICK), BF16),
            pltpu.SemaphoreType.DMA((BRICKS,)),
        ],
        out_shape=jax.ShapeDtypeStruct((SNAPS, FIELDS, BRICKS * PER_BRICK), BF16),
        compiler_params=params(32),
        name="atoms",
    )(own, below, above, spread, hots, columns)


def on_device(atom_values, atom_cell, brick_column):
    count = lax.axis_size("gx")
    to_lower = [((i + 1) % count, i) for i in range(count)]
    to_upper = [(i, (i + 1) % count) for i in range(count)]
    cells = atom_cell.reshape(BRICKS * LANES, 128)
    columns = brick_column.reshape(1, BRICKS)
    low, high = face_sums(atom_values, cells, columns)
    from_above = lax.ppermute(low, "gx", to_lower)
    from_below = lax.ppermute(high, "gx", to_upper)
    head, rest, faces, gram = local_sums(atom_values, cells, brick_column, low)
    packed = add_over_devices(packed_gram(gram, faces, from_below, from_above))
    basis, own, down, up = coefficients(packed, head, rest)
    above = lax.ppermute(down, "gx", to_lower)
    below = lax.ppermute(up, "gx", to_upper)
    spread, hots = prepare(basis, cells)
    return atom_fields(columns, own, below, above, spread, hots)


def solution(mesh):
    in_specs = (P(None, None, ("gx", "gz")), P(("gx", "gz")), P(("gx", "gz")))
    out_specs = P(None, None, ("gx", "gz"))
    return jax.shard_map(on_device, mesh=mesh, in_specs=in_specs, out_specs=out_specs, check_vma=False)
```

time: 90.7 us -> 85.5 us (0.943)
  blocking collectives: 0 us -> 38.1 us
  waiting for transfers between devices: 27.8 us -> 3.31 us
  starting transfers between devices: 31 us -> 14 us
  local copies, waits for them, and re-layouts: 6.87 us -> 1.14 us
  Pallas kernels: 24.6 us -> 28.4 us
    all_to_all x0 -> x3, blocking collectives: none -> 38.1 us  [trade(): lax.all_to_all(parts, axes, 0, 0, axis_index_groups=groups, tiled=True)]
    ppermute x9 -> x0, waiting for transfers between devices: 20.3 us -> none  [move(): lax.ppermute(y, ('gx', 'gz'), [(number[place], number[target(*place)]) fo...]
    ppermute x9 -> x0, starting transfers between devices: 15.6 us -> none  [move(): lax.ppermute(y, ('gx', 'gz'), [(number[place], number[target(*place)]) fo...]
    unnamed x16 -> x6, local copies, waits for them, and re-layouts: 6.87 us -> 1.12 us
    pallas_call x5, Pallas kernels: 20.1 us -> 24.4 us  [the longest x1 11.6 us: local_sums(): pl.pallas_call(local_kernel, in_specs=[SMEM, HBM, VMEM, HBM], out_specs=[...]
    ppermute x1, waiting for transfers between devices: 4.2 us -> 1.7 us  [on_device(): from_below = lax.ppermute(high, 'gx', to_upper)]
    ppermute x1, starting transfers between devices: 6.54 us -> 4.45 us  [on_device(): above = lax.ppermute(down, 'gx', to_lower)]
    ppermute x1, waiting for transfers between devices: 3.22 us -> 1.61 us  [on_device(): below = lax.ppermute(up, 'gx', to_upper)]
  transfers between devices with their start and end apart: 13 -> 4, of which waited for: 11 -> 2; matrix products, arithmetic and copies ran while one was open for 0% -> 0% of each run, Pallas kernels for 11% -> 15%
where the time goes in v3:
time: 85.5 us; the launch traced here: 85.2 us
  blocking collectives  38.1 us (45%)
  Pallas kernels  28.4 us (33%)
  starting transfers between devices  14 us (16%)
  waiting for transfers between devices  3.31 us (4%)
  local copies, waits for them, and re-layouts  1.14 us (1%)
    all_to_all x3, blocking collectives, trade(): lax.all_to_all(parts, axes, 0, 0, axis_index_groups=groups, tiled=True)  38.1 us
    pallas_call x1, Pallas kernels, local_sums(): pl.pallas_call(local_kernel, in_specs=[SMEM, HBM, VMEM, HBM], out_specs=[...  11.6 us
    ppermute x1, starting transfers between devices, on_device(): from_above = lax.ppermute(low, 'gx', to_lower)  6.4 us
    pallas_call x1, Pallas kernels, coefficients(): pl.pallas_call(coefs_kernel, in_specs=[VMEM, HBM, HBM], out_specs=[VMEM]...  5.15 us
    pallas_call x1, Pallas kernels, face_sums(): pl.pallas_call(faces_kernel, in_specs=[HBM] * 3, out_specs=[HBM] * 2, scr...  5.03 us
    ppermute x1, starting transfers between devices, on_device(): above = lax.ppermute(down, 'gx', to_lower)  4.45 us
    pallas_call x1, Pallas kernels, atom_fields(): pl.pallas_call(atoms_kernel, in_specs=[VMEM] * 6, out_specs=HBM, scratch_...  4.02 us
    ppermute x1, starting transfers between devices, on_device(): from_below = lax.ppermute(high, 'gx', to_upper)  2.54 us
  transfers between devices with their start and end apart: 4, of which 2 were waited for; matrix products, arithmetic and copies ran while one was open for 0% of the time, Pallas kernels for 15%

profile of v3, /device:TPU:1, one launch (start us, length us, event | category | flops | bytes accessed | tf_op | source)
XLA Modules:
  0.0 85.2 jit_solution(14597822658760990977)
XLA Ops:
  0.0 0.0 copy-start.1
  0.0 0.0 copy-start
  0.0 5.0 %faces.1 = (bf16[640,512]{1,0:T(8,128)(2,1)}, bf16[640,512]{1,0:T(8,128)(2,1)}) custom-call(bf16[160,4,4096]{2,1,0:T(4,128)(2,1)} %values_hbm.3, s32[32,128]{1,0:T(8,128)} %bitcast.6, s32[1,8]{1,0:T(1,128)} %bitcast.9), custom_call_target="tpu_custom_call" | custom-call | tf_op jit(solution)/shard_map/faces/pallas_call | solution.py:108
  5.0 2.5 %collective-permute-start = (bf16[640,512]{1,0:T(8,128)(2,1)}, bf16[640,512]{1,0:T(8,128)(2,1)S(1)}, u32[]{:S(2)}, u32[]{:S(2)}) collective-permute-start(bf16[640,512]{1,0:T(8,128)(2,1)} %get-tuple-element.20), channel_id=1, source_target_pairs={{0,8},{8,16},{16,24},{24,32},{32,40},{40,48},{48,56},{56,64},{64,7... | collective-permute-start | bytes 1966088 | tf_op jit(solution)/shard_map/ppermute | solution.py:405
  7.6 6.4 %collective-permute-start.1 = (bf16[640,512]{1,0:T(8,128)(2,1)}, bf16[640,512]{1,0:T(8,128)(2,1)S(1)}, u32[]{:S(2)}, u32[]{:S(2)}) collective-permute-start(bf16[640,512]{1,0:T(8,128)(2,1)} %get-tuple-element.17.after), channel_id=1, source_target_pairs={{8,0},{16,8},{24,16},{32,24},{40,32},{48,40},{56,48},{64,56},{72,6... | collective-permute-start | bytes 1966088 | tf_op jit(solution)/shard_map/ppermute | solution.py:404
  14.0 0.0 copy-done.1
  14.0 0.0 copy-done
  14.0 0.0 copy-start.2
  14.0 1.1 %copy-done.2 = bf16[640,512]{1,0:T(8,128)(2,1)S(1)} copy-done((bf16[640,512]{1,0:T(8,128)(2,1)S(1)}, bf16[640,512]{1,0:T(8,128)(2,1)}, u32[]{:S(2)}) %copy-start.2) | copy-done | bytes 655384
  15.1 11.6 %local.1 = (bf16[6,640,512]{2,1,0:T(8,128)(2,1)}, bf16[6,640,512]{2,1,0:T(8,128)(2,1)}, bf16[4,640,512]{2,1,0:T(8,128)(2,1)S(1)}, f32[160,160]{1,0:T(8,128)S(1)}) custom-call(s32[8]{0:T(128)S(1)} %copy-done.1, bf16[160,4,4096]{2,1,0:T(4,128)(2,1)} %values_hbm.3, s32[32,128]{1,0:T(8,128)S(1)} %bitcast.7, bf16[640,512]{1,0:T(8,128)(2,1)S(1)} %copy-done.2), custom_call_target="tpu_custom_call" | custom-call | flops 6000000000 | bytes 14000000 | tf_op jit(solution)/shard_map/local/pallas_call | solution.py:164
  26.7 1.7 %collective-permute-done.from_below = bf16[640,512]{1,0:T(8,128)(2,1)S(1)} collective-permute-done((bf16[640,512]{1,0:T(8,128)(2,1)}, bf16[640,512]{1,0:T(8,128)(2,1)S(1)}, u32[]{:S(2)}, u32[]{:S(2)}) %collective-permute-start) | collective-permute-done | bytes 655392 | tf_op jit(solution)/shard_map/ppermute | solution.py:405
  28.4 0.0 collective-permute-done.1.from_above
  28.4 1.0 %cross.1 = f32[128,128]{1,0:T(8,128)S(1)} custom-call(f32[160,160]{1,0:T(8,128)S(1)} %get-tuple-element.18.gram_ref, bf16[4,640,512]{2,1,0:T(8,128)(2,1)S(1)} %get-tuple-element.19.face_ref, bf16[640,512]{1,0:T(8,128)(2,1)S(1)} %collective-permute-done.from_below, bf16[640,512]{1,0:T(8,128)(2,1)S(1)} %collective-permute-done.1.from_above), custom_call_target="tpu_custom_call" | custom-call | tf_op jit(solution)/shard_map/cross/pallas_call | solution.py:229
  29.4 13.3 %all_to_all.15 = f32[32,4,128]{2,1,0:T(4,128)S(1)} all-to-all(f32[32,4,128]{2,1,0:T(4,128)S(1)} %bitcast.5), channel_id=1, replica_groups={{0,1,2,3,4,5,6,7,64,65,66,67,68,69,70,71,128,129,130,131,132,133,134,13..., dimensions={0} | all-to-all | bytes 131072 | tf_op jit(solution)/shard_map/all_to_all | solution.py:247
  42.7 12.5 %all_to_all.16 = f32[8,4,128]{2,1,0:T(4,128)S(1)} all-to-all(f32[8,4,128]{2,1,0:T(4,128)S(1)} %broadcast_in_dim.6), channel_id=1, replica_groups={{0,8,16,24,32,40,48,56},{1,9,17,25,33,41,49,57},{2,10,18,26,34,42,50,58..., dimensions={0} | all-to-all | bytes 32768 | tf_op jit(solution)/shard_map/all_to_all | solution.py:247
  55.2 12.3 %all_to_all.17 = f32[32,4,128]{2,1,0:T(4,128)S(1)} all-to-all(f32[32,4,128]{2,1,0:T(4,128)S(1)} %broadcast_in_dim.7), channel_id=1, replica_groups={{0,1,2,3,4,5,6,7,64,65,66,67,68,69,70,71,128,129,130,131,132,133,134,13..., dimensions={0} | all-to-all | bytes 131072 | tf_op jit(solution)/shard_map/all_to_all | solution.py:247
  67.5 5.2 %coefs.1 = (f32[8,160]{1,0:T(8,128)S(1)}, f32[32,3072]{1,0:T(8,128)S(1)}, f32[32,1024]{1,0:T(8,128)S(1)}, f32[32,1024]{1,0:T(8,128)S(1)}) custom-call(f32[128,128]{1,0:T(8,128)S(1)} %bitcast.4, bf16[6,640,512]{2,1,0:T(8,128)(2,1)} %get-tuple-element.21.head_hbm, bf16[6,640,512]{2,1,0:T(8,128)(2,1)} %get-tuple-element.22.rest_hbm), custom_call_target="tpu_custom_call" | custom-call | tf_op jit(solution)/shard_map/coefs/pallas_call | solution.py:304
  72.7 0.6 collective-permute-start.2
  73.3 4.5 %collective-permute-start.3 = (f32[32,1024]{1,0:T(8,128)S(1)}, f32[32,1024]{1,0:T(8,128)S(1)}, u32[]{:S(2)}, u32[]{:S(2)}) collective-permute-start(f32[32,1024]{1,0:T(8,128)S(1)} %get-tuple-element.25), channel_id=1, source_target_pairs={{8,0},{16,8},{24,16},{32,24},{40,32},{48,40},{56,48},{64,56},{72,6... | collective-permute-start | bytes 393224 | tf_op jit(solution)/shard_map/ppermute | solution.py:409
  77.8 1.6 %prepare.1 = (bf16[640,128]{1,0:T(8,128)(2,1)S(1)}, bf16[8,512,512]{2,1,0:T(8,128)(2,1)S(1)}) custom-call(f32[8,160]{1,0:T(8,128)S(1)} %get-tuple-element.26.basis_ref, s32[32,128]{1,0:T(8,128)S(1)} %bitcast.8), custom_call_target="tpu_custom_call" | custom-call | tf_op jit(solution)/shard_map/prepare/pallas_call | solution.py:341
  79.4 1.6 %collective-permute-done.2.below_ref = f32[32,1024]{1,0:T(8,128)S(1)} collective-permute-done((f32[32,1024]{1,0:T(8,128)S(1)}, f32[32,1024]{1,0:T(8,128)S(1)}, u32[]{:S(2)}, u32[]{:S(2)}) %collective-permute-start.2) | collective-permute-done | bytes 131104 | tf_op jit(solution)/shard_map/ppermute | solution.py:410
  81.0 0.0 collective-permute-done.3.above_ref
  81.0 4.0 %atoms.1 = bf16[160,4,4096]{2,1,0:T(4,128)(2,1)} custom-call(f32[32,3072]{1,0:T(8,128)S(1)} %get-tuple-element.23.own_ref, f32[32,1024]{1,0:T(8,128)S(1)} %collective-permute-done.2.below_ref, f32[32,1024]{1,0:T(8,128)S(1)} %collective-permute-done.3.above_ref, bf16[640,128]{1,0:T(8,128)(2,1)S(1)} %get-tuple-element.27.spread_ref, ...), custom_call_target="tpu_custom_call" | custom-call | tf_op jit(solution)/shard_map/atoms/pallas_call | solution.py:383
  (4 shorter events, 0.1 us)
Async XLA Ops:
  0.0 14.0 %copy-start.1 = (s32[8]{0:T(128)S(1)}, s32[8]{0:T(128)}, u32[]{:S(2)}) copy-start(s32[8]{0:T(128)} %column_ref.1) | copy-start | bytes 100
  0.0 14.0 %copy-start = (s32[4096]{0:T(1024)S(1)}, s32[4096]{0:T(1024)}, u32[]{:S(2)}) copy-start(s32[4096]{0:T(1024)} %param.4) | copy-start | bytes 49156
  5.0 23.3 %collective-permute-start = (bf16[640,512]{1,0:T(8,128)(2,1)}, bf16[640,512]{1,0:T(8,128)(2,1)S(1)}, u32[]{:S(2)}, u32[]{:S(2)}) collective-permute-start(bf16[640,512]{1,0:T(8,128)(2,1)} %get-tuple-element.20), channel_id=1, source_target_pairs={{0,8},{8,16},{16,24},{24,32},{32,40},{40,48},{48,56},{56,64},{64,7... | collective-permute-start | bytes 1966088 | tf_op jit(solution)/shard_map/ppermute | solution.py:405
  7.6 20.8 %collective-permute-start.1 = (bf16[640,512]{1,0:T(8,128)(2,1)}, bf16[640,512]{1,0:T(8,128)(2,1)S(1)}, u32[]{:S(2)}, u32[]{:S(2)}) collective-permute-start(bf16[640,512]{1,0:T(8,128)(2,1)} %get-tuple-element.17.after), channel_id=1, source_target_pairs={{8,0},{16,8},{24,16},{32,24},{40,32},{48,40},{56,48},{64,56},{72,6... | collective-permute-start | bytes 1966088 | tf_op jit(solution)/shard_map/ppermute | solution.py:404
  14.0 1.1 %copy-start.2 = (bf16[640,512]{1,0:T(8,128)(2,1)S(1)}, bf16[640,512]{1,0:T(8,128)(2,1)}, u32[]{:S(2)}) copy-start(bf16[640,512]{1,0:T(8,128)(2,1)} %get-tuple-element.17.after) | copy-start | bytes 1966084
  72.7 8.3 %collective-permute-start.2 = (f32[32,1024]{1,0:T(8,128)S(1)}, f32[32,1024]{1,0:T(8,128)S(1)}, u32[]{:S(2)}, u32[]{:S(2)}) collective-permute-start(f32[32,1024]{1,0:T(8,128)S(1)} %get-tuple-element.24), channel_id=1, source_target_pairs={{0,8},{8,16},{16,24},{24,32},{32,40},{40,48},{48,56},{56,64},{64,7... | collective-permute-start | bytes 393224 | tf_op jit(solution)/shard_map/ppermute | solution.py:410
  73.3 7.7 %collective-permute-start.3 = (f32[32,1024]{1,0:T(8,128)S(1)}, f32[32,1024]{1,0:T(8,128)S(1)}, u32[]{:S(2)}, u32[]{:S(2)}) collective-permute-start(f32[32,1024]{1,0:T(8,128)S(1)} %get-tuple-element.25), channel_id=1, source_target_pairs={{8,0},{16,8},{24,16},{32,24},{40,32},{48,40},{56,48},{64,56},{72,6... | collective-permute-start | bytes 393224 | tf_op jit(solution)/shard_map/ppermute | solution.py:409

commit v4 on v3

--- a/solution.py
+++ b/solution.py
@@ -1,3 +1,5 @@
+import math
+
 import jax
 import jax.numpy as jnp
 from jax import lax
@@ -16,6 +18,9 @@
 PER_BRICK = 512
 BRICKS = 8
 COEFS = MODES * FIELDS
+WIRE = ROWS + 16
+TOP = 32767.0
+STEPS = 8 / math.log(2)
 SPLIT = 128
 TAIL = SNAPS - SPLIT
 LANES = CW // 128
@@ -65,6 +70,26 @@
 def brick_copy(values_hbm, held, sems, brick, slot):
     source = values_hbm.at[:, :, pl.ds(brick * PER_BRICK, PER_BRICK)]
     return pltpu.make_async_copy(source, held.at[slot], sems.at[slot])
+
+
+def encode(total, out_ref):
+    for t in range(LANES):
+        lanes = slice(t * 128, (t + 1) * 128)
+        most = jnp.max(jnp.abs(total[t]), axis=0, keepdims=True)
+        code = jnp.ceil(jnp.log(jnp.maximum(most, 1e-30)) * STEPS)
+        scale = jnp.exp(code * (-1 / STEPS)) * TOP
+        for f in range(FIELDS):
+            steps = jnp.round(total[t, pl.ds(f, SNAPS, stride=FIELDS), :] * scale)
+            out_ref[f * SNAPS : (f + 1) * SNAPS, lanes] = jnp.clip(steps, -TOP, TOP).astype(jnp.int32).astype(jnp.int16)
+        out_ref[ROWS:, lanes] = jnp.broadcast_to(code, (WIRE - ROWS, 128)).astype(jnp.int32).astype(jnp.int16)
+
+
+def wire_steps(wire, rows):
+    return wire[rows, :].astype(jnp.int32).astype(F32)
+
+
+def wire_scale(wire):
+    return jnp.exp(wire_steps(wire, slice(ROWS, WIRE))[:1] * (1 / STEPS)) * (1 / TOP)
 
 
 HBM = pl.BlockSpec(memory_space=pltpu.HBM)
@@ -96,15 +121,14 @@
             sums = part if sums is None else sums + part
         for t in range(LANES):
             total[i, t] = sums[:, t * 128 : (t + 1) * 128]
-        for f in range(FIELDS):
-            face[i, f * SNAPS : (f + 1) * SNAPS, :] = one_field(total.at[i], f).astype(BF16)
+        encode(total.at[i], face.at[i])
         outputs[i].start()
     for copy in outputs:
         copy.wait()
 
 
 def face_sums(values, cells, columns):
-    shape = jax.ShapeDtypeStruct((ROWS, CW), BF16)
+    shape = jax.ShapeDtypeStruct((WIRE, CW), jnp.int16)
     return pl.pallas_call(
         faces_kernel,
         in_specs=[HBM] * 3,
@@ -112,7 +136,7 @@
         scratch_shapes=[
             pltpu.VMEM((4, SNAPS, FIELDS, PER_BRICK), BF16),
             pltpu.VMEM((2, LANES, ROWS, 128), F32),
-            pltpu.VMEM((2, ROWS, CW), BF16),
+            pltpu.VMEM((2, WIRE, CW), jnp.int16),
             pltpu.VMEM((BRICKS * LANES, 128), jnp.int32),
             pltpu.VMEM((1, BRICKS), jnp.int32),
             pltpu.SemaphoreType.DMA((4,)),
@@ -125,21 +149,29 @@
     )(values, cells, columns)
 
 
-def local_kernel(column_ref, values_hbm, cells, after, head_hbm, rest_hbm, face_ref, gram_ref, held, total, heads, rests, sems, out_sems):
+def local_kernel(
+    column_ref, values_hbm, cells, after, head_hbm, rest_hbm, hots_hbm, face_ref, gram_ref, down_ref, up_ref,
+    held, total, heads, rests, hots, sems, out_sems, hot_sems
+):
     copies = [brick_copy(values_hbm, held, sems, brick, brick) for brick in range(BRICKS)]
     for copy in copies:
         copy.start()
+    outputs = []
     total[...] = jnp.zeros_like(total)
     for brick in range(BRICKS):
         hot = cell_hot(cells, brick)
+        hots[brick] = hot
+        outputs.append(pltpu.make_async_copy(hots.at[brick], hots_hbm.at[brick], hot_sems.at[brick]))
+        outputs[-1].start()
         copies[brick].wait()
         sums = dot_nt(held[brick].reshape(ROWS, PER_BRICK), hot)
         column = column_ref[brick]
         for t in range(LANES):
             total[column, t] += sums[:, t * 128 : (t + 1) * 128]
+    encode(total.at[1], down_ref)
+    encode(total.at[CX], up_ref)
     same = jnp.zeros((SNAPS, SNAPS), F32)
     mixed = jnp.zeros((SNAPS, SNAPS), F32)
-    outputs = []
     for k in range(EXT):
         for f in range(FIELDS):
             rows = slice(f * SNAPS, (f + 1) * SNAPS)
@@ -161,25 +193,31 @@
 
 def local_sums(values, cells, columns, after):
     half = jax.ShapeDtypeStruct((EXT, ROWS, CW), BF16)
+    wire = jax.ShapeDtypeStruct((WIRE, CW), jnp.int16)
     return pl.pallas_call(
         local_kernel,
         in_specs=[SMEM, HBM, VMEM, HBM],
-        out_specs=[HBM, HBM, VMEM, VMEM],
+        out_specs=[HBM] * 3 + [VMEM] * 4,
         scratch_shapes=[
             pltpu.VMEM((BRICKS, SNAPS, FIELDS, PER_BRICK), BF16),
             pltpu.VMEM((EXT, LANES, ROWS, 128), F32),
             pltpu.VMEM((EXT, ROWS, CW), BF16),
             pltpu.VMEM((EXT, ROWS, CW), BF16),
+            pltpu.VMEM((BRICKS, CW, PER_BRICK), BF16),
             pltpu.SemaphoreType.DMA((BRICKS,)),
             pltpu.SemaphoreType.DMA((2, EXT)),
+            pltpu.SemaphoreType.DMA((BRICKS,)),
         ],
         out_shape=[
             half,
             half,
+            jax.ShapeDtypeStruct((BRICKS, CW, PER_BRICK), BF16),
             jax.ShapeDtypeStruct((4, ROWS, CW), BF16),
             jax.ShapeDtypeStruct((SNAPS, SNAPS), F32),
+            wire,
+            wire,
         ],
-        compiler_params=params(50),
+        compiler_params=params(48),
         cost_estimate=pl.CostEstimate(flops=6_000_000_000, bytes_accessed=14_000_000, transcendentals=0),
         name="local",
     )(columns, values, cells, after)
@@ -217,11 +255,13 @@
 
 def cross_kernel(gram_ref, face_ref, from_below, from_above, packed_ref):
     cross = jnp.zeros((SNAPS, SNAPS), F32)
-    for f in range(FIELDS):
-        rows = slice(f * SNAPS, (f + 1) * SNAPS)
-        for i, received in enumerate((from_below, from_above)):
-            other = received[rows, :]
-            cross += dot_nt(face_ref[2 * i, rows, :], other) + dot_nt(face_ref[2 * i + 1, rows, :], other)
+    for i, received in enumerate((from_below, from_above)):
+        scale = wire_scale(received)
+        for f in range(FIELDS):
+            rows = slice(f * SNAPS, (f + 1) * SNAPS)
+            head, rest = halves(wire_steps(received, rows) * scale)
+            own = face_ref[2 * i, rows, :]
+            cross += dot_nt(own, head) + dot_nt(own, rest) + dot_nt(face_ref[2 * i + 1, rows, :], head)
     packed_ref[...] = pack(gram_ref[...] + cross + cross.T)
 
 
@@ -269,129 +309,92 @@
     return jnp.concatenate([part * scale for part in parts], axis=1)[:, :SNAPS]
 
 
-def coefs_kernel(packed_ref, head_hbm, rest_hbm, basis_ref, own_ref, down_ref, up_ref, heads, rests, sems):
-    copies = [
-        pltpu.make_async_copy(head_hbm, heads, sems.at[0]),
-        pltpu.make_async_copy(rest_hbm, rests, sems.at[1]),
-    ]
-    for copy in copies:
+def spread_matrix(basis):
+    snap = lax.broadcasted_iota(jnp.int32, (SNAPS, ROWS), 0)
+    column = lax.broadcasted_iota(jnp.int32, (SNAPS, ROWS), 1)
+    repeat = (snap == column // FIELDS).astype(F32).astype(BF16)
+    both = dot(jnp.concatenate(halves(basis), axis=0), repeat)
+    field = lax.broadcasted_iota(jnp.int32, (COEFS, ROWS), 0) // MODES
+    mine = field == lax.broadcasted_iota(jnp.int32, (COEFS, ROWS), 1) % FIELDS
+    head = jnp.where(mine, jnp.concatenate([both[:MODES]] * FIELDS, axis=0), 0.0)
+    rest = jnp.where(mine, jnp.concatenate([both[MODES:]] * FIELDS, axis=0), 0.0)
+    return jnp.concatenate([head, head, rest, jnp.zeros_like(rest)], axis=0).T.astype(BF16)
+
+
+def output_kernel(
+    packed_ref, column_hbm, head_hbm, rest_hbm, hots_hbm, *refs
+):
+    wires_hbm, out_hbm = refs[:4], refs[4]
+    heads, rests, hots, wires, columns, held, sems, hot_sems, out_sems = refs[5:]
+    sources = (head_hbm, rest_hbm) + wires_hbm + (column_hbm,)
+    places = (heads, rests) + tuple(wires.at[i] for i in range(4)) + (columns,)
+    copies = [pltpu.make_async_copy(a, b, sems.at[i]) for i, (a, b) in enumerate(zip(sources, places))]
+    hot_copies = [pltpu.make_async_copy(hots_hbm.at[i], hots.at[i], hot_sems.at[i]) for i in range(BRICKS)]
+    for copy in copies + hot_copies:
         copy.start()
     gram = unpack(packed_ref[...])
     basis = gram[:MODES, :]
     for _ in range(SWEEPS):
         basis = orthonormal(exact_dot(basis, gram))
-    basis_ref[...] = basis
     wide = jnp.concatenate([basis] * FIELDS, axis=1)
     tall = jnp.concatenate([wide] * FIELDS, axis=0)
     row_field = lax.broadcasted_iota(jnp.int32, (COEFS, ROWS), 0) // MODES
     col_field = lax.broadcasted_iota(jnp.int32, (COEFS, ROWS), 1) // SNAPS
     head, rest = halves(jnp.where(row_field == col_field, tall, 0.0))
     both = jnp.concatenate([head, rest], axis=0)
+    spread = spread_matrix(basis)
+
+    def coefficients(heads_of, rests_of):
+        pair = dot(both, heads_of)
+        return pair[:COEFS] + pair[COEFS:] + dot(head, rests_of)
+
     for copy in copies:
         copy.wait()
+    whole = []
     for k in range(EXT):
-        pair = dot(both, heads[k])
-        own = pair[:COEFS] + pair[COEFS:] + dot(head, rests[k])
-        own_ref[:, k * CW : (k + 1) * CW] = own
-        if k < 2:
-            down_ref[:, k * CW : (k + 1) * CW] = own
-        if k >= CX:
-            up_ref[:, (k - CX) * CW : (k - CX + 1) * CW] = own
-
-
-def coefficients(packed, head, rest):
-    side = jax.ShapeDtypeStruct((COEFS, 2 * CW), F32)
+        value = coefficients(heads[k], rests[k])
+        if k in (0, 1, CX, CX + 1):
+            wire = wires.at[(0, 1, 0, 0, 2, 3)[k]]
+            value += coefficients(*halves(wire_steps(wire, slice(0, ROWS)))) * wire_scale(wire)
+        whole.append(jnp.concatenate(halves(value), axis=0))
+    blank = jnp.zeros((COEFS, PER_BRICK), BF16)
+    outputs = []
+    for brick in range(BRICKS):
+        column = columns[:, brick : brick + 1]
+        mine = whole[0]
+        for k in range(1, EXT):
+            mine = jnp.where(column == k, whole[k], mine)
+        hot_copies[brick].wait()
+        picked = dot(mine, hots[brick]).astype(BF16)
+        stacked = jnp.concatenate([picked, picked[:COEFS], blank], axis=0)
+        held[brick] = dot(spread, stacked).astype(BF16).reshape(SNAPS, FIELDS, PER_BRICK)
+        target = out_hbm.at[:, :, pl.ds(brick * PER_BRICK, PER_BRICK)]
+        outputs.append(pltpu.make_async_copy(held.at[brick], target, out_sems.at[brick]))
+        outputs[-1].start()
+    for copy in outputs:
+        copy.wait()
+
+
+def atom_fields(packed, columns, head, rest, hots, wires):
     return pl.pallas_call(
-        coefs_kernel,
-        in_specs=[VMEM, HBM, HBM],
-        out_specs=[VMEM] * 4,
+        output_kernel,
+        in_specs=[VMEM] + [HBM] * 8,
+        out_specs=HBM,
         scratch_shapes=[
             pltpu.VMEM((EXT, ROWS, CW), BF16),
             pltpu.VMEM((EXT, ROWS, CW), BF16),
-            pltpu.SemaphoreType.DMA((2,)),
-        ],
-        out_shape=[
-            jax.ShapeDtypeStruct((MODES, SNAPS), F32),
-            jax.ShapeDtypeStruct((COEFS, EXT * CW), F32),
-            side,
-            side,
-        ],
-        compiler_params=params(52),
-        name="coefs",
-    )(packed, head, rest)
-
-
-def prepare_kernel(basis_ref, cells, spread_ref, hots_ref):
-    head, rest = halves(basis_ref[...])
-    snap = lax.broadcasted_iota(jnp.int32, (SNAPS, ROWS), 0)
-    column = lax.broadcasted_iota(jnp.int32, (SNAPS, ROWS), 1)
-    repeat = (snap == column // FIELDS).astype(F32).astype(BF16)
-    both = dot(jnp.concatenate([head, rest], axis=0), repeat)
-    field = lax.broadcasted_iota(jnp.int32, (COEFS, ROWS), 0) // MODES
-    mine = field == lax.broadcasted_iota(jnp.int32, (COEFS, ROWS), 1) % FIELDS
-    head = jnp.where(mine, jnp.concatenate([both[:MODES]] * FIELDS, axis=0), 0.0)
-    rest = jnp.where(mine, jnp.concatenate([both[MODES:]] * FIELDS, axis=0), 0.0)
-    stacked = jnp.concatenate([head, head, rest, jnp.zeros_like(rest)], axis=0)
-    spread_ref[...] = stacked.T.astype(BF16)
-    for brick in range(BRICKS):
-        hots_ref[brick] = cell_hot(cells, brick)
-
-
-def prepare(basis, cells):
-    return pl.pallas_call(
-        prepare_kernel,
-        in_specs=[VMEM, VMEM],
-        out_specs=[VMEM, VMEM],
-        out_shape=[
-            jax.ShapeDtypeStruct((ROWS, 4 * COEFS), BF16),
-            jax.ShapeDtypeStruct((BRICKS, CW, PER_BRICK), BF16),
-        ],
-        compiler_params=params(16),
-        name="prepare",
-    )(basis, cells)
-
-
-def atoms_kernel(own_ref, below_ref, above_ref, spread_ref, hots_ref, column_ref, out_hbm, held, sems):
-    whole = []
-    for k in range(EXT):
-        value = own_ref[:, k * CW : (k + 1) * CW]
-        if k < 2:
-            value = value + below_ref[:, k * CW : (k + 1) * CW]
-        if k >= CX:
-            value = value + above_ref[:, (k - CX) * CW : (k - CX + 1) * CW]
-        whole.append(jnp.concatenate(halves(value), axis=0))
-    blank = jnp.zeros((COEFS, PER_BRICK), BF16)
-    copies = []
-    for brick in range(BRICKS):
-        column = column_ref[:, brick : brick + 1]
-        mine = whole[0]
-        for k in range(1, EXT):
-            mine = jnp.where(column == k, whole[k], mine)
-        picked = dot(mine, hots_ref[brick]).astype(BF16)
-        stacked = jnp.concatenate([picked, picked[:COEFS], blank], axis=0)
-        fields = dot(spread_ref[...], stacked).astype(BF16)
-        held[brick] = fields.reshape(SNAPS, FIELDS, PER_BRICK)
-        target = out_hbm.at[:, :, pl.ds(brick * PER_BRICK, PER_BRICK)]
-        copy = pltpu.make_async_copy(held.at[brick], target, sems.at[brick])
-        copy.start()
-        copies.append(copy)
-    for copy in copies:
-        copy.wait()
-
-
-def atom_fields(columns, own, below, above, spread, hots):
-    return pl.pallas_call(
-        atoms_kernel,
-        in_specs=[VMEM] * 6,
-        out_specs=HBM,
-        scratch_shapes=[
+            pltpu.VMEM((BRICKS, CW, PER_BRICK), BF16),
+            pltpu.VMEM((4, WIRE, CW), jnp.int16),
+            pltpu.VMEM((1, BRICKS), jnp.int32),
             pltpu.VMEM((BRICKS, SNAPS, FIELDS, PER_BRICK), BF16),
+            pltpu.SemaphoreType.DMA((7,)),
+            pltpu.SemaphoreType.DMA((BRICKS,)),
             pltpu.SemaphoreType.DMA((BRICKS,)),
         ],
         out_shape=jax.ShapeDtypeStruct((SNAPS, FIELDS, BRICKS * PER_BRICK), BF16),
-        compiler_params=params(32),
-        name="atoms",
-    )(own, below, above, spread, hots, columns)
+        compiler_params=params(51),
+        name="output",
+    )(packed, columns, head, rest, hots, *wires)
 
 
 def on_device(atom_values, atom_cell, brick_column):
@@ -403,13 +406,12 @@
     low, high = face_sums(atom_values, cells, columns)
     from_above = lax.ppermute(low, "gx", to_lower)
     from_below = lax.ppermute(high, "gx", to_upper)
-    head, rest, faces, gram = local_sums(atom_values, cells, brick_column, low)
+    head, rest, hots, faces, gram, down, up = local_sums(atom_values, cells, brick_column, low)
+    second_above = lax.ppermute(down, "gx", to_lower)
+    second_below = lax.ppermute(up, "gx", to_upper)
     packed = add_over_devices(packed_gram(gram, faces, from_below, from_above))
-    basis, own, down, up = coefficients(packed, head, rest)
-    above = lax.ppermute(down, "gx", to_lower)
-    below = lax.ppermute(up, "gx", to_upper)
-    spread, hots = prepare(basis, cells)
-    return atom_fields(columns, own, below, above, spread, hots)
+    wires = (second_below, from_below, from_above, second_above)
+    return atom_fields(packed, columns, head, rest, hots, wires)
 
 
 def solution(mesh):

time: 85.5 us -> 90 us (1.053)
  blocking collectives: 38.1 us -> 26.6 us
  starting transfers between devices: 14 us -> 21.6 us
  waiting for transfers between devices: 3.31 us -> 7.36 us
  Pallas kernels: 28.4 us -> 32 us
    all_to_all x3 -> x2, blocking collectives: 38.1 us -> 26.6 us  [trade(): lax.all_to_all(parts, axes, 0, 0, axis_index_groups=groups, tiled=True)]
    all_to_all x0 -> x1, starting transfers between devices: none -> 7.82 us  [trade(): lax.all_to_all(parts, axes, 0, 0, axis_index_groups=groups, tiled=True)]
    all_to_all x0 -> x1, waiting for transfers between devices: none -> 7.34 us  [trade(): lax.all_to_all(parts, axes, 0, 0, axis_index_groups=groups, tiled=True)]
    pallas_call x1, Pallas kernels: 11.6 us -> 13.9 us  [local_sums(): pl.pallas_call(local_kernel, in_specs=[SMEM, HBM, VMEM, HBM], out_specs=[...]
    ppermute x1, waiting for transfers between devices: 1.7 us -> 0.01 us  [on_device(): from_below = lax.ppermute(high, 'gx', to_upper)]
    ppermute x2, waiting for transfers between devices: 1.61 us -> 0.01 us  [the longest x1 0.01 us: on_device(): second_below = lax.ppermute(up, 'gx', to_upper)]
    pallas_call x3 -> x1, Pallas kernels: 10.8 us -> 11.2 us  [atom_fields(): pl.pallas_call(output_kernel, in_specs=[VMEM] + [HBM] * 8, out_specs=HBM,...]
  transfers between devices with their start and end apart: 4 -> 5, of which waited for: 2 -> 1; matrix products, arithmetic and copies ran while one was open for 0% -> 1% of each run, Pallas kernels for 15% -> 17%
where the time goes in v4:
time: 90 us; the launch traced here: 89.7 us
  Pallas kernels  32 us (36%)
  blocking collectives  26.6 us (30%)
  starting transfers between devices  21.6 us (24%)
  waiting for transfers between devices  7.36 us (8%)
  local copies, waits for them, and re-layouts  1.78 us (2%)
    all_to_all x2, blocking collectives, trade(): lax.all_to_all(parts, axes, 0, 0, axis_index_groups=groups, tiled=True)  26.6 us
    pallas_call x1, Pallas kernels, local_sums(): pl.pallas_call(local_kernel, in_specs=[SMEM, HBM, VMEM, HBM], out_specs=[...  13.9 us
    pallas_call x1, Pallas kernels, atom_fields(): pl.pallas_call(output_kernel, in_specs=[VMEM] + [HBM] * 8, out_specs=HBM,...  11.2 us
    all_to_all x1, starting transfers between devices, trade(): lax.all_to_all(parts, axes, 0, 0, axis_index_groups=groups, tiled=True)  7.82 us
    all_to_all x1, waiting for transfers between devices, trade(): lax.all_to_all(parts, axes, 0, 0, axis_index_groups=groups, tiled=True)  7.34 us
    ppermute x1, starting transfers between devices, on_device(): from_above = lax.ppermute(low, 'gx', to_lower)  6.4 us
    pallas_call x1, Pallas kernels, face_sums(): pl.pallas_call(faces_kernel, in_specs=[HBM] * 3, out_specs=[HBM] * 2, scr...  5.45 us
    ppermute x1, starting transfers between devices, on_device(): second_above = lax.ppermute(down, 'gx', to_lower)  4.77 us
  transfers between devices with their start and end apart: 5, of which 1 were waited for; matrix products, arithmetic and copies ran while one was open for 1% of the time, Pallas kernels for 17%

profile of v4, /device:TPU:1, one launch (start us, length us, event | category | flops | bytes accessed | tf_op | source)
XLA Modules:
  0.0 89.7 jit_solution(16700365079133663460)
XLA Ops:
  0.0 0.0 copy-start.1
  0.0 0.0 copy-start
  0.0 5.4 %faces.1 = (s16[656,512]{1,0:T(8,128)(2,1)}, s16[656,512]{1,0:T(8,128)(2,1)}) custom-call(bf16[160,4,4096]{2,1,0:T(4,128)(2,1)} %values_hbm.3, s32[32,128]{1,0:T(8,128)} %bitcast.6, s32[1,8]{1,0:T(1,128)} %bitcast.8), custom_call_target="tpu_custom_call" | custom-call | tf_op jit(solution)/shard_map/faces/pallas_call | solution.py:132
  5.5 2.5 %collective-permute-start = (s16[656,512]{1,0:T(8,128)(2,1)}, s16[656,512]{1,0:T(8,128)(2,1)S(1)}, u32[]{:S(2)}, u32[]{:S(2)}) collective-permute-start(s16[656,512]{1,0:T(8,128)(2,1)} %get-tuple-element.17), channel_id=1, source_target_pairs={{0,8},{8,16},{16,24},{24,32},{32,40},{40,48},{48,56},{56,64},{64,7... | collective-permute-start | bytes 2015240 | tf_op jit(solution)/shard_map/ppermute | solution.py:408
  8.0 6.4 %collective-permute-start.1 = (s16[656,512]{1,0:T(8,128)(2,1)}, s16[656,512]{1,0:T(8,128)(2,1)S(1)}, u32[]{:S(2)}, u32[]{:S(2)}) collective-permute-start(s16[656,512]{1,0:T(8,128)(2,1)} %get-tuple-element.14.after), channel_id=1, source_target_pairs={{8,0},{16,8},{24,16},{32,24},{40,32},{48,40},{56,48},{64,56},{72,6... | collective-permute-start | bytes 2015240 | tf_op jit(solution)/shard_map/ppermute | solution.py:407
  14.4 0.0 copy-done.1
  14.4 0.0 copy-done
  14.4 0.0 copy-start.2
  14.4 1.1 %copy-done.2 = s16[656,512]{1,0:T(8,128)(2,1)S(1)} copy-done((s16[656,512]{1,0:T(8,128)(2,1)S(1)}, s16[656,512]{1,0:T(8,128)(2,1)}, u32[]{:S(2)}) %copy-start.2) | copy-done | bytes 671768
  15.5 13.9 %local.1 = (bf16[6,640,512]{2,1,0:T(8,128)(2,1)}, bf16[6,640,512]{2,1,0:T(8,128)(2,1)}, bf16[8,512,512]{2,1,0:T(8,128)(2,1)}, bf16[4,640,512]{2,1,0:T(8,128)(2,1...) custom-call(s32[8]{0:T(128)S(1)} %copy-done.1, ...), custom_call_target="tpu_custom_call" | custom-call | flops 6000000000 | bytes 14000000 | tf_op jit(solution)/shard_map/local/pallas_call | solution.py:197
  29.5 0.1 collective-permute-start.2
  29.6 4.8 %collective-permute-start.3 = (s16[656,512]{1,0:T(8,128)(2,1)S(1)}, s16[656,512]{1,0:T(8,128)(2,1)S(1)}, u32[]{:S(2)}, u32[]{:S(2)}) collective-permute-start(s16[656,512]{1,0:T(8,128)(2,1)S(1)} %get-tuple-element.22), channel_id=1, source_target_pairs={{8,0},{16,8},{24,16},{32,24},{40,32},{48,40},{56,48},{64,56},{72,6... | collective-permute-start | bytes 2015240 | tf_op jit(solution)/shard_map/ppermute | solution.py:410
  34.3 0.0 collective-permute-done.from_below.refs_1_
  34.3 0.0 collective-permute-done.1.from_above.refs_2_
  34.3 1.5 %cross.1 = f32[128,128]{1,0:T(8,128)S(1)} custom-call(f32[160,160]{1,0:T(8,128)S(1)} %get-tuple-element.15.gram_ref, bf16[4,640,512]{2,1,0:T(8,128)(2,1)S(1)} %get-tuple-element.16.face_ref, s16[656,512]{1,0:T(8,128)(2,1)S(1)} %collective-permute-done.from_below.refs_1_, s16[656,512]{1,0:T(8,128)(2,1)S(1)} %collective-permute-done.1.from_above.refs_2_), custom_call_target="tpu_custom_call" | custom-call | tf_op jit(solution)/shard_map/cross/pallas_call | solution.py:269
  35.8 17.6 %all_to_all.15 = f32[32,4,128]{2,1,0:T(4,128)S(1)} all-to-all(f32[32,4,128]{2,1,0:T(4,128)S(1)} %bitcast.5), channel_id=1, replica_groups={{0,1,2,3,4,5,6,7,64,65,66,67,68,69,70,71,128,129,130,131,132,133,134,13..., dimensions={0} | all-to-all | bytes 131072 | tf_op jit(solution)/shard_map/all_to_all | solution.py:287
  53.5 9.0 %all_to_all.16 = f32[8,4,128]{2,1,0:T(4,128)S(1)} all-to-all(f32[8,4,128]{2,1,0:T(4,128)S(1)} %broadcast_in_dim.6), channel_id=1, replica_groups={{0,8,16,24,32,40,48,56},{1,9,17,25,33,41,49,57},{2,10,18,26,34,42,50,58..., dimensions={0} | all-to-all | bytes 32768 | tf_op jit(solution)/shard_map/all_to_all | solution.py:287
  62.5 0.6 broadcast_in_dim.7
  63.2 7.8 %all-to-all-start.2 = ((f32[32,4,128]{2,1,0:T(4,128)}), f32[32,4,128]{2,1,0:T(4,128)S(1)}, u32[]{:S(2)}, u32[]{:S(2)}) async-start(f32[32,4,128]{2,1,0:T(4,128)} %broadcast_in_dim.7), calls=%async_computation.2 | async-start | bytes 131072 | tf_op jit(solution)/shard_map/all_to_all | solution.py:287
  71.0 0.0 collective-permute-done.2.refs_0_
  71.0 0.0 collective-permute-done.3.refs_3_
  71.0 7.3 %all-to-all-done.2 = f32[32,4,128]{2,1,0:T(4,128)S(1)} async-done(((f32[32,4,128]{2,1,0:T(4,128)}), f32[32,4,128]{2,1,0:T(4,128)S(1)}, u32[]{:S(2)}, u32[]{:S(2)}) %all-to-all-start.2) | async-done | bytes 65568 | tf_op jit(solution)/shard_map/all_to_all | solution.py:287
  78.4 11.2 %output.1 = bf16[160,4,4096]{2,1,0:T(4,128)(2,1)} custom-call(f32[128,128]{1,0:T(8,128)S(1)} %bitcast.4, s32[1,8]{1,0:T(1,128)S(1)} %bitcast.9, bf16[6,640,512]{2,1,0:T(8,128)(2,1)} %get-tuple-element.18.head_hbm, bf16[6,640,512]{2,1,0:T(8,128)(2,1)} %get-tuple-element.19.rest_hbm, bf16[8,512,512]{2,1,0:T(8,128)(2,1)} %get-tuple-element.20.hots_hbm, ...), custom_call_target="tpu_custom_call" | custom-call | tf_op jit(solution)/shard_map/output/pallas_call | solution.py:379
  (3 shorter events, 0.1 us)
Async XLA Ops:
  0.0 14.4 %copy-start.1 = (s32[8]{0:T(128)S(1)}, s32[8]{0:T(128)}, u32[]{:S(2)}) copy-start(s32[8]{0:T(128)} %column_ref.1) | copy-start | bytes 100
  0.0 14.4 %copy-start = (s32[4096]{0:T(1024)S(1)}, s32[4096]{0:T(1024)}, u32[]{:S(2)}) copy-start(s32[4096]{0:T(1024)} %param.4) | copy-start | bytes 49156
  5.5 28.9 %collective-permute-start = (s16[656,512]{1,0:T(8,128)(2,1)}, s16[656,512]{1,0:T(8,128)(2,1)S(1)}, u32[]{:S(2)}, u32[]{:S(2)}) collective-permute-start(s16[656,512]{1,0:T(8,128)(2,1)} %get-tuple-element.17), channel_id=1, source_target_pairs={{0,8},{8,16},{16,24},{24,32},{32,40},{40,48},{48,56},{56,64},{64,7... | collective-permute-start | bytes 2015240 | tf_op jit(solution)/shard_map/ppermute | solution.py:408
  8.0 26.3 %collective-permute-start.1 = (s16[656,512]{1,0:T(8,128)(2,1)}, s16[656,512]{1,0:T(8,128)(2,1)S(1)}, u32[]{:S(2)}, u32[]{:S(2)}) collective-permute-start(s16[656,512]{1,0:T(8,128)(2,1)} %get-tuple-element.14.after), channel_id=1, source_target_pairs={{8,0},{16,8},{24,16},{32,24},{40,32},{48,40},{56,48},{64,56},{72,6... | collective-permute-start | bytes 2015240 | tf_op jit(solution)/shard_map/ppermute | solution.py:407
  14.4 1.1 %copy-start.2 = (s16[656,512]{1,0:T(8,128)(2,1)S(1)}, s16[656,512]{1,0:T(8,128)(2,1)}, u32[]{:S(2)}) copy-start(s16[656,512]{1,0:T(8,128)(2,1)} %get-tuple-element.14.after) | copy-start | bytes 2015236
  29.5 41.5 %collective-permute-start.2 = (s16[656,512]{1,0:T(8,128)(2,1)}, s16[656,512]{1,0:T(8,128)(2,1)S(1)}, u32[]{:S(2)}, u32[]{:S(2)}) collective-permute-start(s16[656,512]{1,0:T(8,128)(2,1)} %get-tuple-element.21), channel_id=1, source_target_pairs={{0,8},{8,16},{16,24},{24,32},{32,40},{40,48},{48,56},{56,64},{64,7... | collective-permute-start | bytes 2015240 | tf_op jit(solution)/shard_map/ppermute | solution.py:411
  29.6 41.4 %collective-permute-start.3 = (s16[656,512]{1,0:T(8,128)(2,1)S(1)}, s16[656,512]{1,0:T(8,128)(2,1)S(1)}, u32[]{:S(2)}, u32[]{:S(2)}) collective-permute-start(s16[656,512]{1,0:T(8,128)(2,1)S(1)} %get-tuple-element.22), channel_id=1, source_target_pairs={{8,0},{16,8},{24,16},{32,24},{40,32},{48,40},{56,48},{64,56},{72,6... | collective-permute-start | bytes 2015240 | tf_op jit(solution)/shard_map/ppermute | solution.py:410
  63.2 15.2 %all-to-all-start.2 = ((f32[32,4,128]{2,1,0:T(4,128)}), f32[32,4,128]{2,1,0:T(4,128)S(1)}, u32[]{:S(2)}, u32[]{:S(2)}) async-start(f32[32,4,128]{2,1,0:T(4,128)} %broadcast_in_dim.7), calls=%async_computation.2 | async-start | bytes 131072 | tf_op jit(solution)/shard_map/all_to_all | solution.py:287

commit v5 on v4

--- a/solution.py
+++ b/solution.py
@@ -97,7 +97,9 @@
 SMEM = pl.BlockSpec(memory_space=pltpu.SMEM)
 
 
-def faces_kernel(values_hbm, cells_hbm, column_hbm, low_hbm, high_hbm, held, total, face, cells, columns, sems, small, out_sems):
+def faces_kernel(
+    values_hbm, cells_hbm, column_hbm, low_hbm, high_hbm, passed_hbm, held, total, face, cells, columns, sems, small, out_sems
+):
     bricks = (0, 1, BRICKS - 2, BRICKS - 1)
     targets = ((0, low_hbm), (EXT - 1, high_hbm))
     inputs = [
@@ -110,6 +112,8 @@
         copy.start()
     for copy in inputs:
         copy.wait()
+    outputs.append(pltpu.make_async_copy(cells, passed_hbm, out_sems.at[2]))
+    outputs[2].start()
     hots = [
         cell_hot(cells, brick, columns[:, brick : brick + 1] == targets[slot // 2][0]) for slot, brick in enumerate(bricks)
     ]
@@ -132,7 +136,7 @@
     return pl.pallas_call(
         faces_kernel,
         in_specs=[HBM] * 3,
-        out_specs=[HBM] * 2,
+        out_specs=[HBM] * 3,
         scratch_shapes=[
             pltpu.VMEM((4, SNAPS, FIELDS, PER_BRICK), BF16),
             pltpu.VMEM((2, LANES, ROWS, 128), F32),
@@ -141,23 +145,26 @@
             pltpu.VMEM((1, BRICKS), jnp.int32),
             pltpu.SemaphoreType.DMA((4,)),
             pltpu.SemaphoreType.DMA((2,)),
-            pltpu.SemaphoreType.DMA((2,)),
-        ],
-        out_shape=[shape, shape],
+            pltpu.SemaphoreType.DMA((3,)),
+        ],
+        out_shape=[shape, shape, jax.ShapeDtypeStruct((BRICKS * LANES, 128), jnp.int32)],
         compiler_params=params(63),
         name="faces",
     )(values, cells, columns)
 
 
 def local_kernel(
-    column_ref, values_hbm, cells, after, head_hbm, rest_hbm, hots_hbm, face_ref, gram_ref, down_ref, up_ref,
-    held, total, heads, rests, hots, sems, out_sems, hot_sems
+    column_ref, values_hbm, cells_hbm, head_hbm, rest_hbm, hots_hbm, face_ref, gram_ref,
+    cells, held, total, heads, rests, hots, sems, out_sems, hot_sems, small
 ):
+    ids = pltpu.make_async_copy(cells_hbm, cells, small)
+    ids.start()
     copies = [brick_copy(values_hbm, held, sems, brick, brick) for brick in range(BRICKS)]
     for copy in copies:
         copy.start()
     outputs = []
     total[...] = jnp.zeros_like(total)
+    ids.wait()
     for brick in range(BRICKS):
         hot = cell_hot(cells, brick)
         hots[brick] = hot
@@ -168,8 +175,6 @@
         column = column_ref[brick]
         for t in range(LANES):
             total[column, t] += sums[:, t * 128 : (t + 1) * 128]
-    encode(total.at[1], down_ref)
-    encode(total.at[CX], up_ref)
     same = jnp.zeros((SNAPS, SNAPS), F32)
     mixed = jnp.zeros((SNAPS, SNAPS), F32)
     for k in range(EXT):
@@ -191,14 +196,14 @@
         copy.wait()
 
 
-def local_sums(values, cells, columns, after):
+def local_sums(values, cells, columns):
     half = jax.ShapeDtypeStruct((EXT, ROWS, CW), BF16)
-    wire = jax.ShapeDtypeStruct((WIRE, CW), jnp.int16)
     return pl.pallas_call(
         local_kernel,
-        in_specs=[SMEM, HBM, VMEM, HBM],
-        out_specs=[HBM] * 3 + [VMEM] * 4,
+        in_specs=[SMEM, HBM, HBM],
+        out_specs=[HBM] * 3 + [VMEM] * 2,
         scratch_shapes=[
+            pltpu.VMEM((BRICKS * LANES, 128), jnp.int32),
             pltpu.VMEM((BRICKS, SNAPS, FIELDS, PER_BRICK), BF16),
             pltpu.VMEM((EXT, LANES, ROWS, 128), F32),
             pltpu.VMEM((EXT, ROWS, CW), BF16),
@@ -207,6 +212,7 @@
             pltpu.SemaphoreType.DMA((BRICKS,)),
             pltpu.SemaphoreType.DMA((2, EXT)),
             pltpu.SemaphoreType.DMA((BRICKS,)),
+            pltpu.SemaphoreType.DMA,
         ],
         out_shape=[
             half,
@@ -214,13 +220,11 @@
             jax.ShapeDtypeStruct((BRICKS, CW, PER_BRICK), BF16),
             jax.ShapeDtypeStruct((4, ROWS, CW), BF16),
             jax.ShapeDtypeStruct((SNAPS, SNAPS), F32),
-            wire,
-            wire,
         ],
         compiler_params=params(48),
         cost_estimate=pl.CostEstimate(flops=6_000_000_000, bytes_accessed=14_000_000, transcendentals=0),
         name="local",
-    )(columns, values, cells, after)
+    )(columns, values, cells)
 
 
 def pack(gram):
@@ -321,80 +325,180 @@
     return jnp.concatenate([head, head, rest, jnp.zeros_like(rest)], axis=0).T.astype(BF16)
 
 
-def output_kernel(
-    packed_ref, column_hbm, head_hbm, rest_hbm, hots_hbm, *refs
-):
-    wires_hbm, out_hbm = refs[:4], refs[4]
-    heads, rests, hots, wires, columns, held, sems, hot_sems, out_sems = refs[5:]
-    sources = (head_hbm, rest_hbm) + wires_hbm + (column_hbm,)
-    places = (heads, rests) + tuple(wires.at[i] for i in range(4)) + (columns,)
-    copies = [pltpu.make_async_copy(a, b, sems.at[i]) for i, (a, b) in enumerate(zip(sources, places))]
-    hot_copies = [pltpu.make_async_copy(hots_hbm.at[i], hots.at[i], hot_sems.at[i]) for i in range(BRICKS)]
-    for copy in copies + hot_copies:
+def start(copies):
+    for copy in copies:
         copy.start()
+    return copies
+
+
+def wait(copies):
+    for copy in copies:
+        copy.wait()
+
+
+def by_field(basis):
+    tall = jnp.concatenate([jnp.concatenate([basis] * FIELDS, axis=1)] * FIELDS, axis=0)
+    row_field = lax.broadcasted_iota(jnp.int32, (COEFS, ROWS), 0) // MODES
+    col_field = lax.broadcasted_iota(jnp.int32, (COEFS, ROWS), 1) // SNAPS
+    return jnp.concatenate(halves(jnp.where(row_field == col_field, tall, 0.0)), axis=0)
+
+
+def coefficients(both, head, rest):
+    pair = dot(both, head)
+    return pair[:COEFS] + pair[COEFS:] + dot(both[:COEFS], rest)
+
+
+def basis_kernel(packed_ref, head_hbm, rest_hbm, basis_ref, down_ref, up_ref, heads, rests, sems):
+    copies = []
+    for i, k in enumerate((1, CX)):
+        copies.append(pltpu.make_async_copy(head_hbm.at[k], heads.at[i], sems.at[0, i]))
+        copies.append(pltpu.make_async_copy(rest_hbm.at[k], rests.at[i], sems.at[1, i]))
+    start(copies)
     gram = unpack(packed_ref[...])
     basis = gram[:MODES, :]
     for _ in range(SWEEPS):
         basis = orthonormal(exact_dot(basis, gram))
-    wide = jnp.concatenate([basis] * FIELDS, axis=1)
-    tall = jnp.concatenate([wide] * FIELDS, axis=0)
-    row_field = lax.broadcasted_iota(jnp.int32, (COEFS, ROWS), 0) // MODES
-    col_field = lax.broadcasted_iota(jnp.int32, (COEFS, ROWS), 1) // SNAPS
-    head, rest = halves(jnp.where(row_field == col_field, tall, 0.0))
-    both = jnp.concatenate([head, rest], axis=0)
-    spread = spread_matrix(basis)
-
-    def coefficients(heads_of, rests_of):
-        pair = dot(both, heads_of)
-        return pair[:COEFS] + pair[COEFS:] + dot(head, rests_of)
-
-    for copy in copies:
-        copy.wait()
-    whole = []
+    basis_ref[...] = basis
+    both = by_field(basis)
+    wait(copies)
+    down_ref[...] = coefficients(both, heads[0], rests[0])
+    up_ref[...] = coefficients(both, heads[1], rests[1])
+
+
+def basis_and_faces(packed, head, rest):
+    side = jax.ShapeDtypeStruct((COEFS, CW), F32)
+    return pl.pallas_call(
+        basis_kernel,
+        in_specs=[VMEM, HBM, HBM],
+        out_specs=[VMEM] * 3,
+        scratch_shapes=[
+            pltpu.VMEM((2, ROWS, CW), BF16),
+            pltpu.VMEM((2, ROWS, CW), BF16),
+            pltpu.SemaphoreType.DMA((2, 2)),
+        ],
+        out_shape=[jax.ShapeDtypeStruct((MODES, SNAPS), F32), side, side],
+        compiler_params=params(52),
+        name="basis",
+    )(packed, head, rest)
+
+
+def column_of(columns, brick, whole):
+    mine = whole[0]
+    for k in range(1, EXT):
+        mine = jnp.where(columns[:, brick : brick + 1] == k, whole[k], mine)
+    return mine
+
+
+def write_brick(brick, column, hot, spread, held, out_hbm, sem):
+    picked = dot(column, hot).astype(BF16)
+    blank = jnp.zeros((COEFS, PER_BRICK), BF16)
+    stacked = jnp.concatenate([picked, picked[:COEFS], blank], axis=0)
+    held[...] = dot(spread, stacked).astype(BF16).reshape(SNAPS, FIELDS, PER_BRICK)
+    copy = pltpu.make_async_copy(held, out_hbm.at[:, :, pl.ds(brick * PER_BRICK, PER_BRICK)], sem)
+    copy.start()
+    return copy
+
+
+INNER = range(2, BRICKS - 2)
+OUTER = (0, 1, BRICKS - 2, BRICKS - 1)
+
+
+def inner_kernel(
+    basis_ref, down_ref, up_ref, from_below, from_above, column_hbm, head_hbm, rest_hbm, hots_hbm,
+    out_hbm, whole_ref, ends_ref, spread_ref, edge_hots, passed_ref,
+    heads, rests, hots, held, sems, hot_sems, edge_sems, small, out_sems
+):
+    own = (2, 3, 0, EXT - 1)
+    columns = pltpu.make_async_copy(column_hbm, passed_ref, small)
+    columns.start()
+    copies = []
+    for i, k in enumerate(own):
+        copies.append(pltpu.make_async_copy(head_hbm.at[k], heads.at[i], sems.at[0, i]))
+        copies.append(pltpu.make_async_copy(rest_hbm.at[k], rests.at[i], sems.at[1, i]))
+    start(copies)
+    hot_copies = start([pltpu.make_async_copy(hots_hbm.at[b], hots.at[i], hot_sems.at[i]) for i, b in enumerate(INNER)])
+    edge_copies = start([pltpu.make_async_copy(hots_hbm.at[b], edge_hots.at[i], edge_sems.at[i]) for i, b in enumerate(OUTER)])
+    both = by_field(basis_ref[...])
+    spread_ref[...] = spread_matrix(basis_ref[...])
+    whole = [jnp.zeros((2 * COEFS, CW), BF16)] * EXT
+    for k, mine, wire in ((1, down_ref, from_below), (CX, up_ref, from_above)):
+        other = coefficients(both, *halves(wire_steps(wire, slice(0, ROWS))))
+        whole[k] = jnp.concatenate(halves(mine[...] + other * wire_scale(wire)), axis=0)
+    wait(copies)
+    for i, k in enumerate(own):
+        value = coefficients(both, heads[i], rests[i])
+        if i < 2:
+            whole[k] = jnp.concatenate(halves(value), axis=0)
+        else:
+            ends_ref[i - 2] = value
     for k in range(EXT):
-        value = coefficients(heads[k], rests[k])
-        if k in (0, 1, CX, CX + 1):
-            wire = wires.at[(0, 1, 0, 0, 2, 3)[k]]
-            value += coefficients(*halves(wire_steps(wire, slice(0, ROWS)))) * wire_scale(wire)
-        whole.append(jnp.concatenate(halves(value), axis=0))
-    blank = jnp.zeros((COEFS, PER_BRICK), BF16)
+        whole_ref[k] = whole[k]
+    columns.wait()
     outputs = []
-    for brick in range(BRICKS):
-        column = columns[:, brick : brick + 1]
-        mine = whole[0]
-        for k in range(1, EXT):
-            mine = jnp.where(column == k, whole[k], mine)
-        hot_copies[brick].wait()
-        picked = dot(mine, hots[brick]).astype(BF16)
-        stacked = jnp.concatenate([picked, picked[:COEFS], blank], axis=0)
-        held[brick] = dot(spread, stacked).astype(BF16).reshape(SNAPS, FIELDS, PER_BRICK)
-        target = out_hbm.at[:, :, pl.ds(brick * PER_BRICK, PER_BRICK)]
-        outputs.append(pltpu.make_async_copy(held.at[brick], target, out_sems.at[brick]))
-        outputs[-1].start()
-    for copy in outputs:
-        copy.wait()
-
-
-def atom_fields(packed, columns, head, rest, hots, wires):
+    for i, brick in enumerate(INNER):
+        hot_copies[i].wait()
+        column = column_of(passed_ref, brick, whole)
+        outputs.append(write_brick(brick, column, hots[i], spread_ref[...], held.at[i], out_hbm, out_sems.at[i]))
+    wait(edge_copies)
+    wait(outputs)
+
+
+def inner_fields(basis, down, up, from_below, from_above, columns, head, rest, hots):
     return pl.pallas_call(
-        output_kernel,
-        in_specs=[VMEM] + [HBM] * 8,
+        inner_kernel,
+        in_specs=[VMEM] * 5 + [HBM] * 4,
+        out_specs=[HBM] + [VMEM] * 5,
+        scratch_shapes=[
+            pltpu.VMEM((4, ROWS, CW), BF16),
+            pltpu.VMEM((4, ROWS, CW), BF16),
+            pltpu.VMEM((4, CW, PER_BRICK), BF16),
+            pltpu.VMEM((4, SNAPS, FIELDS, PER_BRICK), BF16),
+            pltpu.SemaphoreType.DMA((2, 4)),
+            pltpu.SemaphoreType.DMA((4,)),
+            pltpu.SemaphoreType.DMA((4,)),
+            pltpu.SemaphoreType.DMA,
+            pltpu.SemaphoreType.DMA((4,)),
+        ],
+        out_shape=[
+            jax.ShapeDtypeStruct((SNAPS, FIELDS, BRICKS * PER_BRICK), BF16),
+            jax.ShapeDtypeStruct((EXT, 2 * COEFS, CW), BF16),
+            jax.ShapeDtypeStruct((2, COEFS, CW), F32),
+            jax.ShapeDtypeStruct((ROWS, 4 * COEFS), BF16),
+            jax.ShapeDtypeStruct((4, CW, PER_BRICK), BF16),
+            jax.ShapeDtypeStruct((1, BRICKS), jnp.int32),
+        ],
+        compiler_params=params(48),
+        cost_estimate=pl.CostEstimate(flops=4_000_000_000, bytes_accessed=14_000_000, transcendentals=0),
+        name="inner",
+    )(basis, down, up, from_below, from_above, columns, head, rest, hots)
+
+
+def outer_kernel(filled_hbm, whole_ref, ends_ref, below, above, spread_ref, hots, columns, out_hbm, held, out_sems):
+    del filled_hbm
+    whole = [whole_ref[k] for k in range(EXT)]
+    for k, received in ((0, below), (EXT - 1, above)):
+        whole[k] = jnp.concatenate(halves(ends_ref[k // CX] + received[...]), axis=0)
+    outputs = []
+    for i, brick in enumerate(OUTER):
+        column = column_of(columns, brick, whole)
+        outputs.append(write_brick(brick, column, hots[i], spread_ref[...], held.at[i], out_hbm, out_sems.at[i]))
+    wait(outputs)
+
+
+def outer_fields(filled, whole, ends, below, above, spread, hots, columns):
+    return pl.pallas_call(
+        outer_kernel,
+        in_specs=[HBM] + [VMEM] * 7,
         out_specs=HBM,
         scratch_shapes=[
-            pltpu.VMEM((EXT, ROWS, CW), BF16),
-            pltpu.VMEM((EXT, ROWS, CW), BF16),
-            pltpu.VMEM((BRICKS, CW, PER_BRICK), BF16),
-            pltpu.VMEM((4, WIRE, CW), jnp.int16),
-            pltpu.VMEM((1, BRICKS), jnp.int32),
-            pltpu.VMEM((BRICKS, SNAPS, FIELDS, PER_BRICK), BF16),
-            pltpu.SemaphoreType.DMA((7,)),
-            pltpu.SemaphoreType.DMA((BRICKS,)),
-            pltpu.SemaphoreType.DMA((BRICKS,)),
-        ],
-        out_shape=jax.ShapeDtypeStruct((SNAPS, FIELDS, BRICKS * PER_BRICK), BF16),
-        compiler_params=params(51),
-        name="output",
-    )(packed, columns, head, rest, hots, *wires)
+            pltpu.VMEM((4, SNAPS, FIELDS, PER_BRICK), BF16),
+            pltpu.SemaphoreType.DMA((4,)),
+        ],
+        out_shape=jax.ShapeDtypeStruct(filled.shape, BF16),
+        input_output_aliases={0: 0},
+        compiler_params=params(32),
+        name="outer",
+    )(filled, whole, ends, below, above, spread, hots, columns)
 
 
 def on_device(atom_values, atom_cell, brick_column):
@@ -403,15 +507,18 @@
     to_upper = [(i, (i + 1) % count) for i in range(count)]
     cells = atom_cell.reshape(BRICKS * LANES, 128)
     columns = brick_column.reshape(1, BRICKS)
-    low, high = face_sums(atom_values, cells, columns)
+    low, high, passed = face_sums(atom_values, cells, columns)
     from_above = lax.ppermute(low, "gx", to_lower)
     from_below = lax.ppermute(high, "gx", to_upper)
-    head, rest, hots, faces, gram, down, up = local_sums(atom_values, cells, brick_column, low)
-    second_above = lax.ppermute(down, "gx", to_lower)
-    second_below = lax.ppermute(up, "gx", to_upper)
+    head, rest, hots, faces, gram = local_sums(atom_values, passed, brick_column)
     packed = add_over_devices(packed_gram(gram, faces, from_below, from_above))
-    wires = (second_below, from_below, from_above, second_above)
-    return atom_fields(packed, columns, head, rest, hots, wires)
+    basis, down, up = basis_and_faces(packed, head, rest)
+    above = lax.ppermute(down, "gx", to_lower)
+    below = lax.ppermute(up, "gx", to_upper)
+    filled, whole, ends, spread, edge_hots, columns = inner_fields(
+        basis, down, up, from_below, from_above, columns, head, rest, hots
+    )
+    return outer_fields(filled, whole, ends, below, above, spread, edge_hots, columns)
 
 
 def solution(mesh):

time: 90 us -> 84.6 us (0.940)
  blocking collectives: 26.6 us -> 38.1 us
  starting transfers between devices: 21.6 us -> 10.5 us
  waiting for transfers between devices: 7.36 us -> 1.35 us
  Pallas kernels: 32 us -> 33.4 us
  local copies, waits for them, and re-layouts: 1.78 us -> 0.74 us
    all_to_all x2 -> x3, blocking collectives: 26.6 us -> 38.1 us  [trade(): lax.all_to_all(parts, axes, 0, 0, axis_index_groups=groups, tiled=True)]
    all_to_all x1 -> x0, starting transfers between devices: 7.82 us -> none  [trade(): lax.all_to_all(parts, axes, 0, 0, axis_index_groups=groups, tiled=True)]
    all_to_all x1 -> x0, waiting for transfers between devices: 7.34 us -> none  [trade(): lax.all_to_all(parts, axes, 0, 0, axis_index_groups=groups, tiled=True)]
    ppermute x2, starting transfers between devices: 4.86 us -> 1.54 us  [the longest x1 0.92 us: on_device(): above = lax.ppermute(down, 'gx', to_lower)]
    pallas_call x3 -> x5, Pallas kernels: 30.5 us -> 31.9 us  [the longest x1 12.7 us: local_sums(): pl.pallas_call(local_kernel, in_specs=[SMEM, HBM, HBM], out_specs=[HBM] *...]
    ppermute x1, waiting for transfers between devices: 0.01 us -> 1.34 us  [on_device(): from_below = lax.ppermute(high, 'gx', to_upper)]
  transfers between devices with their start and end apart: 5 -> 4, of which waited for: 1 -> 1; matrix products, arithmetic and copies ran while one was open for 1% -> 0% of each run, Pallas kernels for 17% -> 24%
where the time goes in v5:
time: 84.6 us; the launch traced here: 84.3 us
  blocking collectives  38.1 us (45%)
  Pallas kernels  33.4 us (39%)
  starting transfers between devices  10.5 us (12%)
  waiting for transfers between devices  1.35 us (2%)
    all_to_all x3, blocking collectives, trade(): lax.all_to_all(parts, axes, 0, 0, axis_index_groups=groups, tiled=True)  38.1 us
    pallas_call x1, Pallas kernels, local_sums(): pl.pallas_call(local_kernel, in_specs=[SMEM, HBM, HBM], out_specs=[HBM] *...  12.7 us
    pallas_call x1, Pallas kernels, inner_fields(): pl.pallas_call(inner_kernel, in_specs=[VMEM] * 5 + [HBM] * 4, out_specs=[...  7.78 us
    ppermute x1, starting transfers between devices, on_device(): from_above = lax.ppermute(low, 'gx', to_lower)  6.39 us
    pallas_call x1, Pallas kernels, face_sums(): pl.pallas_call(faces_kernel, in_specs=[HBM] * 3, out_specs=[HBM] * 3, scr...  5.27 us
    pallas_call x1, Pallas kernels, basis_and_faces(): pl.pallas_call(basis_kernel, in_specs=[VMEM, HBM, HBM], out_specs=[VMEM]...  3.65 us
    ppermute x1, starting transfers between devices, on_device(): from_below = lax.ppermute(high, 'gx', to_upper)  2.55 us
    pallas_call x1, Pallas kernels, outer_fields(): pl.pallas_call(outer_kernel, in_specs=[HBM] + [VMEM] * 7, out_specs=HBM,...  2.52 us
  transfers between devices with their start and end apart: 4, of which 1 were waited for; matrix products, arithmetic and copies ran while one was open for 0% of the time, Pallas kernels for 24%

profile of v5, /device:TPU:1, one launch (start us, length us, event | category | flops | bytes accessed | tf_op | source)
XLA Modules:
  0.0 84.3 jit_solution(13094069413860114317)
XLA Ops:
  0.0 0.0 copy-start
  0.0 5.3 %faces.1 = (s16[656,512]{1,0:T(8,128)(2,1)}, s16[656,512]{1,0:T(8,128)(2,1)}, s32[32,128]{1,0:T(8,128)}) custom-call(bf16[160,4,4096]{2,1,0:T(4,128)(2,1)} %values_hbm.3, s32[32,128]{1,0:T(8,128)} %bitcast.8, s32[1,8]{1,0:T(1,128)} %bitcast.6), custom_call_target="tpu_custom_call" | custom-call | tf_op jit(solution)/shard_map/faces/pallas_call | solution.py:136
  5.3 2.6 %collective-permute-start = (s16[656,512]{1,0:T(8,128)(2,1)}, s16[656,512]{1,0:T(8,128)(2,1)S(1)}, u32[]{:S(2)}, u32[]{:S(2)}) collective-permute-start(s16[656,512]{1,0:T(8,128)(2,1)} %get-tuple-element.25), channel_id=1, source_target_pairs={{0,8},{8,16},{16,24},{24,32},{32,40},{40,48},{48,56},{56,64},{64,7... | collective-permute-start | bytes 2015240 | tf_op jit(solution)/shard_map/ppermute | solution.py:512
  7.8 6.4 %collective-permute-start.1 = (s16[656,512]{1,0:T(8,128)(2,1)}, s16[656,512]{1,0:T(8,128)(2,1)S(1)}, u32[]{:S(2)}, u32[]{:S(2)}) collective-permute-start(s16[656,512]{1,0:T(8,128)(2,1)} %get-tuple-element.26), channel_id=1, source_target_pairs={{8,0},{16,8},{24,16},{32,24},{40,32},{48,40},{56,48},{64,56},{72,6... | collective-permute-start | bytes 2015240 | tf_op jit(solution)/shard_map/ppermute | solution.py:511
  14.2 0.0 copy-done
  14.2 0.0 copy-start.1
  14.2 0.7 copy-done.1
  14.9 12.7 %local.1 = (bf16[6,640,512]{2,1,0:T(8,128)(2,1)}, bf16[6,640,512]{2,1,0:T(8,128)(2,1)}, bf16[8,512,512]{2,1,0:T(8,128)(2,1)}, bf16[4,640,512]{2,1,0:T(8,128)(2,1)S(1)}, f32[160,160]{1,0:T(8,128)S(1)}) custom-call(s32[8]{0:T(128)S(1)} %copy-done, bf16[160,4,4096]{2,1,0:T(4,128)(2,1)} %values_hbm.3, s32[32,128]{1,0:T(8,128)S(1)} %copy-done.1), custom_call_target="tpu_custom_call" | custom-call | flops 6000000000 | bytes 14000000 | tf_op jit(solution)/shard_map/local/pallas_call | solution.py:201
  27.6 1.3 %collective-permute-done.from_below = s16[656,512]{1,0:T(8,128)(2,1)S(1)} collective-permute-done((s16[656,512]{1,0:T(8,128)(2,1)}, s16[656,512]{1,0:T(8,128)(2,1)S(1)}, u32[]{:S(2)}, u32[]{:S(2)}) %collective-permute-start) | collective-permute-done | bytes 671776 | tf_op jit(solution)/shard_map/ppermute | solution.py:512
  29.0 0.0 collective-permute-done.1.from_above
  29.0 1.5 %cross.1 = f32[128,128]{1,0:T(8,128)S(1)} custom-call(f32[160,160]{1,0:T(8,128)S(1)} %get-tuple-element.23.gram_ref, bf16[4,640,512]{2,1,0:T(8,128)(2,1)S(1)} %get-tuple-element.24.face_ref, s16[656,512]{1,0:T(8,128)(2,1)S(1)} %collective-permute-done.from_below, s16[656,512]{1,0:T(8,128)(2,1)S(1)} %collective-permute-done.1.from_above), custom_call_target="tpu_custom_call" | custom-call | tf_op jit(solution)/shard_map/cross/pallas_call | solution.py:273
  30.5 13.3 %all_to_all.15 = f32[32,4,128]{2,1,0:T(4,128)S(1)} all-to-all(f32[32,4,128]{2,1,0:T(4,128)S(1)} %bitcast.5), channel_id=1, replica_groups={{0,1,2,3,4,5,6,7,64,65,66,67,68,69,70,71,128,129,130,131,132,133,134,13..., dimensions={0} | all-to-all | bytes 131072 | tf_op jit(solution)/shard_map/all_to_all | solution.py:291
  43.8 12.5 %all_to_all.16 = f32[8,4,128]{2,1,0:T(4,128)S(1)} all-to-all(f32[8,4,128]{2,1,0:T(4,128)S(1)} %broadcast_in_dim.6), channel_id=1, replica_groups={{0,8,16,24,32,40,48,56},{1,9,17,25,33,41,49,57},{2,10,18,26,34,42,50,58..., dimensions={0} | all-to-all | bytes 32768 | tf_op jit(solution)/shard_map/all_to_all | solution.py:291
  56.3 12.3 %all_to_all.17 = f32[32,4,128]{2,1,0:T(4,128)S(1)} all-to-all(f32[32,4,128]{2,1,0:T(4,128)S(1)} %broadcast_in_dim.7), channel_id=1, replica_groups={{0,1,2,3,4,5,6,7,64,65,66,67,68,69,70,71,128,129,130,131,132,133,134,13..., dimensions={0} | all-to-all | bytes 131072 | tf_op jit(solution)/shard_map/all_to_all | solution.py:291
  68.6 3.6 %basis.1 = (f32[8,160]{1,0:T(8,128)S(1)}, f32[32,512]{1,0:T(8,128)S(1)}, f32[32,512]{1,0:T(8,128)S(1)}) custom-call(f32[128,128]{1,0:T(8,128)S(1)} %bitcast.4, bf16[6,640,512]{2,1,0:T(8,128)(2,1)} %get-tuple-element.27.head_hbm, bf16[6,640,512]{2,1,0:T(8,128)(2,1)} %get-tuple-element.28.rest_hbm), custom_call_target="tpu_custom_call" | custom-call | tf_op jit(solution)/shard_map/basis/pallas_call | solution.py:370
  72.3 0.9 %collective-permute-start.3 = (f32[32,512]{1,0:T(8,128)S(1)}, f32[32,512]{1,0:T(8,128)S(1)}, u32[]{:S(2)}, u32[]{:S(2)}) collective-permute-start(f32[32,512]{1,0:T(8,128)S(1)} %get-tuple-element.30.down_ref), channel_id=1, source_target_pairs={{8,0},{16,8},{24,16},{32,24},{40,32},{48,40},{56,48},{64,56},{72,6... | collective-permute-start | bytes 196616 | tf_op jit(solution)/shard_map/ppermute | solution.py:516
  73.2 0.6 collective-permute-start.2
  73.8 7.8 %inner.1 = (bf16[160,4,4096]{2,1,0:T(4,128)(2,1)}, bf16[6,64,512]{2,1,0:T(8,128)(2,1)S(1)}, f32[2,32,512]{2,1,0:T(8,128)S(1)}, bf16[640,128]{1,0:T(8,128)(2,1)S(...) custom-call(f32[8,160]{1,0:T(8,128)S(1)} %get-tuple-element.29.basis_ref, ...), custom_call_target="tpu_custom_call" | custom-call | flops 4000000000 | bytes 14000000 | tf_op jit(solution)/shard_map/inner/pallas_call | solution.py:447
  81.6 0.0 collective-permute-done.3.above
  81.6 0.0 collective-permute-done.2.below
  81.6 2.5 %outer.1 = bf16[160,4,4096]{2,1,0:T(4,128)(2,1)} custom-call(bf16[160,4,4096]{2,1,0:T(4,128)(2,1)} %get-tuple-element.33.filled_hbm, bf16[6,64,512]{2,1,0:T(8,128)(2,1)S(1)} %get-tuple-element.34.whole_ref, f32[2,32,512]{2,1,0:T(8,128)S(1)} %get-tuple-element.35.ends_ref, ...), custom_call_target="tpu_custom_call", output_to_operand_aliasing={{}: (0, {})} | custom-call | tf_op jit(solution)/shard_map/outer/pallas_call | solution.py:489
  (4 shorter events, 0.1 us)
Async XLA Ops:
  0.0 14.2 %copy-start = (s32[8]{0:T(128)S(1)}, s32[8]{0:T(128)}, u32[]{:S(2)}) copy-start(s32[8]{0:T(128)} %column_ref.1) | copy-start | bytes 100
  5.3 23.7 %collective-permute-start = (s16[656,512]{1,0:T(8,128)(2,1)}, s16[656,512]{1,0:T(8,128)(2,1)S(1)}, u32[]{:S(2)}, u32[]{:S(2)}) collective-permute-start(s16[656,512]{1,0:T(8,128)(2,1)} %get-tuple-element.25), channel_id=1, source_target_pairs={{0,8},{8,16},{16,24},{24,32},{32,40},{40,48},{48,56},{56,64},{64,7... | collective-permute-start | bytes 2015240 | tf_op jit(solution)/shard_map/ppermute | solution.py:512
  7.8 21.1 %collective-permute-start.1 = (s16[656,512]{1,0:T(8,128)(2,1)}, s16[656,512]{1,0:T(8,128)(2,1)S(1)}, u32[]{:S(2)}, u32[]{:S(2)}) collective-permute-start(s16[656,512]{1,0:T(8,128)(2,1)} %get-tuple-element.26), channel_id=1, source_target_pairs={{8,0},{16,8},{24,16},{32,24},{40,32},{48,40},{56,48},{64,56},{72,6... | collective-permute-start | bytes 2015240 | tf_op jit(solution)/shard_map/ppermute | solution.py:511
  14.2 0.7 copy-start.1
  72.3 9.3 %collective-permute-start.3 = (f32[32,512]{1,0:T(8,128)S(1)}, f32[32,512]{1,0:T(8,128)S(1)}, u32[]{:S(2)}, u32[]{:S(2)}) collective-permute-start(f32[32,512]{1,0:T(8,128)S(1)} %get-tuple-element.30.down_ref), channel_id=1, source_target_pairs={{8,0},{16,8},{24,16},{32,24},{40,32},{48,40},{56,48},{64,56},{72,6... | collective-permute-start | bytes 196616 | tf_op jit(solution)/shard_map/ppermute | solution.py:516
  73.2 8.4 %collective-permute-start.2 = (f32[32,512]{1,0:T(8,128)S(1)}, f32[32,512]{1,0:T(8,128)S(1)}, u32[]{:S(2)}, u32[]{:S(2)}) collective-permute-start(f32[32,512]{1,0:T(8,128)S(1)} %get-tuple-element.31.up_ref), channel_id=1, source_target_pairs={{0,8},{8,16},{16,24},{24,32},{32,40},{40,48},{48,56},{56,64},{64,7... | collective-permute-start | bytes 196616 | tf_op jit(solution)/shard_map/ppermute | solution.py:517

commit v6 on v5

--- a/solution.py
+++ b/solution.py
@@ -154,22 +154,18 @@
 
 
 def local_kernel(
-    column_ref, values_hbm, cells_hbm, head_hbm, rest_hbm, hots_hbm, face_ref, gram_ref,
-    cells, held, total, heads, rests, hots, sems, out_sems, hot_sems, small
+    column_ref, values_hbm, cells_hbm, heads, rests, hots, gram_ref, cells, held, total, sems, small
 ):
     ids = pltpu.make_async_copy(cells_hbm, cells, small)
     ids.start()
     copies = [brick_copy(values_hbm, held, sems, brick, brick) for brick in range(BRICKS)]
     for copy in copies:
         copy.start()
-    outputs = []
     total[...] = jnp.zeros_like(total)
     ids.wait()
     for brick in range(BRICKS):
         hot = cell_hot(cells, brick)
         hots[brick] = hot
-        outputs.append(pltpu.make_async_copy(hots.at[brick], hots_hbm.at[brick], hot_sems.at[brick]))
-        outputs[-1].start()
         copies[brick].wait()
         sums = dot_nt(held[brick].reshape(ROWS, PER_BRICK), hot)
         column = column_ref[brick]
@@ -183,17 +179,9 @@
             head, rest = halves(one_field(total.at[k], f))
             heads[k, rows, :] = head
             rests[k, rows, :] = rest
-            if k in (1, CX):
-                face_ref[2 * (k // CX), rows, :] = head
-                face_ref[2 * (k // CX) + 1, rows, :] = rest
             same += dot_nt(head, head)
             mixed += dot_nt(head, rest)
-        for i, (source, target) in enumerate(((heads, head_hbm), (rests, rest_hbm))):
-            outputs.append(pltpu.make_async_copy(source.at[k], target.at[k], out_sems.at[i, k]))
-            outputs[-1].start()
     gram_ref[...] = same + mixed + mixed.T
-    for copy in outputs:
-        copy.wait()
 
 
 def local_sums(values, cells, columns):
@@ -201,16 +189,11 @@
     return pl.pallas_call(
         local_kernel,
         in_specs=[SMEM, HBM, HBM],
-        out_specs=[HBM] * 3 + [VMEM] * 2,
+        out_specs=[VMEM] * 4,
         scratch_shapes=[
             pltpu.VMEM((BRICKS * LANES, 128), jnp.int32),
             pltpu.VMEM((BRICKS, SNAPS, FIELDS, PER_BRICK), BF16),
             pltpu.VMEM((EXT, LANES, ROWS, 128), F32),
-            pltpu.VMEM((EXT, ROWS, CW), BF16),
-            pltpu.VMEM((EXT, ROWS, CW), BF16),
-            pltpu.VMEM((BRICKS, CW, PER_BRICK), BF16),
-            pltpu.SemaphoreType.DMA((BRICKS,)),
-            pltpu.SemaphoreType.DMA((2, EXT)),
             pltpu.SemaphoreType.DMA((BRICKS,)),
             pltpu.SemaphoreType.DMA,
         ],
@@ -218,10 +201,9 @@
             half,
             half,
             jax.ShapeDtypeStruct((BRICKS, CW, PER_BRICK), BF16),
-            jax.ShapeDtypeStruct((4, ROWS, CW), BF16),
             jax.ShapeDtypeStruct((SNAPS, SNAPS), F32),
         ],
-        compiler_params=params(48),
+        compiler_params=params(42),
         cost_estimate=pl.CostEstimate(flops=6_000_000_000, bytes_accessed=14_000_000, transcendentals=0),
         name="local",
     )(columns, values, cells)
@@ -257,27 +239,42 @@
     return jnp.concatenate([top, bottom], axis=0)
 
 
-def cross_kernel(gram_ref, face_ref, from_below, from_above, packed_ref):
+def cross_kernel(gram_ref, heads, rests, from_below, from_above, packed_ref):
     cross = jnp.zeros((SNAPS, SNAPS), F32)
-    for i, received in enumerate((from_below, from_above)):
+    for k, received in ((1, from_below), (CX, from_above)):
         scale = wire_scale(received)
         for f in range(FIELDS):
             rows = slice(f * SNAPS, (f + 1) * SNAPS)
             head, rest = halves(wire_steps(received, rows) * scale)
-            own = face_ref[2 * i, rows, :]
-            cross += dot_nt(own, head) + dot_nt(own, rest) + dot_nt(face_ref[2 * i + 1, rows, :], head)
+            own = heads[k, rows, :]
+            cross += dot_nt(own, head) + dot_nt(own, rest) + dot_nt(rests[k, rows, :], head)
     packed_ref[...] = pack(gram_ref[...] + cross + cross.T)
 
 
-def packed_gram(gram, faces, from_below, from_above):
+def packed_gram(gram, heads, rests, from_below, from_above):
     return pl.pallas_call(
         cross_kernel,
-        in_specs=[VMEM] * 4,
+        in_specs=[VMEM] * 5,
         out_specs=VMEM,
         out_shape=jax.ShapeDtypeStruct((SPLIT, SPLIT), F32),
         compiler_params=params(16),
         name="cross",
-    )(gram, faces, from_below, from_above)
+    )(gram, heads, rests, from_below, from_above)
+
+
+def sum_kernel(parts, out_ref):
+    out_ref[...] = jnp.broadcast_to(parts[...].sum(0), out_ref.shape)
+
+
+def summed_copies(parts, copies):
+    return pl.pallas_call(
+        sum_kernel,
+        in_specs=[VMEM],
+        out_specs=VMEM,
+        out_shape=jax.ShapeDtypeStruct((copies,) + parts.shape[1:], F32),
+        compiler_params=params(2),
+        name="sum",
+    )(parts)
 
 
 def add_over_devices(x):
@@ -291,9 +288,9 @@
         return lax.all_to_all(parts, axes, 0, 0, axis_index_groups=groups, tiled=True)
 
     shape = (SPLIT // size, SPLIT)
-    mine = trade(x.reshape((size,) + shape), planes).sum(0)
-    mine = trade(jnp.broadcast_to(mine, (depth,) + shape), lines).sum(0)
-    return trade(jnp.broadcast_to(mine, (size,) + shape), planes).reshape(SPLIT, SPLIT)
+    mine = summed_copies(trade(x.reshape((size,) + shape), planes), depth)
+    mine = summed_copies(trade(mine, lines), size)
+    return trade(mine, planes).reshape(SPLIT, SPLIT)
 
 
 def orthonormal(basis):
@@ -348,38 +345,27 @@
     return pair[:COEFS] + pair[COEFS:] + dot(both[:COEFS], rest)
 
 
-def basis_kernel(packed_ref, head_hbm, rest_hbm, basis_ref, down_ref, up_ref, heads, rests, sems):
-    copies = []
-    for i, k in enumerate((1, CX)):
-        copies.append(pltpu.make_async_copy(head_hbm.at[k], heads.at[i], sems.at[0, i]))
-        copies.append(pltpu.make_async_copy(rest_hbm.at[k], rests.at[i], sems.at[1, i]))
-    start(copies)
+def basis_kernel(packed_ref, heads, rests, basis_ref, down_ref, up_ref):
     gram = unpack(packed_ref[...])
     basis = gram[:MODES, :]
     for _ in range(SWEEPS):
         basis = orthonormal(exact_dot(basis, gram))
     basis_ref[...] = basis
     both = by_field(basis)
-    wait(copies)
-    down_ref[...] = coefficients(both, heads[0], rests[0])
-    up_ref[...] = coefficients(both, heads[1], rests[1])
-
-
-def basis_and_faces(packed, head, rest):
+    down_ref[...] = coefficients(both, heads[1], rests[1])
+    up_ref[...] = coefficients(both, heads[CX], rests[CX])
+
+
+def basis_and_faces(packed, heads, rests):
     side = jax.ShapeDtypeStruct((COEFS, CW), F32)
     return pl.pallas_call(
         basis_kernel,
-        in_specs=[VMEM, HBM, HBM],
+        in_specs=[VMEM] * 3,
         out_specs=[VMEM] * 3,
-        scratch_shapes=[
-            pltpu.VMEM((2, ROWS, CW), BF16),
-            pltpu.VMEM((2, ROWS, CW), BF16),
-            pltpu.SemaphoreType.DMA((2, 2)),
-        ],
         out_shape=[jax.ShapeDtypeStruct((MODES, SNAPS), F32), side, side],
-        compiler_params=params(52),
+        compiler_params=params(16),
         name="basis",
-    )(packed, head, rest)
+    )(packed, heads, rests)
 
 
 def column_of(columns, brick, whole):
@@ -404,59 +390,35 @@
 
 
 def inner_kernel(
-    basis_ref, down_ref, up_ref, from_below, from_above, column_hbm, head_hbm, rest_hbm, hots_hbm,
-    out_hbm, whole_ref, ends_ref, spread_ref, edge_hots, passed_ref,
-    heads, rests, hots, held, sems, hot_sems, edge_sems, small, out_sems
+    basis_ref, down_ref, up_ref, from_below, from_above, columns, heads, rests, hots,
+    out_hbm, whole_ref, ends_ref, spread_ref, held, out_sems
 ):
-    own = (2, 3, 0, EXT - 1)
-    columns = pltpu.make_async_copy(column_hbm, passed_ref, small)
-    columns.start()
-    copies = []
-    for i, k in enumerate(own):
-        copies.append(pltpu.make_async_copy(head_hbm.at[k], heads.at[i], sems.at[0, i]))
-        copies.append(pltpu.make_async_copy(rest_hbm.at[k], rests.at[i], sems.at[1, i]))
-    start(copies)
-    hot_copies = start([pltpu.make_async_copy(hots_hbm.at[b], hots.at[i], hot_sems.at[i]) for i, b in enumerate(INNER)])
-    edge_copies = start([pltpu.make_async_copy(hots_hbm.at[b], edge_hots.at[i], edge_sems.at[i]) for i, b in enumerate(OUTER)])
     both = by_field(basis_ref[...])
     spread_ref[...] = spread_matrix(basis_ref[...])
     whole = [jnp.zeros((2 * COEFS, CW), BF16)] * EXT
     for k, mine, wire in ((1, down_ref, from_below), (CX, up_ref, from_above)):
         other = coefficients(both, *halves(wire_steps(wire, slice(0, ROWS))))
         whole[k] = jnp.concatenate(halves(mine[...] + other * wire_scale(wire)), axis=0)
-    wait(copies)
-    for i, k in enumerate(own):
-        value = coefficients(both, heads[i], rests[i])
-        if i < 2:
-            whole[k] = jnp.concatenate(halves(value), axis=0)
-        else:
-            ends_ref[i - 2] = value
+    for k in (2, 3):
+        whole[k] = jnp.concatenate(halves(coefficients(both, heads[k], rests[k])), axis=0)
+    outputs = []
+    for i, brick in enumerate(INNER):
+        column = column_of(columns, brick, whole)
+        outputs.append(write_brick(brick, column, hots[brick], spread_ref[...], held.at[i], out_hbm, out_sems.at[i]))
     for k in range(EXT):
         whole_ref[k] = whole[k]
-    columns.wait()
-    outputs = []
-    for i, brick in enumerate(INNER):
-        hot_copies[i].wait()
-        column = column_of(passed_ref, brick, whole)
-        outputs.append(write_brick(brick, column, hots[i], spread_ref[...], held.at[i], out_hbm, out_sems.at[i]))
-    wait(edge_copies)
+    for i, k in enumerate((0, EXT - 1)):
+        ends_ref[i] = coefficients(both, heads[k], rests[k])
     wait(outputs)
 
 
-def inner_fields(basis, down, up, from_below, from_above, columns, head, rest, hots):
+def inner_fields(basis, down, up, from_below, from_above, columns, heads, rests, hots):
     return pl.pallas_call(
         inner_kernel,
-        in_specs=[VMEM] * 5 + [HBM] * 4,
-        out_specs=[HBM] + [VMEM] * 5,
+        in_specs=[VMEM] * 9,
+        out_specs=[HBM] + [VMEM] * 3,
         scratch_shapes=[
-            pltpu.VMEM((4, ROWS, CW), BF16),
-            pltpu.VMEM((4, ROWS, CW), BF16),
-            pltpu.VMEM((4, CW, PER_BRICK), BF16),
             pltpu.VMEM((4, SNAPS, FIELDS, PER_BRICK), BF16),
-            pltpu.SemaphoreType.DMA((2, 4)),
-            pltpu.SemaphoreType.DMA((4,)),
-            pltpu.SemaphoreType.DMA((4,)),
-            pltpu.SemaphoreType.DMA,
             pltpu.SemaphoreType.DMA((4,)),
         ],
         out_shape=[
@@ -464,13 +426,11 @@
             jax.ShapeDtypeStruct((EXT, 2 * COEFS, CW), BF16),
             jax.ShapeDtypeStruct((2, COEFS, CW), F32),
             jax.ShapeDtypeStruct((ROWS, 4 * COEFS), BF16),
-            jax.ShapeDtypeStruct((4, CW, PER_BRICK), BF16),
-            jax.ShapeDtypeStruct((1, BRICKS), jnp.int32),
-        ],
-        compiler_params=params(48),
+        ],
+        compiler_params=params(24),
         cost_estimate=pl.CostEstimate(flops=4_000_000_000, bytes_accessed=14_000_000, transcendentals=0),
         name="inner",
-    )(basis, down, up, from_below, from_above, columns, head, rest, hots)
+    )(basis, down, up, from_below, from_above, columns, heads, rests, hots)
 
 
 def outer_kernel(filled_hbm, whole_ref, ends_ref, below, above, spread_ref, hots, columns, out_hbm, held, out_sems):
@@ -481,7 +441,7 @@
     outputs = []
     for i, brick in enumerate(OUTER):
         column = column_of(columns, brick, whole)
-        outputs.append(write_brick(brick, column, hots[i], spread_ref[...], held.at[i], out_hbm, out_sems.at[i]))
+        outputs.append(write_brick(brick, column, hots[brick], spread_ref[...], held.at[i], out_hbm, out_sems.at[i]))
     wait(outputs)
 
 
@@ -510,15 +470,13 @@
     low, high, passed = face_sums(atom_values, cells, columns)
     from_above = lax.ppermute(low, "gx", to_lower)
     from_below = lax.ppermute(high, "gx", to_upper)
-    head, rest, hots, faces, gram = local_sums(atom_values, passed, brick_column)
-    packed = add_over_devices(packed_gram(gram, faces, from_below, from_above))
-    basis, down, up = basis_and_faces(packed, head, rest)
+    heads, rests, hots, gram = local_sums(atom_values, passed, brick_column)
+    packed = add_over_devices(packed_gram(gram, heads, rests, from_below, from_above))
+    basis, down, up = basis_and_faces(packed, heads, rests)
     above = lax.ppermute(down, "gx", to_lower)
     below = lax.ppermute(up, "gx", to_upper)
-    filled, whole, ends, spread, edge_hots, columns = inner_fields(
-        basis, down, up, from_below, from_above, columns, head, rest, hots
-    )
-    return outer_fields(filled, whole, ends, below, above, spread, edge_hots, columns)
+    filled, whole, ends, spread = inner_fields(basis, down, up, from_below, from_above, columns, heads, rests, hots)
+    return outer_fields(filled, whole, ends, below, above, spread, hots, columns)
 
 
 def solution(mesh):

time: 84.6 us -> 81.3 us (0.961)
  Pallas kernels: 33.4 us -> 25.9 us
  waiting for transfers between devices: 1.35 us -> 5.64 us
    pallas_call x4 -> x6, Pallas kernels: 25.6 us -> 18 us  [the longest x1 10.5 us: local_sums(): pl.pallas_call(local_kernel, in_specs=[SMEM, HBM, HBM], out_specs=[VMEM]...]
    ppermute x1, waiting for transfers between devices: 1.34 us -> 3.52 us  [on_device(): from_below = lax.ppermute(high, 'gx', to_upper)]
    ppermute x1, waiting for transfers between devices: 0.01 us -> 2.12 us  [on_device(): below = lax.ppermute(up, 'gx', to_upper)]
  transfers between devices with their start and end apart: 4 -> 4, of which waited for: 1 -> 2; matrix products, arithmetic and copies ran while one was open for 0% -> 0% of each run, Pallas kernels for 24% -> 17%
where the time goes in v6:
time: 81.3 us; the launch traced here: 81 us
  blocking collectives  38.1 us (47%)
  Pallas kernels  25.9 us (32%)
  starting transfers between devices  10.5 us (13%)
  waiting for transfers between devices  5.64 us (7%)
    all_to_all x3, blocking collectives, trade(): lax.all_to_all(parts, axes, 0, 0, axis_index_groups=groups, tiled=True)  38.1 us
    pallas_call x1, Pallas kernels, local_sums(): pl.pallas_call(local_kernel, in_specs=[SMEM, HBM, HBM], out_specs=[VMEM]...  10.5 us
    ppermute x1, starting transfers between devices, on_device(): from_above = lax.ppermute(low, 'gx', to_lower)  6.4 us
    pallas_call x1, Pallas kernels, face_sums(): pl.pallas_call(faces_kernel, in_specs=[HBM] * 3, out_specs=[HBM] * 3, scr...  5.37 us
    pallas_call x1, Pallas kernels, inner_fields(): pl.pallas_call(inner_kernel, in_specs=[VMEM] * 9, out_specs=[HBM] + [VMEM...  3.67 us
    ppermute x1, waiting for transfers between devices, on_device(): from_below = lax.ppermute(high, 'gx', to_upper)  3.52 us
    ppermute x1, starting transfers between devices, on_device(): from_below = lax.ppermute(high, 'gx', to_upper)  2.53 us
    pallas_call x1, Pallas kernels, outer_fields(): pl.pallas_call(outer_kernel, in_specs=[HBM] + [VMEM] * 7, out_specs=HBM,...  2.51 us
  transfers between devices with their start and end apart: 4, of which 2 were waited for; matrix products, arithmetic and copies ran while one was open for 0% of the time, Pallas kernels for 17%

profile of v6, /device:TPU:1, one launch (start us, length us, event | category | flops | bytes accessed | tf_op | source)
XLA Modules:
  0.0 81.0 jit_solution(2218978923433972833)
XLA Ops:
  0.0 0.0 copy-start
  0.0 5.4 %faces.1 = (s16[656,512]{1,0:T(8,128)(2,1)}, s16[656,512]{1,0:T(8,128)(2,1)}, s32[32,128]{1,0:T(8,128)}) custom-call(bf16[160,4,4096]{2,1,0:T(4,128)(2,1)} %values_hbm.3, s32[32,128]{1,0:T(8,128)} %bitcast.9, s32[1,8]{1,0:T(1,128)} %bitcast.6), custom_call_target="tpu_custom_call" | custom-call | tf_op jit(solution)/shard_map/faces/pallas_call | solution.py:136
  5.4 2.5 %collective-permute-start = (s16[656,512]{1,0:T(8,128)(2,1)}, s16[656,512]{1,0:T(8,128)(2,1)S(1)}, u32[]{:S(2)}, u32[]{:S(2)}) collective-permute-start(s16[656,512]{1,0:T(8,128)(2,1)} %get-tuple-element.23), channel_id=1, source_target_pairs={{0,8},{8,16},{16,24},{24,32},{32,40},{40,48},{48,56},{56,64},{64,7... | collective-permute-start | bytes 2015240 | tf_op jit(solution)/shard_map/ppermute | solution.py:472
  7.9 6.4 %collective-permute-start.1 = (s16[656,512]{1,0:T(8,128)(2,1)}, s16[656,512]{1,0:T(8,128)(2,1)S(1)}, u32[]{:S(2)}, u32[]{:S(2)}) collective-permute-start(s16[656,512]{1,0:T(8,128)(2,1)} %get-tuple-element.24), channel_id=1, source_target_pairs={{8,0},{16,8},{24,16},{32,24},{40,32},{48,40},{56,48},{64,56},{72,6... | collective-permute-start | bytes 2015240 | tf_op jit(solution)/shard_map/ppermute | solution.py:471
  14.3 0.0 copy-done
  14.3 0.0 copy-start.1
  14.3 0.7 copy-done.1
  15.0 10.5 %local.1 = (bf16[6,640,512]{2,1,0:T(8,128)(2,1)S(1)}, bf16[6,640,512]{2,1,0:T(8,128)(2,1)S(1)}, bf16[8,512,512]{2,1,0:T(8,128)(2,1)S(1)}, f32[160,160]{1,0:T(8,128)S(1)}) custom-call(s32[8]{0:T(128)S(1)} %copy-done, bf16[160,4,4096]{2,1,0:T(4,128)(2,1)} %values_hbm.3, s32[32,128]{1,0:T(8,128)S(1)} %copy-done.1), custom_call_target="tpu_custom_call" | custom-call | flops 6000000000 | bytes 14000000 | tf_op jit(solution)/shard_map/local/pallas_call | solution.py:189
  25.5 3.5 %collective-permute-done.from_below = s16[656,512]{1,0:T(8,128)(2,1)S(1)} collective-permute-done((s16[656,512]{1,0:T(8,128)(2,1)}, s16[656,512]{1,0:T(8,128)(2,1)S(1)}, u32[]{:S(2)}, u32[]{:S(2)}) %collective-permute-start) | collective-permute-done | bytes 671776 | tf_op jit(solution)/shard_map/ppermute | solution.py:472
  29.1 0.0 collective-permute-done.1.from_above
  29.1 1.5 %cross.1 = f32[128,128]{1,0:T(8,128)S(1)} custom-call(f32[160,160]{1,0:T(8,128)S(1)} %get-tuple-element.20.gram_ref, bf16[6,640,512]{2,1,0:T(8,128)(2,1)S(1)} %get-tuple-element.21.heads, bf16[6,640,512]{2,1,0:T(8,128)(2,1)S(1)} %get-tuple-element.22.rests, s16[656,512]{1,0:T(8,128)(2,1)S(1)} %collective-permute-done.from_below, ...), custom_call_target="tpu_custom_call" | custom-call | tf_op jit(solution)/shard_map/cross/pallas_call | solution.py:255
  30.6 13.3 %all_to_all.15.parts = f32[32,4,128]{2,1,0:T(4,128)S(1)} all-to-all(f32[32,4,128]{2,1,0:T(4,128)S(1)} %bitcast.5), channel_id=1, replica_groups={{0,1,2,3,4,5,6,7,64,65,66,67,68,69,70,71,128,129,130,131,132,133,134,13..., dimensions={0} | all-to-all | bytes 131072 | tf_op jit(solution)/shard_map/all_to_all | solution.py:288
  43.9 12.5 %all_to_all.16.parts = f32[8,4,128]{2,1,0:T(4,128)S(1)} all-to-all(f32[8,4,128]{2,1,0:T(4,128)S(1)} %sum.2), channel_id=1, replica_groups={{0,8,16,24,32,40,48,56},{1,9,17,25,33,41,49,57},{2,10,18,26,34,42,50,58..., dimensions={0} | all-to-all | bytes 32768 | tf_op jit(solution)/shard_map/all_to_all | solution.py:288
  56.4 12.3 %all_to_all.17 = f32[32,4,128]{2,1,0:T(4,128)S(1)} all-to-all(f32[32,4,128]{2,1,0:T(4,128)S(1)} %sum.3), channel_id=1, replica_groups={{0,1,2,3,4,5,6,7,64,65,66,67,68,69,70,71,128,129,130,131,132,133,134,13..., dimensions={0} | all-to-all | bytes 131072 | tf_op jit(solution)/shard_map/all_to_all | solution.py:288
  68.7 2.3 %basis.1 = (f32[8,160]{1,0:T(8,128)S(1)}, f32[32,512]{1,0:T(8,128)S(1)}, f32[32,512]{1,0:T(8,128)S(1)}) custom-call(f32[128,128]{1,0:T(8,128)S(1)} %bitcast.4, bf16[6,640,512]{2,1,0:T(8,128)(2,1)S(1)} %get-tuple-element.21.heads, bf16[6,640,512]{2,1,0:T(8,128)(2,1)S(1)} %get-tuple-element.22.rests), custom_call_target="tpu_custom_call" | custom-call | tf_op jit(solution)/shard_map/basis/pallas_call | solution.py:361
  71.0 0.9 %collective-permute-start.3 = (f32[32,512]{1,0:T(8,128)S(1)}, f32[32,512]{1,0:T(8,128)S(1)}, u32[]{:S(2)}, u32[]{:S(2)}) collective-permute-start(f32[32,512]{1,0:T(8,128)S(1)} %get-tuple-element.26.down_ref), channel_id=1, source_target_pairs={{8,0},{16,8},{24,16},{32,24},{40,32},{48,40},{56,48},{64,56},{72,6... | collective-permute-start | bytes 196616 | tf_op jit(solution)/shard_map/ppermute | solution.py:476
  71.9 0.6 collective-permute-start.2
  72.5 3.7 %inner.1 = (bf16[160,4,4096]{2,1,0:T(4,128)(2,1)}, bf16[6,64,512]{2,1,0:T(8,128)(2,1)S(1)}, f32[2,32,512]{2,1,0:T(8,128)S(1)}, bf16[640,128]{1,0:T(8,128)(2,1)S(1)}) custom-call(f32[8,160]{1,0:T(8,128)S(1)} %get-tuple-element.25.basis_ref, f32[32,512]{1,0:T(8,128)S(1)} %get-tuple-element.26.down_ref, f32[32,512]{1,0:T(8,128)S(1)} %get-tuple-element.27.up_ref, ...), custom_call_target="tpu_custom_call" | custom-call | flops 4000000000 | bytes 14000000 | tf_op jit(solution)/shard_map/inner/pallas_call | solution.py:416
  76.2 0.0 collective-permute-done.3.above
  76.2 2.1 %collective-permute-done.2.below = f32[32,512]{1,0:T(8,128)S(1)} collective-permute-done((f32[32,512]{1,0:T(8,128)S(1)}, f32[32,512]{1,0:T(8,128)S(1)}, u32[]{:S(2)}, u32[]{:S(2)}) %collective-permute-start.2) | collective-permute-done | bytes 65568 | tf_op jit(solution)/shard_map/ppermute | solution.py:477
  78.3 2.5 %outer.1 = bf16[160,4,4096]{2,1,0:T(4,128)(2,1)} custom-call(bf16[160,4,4096]{2,1,0:T(4,128)(2,1)} %get-tuple-element.29.filled_hbm, bf16[6,64,512]{2,1,0:T(8,128)(2,1)S(1)} %get-tuple-element.30.whole_ref, f32[2,32,512]{2,1,0:T(8,128)S(1)} %get-tuple-element.31.ends_ref, ...), custom_call_target="tpu_custom_call", output_to_operand_aliasing={{}: (0, {})} | custom-call | tf_op jit(solution)/shard_map/outer/pallas_call | solution.py:449
  (2 shorter events, 0.1 us)
Async XLA Ops:
  0.0 14.3 %copy-start = (s32[8]{0:T(128)S(1)}, s32[8]{0:T(128)}, u32[]{:S(2)}) copy-start(s32[8]{0:T(128)} %column_ref.1) | copy-start | bytes 100
  5.4 23.7 %collective-permute-start = (s16[656,512]{1,0:T(8,128)(2,1)}, s16[656,512]{1,0:T(8,128)(2,1)S(1)}, u32[]{:S(2)}, u32[]{:S(2)}) collective-permute-start(s16[656,512]{1,0:T(8,128)(2,1)} %get-tuple-element.23), channel_id=1, source_target_pairs={{0,8},{8,16},{16,24},{24,32},{32,40},{40,48},{48,56},{56,64},{64,7... | collective-permute-start | bytes 2015240 | tf_op jit(solution)/shard_map/ppermute | solution.py:472
  7.9 21.2 %collective-permute-start.1 = (s16[656,512]{1,0:T(8,128)(2,1)}, s16[656,512]{1,0:T(8,128)(2,1)S(1)}, u32[]{:S(2)}, u32[]{:S(2)}) collective-permute-start(s16[656,512]{1,0:T(8,128)(2,1)} %get-tuple-element.24), channel_id=1, source_target_pairs={{8,0},{16,8},{24,16},{32,24},{40,32},{48,40},{56,48},{64,56},{72,6... | collective-permute-start | bytes 2015240 | tf_op jit(solution)/shard_map/ppermute | solution.py:471
  14.3 0.7 copy-start.1
  71.0 5.2 %collective-permute-start.3 = (f32[32,512]{1,0:T(8,128)S(1)}, f32[32,512]{1,0:T(8,128)S(1)}, u32[]{:S(2)}, u32[]{:S(2)}) collective-permute-start(f32[32,512]{1,0:T(8,128)S(1)} %get-tuple-element.26.down_ref), channel_id=1, source_target_pairs={{8,0},{16,8},{24,16},{32,24},{40,32},{48,40},{56,48},{64,56},{72,6... | collective-permute-start | bytes 196616 | tf_op jit(solution)/shard_map/ppermute | solution.py:476
  71.9 6.4 %collective-permute-start.2 = (f32[32,512]{1,0:T(8,128)S(1)}, f32[32,512]{1,0:T(8,128)S(1)}, u32[]{:S(2)}, u32[]{:S(2)}) collective-permute-start(f32[32,512]{1,0:T(8,128)S(1)} %get-tuple-element.27.up_ref), channel_id=1, source_target_pairs={{0,8},{8,16},{16,24},{24,32},{32,40},{40,48},{48,56},{56,64},{64,7... | collective-permute-start | bytes 196616 | tf_op jit(solution)/shard_map/ppermute | solution.py:477

commit v7 on v6

--- a/solution.py
+++ b/solution.py
@@ -97,23 +97,18 @@
 SMEM = pl.BlockSpec(memory_space=pltpu.SMEM)
 
 
-def faces_kernel(
-    values_hbm, cells_hbm, column_hbm, low_hbm, high_hbm, passed_hbm, held, total, face, cells, columns, sems, small, out_sems
-):
+def faces_kernel(values_hbm, cells_hbm, column_hbm, low_ref, high_ref, cells, total, held, columns, sems, small):
     bricks = (0, 1, BRICKS - 2, BRICKS - 1)
-    targets = ((0, low_hbm), (EXT - 1, high_hbm))
+    targets = ((0, low_ref), (EXT - 1, high_ref))
     inputs = [
         pltpu.make_async_copy(cells_hbm, cells, small.at[0]),
         pltpu.make_async_copy(column_hbm, columns, small.at[1]),
     ]
     copies = [brick_copy(values_hbm, held, sems, brick, slot) for slot, brick in enumerate(bricks)]
-    outputs = [pltpu.make_async_copy(face.at[i], out, out_sems.at[i]) for i, (_, out) in enumerate(targets)]
     for copy in inputs + copies:
         copy.start()
     for copy in inputs:
         copy.wait()
-    outputs.append(pltpu.make_async_copy(cells, passed_hbm, out_sems.at[2]))
-    outputs[2].start()
     hots = [
         cell_hot(cells, brick, columns[:, brick : brick + 1] == targets[slot // 2][0]) for slot, brick in enumerate(bricks)
     ]
@@ -125,10 +120,7 @@
             sums = part if sums is None else sums + part
         for t in range(LANES):
             total[i, t] = sums[:, t * 128 : (t + 1) * 128]
-        encode(total.at[i], face.at[i])
-        outputs[i].start()
-    for copy in outputs:
-        copy.wait()
+        encode(total.at[i], targets[i][1])
 
 
 def face_sums(values, cells, columns):
@@ -136,47 +128,47 @@
     return pl.pallas_call(
         faces_kernel,
         in_specs=[HBM] * 3,
-        out_specs=[HBM] * 3,
+        out_specs=[VMEM] * 4,
         scratch_shapes=[
             pltpu.VMEM((4, SNAPS, FIELDS, PER_BRICK), BF16),
-            pltpu.VMEM((2, LANES, ROWS, 128), F32),
-            pltpu.VMEM((2, WIRE, CW), jnp.int16),
-            pltpu.VMEM((BRICKS * LANES, 128), jnp.int32),
             pltpu.VMEM((1, BRICKS), jnp.int32),
             pltpu.SemaphoreType.DMA((4,)),
             pltpu.SemaphoreType.DMA((2,)),
-            pltpu.SemaphoreType.DMA((3,)),
-        ],
-        out_shape=[shape, shape, jax.ShapeDtypeStruct((BRICKS * LANES, 128), jnp.int32)],
-        compiler_params=params(63),
+        ],
+        out_shape=[
+            shape,
+            shape,
+            jax.ShapeDtypeStruct((BRICKS * LANES, 128), jnp.int32),
+            jax.ShapeDtypeStruct((2, LANES, ROWS, 128), F32),
+        ],
+        compiler_params=params(50),
         name="faces",
     )(values, cells, columns)
 
 
-def local_kernel(
-    column_ref, values_hbm, cells_hbm, heads, rests, hots, gram_ref, cells, held, total, sems, small
-):
-    ids = pltpu.make_async_copy(cells_hbm, cells, small)
-    ids.start()
-    copies = [brick_copy(values_hbm, held, sems, brick, brick) for brick in range(BRICKS)]
+def local_kernel(column_ref, values_hbm, cells, faces, heads, rests, hots, gram_ref, held, total, sems):
+    copies = [brick_copy(values_hbm, held, sems, brick, brick - 1) for brick in range(1, BRICKS - 1)]
     for copy in copies:
         copy.start()
     total[...] = jnp.zeros_like(total)
-    ids.wait()
     for brick in range(BRICKS):
         hot = cell_hot(cells, brick)
         hots[brick] = hot
-        copies[brick].wait()
-        sums = dot_nt(held[brick].reshape(ROWS, PER_BRICK), hot)
+        if brick in (0, BRICKS - 1):
+            continue
+        copies[brick - 1].wait()
+        sums = dot_nt(held[brick - 1].reshape(ROWS, PER_BRICK), hot)
         column = column_ref[brick]
+        place = jnp.where(column == EXT - 1, 0, column)
         for t in range(LANES):
-            total[column, t] += sums[:, t * 128 : (t + 1) * 128]
+            total[place, t] += sums[:, t * 128 : (t + 1) * 128]
     same = jnp.zeros((SNAPS, SNAPS), F32)
     mixed = jnp.zeros((SNAPS, SNAPS), F32)
     for k in range(EXT):
+        source = faces.at[k // CX] if k in (0, EXT - 1) else total.at[k]
         for f in range(FIELDS):
             rows = slice(f * SNAPS, (f + 1) * SNAPS)
-            head, rest = halves(one_field(total.at[k], f))
+            head, rest = halves(one_field(source, f))
             heads[k, rows, :] = head
             rests[k, rows, :] = rest
             same += dot_nt(head, head)
@@ -184,18 +176,16 @@
     gram_ref[...] = same + mixed + mixed.T
 
 
-def local_sums(values, cells, columns):
+def local_sums(values, cells, columns, faces):
     half = jax.ShapeDtypeStruct((EXT, ROWS, CW), BF16)
     return pl.pallas_call(
         local_kernel,
-        in_specs=[SMEM, HBM, HBM],
+        in_specs=[SMEM, HBM, VMEM, VMEM],
         out_specs=[VMEM] * 4,
         scratch_shapes=[
-            pltpu.VMEM((BRICKS * LANES, 128), jnp.int32),
-            pltpu.VMEM((BRICKS, SNAPS, FIELDS, PER_BRICK), BF16),
-            pltpu.VMEM((EXT, LANES, ROWS, 128), F32),
-            pltpu.SemaphoreType.DMA((BRICKS,)),
-            pltpu.SemaphoreType.DMA,
+            pltpu.VMEM((BRICKS - 2, SNAPS, FIELDS, PER_BRICK), BF16),
+            pltpu.VMEM((CX + 1, LANES, ROWS, 128), F32),
+            pltpu.SemaphoreType.DMA((BRICKS - 2,)),
         ],
         out_shape=[
             half,
@@ -203,10 +193,10 @@
             jax.ShapeDtypeStruct((BRICKS, CW, PER_BRICK), BF16),
             jax.ShapeDtypeStruct((SNAPS, SNAPS), F32),
         ],
-        compiler_params=params(42),
+        compiler_params=params(39),
         cost_estimate=pl.CostEstimate(flops=6_000_000_000, bytes_accessed=14_000_000, transcendentals=0),
         name="local",
-    )(columns, values, cells)
+    )(columns, values, cells, faces)
 
 
 def pack(gram):
@@ -239,7 +229,7 @@
     return jnp.concatenate([top, bottom], axis=0)
 
 
-def cross_kernel(gram_ref, heads, rests, from_below, from_above, packed_ref):
+def cross_kernel(gram_ref, heads, rests, from_below, from_above, mine_ref, other_ref):
     cross = jnp.zeros((SNAPS, SNAPS), F32)
     for k, received in ((1, from_below), (CX, from_above)):
         scale = wire_scale(received)
@@ -248,49 +238,75 @@
             head, rest = halves(wire_steps(received, rows) * scale)
             own = heads[k, rows, :]
             cross += dot_nt(own, head) + dot_nt(own, rest) + dot_nt(rests[k, rows, :], head)
-    packed_ref[...] = pack(gram_ref[...] + cross + cross.T)
+    packed = pack(gram_ref[...] + cross + cross.T)
+    first = on_first_core()
+    mine_ref[...] = jnp.where(first, packed[: SPLIT // 2], packed[SPLIT // 2 :])
+    other_ref[...] = jnp.where(first, packed[SPLIT // 2 :], packed[: SPLIT // 2])
 
 
 def packed_gram(gram, heads, rests, from_below, from_above):
     return pl.pallas_call(
         cross_kernel,
         in_specs=[VMEM] * 5,
-        out_specs=VMEM,
-        out_shape=jax.ShapeDtypeStruct((SPLIT, SPLIT), F32),
+        out_specs=[VMEM] * 2,
+        out_shape=[jax.ShapeDtypeStruct((SPLIT // 2, SPLIT), F32)] * 2,
         compiler_params=params(16),
         name="cross",
     )(gram, heads, rests, from_below, from_above)
 
 
-def sum_kernel(parts, out_ref):
-    out_ref[...] = jnp.broadcast_to(parts[...].sum(0), out_ref.shape)
-
-
-def summed_copies(parts, copies):
-    return pl.pallas_call(
-        sum_kernel,
-        in_specs=[VMEM],
+def on_first_core():
+    return lax.rem(lax.axis_index("gz"), 2) == 0
+
+
+def tree_sum(terms):
+    while len(terms) > 1:
+        terms = [a + b for a, b in zip(terms[::2], terms[1::2])]
+    return terms[0]
+
+
+def terms_kernel(*refs):
+    out_ref = refs[-1]
+    out_ref[...] = jnp.broadcast_to(tree_sum([ref[...] for ref in refs[:-1]]), out_ref.shape)
+
+
+def parts_kernel(parts, out_ref):
+    out_ref[...] = tree_sum([parts[i] for i in range(parts.shape[0])])
+
+
+def small_sum(kernel, terms, shape):
+    return pl.pallas_call(
+        kernel,
+        in_specs=[VMEM] * len(terms),
         out_specs=VMEM,
-        out_shape=jax.ShapeDtypeStruct((copies,) + parts.shape[1:], F32),
-        compiler_params=params(2),
+        out_shape=jax.ShapeDtypeStruct(shape, F32),
+        compiler_params=params(4),
         name="sum",
-    )(parts)
-
-
-def add_over_devices(x):
+    )(*terms)
+
+
+def add_over_devices(mine, other):
     axes = ("gx", "gz")
     depth = 8
-    planes = [[i * 8 + j for i in range(z, 32, depth) for j in range(8)] for z in range(depth)]
-    lines = [list(line) for line in zip(*planes)]
-    size = len(planes[0])
-
-    def trade(parts, groups):
-        return lax.all_to_all(parts, axes, 0, 0, axis_index_groups=groups, tiled=True)
-
-    shape = (SPLIT // size, SPLIT)
-    mine = summed_copies(trade(x.reshape((size,) + shape), planes), depth)
-    mine = summed_copies(trade(mine, lines), size)
-    return trade(mine, planes).reshape(SPLIT, SPLIT)
+    places = [(a, z, y, c) for a in range(4) for z in range(depth) for y in range(4) for c in range(2)]
+    number = {place: i for i, place in enumerate(places)}
+    lines = [[number[a, z, y, c] for z in range(depth)] for a in range(4) for y in range(4) for c in range(2)]
+
+    def move(x, target):
+        return lax.ppermute(x, axes, [(number[place], number[target(*place)]) for place in places])
+
+    def swap(x):
+        return move(x, lambda a, z, y, c: (a, z, y, 1 - c))
+
+    shape = mine.shape
+    mine = small_sum(terms_kernel, [mine, swap(other)], shape)
+    others = [move(mine, lambda a, z, y, c, k=k: (a ^ k, z, y, c)) for k in (1, 2, 3)]
+    mine = small_sum(terms_kernel, [mine] + others, shape)
+    others = [move(mine, lambda a, z, y, c, k=k: (a, z, y ^ k, c)) for k in (1, 2, 3)]
+    copies = small_sum(terms_kernel, [mine] + others, (depth,) + shape)
+    parts = lax.all_to_all(copies, axes, 0, 0, axis_index_groups=lines, tiled=True)
+    mine = small_sum(parts_kernel, [parts], shape)
+    return mine, swap(mine)
 
 
 def orthonormal(basis):
@@ -345,8 +361,10 @@
     return pair[:COEFS] + pair[COEFS:] + dot(both[:COEFS], rest)
 
 
-def basis_kernel(packed_ref, heads, rests, basis_ref, down_ref, up_ref):
-    gram = unpack(packed_ref[...])
+def basis_kernel(mine_ref, other_ref, heads, rests, basis_ref, down_ref, up_ref):
+    first = on_first_core()
+    mine, other = mine_ref[...], other_ref[...]
+    gram = unpack(jnp.concatenate([jnp.where(first, mine, other), jnp.where(first, other, mine)], axis=0))
     basis = gram[:MODES, :]
     for _ in range(SWEEPS):
         basis = orthonormal(exact_dot(basis, gram))
@@ -356,16 +374,16 @@
     up_ref[...] = coefficients(both, heads[CX], rests[CX])
 
 
-def basis_and_faces(packed, heads, rests):
+def basis_and_faces(mine, other, heads, rests):
     side = jax.ShapeDtypeStruct((COEFS, CW), F32)
     return pl.pallas_call(
         basis_kernel,
-        in_specs=[VMEM] * 3,
+        in_specs=[VMEM] * 4,
         out_specs=[VMEM] * 3,
         out_shape=[jax.ShapeDtypeStruct((MODES, SNAPS), F32), side, side],
         compiler_params=params(16),
         name="basis",
-    )(packed, heads, rests)
+    )(mine, other, heads, rests)
 
 
 def column_of(columns, brick, whole):
@@ -467,12 +485,12 @@
     to_upper = [(i, (i + 1) % count) for i in range(count)]
     cells = atom_cell.reshape(BRICKS * LANES, 128)
     columns = brick_column.reshape(1, BRICKS)
-    low, high, passed = face_sums(atom_values, cells, columns)
+    low, high, passed, totals = face_sums(atom_values, cells, columns)
     from_above = lax.ppermute(low, "gx", to_lower)
     from_below = lax.ppermute(high, "gx", to_upper)
-    heads, rests, hots, gram = local_sums(atom_values, passed, brick_column)
-    packed = add_over_devices(packed_gram(gram, heads, rests, from_below, from_above))
-    basis, down, up = basis_and_faces(packed, heads, rests)
+    heads, rests, hots, gram = local_sums(atom_values, passed, brick_column, totals)
+    mine, other = add_over_devices(*packed_gram(gram, heads, rests, from_below, from_above))
+    basis, down, up = basis_and_faces(mine, other, heads, rests)
     above = lax.ppermute(down, "gx", to_lower)
     below = lax.ppermute(up, "gx", to_upper)
     filled, whole, ends, spread = inner_fields(basis, down, up, from_below, from_above, columns, heads, rests, hots)

time: 81.3 us -> 76.9 us (0.946)
  blocking collectives: 38.1 us -> 14.9 us
  starting transfers between devices: 10.5 us -> 23.4 us
  waiting for transfers between devices: 5.64 us -> 14.4 us
  Pallas kernels: 25.9 us -> 22.4 us
    all_to_all x3 -> x1, blocking collectives: 38.1 us -> 14.9 us  [add_over_devices(): lax.all_to_all(copies, axes, 0, 0, axis_index_groups=lines, tiled=True)]
    ppermute x0 -> x8, starting transfers between devices: none -> 12.9 us  [move(): lax.ppermute(x, axes, [(number[place], number[target(*place)]) for place...]
    ppermute x0 -> x8, waiting for transfers between devices: none -> 7.26 us  [move(): lax.ppermute(x, axes, [(number[place], number[target(*place)]) for place...]
    pallas_call x6 -> x8, Pallas kernels: 19.7 us -> 16.2 us  [the longest x1 8.77 us: local_sums(): pl.pallas_call(local_kernel, in_specs=[SMEM, HBM, VMEM, VMEM], out_specs=...]
    ppermute x1, waiting for transfers between devices: 3.52 us -> 5.76 us  [on_device(): from_below = lax.ppermute(high, 'gx', to_upper)]
    ppermute x1, starting transfers between devices: 0.9 us -> 0.06 us  [on_device(): above = lax.ppermute(down, 'gx', to_lower)]
    ppermute x1, starting transfers between devices: 0.63 us -> 1.45 us  [on_device(): below = lax.ppermute(up, 'gx', to_upper)]
  transfers between devices with their start and end apart: 4 -> 12, of which waited for: 2 -> 9; matrix products, arithmetic and copies ran while one was open for 0% -> 0% of each run, Pallas kernels for 17% -> 16%
where the time goes in v7:
time: 76.9 us; the launch traced here: 76.7 us
  starting transfers between devices  23.4 us (30%)
  Pallas kernels  22.4 us (29%)
  blocking collectives  14.9 us (19%)
  waiting for transfers between devices  14.4 us (19%)
  local copies, waits for them, and re-layouts  1.39 us (2%)
    all_to_all x1, blocking collectives, add_over_devices(): lax.all_to_all(copies, axes, 0, 0, axis_index_groups=lines, tiled=True)  14.9 us
    ppermute x8, starting transfers between devices, move(): lax.ppermute(x, axes, [(number[place], number[target(*place)]) for place...  12.9 us
    pallas_call x1, Pallas kernels, local_sums(): pl.pallas_call(local_kernel, in_specs=[SMEM, HBM, VMEM, VMEM], out_specs=...  8.77 us
    ppermute x8, waiting for transfers between devices, move(): lax.ppermute(x, axes, [(number[place], number[target(*place)]) for place...  7.26 us
    ppermute x1, starting transfers between devices, on_device(): from_above = lax.ppermute(low, 'gx', to_lower)  6.4 us
    ppermute x1, waiting for transfers between devices, on_device(): from_below = lax.ppermute(high, 'gx', to_upper)  5.76 us
    pallas_call x1, Pallas kernels, inner_fields(): pl.pallas_call(inner_kernel, in_specs=[VMEM] * 9, out_specs=[HBM] + [VMEM...  3.67 us
    pallas_call x1, Pallas kernels, face_sums(): pl.pallas_call(faces_kernel, in_specs=[HBM] * 3, out_specs=[VMEM] * 4, sc...  3.6 us
  transfers between devices with their start and end apart: 12, of which 9 were waited for; matrix products, arithmetic and copies ran while one was open for 0% of the time, Pallas kernels for 16%

profile of v7, /device:TPU:1, one launch (start us, length us, event | category | flops | bytes accessed | tf_op | source)
XLA Modules:
  0.0 76.7 jit_solution(6253403562252080701)
XLA Ops:
  0.0 0.7 copy-done
  0.7 0.7 copy-done.1
  1.4 3.6 %faces.1 = (s16[656,512]{1,0:T(8,128)(2,1)S(1)}, s16[656,512]{1,0:T(8,128)(2,1)S(1)}, s32[32,128]{1,0:T(8,128)S(1)}, f32[2,4,640,128]{3,2,1,0:T(8,128)S(1)}) custom-call(bf16[160,4,4096]{2,1,0:T(4,128)(2,1)} %values_hbm.3, s32[32,128]{1,0:T(8,128)S(1)} %bitcast.2, s32[1,8]{1,0:T(1,128)S(1)} %bitcast.3), custom_call_target="tpu_custom_call" | custom-call | tf_op jit(solution)/shard_map/faces/pallas_call | solution.py:128
  5.0 2.5 %collective-permute-start = (s16[656,512]{1,0:T(8,128)(2,1)S(1)}, s16[656,512]{1,0:T(8,128)(2,1)S(1)}, u32[]{:S(2)}, u32[]{:S(2)}) collective-permute-start(s16[656,512]{1,0:T(8,128)(2,1)S(1)} %get-tuple-element.27), channel_id=1, source_target_pairs={{0,8},{8,16},{16,24},{24,32},{32,40},{40,48},{48,56},{56,64},{64,7... | collective-permute-start | bytes 2015240 | tf_op jit(solution)/shard_map/ppermute | solution.py:490
  7.5 6.4 %collective-permute-start.1 = (s16[656,512]{1,0:T(8,128)(2,1)S(1)}, s16[656,512]{1,0:T(8,128)(2,1)S(1)}, u32[]{:S(2)}, u32[]{:S(2)}) collective-permute-start(s16[656,512]{1,0:T(8,128)(2,1)S(1)} %get-tuple-element.28), channel_id=1, source_target_pairs={{8,0},{16,8},{24,16},{32,24},{40,32},{48,40},{56,48},{64,56},{72,6... | collective-permute-start | bytes 2015240 | tf_op jit(solution)/shard_map/ppermute | solution.py:489
  14.0 8.8 %local.1 = (bf16[6,640,512]{2,1,0:T(8,128)(2,1)S(1)}, bf16[6,640,512]{2,1,0:T(8,128)(2,1)S(1)}, bf16[8,512,512]{2,1,0:T(8,128)(2,1)S(1)}, f32[160,160]{1,0:T(8,128)S(1)}) custom-call(s32[8]{0:T(128)S(1)} %copy-done.2, bf16[160,4,4096]{2,1,0:T(4,128)(2,1)} %values_hbm.3, s32[32,128]{1,0:T(8,128)S(1)} %get-tuple-element.22.cells, ...), custom_call_target="tpu_custom_call" | custom-call | flops 6000000000 | bytes 14000000 | tf_op jit(solution)/shard_map/local/pallas_call | solution.py:181
  22.7 5.8 %collective-permute-done.from_below = s16[656,512]{1,0:T(8,128)(2,1)S(1)} collective-permute-done((s16[656,512]{1,0:T(8,128)(2,1)S(1)}, s16[656,512]{1,0:T(8,128)(2,1)S(1)}, u32[]{:S(2)}, u32[]{:S(2)}) %collective-permute-start) | collective-permute-done | bytes 671776 | tf_op jit(solution)/shard_map/ppermute | solution.py:490
  28.5 1.5 %cross.1 = (f32[64,128]{1,0:T(8,128)S(1)}, f32[64,128]{1,0:T(8,128)S(1)}) custom-call(f32[160,160]{1,0:T(8,128)S(1)} %get-tuple-element.24.gram_ref, bf16[6,640,512]{2,1,0:T(8,128)(2,1)S(1)} %get-tuple-element.25.heads, bf16[6,640,512]{2,1,0:T(8,128)(2,1)S(1)} %get-tuple-element.26.rests, s16[656,512]{1,0:T(8,128)(2,1)S(1)} %collective-permute-done.from_below, ...), custom_call_target="tpu_custom_call" | custom-call | tf_op jit(solution)/shard_map/cross/pallas_call | solution.py:248
  30.0 1.3 %collective-permute-start.2 = (f32[64,128]{1,0:T(8,128)S(1)}, f32[64,128]{1,0:T(8,128)S(1)}, u32[]{:S(2)}, u32[]{:S(2)}) collective-permute-start(f32[64,128]{1,0:T(8,128)S(1)} %get-tuple-element.30), channel_id=1, source_target_pairs={{0,1},{1,0},{2,3},{3,2},{4,5},{5,4},{6,7},{7,6},{8,9},{9,8},{10,11... | collective-permute-start | bytes 98312 | tf_op jit(solution)/shard_map/ppermute | solution.py:296
  31.3 0.9 %collective-permute-done.2.refs_1_ = f32[64,128]{1,0:T(8,128)S(1)} collective-permute-done((f32[64,128]{1,0:T(8,128)S(1)}, f32[64,128]{1,0:T(8,128)S(1)}, u32[]{:S(2)}, u32[]{:S(2)}) %collective-permute-start.2) | collective-permute-done | bytes 32800 | tf_op jit(solution)/shard_map/ppermute | solution.py:296
  32.2 0.6 collective-permute-start.5
  32.7 0.2 collective-permute-start.4
  32.9 2.5 %collective-permute-start.3 = (f32[64,128]{1,0:T(8,128)S(1)}, f32[64,128]{1,0:T(8,128)S(1)}, u32[]{:S(2)}, u32[]{:S(2)}) collective-permute-start(f32[64,128]{1,0:T(8,128)S(1)} %sum.4.refs_0_), channel_id=1, source_target_pairs={{0,64},{1,65},{2,66},{3,67},{4,68},{5,69},{6,70},{7,71},{8,72},{9,... | collective-permute-start | bytes 98312 | tf_op jit(solution)/shard_map/ppermute | solution.py:296
  35.4 0.7 collective-permute-done.5.refs_3_
  36.1 1.0 %collective-permute-done.4.refs_2_ = f32[64,128]{1,0:T(8,128)S(1)} collective-permute-done((f32[64,128]{1,0:T(8,128)S(1)}, f32[64,128]{1,0:T(8,128)S(1)}, u32[]{:S(2)}, u32[]{:S(2)}) %collective-permute-start.4) | collective-permute-done | bytes 32800 | tf_op jit(solution)/shard_map/ppermute | solution.py:296
  37.1 0.3 collective-permute-done.3.refs_1_
  37.4 2.8 %collective-permute-start.8 = (f32[64,128]{1,0:T(8,128)S(1)}, f32[64,128]{1,0:T(8,128)S(1)}, u32[]{:S(2)}, u32[]{:S(2)}) collective-permute-start(f32[64,128]{1,0:T(8,128)S(1)} %sum.5.refs_0_), channel_id=1, source_target_pairs={{0,6},{1,7},{2,4},{3,5},{4,2},{5,3},{6,0},{7,1},{8,14},{9,15},{10,... | collective-permute-start | bytes 98312 | tf_op jit(solution)/shard_map/ppermute | solution.py:296
  40.2 0.3 collective-permute-start.7
  40.5 0.3 collective-permute-start.6
  40.9 0.6 collective-permute-done.8.refs_3_
  41.5 3.0 %collective-permute-done.7.refs_2_ = f32[64,128]{1,0:T(8,128)S(1)} collective-permute-done((f32[64,128]{1,0:T(8,128)S(1)}, f32[64,128]{1,0:T(8,128)S(1)}, u32[]{:S(2)}, u32[]{:S(2)}) %collective-permute-start.7) | collective-permute-done | bytes 32800 | tf_op jit(solution)/shard_map/ppermute | solution.py:296
  44.5 0.0 collective-permute-done.6.refs_1_
  44.5 14.9 %all_to_all.5.parts = f32[8,64,128]{2,1,0:T(8,128)S(1)} all-to-all(f32[8,64,128]{2,1,0:T(8,128)S(1)} %sum.6), channel_id=1, replica_groups={{0,8,16,24,32,40,48,56},{1,9,17,25,33,41,49,57},{2,10,18,26,34,42,50,58..., dimensions={0} | all-to-all | bytes 524288 | tf_op jit(solution)/shard_map/all_to_all | solution.py:307
  59.4 4.8 %collective-permute-start.9 = (f32[64,128]{1,0:T(8,128)S(1)}, f32[64,128]{1,0:T(8,128)S(1)}, u32[]{:S(2)}, u32[]{:S(2)}) collective-permute-start(f32[64,128]{1,0:T(8,128)S(1)} %sum.7.mine_ref), channel_id=1, source_target_pairs={{0,1},{1,0},{2,3},{3,2},{4,5},{5,4},{6,7},{7,6},{8,9},{9,8},{10,11... | collective-permute-start | bytes 98312 | tf_op jit(solution)/shard_map/ppermute | solution.py:296
  64.3 0.9 %collective-permute-done.9.other_ref = f32[64,128]{1,0:T(8,128)S(1)} collective-permute-done((f32[64,128]{1,0:T(8,128)S(1)}, f32[64,128]{1,0:T(8,128)S(1)}, u32[]{:S(2)}, u32[]{:S(2)}) %collective-permute-start.9) | collective-permute-done | bytes 32800 | tf_op jit(solution)/shard_map/ppermute | solution.py:296
  65.1 2.3 %basis.1 = (f32[8,160]{1,0:T(8,128)S(1)}, f32[32,512]{1,0:T(8,128)S(1)}, f32[32,512]{1,0:T(8,128)S(1)}) custom-call(f32[64,128]{1,0:T(8,128)S(1)} %sum.7.mine_ref, f32[64,128]{1,0:T(8,128)S(1)} %collective-permute-done.9.other_ref, bf16[6,640,512]{2,1,0:T(8,128)(2,1)S(1)} %get-tuple-element.25.heads, bf16[6,640,512]{2,1,0:T(8,128)(2,1)S(1)} %get-tuple-element.26.rests), custom_call_target="tpu_custom_call" | custom-call | tf_op jit(solution)/shard_map/basis/pallas_call | solution.py:379
  67.4 0.1 collective-permute-start.11
  67.5 1.5 %collective-permute-start.10 = (f32[32,512]{1,0:T(8,128)S(1)}, f32[32,512]{1,0:T(8,128)S(1)}, u32[]{:S(2)}, u32[]{:S(2)}) collective-permute-start(f32[32,512]{1,0:T(8,128)S(1)} %get-tuple-element.33.up_ref), channel_id=1, source_target_pairs={{0,8},{8,16},{16,24},{24,32},{32,40},{40,48},{48,56},{56,64},{64,7... | collective-permute-start | bytes 196616 | tf_op jit(solution)/shard_map/ppermute | solution.py:495
  69.0 3.7 %inner.1 = (bf16[160,4,4096]{2,1,0:T(4,128)(2,1)}, bf16[6,64,512]{2,1,0:T(8,128)(2,1)S(1)}, f32[2,32,512]{2,1,0:T(8,128)S(1)}, bf16[640,128]{1,0:T(8,128)(2,1)S(1)}) custom-call(f32[8,160]{1,0:T(8,128)S(1)} %get-tuple-element.31.basis_ref, f32[32,512]{1,0:T(8,128)S(1)} %get-tuple-element.32.down_ref, f32[32,512]{1,0:T(8,128)S(1)} %get-tuple-element.33.up_ref, ...), custom_call_target="tpu_custom_call" | custom-call | flops 4000000000 | bytes 14000000 | tf_op jit(solution)/shard_map/inner/pallas_call | solution.py:434
  72.6 0.0 collective-permute-done.11.above
  72.7 1.4 %collective-permute-done.10.below = f32[32,512]{1,0:T(8,128)S(1)} collective-permute-done((f32[32,512]{1,0:T(8,128)S(1)}, f32[32,512]{1,0:T(8,128)S(1)}, u32[]{:S(2)}, u32[]{:S(2)}) %collective-permute-start.10) | collective-permute-done | bytes 65568 | tf_op jit(solution)/shard_map/ppermute | solution.py:495
  74.0 2.5 %outer.1 = bf16[160,4,4096]{2,1,0:T(4,128)(2,1)} custom-call(bf16[160,4,4096]{2,1,0:T(4,128)(2,1)} %get-tuple-element.35.filled_hbm, bf16[6,64,512]{2,1,0:T(8,128)(2,1)S(1)} %get-tuple-element.36.whole_ref, f32[2,32,512]{2,1,0:T(8,128)S(1)} %get-tuple-element.37.ends_ref, ...), custom_call_target="tpu_custom_call", output_to_operand_aliasing={{}: (0, {})} | custom-call | tf_op jit(solution)/shard_map/outer/pallas_call | solution.py:467
  (9 shorter events, 0.1 us)
Async XLA Ops:
  0.0 14.0 %copy-start.2 = (s32[8]{0:T(128)S(1)}, s32[8]{0:T(128)}, u32[]{:S(2)}) copy-start(s32[8]{0:T(128)} %column_ref.1) | copy-start | bytes 100
  0.0 0.7 copy-start
  0.7 0.7 copy-start.1
  5.0 23.5 %collective-permute-start = (s16[656,512]{1,0:T(8,128)(2,1)S(1)}, s16[656,512]{1,0:T(8,128)(2,1)S(1)}, u32[]{:S(2)}, u32[]{:S(2)}) collective-permute-start(s16[656,512]{1,0:T(8,128)(2,1)S(1)} %get-tuple-element.27), channel_id=1, source_target_pairs={{0,8},{8,16},{16,24},{24,32},{32,40},{40,48},{48,56},{56,64},{64,7... | collective-permute-start | bytes 2015240 | tf_op jit(solution)/shard_map/ppermute | solution.py:490
  7.5 20.9 %collective-permute-start.1 = (s16[656,512]{1,0:T(8,128)(2,1)S(1)}, s16[656,512]{1,0:T(8,128)(2,1)S(1)}, u32[]{:S(2)}, u32[]{:S(2)}) collective-permute-start(s16[656,512]{1,0:T(8,128)(2,1)S(1)} %get-tuple-element.28), channel_id=1, source_target_pairs={{8,0},{16,8},{24,16},{32,24},{40,32},{48,40},{56,48},{64,56},{72,6... | collective-permute-start | bytes 2015240 | tf_op jit(solution)/shard_map/ppermute | solution.py:489
  30.0 2.2 %collective-permute-start.2 = (f32[64,128]{1,0:T(8,128)S(1)}, f32[64,128]{1,0:T(8,128)S(1)}, u32[]{:S(2)}, u32[]{:S(2)}) collective-permute-start(f32[64,128]{1,0:T(8,128)S(1)} %get-tuple-element.30), channel_id=1, source_target_pairs={{0,1},{1,0},{2,3},{3,2},{4,5},{5,4},{6,7},{7,6},{8,9},{9,8},{10,11... | collective-permute-start | bytes 98312 | tf_op jit(solution)/shard_map/ppermute | solution.py:296
  32.2 4.0 %collective-permute-start.5 = (f32[64,128]{1,0:T(8,128)S(1)}, f32[64,128]{1,0:T(8,128)S(1)}, u32[]{:S(2)}, u32[]{:S(2)}) collective-permute-start(f32[64,128]{1,0:T(8,128)S(1)} %sum.4.refs_0_), channel_id=1, source_target_pairs={{0,192},{1,193},{2,194},{3,195},{4,196},{5,197},{6,198},{7,199},{8... | collective-permute-start | bytes 98312 | tf_op jit(solution)/shard_map/ppermute | solution.py:296
  32.7 4.4 %collective-permute-start.4 = (f32[64,128]{1,0:T(8,128)S(1)}, f32[64,128]{1,0:T(8,128)S(1)}, u32[]{:S(2)}, u32[]{:S(2)}) collective-permute-start(f32[64,128]{1,0:T(8,128)S(1)} %sum.4.refs_0_), channel_id=1, source_target_pairs={{0,128},{1,129},{2,130},{3,131},{4,132},{5,133},{6,134},{7,135},{8... | collective-permute-start | bytes 98312 | tf_op jit(solution)/shard_map/ppermute | solution.py:296
  32.9 4.4 %collective-permute-start.3 = (f32[64,128]{1,0:T(8,128)S(1)}, f32[64,128]{1,0:T(8,128)S(1)}, u32[]{:S(2)}, u32[]{:S(2)}) collective-permute-start(f32[64,128]{1,0:T(8,128)S(1)} %sum.4.refs_0_), channel_id=1, source_target_pairs={{0,64},{1,65},{2,66},{3,67},{4,68},{5,69},{6,70},{7,71},{8,72},{9,... | collective-permute-start | bytes 98312 | tf_op jit(solution)/shard_map/ppermute | solution.py:296
  37.4 4.1 %collective-permute-start.8 = (f32[64,128]{1,0:T(8,128)S(1)}, f32[64,128]{1,0:T(8,128)S(1)}, u32[]{:S(2)}, u32[]{:S(2)}) collective-permute-start(f32[64,128]{1,0:T(8,128)S(1)} %sum.5.refs_0_), channel_id=1, source_target_pairs={{0,6},{1,7},{2,4},{3,5},{4,2},{5,3},{6,0},{7,1},{8,14},{9,15},{10,... | collective-permute-start | bytes 98312 | tf_op jit(solution)/shard_map/ppermute | solution.py:296
  40.2 4.3 %collective-permute-start.7 = (f32[64,128]{1,0:T(8,128)S(1)}, f32[64,128]{1,0:T(8,128)S(1)}, u32[]{:S(2)}, u32[]{:S(2)}) collective-permute-start(f32[64,128]{1,0:T(8,128)S(1)} %sum.5.refs_0_), channel_id=1, source_target_pairs={{0,4},{1,5},{2,6},{3,7},{4,0},{5,1},{6,2},{7,3},{8,12},{9,13},{10,... | collective-permute-start | bytes 98312 | tf_op jit(solution)/shard_map/ppermute | solution.py:296
  40.5 3.9 %collective-permute-start.6 = (f32[64,128]{1,0:T(8,128)S(1)}, f32[64,128]{1,0:T(8,128)S(1)}, u32[]{:S(2)}, u32[]{:S(2)}) collective-permute-start(f32[64,128]{1,0:T(8,128)S(1)} %sum.5.refs_0_), channel_id=1, source_target_pairs={{0,2},{1,3},{2,0},{3,1},{4,6},{5,7},{6,4},{7,5},{8,10},{9,11},{10,... | collective-permute-start | bytes 98312 | tf_op jit(solution)/shard_map/ppermute | solution.py:296
  59.4 5.7 %collective-permute-start.9 = (f32[64,128]{1,0:T(8,128)S(1)}, f32[64,128]{1,0:T(8,128)S(1)}, u32[]{:S(2)}, u32[]{:S(2)}) collective-permute-start(f32[64,128]{1,0:T(8,128)S(1)} %sum.7.mine_ref), channel_id=1, source_target_pairs={{0,1},{1,0},{2,3},{3,2},{4,5},{5,4},{6,7},{7,6},{8,9},{9,8},{10,11... | collective-permute-start | bytes 98312 | tf_op jit(solution)/shard_map/ppermute | solution.py:296
  67.4 5.2 %collective-permute-start.11 = (f32[32,512]{1,0:T(8,128)S(1)}, f32[32,512]{1,0:T(8,128)S(1)}, u32[]{:S(2)}, u32[]{:S(2)}) collective-permute-start(f32[32,512]{1,0:T(8,128)S(1)} %get-tuple-element.32.down_ref), channel_id=1, source_target_pairs={{8,0},{16,8},{24,16},{32,24},{40,32},{48,40},{56,48},{64,56},{72,6... | collective-permute-start | bytes 196616 | tf_op jit(solution)/shard_map/ppermute | solution.py:494
  67.5 6.5 %collective-permute-start.10 = (f32[32,512]{1,0:T(8,128)S(1)}, f32[32,512]{1,0:T(8,128)S(1)}, u32[]{:S(2)}, u32[]{:S(2)}) collective-permute-start(f32[32,512]{1,0:T(8,128)S(1)} %get-tuple-element.33.up_ref), channel_id=1, source_target_pairs={{0,8},{8,16},{16,24},{24,32},{32,40},{40,48},{48,56},{56,64},{64,7... | collective-permute-start | bytes 196616 | tf_op jit(solution)/shard_map/ppermute | solution.py:495

commit v8 on v7

--- a/solution.py
+++ b/solution.py
@@ -1,3 +1,4 @@
+import functools
 import math
 
 import jax
@@ -18,7 +19,9 @@
 PER_BRICK = 512
 BRICKS = 8
 COEFS = MODES * FIELDS
-WIRE = ROWS + 16
+PART = SNAPS // 2
+PART_ROWS = PART * FIELDS
+WIRE = PART_ROWS + 16
 TOP = 32767.0
 STEPS = 8 / math.log(2)
 SPLIT = 128
@@ -63,7 +66,7 @@
 
 
 def one_field(total, field):
-    rows = pl.ds(field, SNAPS, stride=FIELDS)
+    rows = pl.ds(field, total.shape[1] // FIELDS, stride=FIELDS)
     return jnp.concatenate([total[t, rows, :] for t in range(LANES)], axis=1)
 
 
@@ -79,9 +82,9 @@
         code = jnp.ceil(jnp.log(jnp.maximum(most, 1e-30)) * STEPS)
         scale = jnp.exp(code * (-1 / STEPS)) * TOP
         for f in range(FIELDS):
-            steps = jnp.round(total[t, pl.ds(f, SNAPS, stride=FIELDS), :] * scale)
-            out_ref[f * SNAPS : (f + 1) * SNAPS, lanes] = jnp.clip(steps, -TOP, TOP).astype(jnp.int32).astype(jnp.int16)
-        out_ref[ROWS:, lanes] = jnp.broadcast_to(code, (WIRE - ROWS, 128)).astype(jnp.int32).astype(jnp.int16)
+            steps = jnp.round(total[t, pl.ds(f, PART, stride=FIELDS), :] * scale)
+            out_ref[f * PART : (f + 1) * PART, lanes] = jnp.clip(steps, -TOP, TOP).astype(jnp.int32).astype(jnp.int16)
+        out_ref[PART_ROWS:, lanes] = jnp.broadcast_to(code, (WIRE - PART_ROWS, 128)).astype(jnp.int32).astype(jnp.int16)
 
 
 def wire_steps(wire, rows):
@@ -89,7 +92,7 @@
 
 
 def wire_scale(wire):
-    return jnp.exp(wire_steps(wire, slice(ROWS, WIRE))[:1] * (1 / STEPS)) * (1 / TOP)
+    return jnp.exp(wire_steps(wire, slice(PART_ROWS, WIRE))[:1] * (1 / STEPS)) * (1 / TOP)
 
 
 HBM = pl.BlockSpec(memory_space=pltpu.HBM)
@@ -97,14 +100,17 @@
 SMEM = pl.BlockSpec(memory_space=pltpu.SMEM)
 
 
-def faces_kernel(values_hbm, cells_hbm, column_hbm, low_ref, high_ref, cells, total, held, columns, sems, small):
+def faces_kernel(part, values_hbm, cells_hbm, column_hbm, low_ref, high_ref, cells, columns, total, held, sems, small):
     bricks = (0, 1, BRICKS - 2, BRICKS - 1)
     targets = ((0, low_ref), (EXT - 1, high_ref))
     inputs = [
         pltpu.make_async_copy(cells_hbm, cells, small.at[0]),
         pltpu.make_async_copy(column_hbm, columns, small.at[1]),
     ]
-    copies = [brick_copy(values_hbm, held, sems, brick, slot) for slot, brick in enumerate(bricks)]
+    copies = []
+    for slot, brick in enumerate(bricks):
+        source = values_hbm.at[pl.ds(part * PART, PART), :, pl.ds(brick * PER_BRICK, PER_BRICK)]
+        copies.append(pltpu.make_async_copy(source, held.at[slot], sems.at[slot]))
     for copy in inputs + copies:
         copy.start()
     for copy in inputs:
@@ -116,22 +122,21 @@
         sums = None
         for slot in (2 * i, 2 * i + 1):
             copies[slot].wait()
-            part = dot_nt(held[slot].reshape(ROWS, PER_BRICK), hots[slot])
-            sums = part if sums is None else sums + part
+            part_sums = dot_nt(held[slot].reshape(PART_ROWS, PER_BRICK), hots[slot])
+            sums = part_sums if sums is None else sums + part_sums
         for t in range(LANES):
             total[i, t] = sums[:, t * 128 : (t + 1) * 128]
         encode(total.at[i], targets[i][1])
 
 
-def face_sums(values, cells, columns):
+def face_sums(part, values, cells, columns):
     shape = jax.ShapeDtypeStruct((WIRE, CW), jnp.int16)
     return pl.pallas_call(
-        faces_kernel,
+        functools.partial(faces_kernel, part),
         in_specs=[HBM] * 3,
-        out_specs=[VMEM] * 4,
+        out_specs=[VMEM] * 5,
         scratch_shapes=[
-            pltpu.VMEM((4, SNAPS, FIELDS, PER_BRICK), BF16),
-            pltpu.VMEM((1, BRICKS), jnp.int32),
+            pltpu.VMEM((4, PART, FIELDS, PER_BRICK), BF16),
             pltpu.SemaphoreType.DMA((4,)),
             pltpu.SemaphoreType.DMA((2,)),
         ],
@@ -139,14 +144,16 @@
             shape,
             shape,
             jax.ShapeDtypeStruct((BRICKS * LANES, 128), jnp.int32),
-            jax.ShapeDtypeStruct((2, LANES, ROWS, 128), F32),
-        ],
-        compiler_params=params(50),
+            jax.ShapeDtypeStruct((1, BRICKS), jnp.int32),
+            jax.ShapeDtypeStruct((2, LANES, PART_ROWS, 128), F32),
+        ],
+        compiler_params=params((51, 50)[part]),
+        cost_estimate=pl.CostEstimate(flops=1_400_000_000, bytes_accessed=4_000_000, transcendentals=0),
         name="faces",
     )(values, cells, columns)
 
 
-def local_kernel(column_ref, values_hbm, cells, faces, heads, rests, hots, gram_ref, held, total, sems):
+def local_kernel(column_ref, values_hbm, cells, early, late, heads, rests, hots, gram_ref, held, total, sems):
     copies = [brick_copy(values_hbm, held, sems, brick, brick - 1) for brick in range(1, BRICKS - 1)]
     for copy in copies:
         copy.start()
@@ -165,10 +172,13 @@
     same = jnp.zeros((SNAPS, SNAPS), F32)
     mixed = jnp.zeros((SNAPS, SNAPS), F32)
     for k in range(EXT):
-        source = faces.at[k // CX] if k in (0, EXT - 1) else total.at[k]
         for f in range(FIELDS):
             rows = slice(f * SNAPS, (f + 1) * SNAPS)
-            head, rest = halves(one_field(source, f))
+            if k in (0, EXT - 1):
+                sums = jnp.concatenate([one_field(early.at[k // CX], f), one_field(late.at[k // CX], f)], axis=0)
+            else:
+                sums = one_field(total.at[k], f)
+            head, rest = halves(sums)
             heads[k, rows, :] = head
             rests[k, rows, :] = rest
             same += dot_nt(head, head)
@@ -176,11 +186,11 @@
     gram_ref[...] = same + mixed + mixed.T
 
 
-def local_sums(values, cells, columns, faces):
+def local_sums(values, cells, columns, early, late):
     half = jax.ShapeDtypeStruct((EXT, ROWS, CW), BF16)
     return pl.pallas_call(
         local_kernel,
-        in_specs=[SMEM, HBM, VMEM, VMEM],
+        in_specs=[SMEM, HBM, VMEM, VMEM, VMEM],
         out_specs=[VMEM] * 4,
         scratch_shapes=[
             pltpu.VMEM((BRICKS - 2, SNAPS, FIELDS, PER_BRICK), BF16),
@@ -196,7 +206,7 @@
         compiler_params=params(39),
         cost_estimate=pl.CostEstimate(flops=6_000_000_000, bytes_accessed=14_000_000, transcendentals=0),
         name="local",
-    )(columns, values, cells, faces)
+    )(columns, values, cells, early, late)
 
 
 def pack(gram):
@@ -229,30 +239,48 @@
     return jnp.concatenate([top, bottom], axis=0)
 
 
-def cross_kernel(gram_ref, heads, rests, from_below, from_above, mine_ref, other_ref):
+def cross_terms(gram, heads, rests, early, late):
     cross = jnp.zeros((SNAPS, SNAPS), F32)
-    for k, received in ((1, from_below), (CX, from_above)):
-        scale = wire_scale(received)
-        for f in range(FIELDS):
-            rows = slice(f * SNAPS, (f + 1) * SNAPS)
-            head, rest = halves(wire_steps(received, rows) * scale)
-            own = heads[k, rows, :]
-            cross += dot_nt(own, head) + dot_nt(own, rest) + dot_nt(rests[k, rows, :], head)
-    packed = pack(gram_ref[...] + cross + cross.T)
+    scales = [wire_scale(wire) for wire in (early, late)]
+    for f in range(FIELDS):
+        part = slice(f * PART, (f + 1) * PART)
+        steps = [wire_steps(wire, part) * scale for wire, scale in zip((early, late), scales)]
+        head, rest = halves(jnp.concatenate(steps, axis=0))
+        rows = slice(f * SNAPS, (f + 1) * SNAPS)
+        own = heads[rows, :]
+        cross += dot_nt(own, head) + dot_nt(own, rest) + dot_nt(rests[rows, :], head)
+    return gram + cross + cross.T
+
+
+def below_kernel(gram_ref, heads, rests, early, late, out_ref):
+    out_ref[...] = cross_terms(gram_ref[...], heads.at[1], rests.at[1], early, late)
+
+
+def above_kernel(gram_ref, heads, rests, early, late, mine_ref, other_ref):
+    packed = pack(cross_terms(gram_ref[...], heads.at[CX], rests.at[CX], early, late))
     first = on_first_core()
     mine_ref[...] = jnp.where(first, packed[: SPLIT // 2], packed[SPLIT // 2 :])
     other_ref[...] = jnp.where(first, packed[SPLIT // 2 :], packed[: SPLIT // 2])
 
 
-def packed_gram(gram, heads, rests, from_below, from_above):
-    return pl.pallas_call(
-        cross_kernel,
+def packed_gram(gram, heads, rests, below, above):
+    common = dict(compiler_params=params(16), cost_estimate=pl.CostEstimate(flops=400_000_000, bytes_accessed=3_000_000, transcendentals=0))
+    gram = pl.pallas_call(
+        below_kernel,
+        in_specs=[VMEM] * 5,
+        out_specs=VMEM,
+        out_shape=jax.ShapeDtypeStruct((SNAPS, SNAPS), F32),
+        name="below",
+        **common,
+    )(gram, heads, rests, *below)
+    return pl.pallas_call(
+        above_kernel,
         in_specs=[VMEM] * 5,
         out_specs=[VMEM] * 2,
         out_shape=[jax.ShapeDtypeStruct((SPLIT // 2, SPLIT), F32)] * 2,
-        compiler_params=params(16),
-        name="cross",
-    )(gram, heads, rests, from_below, from_above)
+        name="above",
+        **common,
+    )(gram, heads, rests, *above)
 
 
 def on_first_core():
@@ -350,9 +378,10 @@
 
 
 def by_field(basis):
+    snaps = basis.shape[1]
     tall = jnp.concatenate([jnp.concatenate([basis] * FIELDS, axis=1)] * FIELDS, axis=0)
-    row_field = lax.broadcasted_iota(jnp.int32, (COEFS, ROWS), 0) // MODES
-    col_field = lax.broadcasted_iota(jnp.int32, (COEFS, ROWS), 1) // SNAPS
+    row_field = lax.broadcasted_iota(jnp.int32, tall.shape, 0) // MODES
+    col_field = lax.broadcasted_iota(jnp.int32, tall.shape, 1) // snaps
     return jnp.concatenate(halves(jnp.where(row_field == col_field, tall, 0.0)), axis=0)
 
 
@@ -408,15 +437,18 @@
 
 
 def inner_kernel(
-    basis_ref, down_ref, up_ref, from_below, from_above, columns, heads, rests, hots,
+    basis_ref, down_ref, up_ref, below_early, below_late, above_early, above_late, columns, heads, rests, hots,
     out_hbm, whole_ref, ends_ref, spread_ref, held, out_sems
 ):
     both = by_field(basis_ref[...])
     spread_ref[...] = spread_matrix(basis_ref[...])
     whole = [jnp.zeros((2 * COEFS, CW), BF16)] * EXT
-    for k, mine, wire in ((1, down_ref, from_below), (CX, up_ref, from_above)):
-        other = coefficients(both, *halves(wire_steps(wire, slice(0, ROWS))))
-        whole[k] = jnp.concatenate(halves(mine[...] + other * wire_scale(wire)), axis=0)
+    parts = [by_field(basis_ref[...][:, h * PART : (h + 1) * PART]) for h in range(2)]
+    for k, mine, wires in ((1, down_ref, (below_early, below_late)), (CX, up_ref, (above_early, above_late))):
+        value = mine[...]
+        for part, wire in zip(parts, wires):
+            value += coefficients(part, *halves(wire_steps(wire, slice(0, PART_ROWS)))) * wire_scale(wire)
+        whole[k] = jnp.concatenate(halves(value), axis=0)
     for k in (2, 3):
         whole[k] = jnp.concatenate(halves(coefficients(both, heads[k], rests[k])), axis=0)
     outputs = []
@@ -430,10 +462,10 @@
     wait(outputs)
 
 
-def inner_fields(basis, down, up, from_below, from_above, columns, heads, rests, hots):
+def inner_fields(basis, down, up, below, above, columns, heads, rests, hots):
     return pl.pallas_call(
         inner_kernel,
-        in_specs=[VMEM] * 9,
+        in_specs=[VMEM] * 11,
         out_specs=[HBM] + [VMEM] * 3,
         scratch_shapes=[
             pltpu.VMEM((4, SNAPS, FIELDS, PER_BRICK), BF16),
@@ -448,7 +480,7 @@
         compiler_params=params(24),
         cost_estimate=pl.CostEstimate(flops=4_000_000_000, bytes_accessed=14_000_000, transcendentals=0),
         name="inner",
-    )(basis, down, up, from_below, from_above, columns, heads, rests, hots)
+    )(basis, down, up, *below, *above, columns, heads, rests, hots)
 
 
 def outer_kernel(filled_hbm, whole_ref, ends_ref, below, above, spread_ref, hots, columns, out_hbm, held, out_sems):
@@ -485,16 +517,19 @@
     to_upper = [(i, (i + 1) % count) for i in range(count)]
     cells = atom_cell.reshape(BRICKS * LANES, 128)
     columns = brick_column.reshape(1, BRICKS)
-    low, high, passed, totals = face_sums(atom_values, cells, columns)
-    from_above = lax.ppermute(low, "gx", to_lower)
-    from_below = lax.ppermute(high, "gx", to_upper)
-    heads, rests, hots, gram = local_sums(atom_values, passed, brick_column, totals)
-    mine, other = add_over_devices(*packed_gram(gram, heads, rests, from_below, from_above))
+    below, above, totals = [], [], []
+    for part in range(2):
+        low, high, cells, columns, total = face_sums(part, atom_values, cells, columns)
+        above.append(lax.ppermute(low, "gx", to_lower))
+        below.append(lax.ppermute(high, "gx", to_upper))
+        totals.append(total)
+    heads, rests, hots, gram = local_sums(atom_values, cells, brick_column, *totals)
+    mine, other = add_over_devices(*packed_gram(gram, heads, rests, below, above))
     basis, down, up = basis_and_faces(mine, other, heads, rests)
-    above = lax.ppermute(down, "gx", to_lower)
-    below = lax.ppermute(up, "gx", to_upper)
-    filled, whole, ends, spread = inner_fields(basis, down, up, from_below, from_above, columns, heads, rests, hots)
-    return outer_fields(filled, whole, ends, below, above, spread, hots, columns)
+    end_above = lax.ppermute(down, "gx", to_lower)
+    end_below = lax.ppermute(up, "gx", to_upper)
+    filled, whole, ends, spread = inner_fields(basis, down, up, below, above, columns, heads, rests, hots)
+    return outer_fields(filled, whole, ends, end_below, end_above, spread, hots, columns)
 
 
 def solution(mesh):

time: 76.9 us -> 75.6 us (0.983)
  waiting for transfers between devices: 14.4 us -> 8.72 us
  starting transfers between devices: 23.4 us -> 28.4 us
  blocking collectives: 14.9 us -> 12.5 us
  Pallas kernels: 22.4 us -> 24.1 us
    ppermute x4 -> x6, waiting for transfers between devices: 7.13 us -> 1.47 us  [the longest x1 1.45 us: on_device(): end_below = lax.ppermute(up, 'gx', to_upper)]
    ppermute x4 -> x6, starting transfers between devices: 10.5 us -> 15.1 us  [the longest x2 11 us: on_device(): above.append(lax.ppermute(low, 'gx', to_lower))]
    all_to_all x1, blocking collectives: 14.9 us -> 12.5 us  [add_over_devices(): lax.all_to_all(copies, axes, 0, 0, axis_index_groups=lines, tiled=True)]
    pallas_call x4 -> x6, Pallas kernels: 17.5 us -> 19.2 us  [the longest x1 8.77 us: local_sums(): pl.pallas_call(local_kernel, in_specs=[SMEM, HBM, VMEM, VMEM, VMEM], out_...]
  transfers between devices with their start and end apart: 12 -> 14, of which waited for: 9 -> 8; matrix products, arithmetic and copies ran while one was open for 0% -> 0% of each run, Pallas kernels for 16% -> 21%
where the time goes in v8:
time: 75.6 us; the launch traced here: 75.3 us
  starting transfers between devices  28.4 us (38%)
  Pallas kernels  24.1 us (32%)
  blocking collectives  12.5 us (17%)
  waiting for transfers between devices  8.72 us (12%)
  local copies, waits for them, and re-layouts  1.38 us (2%)
    ppermute x8, starting transfers between devices, move(): lax.ppermute(x, axes, [(number[place], number[target(*place)]) for place...  13.2 us
    all_to_all x1, blocking collectives, add_over_devices(): lax.all_to_all(copies, axes, 0, 0, axis_index_groups=lines, tiled=True)  12.5 us
    ppermute x2, starting transfers between devices, on_device(): above.append(lax.ppermute(low, 'gx', to_lower))  11 us
    pallas_call x1, Pallas kernels, local_sums(): pl.pallas_call(local_kernel, in_specs=[SMEM, HBM, VMEM, VMEM, VMEM], out_...  8.77 us
    ppermute x8, waiting for transfers between devices, move(): lax.ppermute(x, axes, [(number[place], number[target(*place)]) for place...  7.26 us
    pallas_call x2, Pallas kernels, face_sums(): pl.pallas_call(functools.partial(faces_kernel, part), in_specs=[HBM] * 3,...  4.91 us
    pallas_call x1, Pallas kernels, inner_fields(): pl.pallas_call(inner_kernel, in_specs=[VMEM] * 11, out_specs=[HBM] + [VME...  3.69 us
    ppermute x2, starting transfers between devices, on_device(): below.append(lax.ppermute(high, 'gx', to_upper))  2.63 us
  transfers between devices with their start and end apart: 14, of which 8 were waited for; matrix products, arithmetic and copies ran while one was open for 0% of the time, Pallas kernels for 21%

profile of v8, /device:TPU:1, one launch (start us, length us, event | category | flops | bytes accessed | tf_op | source)
XLA Modules:
  0.0 75.3 jit_solution(4456071542954427232)
XLA Ops:
  0.0 0.7 copy-done
  0.7 0.7 copy-done.1
  1.4 2.5 %faces.2 = (s16[336,512]{1,0:T(8,128)(2,1)S(1)}, s16[336,512]{1,0:T(8,128)(2,1)S(1)}, s32[32,128]{1,0:T(8,128)S(1)}, s32[1,8]{1,0:T(1,128)S(1)}, f32[2,4,320,128]{3,2,1,0:T(8,128)S(1)}) custom-call(bf16[160,4,4096]{2,1,0:T(4,128)(2,1)} %values_hbm.5, s32[32,128]{1,0:T(8,128)S(1)} %bitcast.2, s32[1,8]{1,0:T(1,128)S(1)} %bitcast.3), custom_call_target="tpu_custom_call" | custom-call | flops 1400000000 | bytes 4000000 | tf_op jit(solution)/shard_map/faces/pallas_call | solution.py:134
  3.8 2.5 %collective-permute-start = (s16[336,512]{1,0:T(8,128)(2,1)S(1)}, s16[336,512]{1,0:T(8,128)(2,1)S(1)}, u32[]{:S(2)}, u32[]{:S(2)}) collective-permute-start(s16[336,512]{1,0:T(8,128)(2,1)S(1)} %get-tuple-element.36), channel_id=1, source_target_pairs={{0,8},{8,16},{16,24},{24,32},{32,40},{40,48},{48,56},{56,64},{64,7... | collective-permute-start | bytes 1032200 | tf_op jit(solution)/shard_map/ppermute | solution.py:524
  6.4 6.2 %collective-permute-start.2 = (s16[336,512]{1,0:T(8,128)(2,1)S(1)}, s16[336,512]{1,0:T(8,128)(2,1)S(1)}, u32[]{:S(2)}, u32[]{:S(2)}) collective-permute-start(s16[336,512]{1,0:T(8,128)(2,1)S(1)} %get-tuple-element.38), channel_id=1, source_target_pairs={{8,0},{16,8},{24,16},{32,24},{40,32},{48,40},{56,48},{64,56},{72,6... | collective-permute-start | bytes 1032200 | tf_op jit(solution)/shard_map/ppermute | solution.py:523
  12.6 2.5 %faces.3 = (s16[336,512]{1,0:T(8,128)(2,1)S(1)}, s16[336,512]{1,0:T(8,128)(2,1)S(1)}, s32[32,128]{1,0:T(8,128)S(1)}, s32[1,8]{1,0:T(1,128)S(1)}, f32[2,4,320,128]{3,2,1,0:T(8,128)S(1)}) custom-call(bf16[160,4,4096]{2,1,0:T(4,128)(2,1)} %values_hbm.5, s32[32,128]{1,0:T(8,128)S(1)} %get-tuple-element.28.cells_hbm, s32[1,8]{1,0:T(1,128)S(1)} %get-tuple-element.29.column_hbm), custom_call_target="tpu_custom_call" | custom-call | flops 1400000000 | bytes 4000000 | tf_op jit(solution)/shard_map/faces/pallas_call | solution.py:134
  15.1 0.1 collective-permute-start.1
  15.2 4.8 %collective-permute-start.3 = (s16[336,512]{1,0:T(8,128)(2,1)S(1)}, s16[336,512]{1,0:T(8,128)(2,1)S(1)}, u32[]{:S(2)}, u32[]{:S(2)}) collective-permute-start(s16[336,512]{1,0:T(8,128)(2,1)S(1)} %get-tuple-element.39), channel_id=1, source_target_pairs={{8,0},{16,8},{24,16},{32,24},{40,32},{48,40},{56,48},{64,56},{72,6... | collective-permute-start | bytes 1032200 | tf_op jit(solution)/shard_map/ppermute | solution.py:523
  19.9 8.8 %local.1 = (bf16[6,640,512]{2,1,0:T(8,128)(2,1)S(1)}, bf16[6,640,512]{2,1,0:T(8,128)(2,1)S(1)}, bf16[8,512,512]{2,1,0:T(8,128)(2,1)S(1)}, f32[160,160]{1,0:T(8,128)S(1)}) custom-call(s32[8]{0:T(128)S(1)} %copy-done.2, bf16[160,4,4096]{2,1,0:T(4,128)(2,1)} %values_hbm.5, s32[32,128]{1,0:T(8,128)S(1)} %get-tuple-element.30.cells, ...), custom_call_target="tpu_custom_call" | custom-call | flops 6000000000 | bytes 14000000 | tf_op jit(solution)/shard_map/local/pallas_call | solution.py:191
  28.7 0.9 %below.1.gram_ref = f32[160,160]{1,0:T(8,128)S(1)} custom-call(f32[160,160]{1,0:T(8,128)S(1)} %get-tuple-element.33.gram_ref, bf16[6,640,512]{2,1,0:T(8,128)(2,1)S(1)} %get-tuple-element.34.heads, bf16[6,640,512]{2,1,0:T(8,128)(2,1)S(1)} %get-tuple-element.35.rests, s16[336,512]{1,0:T(8,128)(2,1)S(1)} %collective-permute-done.early.below_early, ...), custom_call_target="tpu_custom_call" | custom-call | flops 400000000 | bytes 3000000 | tf_op jit(solution)/shard_map/below/pallas_call | solution.py:268
  29.6 0.9 %above.1 = (f32[64,128]{1,0:T(8,128)S(1)}, f32[64,128]{1,0:T(8,128)S(1)}) custom-call(f32[160,160]{1,0:T(8,128)S(1)} %below.1.gram_ref, bf16[6,640,512]{2,1,0:T(8,128)(2,1)S(1)} %get-tuple-element.34.heads, bf16[6,640,512]{2,1,0:T(8,128)(2,1)S(1)} %get-tuple-element.35.rests, s16[336,512]{1,0:T(8,128)(2,1)S(1)} %collective-permute-done.2.early.above_early, ...), custom_call_target="tpu_custom_call" | custom-call | flops 400000000 | bytes 3000000 | tf_op jit(solution)/shard_map/above/pallas_call | solution.py:276
  30.6 1.6 %collective-permute-start.4 = (f32[64,128]{1,0:T(8,128)S(1)}, f32[64,128]{1,0:T(8,128)S(1)}, u32[]{:S(2)}, u32[]{:S(2)}) collective-permute-start(f32[64,128]{1,0:T(8,128)S(1)} %get-tuple-element.41), channel_id=1, source_target_pairs={{0,1},{1,0},{2,3},{3,2},{4,5},{5,4},{6,7},{7,6},{8,9},{9,8},{10,11... | collective-permute-start | bytes 98312 | tf_op jit(solution)/shard_map/ppermute | solution.py:324
  32.2 0.9 %collective-permute-done.4.refs_1_ = f32[64,128]{1,0:T(8,128)S(1)} collective-permute-done((f32[64,128]{1,0:T(8,128)S(1)}, f32[64,128]{1,0:T(8,128)S(1)}, u32[]{:S(2)}, u32[]{:S(2)}) %collective-permute-start.4) | collective-permute-done | bytes 32800 | tf_op jit(solution)/shard_map/ppermute | solution.py:324
  33.1 0.1 collective-permute-start.6
  33.2 3.1 %collective-permute-start.5 = (f32[64,128]{1,0:T(8,128)S(1)}, f32[64,128]{1,0:T(8,128)S(1)}, u32[]{:S(2)}, u32[]{:S(2)}) collective-permute-start(f32[64,128]{1,0:T(8,128)S(1)} %sum.4.refs_0_), channel_id=1, source_target_pairs={{0,64},{1,65},{2,66},{3,67},{4,68},{5,69},{6,70},{7,71},{8,72},{9,... | collective-permute-start | bytes 98312 | tf_op jit(solution)/shard_map/ppermute | solution.py:324
  36.3 0.7 collective-permute-done.7.refs_3_
  37.0 0.4 collective-permute-done.6.refs_2_
  37.4 0.8 %collective-permute-done.5.refs_1_ = f32[64,128]{1,0:T(8,128)S(1)} collective-permute-done((f32[64,128]{1,0:T(8,128)S(1)}, f32[64,128]{1,0:T(8,128)S(1)}, u32[]{:S(2)}, u32[]{:S(2)}) %collective-permute-start.5) | collective-permute-done | bytes 32800 | tf_op jit(solution)/shard_map/ppermute | solution.py:324
  38.3 2.8 %collective-permute-start.10 = (f32[64,128]{1,0:T(8,128)S(1)}, f32[64,128]{1,0:T(8,128)S(1)}, u32[]{:S(2)}, u32[]{:S(2)}) collective-permute-start(f32[64,128]{1,0:T(8,128)S(1)} %sum.5.refs_0_), channel_id=1, source_target_pairs={{0,6},{1,7},{2,4},{3,5},{4,2},{5,3},{6,0},{7,1},{8,14},{9,15},{10,... | collective-permute-start | bytes 98312 | tf_op jit(solution)/shard_map/ppermute | solution.py:324
  41.1 0.3 collective-permute-start.9
  41.5 0.3 collective-permute-start.8
  41.8 0.6 collective-permute-done.10.refs_3_
  42.4 3.0 %collective-permute-done.9.refs_2_ = f32[64,128]{1,0:T(8,128)S(1)} collective-permute-done((f32[64,128]{1,0:T(8,128)S(1)}, f32[64,128]{1,0:T(8,128)S(1)}, u32[]{:S(2)}, u32[]{:S(2)}) %collective-permute-start.9) | collective-permute-done | bytes 32800 | tf_op jit(solution)/shard_map/ppermute | solution.py:324
  45.4 12.5 %all_to_all.5.parts = f32[8,64,128]{2,1,0:T(8,128)S(1)} all-to-all(f32[8,64,128]{2,1,0:T(8,128)S(1)} %sum.6), channel_id=1, replica_groups={{0,8,16,24,32,40,48,56},{1,9,17,25,33,41,49,57},{2,10,18,26,34,42,50,58..., dimensions={0} | all-to-all | bytes 524288 | tf_op jit(solution)/shard_map/all_to_all | solution.py:335
  57.9 4.8 %collective-permute-start.11 = (f32[64,128]{1,0:T(8,128)S(1)}, f32[64,128]{1,0:T(8,128)S(1)}, u32[]{:S(2)}, u32[]{:S(2)}) collective-permute-start(f32[64,128]{1,0:T(8,128)S(1)} %sum.7.mine_ref), channel_id=1, source_target_pairs={{0,1},{1,0},{2,3},{3,2},{4,5},{5,4},{6,7},{7,6},{8,9},{9,8},{10,11... | collective-permute-start | bytes 98312 | tf_op jit(solution)/shard_map/ppermute | solution.py:324
  62.8 0.9 %collective-permute-done.11.other_ref = f32[64,128]{1,0:T(8,128)S(1)} collective-permute-done((f32[64,128]{1,0:T(8,128)S(1)}, f32[64,128]{1,0:T(8,128)S(1)}, u32[]{:S(2)}, u32[]{:S(2)}) %collective-permute-start.11) | collective-permute-done | bytes 32800 | tf_op jit(solution)/shard_map/ppermute | solution.py:324
  63.7 2.3 %basis.1 = (f32[8,160]{1,0:T(8,128)S(1)}, f32[32,512]{1,0:T(8,128)S(1)}, f32[32,512]{1,0:T(8,128)S(1)}) custom-call(f32[64,128]{1,0:T(8,128)S(1)} %sum.7.mine_ref, f32[64,128]{1,0:T(8,128)S(1)} %collective-permute-done.11.other_ref, bf16[6,640,512]{2,1,0:T(8,128)(2,1)S(1)} %get-tuple-element.34.heads, bf16[6,640,512]{2,1,0:T(8,128)(2,1)S(1)} %get-tuple-element.35.rests), custom_call_target="tpu_custom_call" | custom-call | tf_op jit(solution)/shard_map/basis/pallas_call | solution.py:408
  66.0 0.2 collective-permute-start.13
  66.2 1.3 %collective-permute-start.12 = (f32[32,512]{1,0:T(8,128)S(1)}, f32[32,512]{1,0:T(8,128)S(1)}, u32[]{:S(2)}, u32[]{:S(2)}) collective-permute-start(f32[32,512]{1,0:T(8,128)S(1)} %get-tuple-element.44.up_ref), channel_id=1, source_target_pairs={{0,8},{8,16},{16,24},{24,32},{32,40},{40,48},{48,56},{56,64},{64,7... | collective-permute-start | bytes 196616 | tf_op jit(solution)/shard_map/ppermute | solution.py:530
  67.5 3.7 %inner.1 = (bf16[160,4,4096]{2,1,0:T(4,128)(2,1)}, bf16[6,64,512]{2,1,0:T(8,128)(2,1)S(1)}, f32[2,32,512]{2,1,0:T(8,128)S(1)}, bf16[640,128]{1,0:T(8,128)(2,1)S(1)}) custom-call(f32[8,160]{1,0:T(8,128)S(1)} %get-tuple-element.42.basis_ref, f32[32,512]{1,0:T(8,128)S(1)} %get-tuple-element.43.down_ref, f32[32,512]{1,0:T(8,128)S(1)} %get-tuple-element.44.up_ref, ...), custom_call_target="tpu_custom_call" | custom-call | flops 4000000000 | bytes 14000000 | tf_op jit(solution)/shard_map/inner/pallas_call | solution.py:466
  71.2 1.5 %collective-permute-done.12.below = f32[32,512]{1,0:T(8,128)S(1)} collective-permute-done((f32[32,512]{1,0:T(8,128)S(1)}, f32[32,512]{1,0:T(8,128)S(1)}, u32[]{:S(2)}, u32[]{:S(2)}) %collective-permute-start.12) | collective-permute-done | bytes 65568 | tf_op jit(solution)/shard_map/ppermute | solution.py:530
  72.6 2.5 %outer.1 = bf16[160,4,4096]{2,1,0:T(4,128)(2,1)} custom-call(bf16[160,4,4096]{2,1,0:T(4,128)(2,1)} %get-tuple-element.47.filled_hbm, bf16[6,64,512]{2,1,0:T(8,128)(2,1)S(1)} %get-tuple-element.48.whole_ref, f32[2,32,512]{2,1,0:T(8,128)S(1)} %get-tuple-element.49.ends_ref, ...), custom_call_target="tpu_custom_call", output_to_operand_aliasing={{}: (0, {})} | custom-call | tf_op jit(solution)/shard_map/outer/pallas_call | solution.py:499
  (15 shorter events, 0.1 us)
Async XLA Ops:
  0.0 0.7 copy-start
  0.7 0.7 copy-start.1
  1.4 18.6 %copy-start.2 = (s32[8]{0:T(128)S(1)}, s32[8]{0:T(128)}, u32[]{:S(2)}) copy-start(s32[8]{0:T(128)} %column_ref.1) | copy-start | bytes 100
  3.8 24.9 %collective-permute-start = (s16[336,512]{1,0:T(8,128)(2,1)S(1)}, s16[336,512]{1,0:T(8,128)(2,1)S(1)}, u32[]{:S(2)}, u32[]{:S(2)}) collective-permute-start(s16[336,512]{1,0:T(8,128)(2,1)S(1)} %get-tuple-element.36), channel_id=1, source_target_pairs={{0,8},{8,16},{16,24},{24,32},{32,40},{40,48},{48,56},{56,64},{64,7... | collective-permute-start | bytes 1032200 | tf_op jit(solution)/shard_map/ppermute | solution.py:524
  6.4 23.2 %collective-permute-start.2 = (s16[336,512]{1,0:T(8,128)(2,1)S(1)}, s16[336,512]{1,0:T(8,128)(2,1)S(1)}, u32[]{:S(2)}, u32[]{:S(2)}) collective-permute-start(s16[336,512]{1,0:T(8,128)(2,1)S(1)} %get-tuple-element.38), channel_id=1, source_target_pairs={{8,0},{16,8},{24,16},{32,24},{40,32},{48,40},{56,48},{64,56},{72,6... | collective-permute-start | bytes 1032200 | tf_op jit(solution)/shard_map/ppermute | solution.py:523
  15.1 13.7 %collective-permute-start.1 = (s16[336,512]{1,0:T(8,128)(2,1)S(1)}, s16[336,512]{1,0:T(8,128)(2,1)S(1)}, u32[]{:S(2)}, u32[]{:S(2)}) collective-permute-start(s16[336,512]{1,0:T(8,128)(2,1)S(1)} %get-tuple-element.37), channel_id=1, source_target_pairs={{0,8},{8,16},{16,24},{24,32},{32,40},{40,48},{48,56},{56,64},{64,7... | collective-permute-start | bytes 1032200 | tf_op jit(solution)/shard_map/ppermute | solution.py:524
  15.2 14.5 %collective-permute-start.3 = (s16[336,512]{1,0:T(8,128)(2,1)S(1)}, s16[336,512]{1,0:T(8,128)(2,1)S(1)}, u32[]{:S(2)}, u32[]{:S(2)}) collective-permute-start(s16[336,512]{1,0:T(8,128)(2,1)S(1)} %get-tuple-element.39), channel_id=1, source_target_pairs={{8,0},{16,8},{24,16},{32,24},{40,32},{48,40},{56,48},{64,56},{72,6... | collective-permute-start | bytes 1032200 | tf_op jit(solution)/shard_map/ppermute | solution.py:523
  30.6 2.5 %collective-permute-start.4 = (f32[64,128]{1,0:T(8,128)S(1)}, f32[64,128]{1,0:T(8,128)S(1)}, u32[]{:S(2)}, u32[]{:S(2)}) collective-permute-start(f32[64,128]{1,0:T(8,128)S(1)} %get-tuple-element.41), channel_id=1, source_target_pairs={{0,1},{1,0},{2,3},{3,2},{4,5},{5,4},{6,7},{7,6},{8,9},{9,8},{10,11... | collective-permute-start | bytes 98312 | tf_op jit(solution)/shard_map/ppermute | solution.py:324
  33.1 4.0 %collective-permute-start.7 = (f32[64,128]{1,0:T(8,128)S(1)}, f32[64,128]{1,0:T(8,128)S(1)}, u32[]{:S(2)}, u32[]{:S(2)}) collective-permute-start(f32[64,128]{1,0:T(8,128)S(1)} %sum.4.refs_0_), channel_id=1, source_target_pairs={{0,192},{1,193},{2,194},{3,195},{4,196},{5,197},{6,198},{7,199},{8... | collective-permute-start | bytes 98312 | tf_op jit(solution)/shard_map/ppermute | solution.py:324
  33.1 4.4 %collective-permute-start.6 = (f32[64,128]{1,0:T(8,128)S(1)}, f32[64,128]{1,0:T(8,128)S(1)}, u32[]{:S(2)}, u32[]{:S(2)}) collective-permute-start(f32[64,128]{1,0:T(8,128)S(1)} %sum.4.refs_0_), channel_id=1, source_target_pairs={{0,128},{1,129},{2,130},{3,131},{4,132},{5,133},{6,134},{7,135},{8... | collective-permute-start | bytes 98312 | tf_op jit(solution)/shard_map/ppermute | solution.py:324
  33.2 5.1 %collective-permute-start.5 = (f32[64,128]{1,0:T(8,128)S(1)}, f32[64,128]{1,0:T(8,128)S(1)}, u32[]{:S(2)}, u32[]{:S(2)}) collective-permute-start(f32[64,128]{1,0:T(8,128)S(1)} %sum.4.refs_0_), channel_id=1, source_target_pairs={{0,64},{1,65},{2,66},{3,67},{4,68},{5,69},{6,70},{7,71},{8,72},{9,... | collective-permute-start | bytes 98312 | tf_op jit(solution)/shard_map/ppermute | solution.py:324
  38.3 4.1 %collective-permute-start.10 = (f32[64,128]{1,0:T(8,128)S(1)}, f32[64,128]{1,0:T(8,128)S(1)}, u32[]{:S(2)}, u32[]{:S(2)}) collective-permute-start(f32[64,128]{1,0:T(8,128)S(1)} %sum.5.refs_0_), channel_id=1, source_target_pairs={{0,6},{1,7},{2,4},{3,5},{4,2},{5,3},{6,0},{7,1},{8,14},{9,15},{10,... | collective-permute-start | bytes 98312 | tf_op jit(solution)/shard_map/ppermute | solution.py:324
  41.1 4.3 %collective-permute-start.9 = (f32[64,128]{1,0:T(8,128)S(1)}, f32[64,128]{1,0:T(8,128)S(1)}, u32[]{:S(2)}, u32[]{:S(2)}) collective-permute-start(f32[64,128]{1,0:T(8,128)S(1)} %sum.5.refs_0_), channel_id=1, source_target_pairs={{0,4},{1,5},{2,6},{3,7},{4,0},{5,1},{6,2},{7,3},{8,12},{9,13},{10,... | collective-permute-start | bytes 98312 | tf_op jit(solution)/shard_map/ppermute | solution.py:324
  41.5 3.9 %collective-permute-start.8 = (f32[64,128]{1,0:T(8,128)S(1)}, f32[64,128]{1,0:T(8,128)S(1)}, u32[]{:S(2)}, u32[]{:S(2)}) collective-permute-start(f32[64,128]{1,0:T(8,128)S(1)} %sum.5.refs_0_), channel_id=1, source_target_pairs={{0,2},{1,3},{2,0},{3,1},{4,6},{5,7},{6,4},{7,5},{8,10},{9,11},{10,... | collective-permute-start | bytes 98312 | tf_op jit(solution)/shard_map/ppermute | solution.py:324
  57.9 5.7 %collective-permute-start.11 = (f32[64,128]{1,0:T(8,128)S(1)}, f32[64,128]{1,0:T(8,128)S(1)}, u32[]{:S(2)}, u32[]{:S(2)}) collective-permute-start(f32[64,128]{1,0:T(8,128)S(1)} %sum.7.mine_ref), channel_id=1, source_target_pairs={{0,1},{1,0},{2,3},{3,2},{4,5},{5,4},{6,7},{7,6},{8,9},{9,8},{10,11... | collective-permute-start | bytes 98312 | tf_op jit(solution)/shard_map/ppermute | solution.py:324
  66.0 5.2 %collective-permute-start.13 = (f32[32,512]{1,0:T(8,128)S(1)}, f32[32,512]{1,0:T(8,128)S(1)}, u32[]{:S(2)}, u32[]{:S(2)}) collective-permute-start(f32[32,512]{1,0:T(8,128)S(1)} %get-tuple-element.43.down_ref), channel_id=1, source_target_pairs={{8,0},{16,8},{24,16},{32,24},{40,32},{48,40},{56,48},{64,56},{72,6... | collective-permute-start | bytes 196616 | tf_op jit(solution)/shard_map/ppermute | solution.py:529
  66.2 6.4 %collective-permute-start.12 = (f32[32,512]{1,0:T(8,128)S(1)}, f32[32,512]{1,0:T(8,128)S(1)}, u32[]{:S(2)}, u32[]{:S(2)}) collective-permute-start(f32[32,512]{1,0:T(8,128)S(1)} %get-tuple-element.44.up_ref), channel_id=1, source_target_pairs={{0,8},{8,16},{16,24},{24,32},{32,40},{40,48},{48,56},{56,64},{64,7... | collective-permute-start | bytes 196616 | tf_op jit(solution)/shard_map/ppermute | solution.py:530

commit v9 on v8

--- a/solution.py
+++ b/solution.py
@@ -95,29 +95,47 @@
     return jnp.exp(wire_steps(wire, slice(PART_ROWS, WIRE))[:1] * (1 / STEPS)) * (1 / TOP)
 
 
+def start(copies):
+    for copy in copies:
+        copy.start()
+
+
+def wait(copies):
+    for copy in copies:
+        copy.wait()
+
+
+def column_id(ids, brick):
+    return ids[BRICKS * LANES : BRICKS * LANES + 1, brick : brick + 1]
+
+
+INNER = range(2, BRICKS - 2)
+OUTER = (0, 1, BRICKS - 2, BRICKS - 1)
 HBM = pl.BlockSpec(memory_space=pltpu.HBM)
 VMEM = pl.BlockSpec(memory_space=pltpu.VMEM)
 SMEM = pl.BlockSpec(memory_space=pltpu.SMEM)
 
 
-def faces_kernel(part, values_hbm, cells_hbm, column_hbm, low_ref, high_ref, cells, columns, total, held, sems, small):
+def faces_kernel(part, values_hbm, ids_ref, low_ref, high_ref, total, *rest):
     bricks = (0, 1, BRICKS - 2, BRICKS - 1)
     targets = ((0, low_ref), (EXT - 1, high_ref))
-    inputs = [
-        pltpu.make_async_copy(cells_hbm, cells, small.at[0]),
-        pltpu.make_async_copy(column_hbm, columns, small.at[1]),
-    ]
+    held, sems = rest[-2:]
     copies = []
     for slot, brick in enumerate(bricks):
         source = values_hbm.at[pl.ds(part * PART, PART), :, pl.ds(brick * PER_BRICK, PER_BRICK)]
         copies.append(pltpu.make_async_copy(source, held.at[slot], sems.at[slot]))
-    for copy in inputs + copies:
-        copy.start()
-    for copy in inputs:
-        copy.wait()
+    start(copies)
+    later = []
+    if part:
+        passed, outer_hots, later_sems = rest[:3]
+        later = [brick_copy(values_hbm, passed, later_sems, brick, i) for i, brick in enumerate(INNER)]
+        start(later)
     hots = [
-        cell_hot(cells, brick, columns[:, brick : brick + 1] == targets[slot // 2][0]) for slot, brick in enumerate(bricks)
+        cell_hot(ids_ref, brick, column_id(ids_ref, brick) == targets[slot // 2][0]) for slot, brick in enumerate(bricks)
     ]
+    if part:
+        outer_hots[0] = hots[0]
+        outer_hots[1] = hots[3]
     for i in range(2):
         sums = None
         for slot in (2 * i, 2 * i + 1):
@@ -127,50 +145,55 @@
         for t in range(LANES):
             total[i, t] = sums[:, t * 128 : (t + 1) * 128]
         encode(total.at[i], targets[i][1])
-
-
-def face_sums(part, values, cells, columns):
+    wait(later)
+
+
+def face_sums(part, values, ids):
     shape = jax.ShapeDtypeStruct((WIRE, CW), jnp.int16)
+    later_shapes = [
+        jax.ShapeDtypeStruct((len(INNER), SNAPS, FIELDS, PER_BRICK), BF16),
+        jax.ShapeDtypeStruct((2, CW, PER_BRICK), BF16),
+    ]
+    later_scratch = [pltpu.SemaphoreType.DMA((len(INNER),))]
     return pl.pallas_call(
         functools.partial(faces_kernel, part),
-        in_specs=[HBM] * 3,
-        out_specs=[VMEM] * 5,
-        scratch_shapes=[
+        in_specs=[HBM, VMEM],
+        out_specs=[VMEM] * (3 + 2 * part),
+        scratch_shapes=later_scratch * part
+        + [
             pltpu.VMEM((4, PART, FIELDS, PER_BRICK), BF16),
             pltpu.SemaphoreType.DMA((4,)),
-            pltpu.SemaphoreType.DMA((2,)),
         ],
-        out_shape=[
-            shape,
-            shape,
-            jax.ShapeDtypeStruct((BRICKS * LANES, 128), jnp.int32),
-            jax.ShapeDtypeStruct((1, BRICKS), jnp.int32),
-            jax.ShapeDtypeStruct((2, LANES, PART_ROWS, 128), F32),
-        ],
-        compiler_params=params((51, 50)[part]),
+        out_shape=[shape, shape, jax.ShapeDtypeStruct((2, LANES, PART_ROWS, 128), F32)] + later_shapes * part,
+        compiler_params=params((51, 46)[part]),
         cost_estimate=pl.CostEstimate(flops=1_400_000_000, bytes_accessed=4_000_000, transcendentals=0),
         name="faces",
-    )(values, cells, columns)
-
-
-def local_kernel(column_ref, values_hbm, cells, early, late, heads, rests, hots, gram_ref, held, total, sems):
-    copies = [brick_copy(values_hbm, held, sems, brick, brick - 1) for brick in range(1, BRICKS - 1)]
-    for copy in copies:
-        copy.start()
+    )(values, ids)
+
+
+def local_kernel(
+    column_ref, values_hbm, ids_ref, early, late, inner, outer_hots, heads, rests, hots, gram_ref, held, total, sems
+):
+    edges = (1, BRICKS - 2)
+    copies = [brick_copy(values_hbm, held, sems, brick, i) for i, brick in enumerate(edges)]
+    start(copies)
     total[...] = jnp.zeros_like(total)
-    for brick in range(BRICKS):
-        hot = cell_hot(cells, brick)
+    hots[0] = outer_hots[0]
+    hots[BRICKS - 1] = outer_hots[1]
+    for brick in tuple(INNER) + edges:
+        hot = cell_hot(ids_ref, brick)
         hots[brick] = hot
-        if brick in (0, BRICKS - 1):
-            continue
-        copies[brick - 1].wait()
-        sums = dot_nt(held[brick - 1].reshape(ROWS, PER_BRICK), hot)
+        if brick in INNER:
+            values = inner[brick - 2]
+        else:
+            copies[edges.index(brick)].wait()
+            values = held[edges.index(brick)]
+        sums = dot_nt(values.reshape(ROWS, PER_BRICK), hot)
         column = column_ref[brick]
         place = jnp.where(column == EXT - 1, 0, column)
         for t in range(LANES):
             total[place, t] += sums[:, t * 128 : (t + 1) * 128]
-    same = jnp.zeros((SNAPS, SNAPS), F32)
-    mixed = jnp.zeros((SNAPS, SNAPS), F32)
+    both = jnp.zeros((2 * SNAPS, SNAPS), F32)
     for k in range(EXT):
         for f in range(FIELDS):
             rows = slice(f * SNAPS, (f + 1) * SNAPS)
@@ -181,21 +204,21 @@
             head, rest = halves(sums)
             heads[k, rows, :] = head
             rests[k, rows, :] = rest
-            same += dot_nt(head, head)
-            mixed += dot_nt(head, rest)
-    gram_ref[...] = same + mixed + mixed.T
-
-
-def local_sums(values, cells, columns, early, late):
+            both += dot_nt(jnp.concatenate([head, rest], axis=0), head)
+    mixed = both[SNAPS:]
+    gram_ref[...] = both[:SNAPS] + mixed + mixed.T
+
+
+def local_sums(values, ids, columns, early, late, inner, outer_hots):
     half = jax.ShapeDtypeStruct((EXT, ROWS, CW), BF16)
     return pl.pallas_call(
         local_kernel,
-        in_specs=[SMEM, HBM, VMEM, VMEM, VMEM],
+        in_specs=[SMEM, HBM] + [VMEM] * 5,
         out_specs=[VMEM] * 4,
         scratch_shapes=[
-            pltpu.VMEM((BRICKS - 2, SNAPS, FIELDS, PER_BRICK), BF16),
+            pltpu.VMEM((2, SNAPS, FIELDS, PER_BRICK), BF16),
             pltpu.VMEM((CX + 1, LANES, ROWS, 128), F32),
-            pltpu.SemaphoreType.DMA((BRICKS - 2,)),
+            pltpu.SemaphoreType.DMA((2,)),
         ],
         out_shape=[
             half,
@@ -203,10 +226,10 @@
             jax.ShapeDtypeStruct((BRICKS, CW, PER_BRICK), BF16),
             jax.ShapeDtypeStruct((SNAPS, SNAPS), F32),
         ],
-        compiler_params=params(39),
+        compiler_params=params(36),
         cost_estimate=pl.CostEstimate(flops=6_000_000_000, bytes_accessed=14_000_000, transcendentals=0),
         name="local",
-    )(columns, values, cells, early, late)
+    )(columns, values, ids, early, late, inner, outer_hots)
 
 
 def pack(gram):
@@ -248,7 +271,8 @@
         head, rest = halves(jnp.concatenate(steps, axis=0))
         rows = slice(f * SNAPS, (f + 1) * SNAPS)
         own = heads[rows, :]
-        cross += dot_nt(own, head) + dot_nt(own, rest) + dot_nt(rests[rows, :], head)
+        pair = dot_nt(jnp.concatenate([own, rests[rows, :]], axis=0), head)
+        cross += pair[:SNAPS] + pair[SNAPS:] + dot_nt(own, rest)
     return gram + cross + cross.T
 
 
@@ -366,17 +390,6 @@
     return jnp.concatenate([head, head, rest, jnp.zeros_like(rest)], axis=0).T.astype(BF16)
 
 
-def start(copies):
-    for copy in copies:
-        copy.start()
-    return copies
-
-
-def wait(copies):
-    for copy in copies:
-        copy.wait()
-
-
 def by_field(basis):
     snaps = basis.shape[1]
     tall = jnp.concatenate([jnp.concatenate([basis] * FIELDS, axis=1)] * FIELDS, axis=0)
@@ -415,10 +428,10 @@
     )(mine, other, heads, rests)
 
 
-def column_of(columns, brick, whole):
+def column_of(ids, brick, whole):
     mine = whole[0]
     for k in range(1, EXT):
-        mine = jnp.where(columns[:, brick : brick + 1] == k, whole[k], mine)
+        mine = jnp.where(column_id(ids, brick) == k, whole[k], mine)
     return mine
 
 
@@ -432,12 +445,8 @@
     return copy
 
 
-INNER = range(2, BRICKS - 2)
-OUTER = (0, 1, BRICKS - 2, BRICKS - 1)
-
-
 def inner_kernel(
-    basis_ref, down_ref, up_ref, below_early, below_late, above_early, above_late, columns, heads, rests, hots,
+    basis_ref, down_ref, up_ref, below_early, below_late, above_early, above_late, ids, heads, rests, hots,
     out_hbm, whole_ref, ends_ref, spread_ref, held, out_sems
 ):
     both = by_field(basis_ref[...])
@@ -453,7 +462,7 @@
         whole[k] = jnp.concatenate(halves(coefficients(both, heads[k], rests[k])), axis=0)
     outputs = []
     for i, brick in enumerate(INNER):
-        column = column_of(columns, brick, whole)
+        column = column_of(ids, brick, whole)
         outputs.append(write_brick(brick, column, hots[brick], spread_ref[...], held.at[i], out_hbm, out_sems.at[i]))
     for k in range(EXT):
         whole_ref[k] = whole[k]
@@ -462,7 +471,7 @@
     wait(outputs)
 
 
-def inner_fields(basis, down, up, below, above, columns, heads, rests, hots):
+def inner_fields(basis, down, up, below, above, ids, heads, rests, hots):
     return pl.pallas_call(
         inner_kernel,
         in_specs=[VMEM] * 11,
@@ -480,22 +489,22 @@
         compiler_params=params(24),
         cost_estimate=pl.CostEstimate(flops=4_000_000_000, bytes_accessed=14_000_000, transcendentals=0),
         name="inner",
-    )(basis, down, up, *below, *above, columns, heads, rests, hots)
-
-
-def outer_kernel(filled_hbm, whole_ref, ends_ref, below, above, spread_ref, hots, columns, out_hbm, held, out_sems):
+    )(basis, down, up, *below, *above, ids, heads, rests, hots)
+
+
+def outer_kernel(filled_hbm, whole_ref, ends_ref, below, above, spread_ref, hots, ids, out_hbm, held, out_sems):
     del filled_hbm
     whole = [whole_ref[k] for k in range(EXT)]
     for k, received in ((0, below), (EXT - 1, above)):
         whole[k] = jnp.concatenate(halves(ends_ref[k // CX] + received[...]), axis=0)
     outputs = []
     for i, brick in enumerate(OUTER):
-        column = column_of(columns, brick, whole)
+        column = column_of(ids, brick, whole)
         outputs.append(write_brick(brick, column, hots[brick], spread_ref[...], held.at[i], out_hbm, out_sems.at[i]))
     wait(outputs)
 
 
-def outer_fields(filled, whole, ends, below, above, spread, hots, columns):
+def outer_fields(filled, whole, ends, below, above, spread, hots, ids):
     return pl.pallas_call(
         outer_kernel,
         in_specs=[HBM] + [VMEM] * 7,
@@ -508,28 +517,28 @@
         input_output_aliases={0: 0},
         compiler_params=params(32),
         name="outer",
-    )(filled, whole, ends, below, above, spread, hots, columns)
+    )(filled, whole, ends, below, above, spread, hots, ids)
 
 
 def on_device(atom_values, atom_cell, brick_column):
     count = lax.axis_size("gx")
     to_lower = [((i + 1) % count, i) for i in range(count)]
     to_upper = [(i, (i + 1) % count) for i in range(count)]
-    cells = atom_cell.reshape(BRICKS * LANES, 128)
-    columns = brick_column.reshape(1, BRICKS)
-    below, above, totals = [], [], []
+    columns = jnp.pad(brick_column.reshape(1, BRICKS), ((0, 7), (0, 128 - BRICKS)))
+    ids = jnp.concatenate([atom_cell.reshape(BRICKS * LANES, 128), columns], axis=0)
+    below, above, totals, extra = [], [], [], []
     for part in range(2):
-        low, high, cells, columns, total = face_sums(part, atom_values, cells, columns)
+        low, high, total, *extra = face_sums(part, atom_values, ids)
         above.append(lax.ppermute(low, "gx", to_lower))
         below.append(lax.ppermute(high, "gx", to_upper))
         totals.append(total)
-    heads, rests, hots, gram = local_sums(atom_values, cells, brick_column, *totals)
+    heads, rests, hots, gram = local_sums(atom_values, ids, brick_column, *totals, *extra)
     mine, other = add_over_devices(*packed_gram(gram, heads, rests, below, above))
     basis, down, up = basis_and_faces(mine, other, heads, rests)
     end_above = lax.ppermute(down, "gx", to_lower)
     end_below = lax.ppermute(up, "gx", to_upper)
-    filled, whole, ends, spread = inner_fields(basis, down, up, below, above, columns, heads, rests, hots)
-    return outer_fields(filled, whole, ends, end_below, end_above, spread, hots, columns)
+    filled, whole, ends, spread = inner_fields(basis, down, up, below, above, ids, heads, rests, hots)
+    return outer_fields(filled, whole, ends, end_below, end_above, spread, hots, ids)
 
 
 def solution(mesh):

time: 75.6 us -> 75.9 us (level)
  local copies, waits for them, and re-layouts: 1.38 us -> 0.01 us
  Pallas kernels: 24.1 us -> 25.4 us
    pallas_call x3, Pallas kernels: 13.7 us -> 15.2 us  [the longest x1 10.1 us: local_sums(): pl.pallas_call(local_kernel, in_specs=[SMEM, HBM] + [VMEM] * 5, out_specs...]
    unnamed x6 -> x2, local copies, waits for them, and re-layouts: 1.38 us -> 0.01 us
  transfers between devices with their start and end apart: 14 -> 14, of which waited for: 8 -> 8; matrix products, arithmetic and copies ran while one was open for 0% -> 0% of each run, Pallas kernels for 21% -> 23%
where the time goes in v9:
time: 75.9 us; the launch traced here: 75.7 us
  starting transfers between devices  28.1 us (37%)
  Pallas kernels  25.4 us (33%)
  blocking collectives  12 us (16%)
  waiting for transfers between devices  9.17 us (12%)
    ppermute x8, starting transfers between devices, move(): lax.ppermute(x, axes, [(number[place], number[target(*place)]) for place...  13 us
    all_to_all x1, blocking collectives, add_over_devices(): lax.all_to_all(copies, axes, 0, 0, axis_index_groups=lines, tiled=True)  12 us
    ppermute x2, starting transfers between devices, on_device(): above.append(lax.ppermute(low, 'gx', to_lower))  11 us
    pallas_call x1, Pallas kernels, local_sums(): pl.pallas_call(local_kernel, in_specs=[SMEM, HBM] + [VMEM] * 5, out_specs...  10.1 us
    ppermute x8, waiting for transfers between devices, move(): lax.ppermute(x, axes, [(number[place], number[target(*place)]) for place...  7.26 us
    pallas_call x2, Pallas kernels, face_sums(): pl.pallas_call(functools.partial(faces_kernel, part), in_specs=[HBM, VMEM...  5.11 us
    pallas_call x1, Pallas kernels, inner_fields(): pl.pallas_call(inner_kernel, in_specs=[VMEM] * 11, out_specs=[HBM] + [VME...  3.56 us
    ppermute x2, starting transfers between devices, on_device(): below.append(lax.ppermute(high, 'gx', to_upper))  2.63 us
  transfers between devices with their start and end apart: 14, of which 8 were waited for; matrix products, arithmetic and copies ran while one was open for 0% of the time, Pallas kernels for 23%

profile of v9, /device:TPU:1, one launch (start us, length us, event | category | flops | bytes accessed | tf_op | source)
XLA Modules:
  0.0 75.7 jit_solution(5711343650337814340)
XLA Ops:
  0.0 0.7 pad_add_fusion.ids_ref.ids
  0.7 2.4 %faces.2 = (s16[336,512]{1,0:T(8,128)(2,1)S(1)}, s16[336,512]{1,0:T(8,128)(2,1)S(1)}, f32[2,4,320,128]{3,2,1,0:T(8,128)S(1)}) custom-call(bf16[160,4,4096]{2,1,0:T(4,128)(2,1)} %values_hbm.5, s32[40,128]{1,0:T(8,128)S(1)} %pad_add_fusion.ids_ref.ids), custom_call_target="tpu_custom_call" | custom-call | flops 1400000000 | bytes 4000000 | tf_op jit(solution)/shard_map/faces/pallas_call | solution.py:158
  3.2 0.0 copy-start
  3.2 2.5 %collective-permute-start = (s16[336,512]{1,0:T(8,128)(2,1)S(1)}, s16[336,512]{1,0:T(8,128)(2,1)S(1)}, u32[]{:S(2)}, u32[]{:S(2)}) collective-permute-start(s16[336,512]{1,0:T(8,128)(2,1)S(1)} %get-tuple-element.33), channel_id=1, source_target_pairs={{0,8},{8,16},{16,24},{24,32},{32,40},{40,48},{48,56},{56,64},{64,7... | collective-permute-start | bytes 1032200 | tf_op jit(solution)/shard_map/ppermute | solution.py:533
  5.7 6.2 %collective-permute-start.2 = (s16[336,512]{1,0:T(8,128)(2,1)S(1)}, s16[336,512]{1,0:T(8,128)(2,1)S(1)}, u32[]{:S(2)}, u32[]{:S(2)}) collective-permute-start(s16[336,512]{1,0:T(8,128)(2,1)S(1)} %get-tuple-element.35), channel_id=1, source_target_pairs={{8,0},{16,8},{24,16},{32,24},{40,32},{48,40},{56,48},{64,56},{72,6... | collective-permute-start | bytes 1032200 | tf_op jit(solution)/shard_map/ppermute | solution.py:532
  12.0 2.7 %faces.3 = (s16[336,512]{1,0:T(8,128)(2,1)S(1)}, s16[336,512]{1,0:T(8,128)(2,1)S(1)}, f32[2,4,320,128]{3,2,1,0:T(8,128)S(1)}, bf16[4,160,4,512]{3,2,1,0:T(4,128)(2,1)S(1)}, bf16[2,512,512]{2,1,0:T(8,128)(2,1)S(1)}) custom-call(bf16[160,4,4096]{2,1,0:T(4,128)(2,1)} %values_hbm.5, s32[40,128]{1,0:T(8,128)S(1)} %pad_add_fusion.ids_ref.ids), custom_call_target="tpu_custom_call" | custom-call | flops 1400000000 | bytes 4000000 | tf_op jit(solution)/shard_map/faces/pallas_call | solution.py:158
  14.6 0.1 collective-permute-start.1
  14.7 4.8 %collective-permute-start.3 = (s16[336,512]{1,0:T(8,128)(2,1)S(1)}, s16[336,512]{1,0:T(8,128)(2,1)S(1)}, u32[]{:S(2)}, u32[]{:S(2)}) collective-permute-start(s16[336,512]{1,0:T(8,128)(2,1)S(1)} %get-tuple-element.36), channel_id=1, source_target_pairs={{8,0},{16,8},{24,16},{32,24},{40,32},{48,40},{56,48},{64,56},{72,6... | collective-permute-start | bytes 1032200 | tf_op jit(solution)/shard_map/ppermute | solution.py:532
  19.5 10.1 %local.1 = (bf16[6,640,512]{2,1,0:T(8,128)(2,1)S(1)}, bf16[6,640,512]{2,1,0:T(8,128)(2,1)S(1)}, bf16[8,512,512]{2,1,0:T(8,128)(2,1)S(1)}, f32[160,160]{1,0:T(8,128)S(1)}) custom-call(s32[8]{0:T(128)S(1)} %copy-done, bf16[160,4,4096]{2,1,0:T(4,128)(2,1)} %values_hbm.5, s32[40,128]{1,0:T(8,128)S(1)} %pad_add_fusion.ids_ref.ids, ...), custom_call_target="tpu_custom_call" | custom-call | flops 6000000000 | bytes 14000000 | tf_op jit(solution)/shard_map/local/pallas_call | solution.py:214
  29.7 0.8 %below.1.gram_ref = f32[160,160]{1,0:T(8,128)S(1)} custom-call(f32[160,160]{1,0:T(8,128)S(1)} %get-tuple-element.30.gram_ref, bf16[6,640,512]{2,1,0:T(8,128)(2,1)S(1)} %get-tuple-element.31.heads, bf16[6,640,512]{2,1,0:T(8,128)(2,1)S(1)} %get-tuple-element.32.rests, s16[336,512]{1,0:T(8,128)(2,1)S(1)} %collective-permute-done.early.below_early, ...), custom_call_target="tpu_custom_call" | custom-call | flops 400000000 | bytes 3000000 | tf_op jit(solution)/shard_map/below/pallas_call | solution.py:292
  30.5 0.9 %above.1 = (f32[64,128]{1,0:T(8,128)S(1)}, f32[64,128]{1,0:T(8,128)S(1)}) custom-call(f32[160,160]{1,0:T(8,128)S(1)} %below.1.gram_ref, bf16[6,640,512]{2,1,0:T(8,128)(2,1)S(1)} %get-tuple-element.31.heads, bf16[6,640,512]{2,1,0:T(8,128)(2,1)S(1)} %get-tuple-element.32.rests, s16[336,512]{1,0:T(8,128)(2,1)S(1)} %collective-permute-done.2.early.above_early, ...), custom_call_target="tpu_custom_call" | custom-call | flops 400000000 | bytes 3000000 | tf_op jit(solution)/shard_map/above/pallas_call | solution.py:300
  31.4 1.6 %collective-permute-start.4 = (f32[64,128]{1,0:T(8,128)S(1)}, f32[64,128]{1,0:T(8,128)S(1)}, u32[]{:S(2)}, u32[]{:S(2)}) collective-permute-start(f32[64,128]{1,0:T(8,128)S(1)} %get-tuple-element.38), channel_id=1, source_target_pairs={{0,1},{1,0},{2,3},{3,2},{4,5},{5,4},{6,7},{7,6},{8,9},{9,8},{10,11... | collective-permute-start | bytes 98312 | tf_op jit(solution)/shard_map/ppermute | solution.py:348
  33.0 0.9 %collective-permute-done.4.refs_1_ = f32[64,128]{1,0:T(8,128)S(1)} collective-permute-done((f32[64,128]{1,0:T(8,128)S(1)}, f32[64,128]{1,0:T(8,128)S(1)}, u32[]{:S(2)}, u32[]{:S(2)}) %collective-permute-start.4) | collective-permute-done | bytes 32800 | tf_op jit(solution)/shard_map/ppermute | solution.py:348
  33.8 0.1 collective-permute-start.6
  33.9 3.1 %collective-permute-start.5 = (f32[64,128]{1,0:T(8,128)S(1)}, f32[64,128]{1,0:T(8,128)S(1)}, u32[]{:S(2)}, u32[]{:S(2)}) collective-permute-start(f32[64,128]{1,0:T(8,128)S(1)} %sum.4.refs_0_), channel_id=1, source_target_pairs={{0,64},{1,65},{2,66},{3,67},{4,68},{5,69},{6,70},{7,71},{8,72},{9,... | collective-permute-start | bytes 98312 | tf_op jit(solution)/shard_map/ppermute | solution.py:348
  37.1 0.7 collective-permute-done.7.refs_3_
  37.8 0.4 collective-permute-done.6.refs_2_
  38.2 0.8 %collective-permute-done.5.refs_1_ = f32[64,128]{1,0:T(8,128)S(1)} collective-permute-done((f32[64,128]{1,0:T(8,128)S(1)}, f32[64,128]{1,0:T(8,128)S(1)}, u32[]{:S(2)}, u32[]{:S(2)}) %collective-permute-start.5) | collective-permute-done | bytes 32800 | tf_op jit(solution)/shard_map/ppermute | solution.py:348
  39.1 2.8 %collective-permute-start.10 = (f32[64,128]{1,0:T(8,128)S(1)}, f32[64,128]{1,0:T(8,128)S(1)}, u32[]{:S(2)}, u32[]{:S(2)}) collective-permute-start(f32[64,128]{1,0:T(8,128)S(1)} %sum.5.refs_0_), channel_id=1, source_target_pairs={{0,6},{1,7},{2,4},{3,5},{4,2},{5,3},{6,0},{7,1},{8,14},{9,15},{10,... | collective-permute-start | bytes 98312 | tf_op jit(solution)/shard_map/ppermute | solution.py:348
  41.9 0.3 collective-permute-start.9
  42.2 0.3 collective-permute-start.8
  42.6 0.6 collective-permute-done.10.refs_3_
  43.2 3.0 %collective-permute-done.9.refs_2_ = f32[64,128]{1,0:T(8,128)S(1)} collective-permute-done((f32[64,128]{1,0:T(8,128)S(1)}, f32[64,128]{1,0:T(8,128)S(1)}, u32[]{:S(2)}, u32[]{:S(2)}) %collective-permute-start.9) | collective-permute-done | bytes 32800 | tf_op jit(solution)/shard_map/ppermute | solution.py:348
  46.2 12.0 %all_to_all.5.parts = f32[8,64,128]{2,1,0:T(8,128)S(1)} all-to-all(f32[8,64,128]{2,1,0:T(8,128)S(1)} %sum.6), channel_id=1, replica_groups={{0,8,16,24,32,40,48,56},{1,9,17,25,33,41,49,57},{2,10,18,26,34,42,50,58..., dimensions={0} | all-to-all | bytes 524288 | tf_op jit(solution)/shard_map/all_to_all | solution.py:359
  58.1 4.6 %collective-permute-start.11 = (f32[64,128]{1,0:T(8,128)S(1)}, f32[64,128]{1,0:T(8,128)S(1)}, u32[]{:S(2)}, u32[]{:S(2)}) collective-permute-start(f32[64,128]{1,0:T(8,128)S(1)} %sum.7.mine_ref), channel_id=1, source_target_pairs={{0,1},{1,0},{2,3},{3,2},{4,5},{5,4},{6,7},{7,6},{8,9},{9,8},{10,11... | collective-permute-start | bytes 98312 | tf_op jit(solution)/shard_map/ppermute | solution.py:348
  62.8 0.9 %collective-permute-done.11.other_ref = f32[64,128]{1,0:T(8,128)S(1)} collective-permute-done((f32[64,128]{1,0:T(8,128)S(1)}, f32[64,128]{1,0:T(8,128)S(1)}, u32[]{:S(2)}, u32[]{:S(2)}) %collective-permute-start.11) | collective-permute-done | bytes 32800 | tf_op jit(solution)/shard_map/ppermute | solution.py:348
  63.6 2.3 %basis.1 = (f32[8,160]{1,0:T(8,128)S(1)}, f32[32,512]{1,0:T(8,128)S(1)}, f32[32,512]{1,0:T(8,128)S(1)}) custom-call(f32[64,128]{1,0:T(8,128)S(1)} %sum.7.mine_ref, f32[64,128]{1,0:T(8,128)S(1)} %collective-permute-done.11.other_ref, bf16[6,640,512]{2,1,0:T(8,128)(2,1)S(1)} %get-tuple-element.31.heads, bf16[6,640,512]{2,1,0:T(8,128)(2,1)S(1)} %get-tuple-element.32.rests), custom_call_target="tpu_custom_call" | custom-call | tf_op jit(solution)/shard_map/basis/pallas_call | solution.py:421
  65.9 0.6 collective-permute-start.13
  66.5 1.0 %collective-permute-start.12 = (f32[32,512]{1,0:T(8,128)S(1)}, f32[32,512]{1,0:T(8,128)S(1)}, u32[]{:S(2)}, u32[]{:S(2)}) collective-permute-start(f32[32,512]{1,0:T(8,128)S(1)} %get-tuple-element.41.up_ref), channel_id=1, source_target_pairs={{0,8},{8,16},{16,24},{24,32},{32,40},{40,48},{48,56},{56,64},{64,7... | collective-permute-start | bytes 196616 | tf_op jit(solution)/shard_map/ppermute | solution.py:539
  67.5 3.6 %inner.1 = (bf16[160,4,4096]{2,1,0:T(4,128)(2,1)}, bf16[6,64,512]{2,1,0:T(8,128)(2,1)S(1)}, f32[2,32,512]{2,1,0:T(8,128)S(1)}, bf16[640,128]{1,0:T(8,128)(2,1)S(1)}) custom-call(f32[8,160]{1,0:T(8,128)S(1)} %get-tuple-element.39.basis_ref, f32[32,512]{1,0:T(8,128)S(1)} %get-tuple-element.40.down_ref, f32[32,512]{1,0:T(8,128)S(1)} %get-tuple-element.41.up_ref, ...), custom_call_target="tpu_custom_call" | custom-call | flops 4000000000 | bytes 14000000 | tf_op jit(solution)/shard_map/inner/pallas_call | solution.py:475
  71.0 1.9 %collective-permute-done.12.below = f32[32,512]{1,0:T(8,128)S(1)} collective-permute-done((f32[32,512]{1,0:T(8,128)S(1)}, f32[32,512]{1,0:T(8,128)S(1)}, u32[]{:S(2)}, u32[]{:S(2)}) %collective-permute-start.12) | collective-permute-done | bytes 65568 | tf_op jit(solution)/shard_map/ppermute | solution.py:539
  72.9 2.5 %outer.1 = bf16[160,4,4096]{2,1,0:T(4,128)(2,1)} custom-call(bf16[160,4,4096]{2,1,0:T(4,128)(2,1)} %get-tuple-element.43.filled_hbm, bf16[6,64,512]{2,1,0:T(8,128)(2,1)S(1)} %get-tuple-element.44.whole_ref, f32[2,32,512]{2,1,0:T(8,128)S(1)} %get-tuple-element.45.ends_ref, ...), custom_call_target="tpu_custom_call", output_to_operand_aliasing={{}: (0, {})} | custom-call | tf_op jit(solution)/shard_map/outer/pallas_call | solution.py:508
  (12 shorter events, 0.1 us)
Async XLA Ops:
  3.2 16.3 %copy-start = (s32[8]{0:T(128)S(1)}, s32[8]{0:T(128)}, u32[]{:S(2)}) copy-start(s32[8]{0:T(128)} %column_ref.1) | copy-start | bytes 100
  3.2 26.5 %collective-permute-start = (s16[336,512]{1,0:T(8,128)(2,1)S(1)}, s16[336,512]{1,0:T(8,128)(2,1)S(1)}, u32[]{:S(2)}, u32[]{:S(2)}) collective-permute-start(s16[336,512]{1,0:T(8,128)(2,1)S(1)} %get-tuple-element.33), channel_id=1, source_target_pairs={{0,8},{8,16},{16,24},{24,32},{32,40},{40,48},{48,56},{56,64},{64,7... | collective-permute-start | bytes 1032200 | tf_op jit(solution)/shard_map/ppermute | solution.py:533
  5.7 24.7 %collective-permute-start.2 = (s16[336,512]{1,0:T(8,128)(2,1)S(1)}, s16[336,512]{1,0:T(8,128)(2,1)S(1)}, u32[]{:S(2)}, u32[]{:S(2)}) collective-permute-start(s16[336,512]{1,0:T(8,128)(2,1)S(1)} %get-tuple-element.35), channel_id=1, source_target_pairs={{8,0},{16,8},{24,16},{32,24},{40,32},{48,40},{56,48},{64,56},{72,6... | collective-permute-start | bytes 1032200 | tf_op jit(solution)/shard_map/ppermute | solution.py:532
  14.6 15.0 %collective-permute-start.1 = (s16[336,512]{1,0:T(8,128)(2,1)S(1)}, s16[336,512]{1,0:T(8,128)(2,1)S(1)}, u32[]{:S(2)}, u32[]{:S(2)}) collective-permute-start(s16[336,512]{1,0:T(8,128)(2,1)S(1)} %get-tuple-element.34), channel_id=1, source_target_pairs={{0,8},{8,16},{16,24},{24,32},{32,40},{40,48},{48,56},{56,64},{64,7... | collective-permute-start | bytes 1032200 | tf_op jit(solution)/shard_map/ppermute | solution.py:533
  14.7 15.8 %collective-permute-start.3 = (s16[336,512]{1,0:T(8,128)(2,1)S(1)}, s16[336,512]{1,0:T(8,128)(2,1)S(1)}, u32[]{:S(2)}, u32[]{:S(2)}) collective-permute-start(s16[336,512]{1,0:T(8,128)(2,1)S(1)} %get-tuple-element.36), channel_id=1, source_target_pairs={{8,0},{16,8},{24,16},{32,24},{40,32},{48,40},{56,48},{64,56},{72,6... | collective-permute-start | bytes 1032200 | tf_op jit(solution)/shard_map/ppermute | solution.py:532
  31.4 2.5 %collective-permute-start.4 = (f32[64,128]{1,0:T(8,128)S(1)}, f32[64,128]{1,0:T(8,128)S(1)}, u32[]{:S(2)}, u32[]{:S(2)}) collective-permute-start(f32[64,128]{1,0:T(8,128)S(1)} %get-tuple-element.38), channel_id=1, source_target_pairs={{0,1},{1,0},{2,3},{3,2},{4,5},{5,4},{6,7},{7,6},{8,9},{9,8},{10,11... | collective-permute-start | bytes 98312 | tf_op jit(solution)/shard_map/ppermute | solution.py:348
  33.8 4.0 %collective-permute-start.7 = (f32[64,128]{1,0:T(8,128)S(1)}, f32[64,128]{1,0:T(8,128)S(1)}, u32[]{:S(2)}, u32[]{:S(2)}) collective-permute-start(f32[64,128]{1,0:T(8,128)S(1)} %sum.4.refs_0_), channel_id=1, source_target_pairs={{0,192},{1,193},{2,194},{3,195},{4,196},{5,197},{6,198},{7,199},{8... | collective-permute-start | bytes 98312 | tf_op jit(solution)/shard_map/ppermute | solution.py:348
  33.8 4.4 %collective-permute-start.6 = (f32[64,128]{1,0:T(8,128)S(1)}, f32[64,128]{1,0:T(8,128)S(1)}, u32[]{:S(2)}, u32[]{:S(2)}) collective-permute-start(f32[64,128]{1,0:T(8,128)S(1)} %sum.4.refs_0_), channel_id=1, source_target_pairs={{0,128},{1,129},{2,130},{3,131},{4,132},{5,133},{6,134},{7,135},{8... | collective-permute-start | bytes 98312 | tf_op jit(solution)/shard_map/ppermute | solution.py:348
  33.9 5.1 %collective-permute-start.5 = (f32[64,128]{1,0:T(8,128)S(1)}, f32[64,128]{1,0:T(8,128)S(1)}, u32[]{:S(2)}, u32[]{:S(2)}) collective-permute-start(f32[64,128]{1,0:T(8,128)S(1)} %sum.4.refs_0_), channel_id=1, source_target_pairs={{0,64},{1,65},{2,66},{3,67},{4,68},{5,69},{6,70},{7,71},{8,72},{9,... | collective-permute-start | bytes 98312 | tf_op jit(solution)/shard_map/ppermute | solution.py:348
  39.1 4.1 %collective-permute-start.10 = (f32[64,128]{1,0:T(8,128)S(1)}, f32[64,128]{1,0:T(8,128)S(1)}, u32[]{:S(2)}, u32[]{:S(2)}) collective-permute-start(f32[64,128]{1,0:T(8,128)S(1)} %sum.5.refs_0_), channel_id=1, source_target_pairs={{0,6},{1,7},{2,4},{3,5},{4,2},{5,3},{6,0},{7,1},{8,14},{9,15},{10,... | collective-permute-start | bytes 98312 | tf_op jit(solution)/shard_map/ppermute | solution.py:348
  41.9 4.3 %collective-permute-start.9 = (f32[64,128]{1,0:T(8,128)S(1)}, f32[64,128]{1,0:T(8,128)S(1)}, u32[]{:S(2)}, u32[]{:S(2)}) collective-permute-start(f32[64,128]{1,0:T(8,128)S(1)} %sum.5.refs_0_), channel_id=1, source_target_pairs={{0,4},{1,5},{2,6},{3,7},{4,0},{5,1},{6,2},{7,3},{8,12},{9,13},{10,... | collective-permute-start | bytes 98312 | tf_op jit(solution)/shard_map/ppermute | solution.py:348
  42.2 3.9 %collective-permute-start.8 = (f32[64,128]{1,0:T(8,128)S(1)}, f32[64,128]{1,0:T(8,128)S(1)}, u32[]{:S(2)}, u32[]{:S(2)}) collective-permute-start(f32[64,128]{1,0:T(8,128)S(1)} %sum.5.refs_0_), channel_id=1, source_target_pairs={{0,2},{1,3},{2,0},{3,1},{4,6},{5,7},{6,4},{7,5},{8,10},{9,11},{10,... | collective-permute-start | bytes 98312 | tf_op jit(solution)/shard_map/ppermute | solution.py:348
  58.1 5.5 %collective-permute-start.11 = (f32[64,128]{1,0:T(8,128)S(1)}, f32[64,128]{1,0:T(8,128)S(1)}, u32[]{:S(2)}, u32[]{:S(2)}) collective-permute-start(f32[64,128]{1,0:T(8,128)S(1)} %sum.7.mine_ref), channel_id=1, source_target_pairs={{0,1},{1,0},{2,3},{3,2},{4,5},{5,4},{6,7},{7,6},{8,9},{9,8},{10,11... | collective-permute-start | bytes 98312 | tf_op jit(solution)/shard_map/ppermute | solution.py:348
  65.9 5.1 %collective-permute-start.13 = (f32[32,512]{1,0:T(8,128)S(1)}, f32[32,512]{1,0:T(8,128)S(1)}, u32[]{:S(2)}, u32[]{:S(2)}) collective-permute-start(f32[32,512]{1,0:T(8,128)S(1)} %get-tuple-element.40.down_ref), channel_id=1, source_target_pairs={{8,0},{16,8},{24,16},{32,24},{40,32},{48,40},{56,48},{64,56},{72,6... | collective-permute-start | bytes 196616 | tf_op jit(solution)/shard_map/ppermute | solution.py:538
  66.5 6.4 %collective-permute-start.12 = (f32[32,512]{1,0:T(8,128)S(1)}, f32[32,512]{1,0:T(8,128)S(1)}, u32[]{:S(2)}, u32[]{:S(2)}) collective-permute-start(f32[32,512]{1,0:T(8,128)S(1)} %get-tuple-element.41.up_ref), channel_id=1, source_target_pairs={{0,8},{8,16},{16,24},{24,32},{32,40},{40,48},{48,56},{56,64},{64,7... | collective-permute-start | bytes 196616 | tf_op jit(solution)/shard_map/ppermute | solution.py:539

commit v10 on v9

--- a/solution.py
+++ b/solution.py
@@ -193,7 +193,8 @@
         place = jnp.where(column == EXT - 1, 0, column)
         for t in range(LANES):
             total[place, t] += sums[:, t * 128 : (t + 1) * 128]
-    both = jnp.zeros((2 * SNAPS, SNAPS), F32)
+    same = jnp.zeros((SNAPS, SNAPS), F32)
+    mixed = jnp.zeros((SNAPS, SNAPS), F32)
     for k in range(EXT):
         for f in range(FIELDS):
             rows = slice(f * SNAPS, (f + 1) * SNAPS)
@@ -204,9 +205,11 @@
             head, rest = halves(sums)
             heads[k, rows, :] = head
             rests[k, rows, :] = rest
-            both += dot_nt(jnp.concatenate([head, rest], axis=0), head)
-    mixed = both[SNAPS:]
-    gram_ref[...] = both[:SNAPS] + mixed + mixed.T
+        for f in range(FIELDS):
+            rows = slice(f * SNAPS, (f + 1) * SNAPS)
+            same += dot_nt(heads[k, rows, :], heads[k, rows, :])
+            mixed += dot_nt(heads[k, rows, :], rests[k, rows, :])
+    gram_ref[...] = same + mixed + mixed.T
 
 
 def local_sums(values, ids, columns, early, late, inner, outer_hots):
@@ -352,10 +355,10 @@
 
     shape = mine.shape
     mine = small_sum(terms_kernel, [mine, swap(other)], shape)
-    others = [move(mine, lambda a, z, y, c, k=k: (a ^ k, z, y, c)) for k in (1, 2, 3)]
-    mine = small_sum(terms_kernel, [mine] + others, shape)
-    others = [move(mine, lambda a, z, y, c, k=k: (a, z, y ^ k, c)) for k in (1, 2, 3)]
-    copies = small_sum(terms_kernel, [mine] + others, (depth,) + shape)
+    one, three, two = [move(mine, lambda a, z, y, c, k=k: (a ^ k, z, y, c)) for k in (1, 3, 2)]
+    mine = small_sum(terms_kernel, [mine, one, three, two], shape)
+    one, three, two = [move(mine, lambda a, z, y, c, k=k: (a, z, y ^ k, c)) for k in (1, 3, 2)]
+    copies = small_sum(terms_kernel, [mine, one, three, two], (depth,) + shape)
     parts = lax.all_to_all(copies, axes, 0, 0, axis_index_groups=lines, tiled=True)
     mine = small_sum(parts_kernel, [parts], shape)
     return mine, swap(mine)

time: 75.9 us -> 75.3 us (level)
  Pallas kernels: 25.4 us -> 22 us
  blocking collectives: 12 us -> 14.2 us
    pallas_call x1, Pallas kernels: 10.1 us -> 6.8 us  [local_sums(): pl.pallas_call(local_kernel, in_specs=[SMEM, HBM] + [VMEM] * 5, out_specs...]
    all_to_all x1, blocking collectives: 12 us -> 14.2 us  [add_over_devices(): lax.all_to_all(copies, axes, 0, 0, axis_index_groups=lines, tiled=True)]
  transfers between devices with their start and end apart: 14 -> 14, of which waited for: 8 -> 8; matrix products, arithmetic and copies ran while one was open for 0% -> 0% of each run, Pallas kernels for 23% -> 18%
where the time goes in v10:
time: 75.3 us; the launch traced here: 75.1 us
  starting transfers between devices  28.4 us (38%)
  Pallas kernels  22 us (29%)
  blocking collectives  14.2 us (19%)
  waiting for transfers between devices  9.43 us (13%)
    all_to_all x1, blocking collectives, add_over_devices(): lax.all_to_all(copies, axes, 0, 0, axis_index_groups=lines, tiled=True)  14.2 us
    ppermute x8, starting transfers between devices, move(): lax.ppermute(x, axes, [(number[place], number[target(*place)]) for place...  13 us
    ppermute x2, starting transfers between devices, on_device(): above.append(lax.ppermute(low, 'gx', to_lower))  11 us
    ppermute x8, waiting for transfers between devices, move(): lax.ppermute(x, axes, [(number[place], number[target(*place)]) for place...  6.86 us
    pallas_call x1, Pallas kernels, local_sums(): pl.pallas_call(local_kernel, in_specs=[SMEM, HBM] + [VMEM] * 5, out_specs...  6.8 us
    pallas_call x2, Pallas kernels, face_sums(): pl.pallas_call(functools.partial(faces_kernel, part), in_specs=[HBM, VMEM...  5.11 us
    pallas_call x1, Pallas kernels, inner_fields(): pl.pallas_call(inner_kernel, in_specs=[VMEM] * 11, out_specs=[HBM] + [VME...  3.55 us
    ppermute x2, starting transfers between devices, on_device(): below.append(lax.ppermute(high, 'gx', to_upper))  2.63 us
  transfers between devices with their start and end apart: 14, of which 8 were waited for; matrix products, arithmetic and copies ran while one was open for 0% of the time, Pallas kernels for 18%

profile of v10, /device:TPU:1, one launch (start us, length us, event | category | flops | bytes accessed | tf_op | source)
XLA Modules:
  0.0 75.1 jit_solution(12087527805442636132)
XLA Ops:
  0.0 0.7 pad_add_fusion.ids_ref.ids
  0.7 2.4 %faces.2 = (s16[336,512]{1,0:T(8,128)(2,1)S(1)}, s16[336,512]{1,0:T(8,128)(2,1)S(1)}, f32[2,4,320,128]{3,2,1,0:T(8,128)S(1)}) custom-call(bf16[160,4,4096]{2,1,0:T(4,128)(2,1)} %values_hbm.5, s32[40,128]{1,0:T(8,128)S(1)} %pad_add_fusion.ids_ref.ids), custom_call_target="tpu_custom_call" | custom-call | flops 1400000000 | bytes 4000000 | tf_op jit(solution)/shard_map/faces/pallas_call | solution.py:158
  3.2 0.0 copy-start
  3.2 2.5 %collective-permute-start = (s16[336,512]{1,0:T(8,128)(2,1)S(1)}, s16[336,512]{1,0:T(8,128)(2,1)S(1)}, u32[]{:S(2)}, u32[]{:S(2)}) collective-permute-start(s16[336,512]{1,0:T(8,128)(2,1)S(1)} %get-tuple-element.33), channel_id=1, source_target_pairs={{0,8},{8,16},{16,24},{24,32},{32,40},{40,48},{48,56},{56,64},{64,7... | collective-permute-start | bytes 1032200 | tf_op jit(solution)/shard_map/ppermute | solution.py:536
  5.7 6.2 %collective-permute-start.2 = (s16[336,512]{1,0:T(8,128)(2,1)S(1)}, s16[336,512]{1,0:T(8,128)(2,1)S(1)}, u32[]{:S(2)}, u32[]{:S(2)}) collective-permute-start(s16[336,512]{1,0:T(8,128)(2,1)S(1)} %get-tuple-element.35), channel_id=1, source_target_pairs={{8,0},{16,8},{24,16},{32,24},{40,32},{48,40},{56,48},{64,56},{72,6... | collective-permute-start | bytes 1032200 | tf_op jit(solution)/shard_map/ppermute | solution.py:535
  12.0 2.7 %faces.3 = (s16[336,512]{1,0:T(8,128)(2,1)S(1)}, s16[336,512]{1,0:T(8,128)(2,1)S(1)}, f32[2,4,320,128]{3,2,1,0:T(8,128)S(1)}, bf16[4,160,4,512]{3,2,1,0:T(4,128)(2,1)S(1)}, bf16[2,512,512]{2,1,0:T(8,128)(2,1)S(1)}) custom-call(bf16[160,4,4096]{2,1,0:T(4,128)(2,1)} %values_hbm.5, s32[40,128]{1,0:T(8,128)S(1)} %pad_add_fusion.ids_ref.ids), custom_call_target="tpu_custom_call" | custom-call | flops 1400000000 | bytes 4000000 | tf_op jit(solution)/shard_map/faces/pallas_call | solution.py:158
  14.6 0.1 collective-permute-start.1
  14.7 4.8 %collective-permute-start.3 = (s16[336,512]{1,0:T(8,128)(2,1)S(1)}, s16[336,512]{1,0:T(8,128)(2,1)S(1)}, u32[]{:S(2)}, u32[]{:S(2)}) collective-permute-start(s16[336,512]{1,0:T(8,128)(2,1)S(1)} %get-tuple-element.36), channel_id=1, source_target_pairs={{8,0},{16,8},{24,16},{32,24},{40,32},{48,40},{56,48},{64,56},{72,6... | collective-permute-start | bytes 1032200 | tf_op jit(solution)/shard_map/ppermute | solution.py:535
  19.5 6.8 %local.1 = (bf16[6,640,512]{2,1,0:T(8,128)(2,1)S(1)}, bf16[6,640,512]{2,1,0:T(8,128)(2,1)S(1)}, bf16[8,512,512]{2,1,0:T(8,128)(2,1)S(1)}, f32[160,160]{1,0:T(8,128)S(1)}) custom-call(s32[8]{0:T(128)S(1)} %copy-done, bf16[160,4,4096]{2,1,0:T(4,128)(2,1)} %values_hbm.5, s32[40,128]{1,0:T(8,128)S(1)} %pad_add_fusion.ids_ref.ids, ...), custom_call_target="tpu_custom_call" | custom-call | flops 6000000000 | bytes 14000000 | tf_op jit(solution)/shard_map/local/pallas_call | solution.py:217
  26.3 0.3 collective-permute-done.1.late.below_late
  26.7 0.8 %below.1.gram_ref = f32[160,160]{1,0:T(8,128)S(1)} custom-call(f32[160,160]{1,0:T(8,128)S(1)} %get-tuple-element.30.gram_ref, bf16[6,640,512]{2,1,0:T(8,128)(2,1)S(1)} %get-tuple-element.31.heads, bf16[6,640,512]{2,1,0:T(8,128)(2,1)S(1)} %get-tuple-element.32.rests, s16[336,512]{1,0:T(8,128)(2,1)S(1)} %collective-permute-done.early.below_early, ...), custom_call_target="tpu_custom_call" | custom-call | flops 400000000 | bytes 3000000 | tf_op jit(solution)/shard_map/below/pallas_call | solution.py:295
  27.5 0.9 %above.1 = (f32[64,128]{1,0:T(8,128)S(1)}, f32[64,128]{1,0:T(8,128)S(1)}) custom-call(f32[160,160]{1,0:T(8,128)S(1)} %below.1.gram_ref, bf16[6,640,512]{2,1,0:T(8,128)(2,1)S(1)} %get-tuple-element.31.heads, bf16[6,640,512]{2,1,0:T(8,128)(2,1)S(1)} %get-tuple-element.32.rests, s16[336,512]{1,0:T(8,128)(2,1)S(1)} %collective-permute-done.2.early.above_early, ...), custom_call_target="tpu_custom_call" | custom-call | flops 400000000 | bytes 3000000 | tf_op jit(solution)/shard_map/above/pallas_call | solution.py:303
  28.3 2.0 %collective-permute-start.4 = (f32[64,128]{1,0:T(8,128)S(1)}, f32[64,128]{1,0:T(8,128)S(1)}, u32[]{:S(2)}, u32[]{:S(2)}) collective-permute-start(f32[64,128]{1,0:T(8,128)S(1)} %get-tuple-element.38), channel_id=1, source_target_pairs={{0,1},{1,0},{2,3},{3,2},{4,5},{5,4},{6,7},{7,6},{8,9},{9,8},{10,11... | collective-permute-start | bytes 98312 | tf_op jit(solution)/shard_map/ppermute | solution.py:351
  30.3 0.9 %collective-permute-done.4.refs_1_ = f32[64,128]{1,0:T(8,128)S(1)} collective-permute-done((f32[64,128]{1,0:T(8,128)S(1)}, f32[64,128]{1,0:T(8,128)S(1)}, u32[]{:S(2)}, u32[]{:S(2)}) %collective-permute-start.4) | collective-permute-done | bytes 32800 | tf_op jit(solution)/shard_map/ppermute | solution.py:351
  31.2 0.3 collective-permute-start.7
  31.4 0.9 %collective-permute-start.6 = (f32[64,128]{1,0:T(8,128)S(1)}, f32[64,128]{1,0:T(8,128)S(1)}, u32[]{:S(2)}, u32[]{:S(2)}) collective-permute-start(f32[64,128]{1,0:T(8,128)S(1)} %sum.4.refs_0_), channel_id=1, source_target_pairs={{0,192},{1,193},{2,194},{3,195},{4,196},{5,197},{6,198},{7,199},{8... | collective-permute-start | bytes 98312 | tf_op jit(solution)/shard_map/ppermute | solution.py:351
  32.3 1.5 %collective-permute-start.5 = (f32[64,128]{1,0:T(8,128)S(1)}, f32[64,128]{1,0:T(8,128)S(1)}, u32[]{:S(2)}, u32[]{:S(2)}) collective-permute-start(f32[64,128]{1,0:T(8,128)S(1)} %sum.4.refs_0_), channel_id=1, source_target_pairs={{0,64},{1,65},{2,66},{3,67},{4,68},{5,69},{6,70},{7,71},{8,72},{9,... | collective-permute-start | bytes 98312 | tf_op jit(solution)/shard_map/ppermute | solution.py:351
  33.8 1.7 %collective-permute-done.7.refs_3_ = f32[64,128]{1,0:T(8,128)S(1)} collective-permute-done((f32[64,128]{1,0:T(8,128)S(1)}, f32[64,128]{1,0:T(8,128)S(1)}, u32[]{:S(2)}, u32[]{:S(2)}) %collective-permute-start.7) | collective-permute-done | bytes 32800 | tf_op jit(solution)/shard_map/ppermute | solution.py:351
  35.6 0.2 collective-permute-done.6.refs_2_
  35.8 3.0 %collective-permute-start.10 = (f32[64,128]{1,0:T(8,128)S(1)}, f32[64,128]{1,0:T(8,128)S(1)}, u32[]{:S(2)}, u32[]{:S(2)}) collective-permute-start(f32[64,128]{1,0:T(8,128)S(1)} %sum.5.refs_0_), channel_id=1, source_target_pairs={{0,4},{1,5},{2,6},{3,7},{4,0},{5,1},{6,2},{7,3},{8,12},{9,13},{10,... | collective-permute-start | bytes 98312 | tf_op jit(solution)/shard_map/ppermute | solution.py:351
  38.8 0.8 %collective-permute-start.9 = (f32[64,128]{1,0:T(8,128)S(1)}, f32[64,128]{1,0:T(8,128)S(1)}, u32[]{:S(2)}, u32[]{:S(2)}) collective-permute-start(f32[64,128]{1,0:T(8,128)S(1)} %sum.5.refs_0_), channel_id=1, source_target_pairs={{0,6},{1,7},{2,4},{3,5},{4,2},{5,3},{6,0},{7,1},{8,14},{9,15},{10,... | collective-permute-start | bytes 98312 | tf_op jit(solution)/shard_map/ppermute | solution.py:351
  39.6 0.6 collective-permute-done.10.refs_3_
  40.1 2.6 %collective-permute-done.9.refs_2_ = f32[64,128]{1,0:T(8,128)S(1)} collective-permute-done((f32[64,128]{1,0:T(8,128)S(1)}, f32[64,128]{1,0:T(8,128)S(1)}, u32[]{:S(2)}, u32[]{:S(2)}) %collective-permute-start.9) | collective-permute-done | bytes 32800 | tf_op jit(solution)/shard_map/ppermute | solution.py:351
  42.8 14.2 %all_to_all.5.parts = f32[8,64,128]{2,1,0:T(8,128)S(1)} all-to-all(f32[8,64,128]{2,1,0:T(8,128)S(1)} %sum.6), channel_id=1, replica_groups={{0,8,16,24,32,40,48,56},{1,9,17,25,33,41,49,57},{2,10,18,26,34,42,50,58..., dimensions={0} | all-to-all | bytes 524288 | tf_op jit(solution)/shard_map/all_to_all | solution.py:362
  57.0 4.6 %collective-permute-start.11 = (f32[64,128]{1,0:T(8,128)S(1)}, f32[64,128]{1,0:T(8,128)S(1)}, u32[]{:S(2)}, u32[]{:S(2)}) collective-permute-start(f32[64,128]{1,0:T(8,128)S(1)} %sum.7.mine_ref), channel_id=1, source_target_pairs={{0,1},{1,0},{2,3},{3,2},{4,5},{5,4},{6,7},{7,6},{8,9},{9,8},{10,11... | collective-permute-start | bytes 98312 | tf_op jit(solution)/shard_map/ppermute | solution.py:351
  61.6 0.9 %collective-permute-done.11.other_ref = f32[64,128]{1,0:T(8,128)S(1)} collective-permute-done((f32[64,128]{1,0:T(8,128)S(1)}, f32[64,128]{1,0:T(8,128)S(1)}, u32[]{:S(2)}, u32[]{:S(2)}) %collective-permute-start.11) | collective-permute-done | bytes 32800 | tf_op jit(solution)/shard_map/ppermute | solution.py:351
  62.5 2.3 %basis.1 = (f32[8,160]{1,0:T(8,128)S(1)}, f32[32,512]{1,0:T(8,128)S(1)}, f32[32,512]{1,0:T(8,128)S(1)}) custom-call(f32[64,128]{1,0:T(8,128)S(1)} %sum.7.mine_ref, f32[64,128]{1,0:T(8,128)S(1)} %collective-permute-done.11.other_ref, bf16[6,640,512]{2,1,0:T(8,128)(2,1)S(1)} %get-tuple-element.31.heads, bf16[6,640,512]{2,1,0:T(8,128)(2,1)S(1)} %get-tuple-element.32.rests), custom_call_target="tpu_custom_call" | custom-call | tf_op jit(solution)/shard_map/basis/pallas_call | solution.py:424
  64.8 1.1 %collective-permute-start.13 = (f32[32,512]{1,0:T(8,128)S(1)}, f32[32,512]{1,0:T(8,128)S(1)}, u32[]{:S(2)}, u32[]{:S(2)}) collective-permute-start(f32[32,512]{1,0:T(8,128)S(1)} %get-tuple-element.40.down_ref), channel_id=1, source_target_pairs={{8,0},{16,8},{24,16},{32,24},{40,32},{48,40},{56,48},{64,56},{72,6... | collective-permute-start | bytes 196616 | tf_op jit(solution)/shard_map/ppermute | solution.py:541
  65.9 0.6 collective-permute-start.12
  66.6 3.6 %inner.1 = (bf16[160,4,4096]{2,1,0:T(4,128)(2,1)}, bf16[6,64,512]{2,1,0:T(8,128)(2,1)S(1)}, f32[2,32,512]{2,1,0:T(8,128)S(1)}, bf16[640,128]{1,0:T(8,128)(2,1)S(1)}) custom-call(f32[8,160]{1,0:T(8,128)S(1)} %get-tuple-element.39.basis_ref, f32[32,512]{1,0:T(8,128)S(1)} %get-tuple-element.40.down_ref, f32[32,512]{1,0:T(8,128)S(1)} %get-tuple-element.41.up_ref, ...), custom_call_target="tpu_custom_call" | custom-call | flops 4000000000 | bytes 14000000 | tf_op jit(solution)/shard_map/inner/pallas_call | solution.py:478
  70.1 2.2 %collective-permute-done.12.below = f32[32,512]{1,0:T(8,128)S(1)} collective-permute-done((f32[32,512]{1,0:T(8,128)S(1)}, f32[32,512]{1,0:T(8,128)S(1)}, u32[]{:S(2)}, u32[]{:S(2)}) %collective-permute-start.12) | collective-permute-done | bytes 65568 | tf_op jit(solution)/shard_map/ppermute | solution.py:542
  72.4 2.5 %outer.1 = bf16[160,4,4096]{2,1,0:T(4,128)(2,1)} custom-call(bf16[160,4,4096]{2,1,0:T(4,128)(2,1)} %get-tuple-element.43.filled_hbm, bf16[6,64,512]{2,1,0:T(8,128)(2,1)S(1)} %get-tuple-element.44.whole_ref, f32[2,32,512]{2,1,0:T(8,128)S(1)} %get-tuple-element.45.ends_ref, ...), custom_call_target="tpu_custom_call", output_to_operand_aliasing={{}: (0, {})} | custom-call | tf_op jit(solution)/shard_map/outer/pallas_call | solution.py:511
  (12 shorter events, 0.1 us)
Async XLA Ops:
  3.2 16.3 %copy-start = (s32[8]{0:T(128)S(1)}, s32[8]{0:T(128)}, u32[]{:S(2)}) copy-start(s32[8]{0:T(128)} %column_ref.1) | copy-start | bytes 100
  3.2 23.1 %collective-permute-start = (s16[336,512]{1,0:T(8,128)(2,1)S(1)}, s16[336,512]{1,0:T(8,128)(2,1)S(1)}, u32[]{:S(2)}, u32[]{:S(2)}) collective-permute-start(s16[336,512]{1,0:T(8,128)(2,1)S(1)} %get-tuple-element.33), channel_id=1, source_target_pairs={{0,8},{8,16},{16,24},{24,32},{32,40},{40,48},{48,56},{56,64},{64,7... | collective-permute-start | bytes 1032200 | tf_op jit(solution)/shard_map/ppermute | solution.py:536
  5.7 21.7 %collective-permute-start.2 = (s16[336,512]{1,0:T(8,128)(2,1)S(1)}, s16[336,512]{1,0:T(8,128)(2,1)S(1)}, u32[]{:S(2)}, u32[]{:S(2)}) collective-permute-start(s16[336,512]{1,0:T(8,128)(2,1)S(1)} %get-tuple-element.35), channel_id=1, source_target_pairs={{8,0},{16,8},{24,16},{32,24},{40,32},{48,40},{56,48},{64,56},{72,6... | collective-permute-start | bytes 1032200 | tf_op jit(solution)/shard_map/ppermute | solution.py:535
  14.6 12.0 %collective-permute-start.1 = (s16[336,512]{1,0:T(8,128)(2,1)S(1)}, s16[336,512]{1,0:T(8,128)(2,1)S(1)}, u32[]{:S(2)}, u32[]{:S(2)}) collective-permute-start(s16[336,512]{1,0:T(8,128)(2,1)S(1)} %get-tuple-element.34), channel_id=1, source_target_pairs={{0,8},{8,16},{16,24},{24,32},{32,40},{40,48},{48,56},{56,64},{64,7... | collective-permute-start | bytes 1032200 | tf_op jit(solution)/shard_map/ppermute | solution.py:536
  14.7 12.7 %collective-permute-start.3 = (s16[336,512]{1,0:T(8,128)(2,1)S(1)}, s16[336,512]{1,0:T(8,128)(2,1)S(1)}, u32[]{:S(2)}, u32[]{:S(2)}) collective-permute-start(s16[336,512]{1,0:T(8,128)(2,1)S(1)} %get-tuple-element.36), channel_id=1, source_target_pairs={{8,0},{16,8},{24,16},{32,24},{40,32},{48,40},{56,48},{64,56},{72,6... | collective-permute-start | bytes 1032200 | tf_op jit(solution)/shard_map/ppermute | solution.py:535
  28.3 2.8 %collective-permute-start.4 = (f32[64,128]{1,0:T(8,128)S(1)}, f32[64,128]{1,0:T(8,128)S(1)}, u32[]{:S(2)}, u32[]{:S(2)}) collective-permute-start(f32[64,128]{1,0:T(8,128)S(1)} %get-tuple-element.38), channel_id=1, source_target_pairs={{0,1},{1,0},{2,3},{3,2},{4,5},{5,4},{6,7},{7,6},{8,9},{9,8},{10,11... | collective-permute-start | bytes 98312 | tf_op jit(solution)/shard_map/ppermute | solution.py:351
  31.2 4.4 %collective-permute-start.7 = (f32[64,128]{1,0:T(8,128)S(1)}, f32[64,128]{1,0:T(8,128)S(1)}, u32[]{:S(2)}, u32[]{:S(2)}) collective-permute-start(f32[64,128]{1,0:T(8,128)S(1)} %sum.4.refs_0_), channel_id=1, source_target_pairs={{0,128},{1,129},{2,130},{3,131},{4,132},{5,133},{6,134},{7,135},{8... | collective-permute-start | bytes 98312 | tf_op jit(solution)/shard_map/ppermute | solution.py:351
  31.4 4.3 %collective-permute-start.6 = (f32[64,128]{1,0:T(8,128)S(1)}, f32[64,128]{1,0:T(8,128)S(1)}, u32[]{:S(2)}, u32[]{:S(2)}) collective-permute-start(f32[64,128]{1,0:T(8,128)S(1)} %sum.4.refs_0_), channel_id=1, source_target_pairs={{0,192},{1,193},{2,194},{3,195},{4,196},{5,197},{6,198},{7,199},{8... | collective-permute-start | bytes 98312 | tf_op jit(solution)/shard_map/ppermute | solution.py:351
  32.3 3.5 %collective-permute-start.5 = (f32[64,128]{1,0:T(8,128)S(1)}, f32[64,128]{1,0:T(8,128)S(1)}, u32[]{:S(2)}, u32[]{:S(2)}) collective-permute-start(f32[64,128]{1,0:T(8,128)S(1)} %sum.4.refs_0_), channel_id=1, source_target_pairs={{0,64},{1,65},{2,66},{3,67},{4,68},{5,69},{6,70},{7,71},{8,72},{9,... | collective-permute-start | bytes 98312 | tf_op jit(solution)/shard_map/ppermute | solution.py:351
  35.8 4.4 %collective-permute-start.10 = (f32[64,128]{1,0:T(8,128)S(1)}, f32[64,128]{1,0:T(8,128)S(1)}, u32[]{:S(2)}, u32[]{:S(2)}) collective-permute-start(f32[64,128]{1,0:T(8,128)S(1)} %sum.5.refs_0_), channel_id=1, source_target_pairs={{0,4},{1,5},{2,6},{3,7},{4,0},{5,1},{6,2},{7,3},{8,12},{9,13},{10,... | collective-permute-start | bytes 98312 | tf_op jit(solution)/shard_map/ppermute | solution.py:351
  38.8 4.0 %collective-permute-start.9 = (f32[64,128]{1,0:T(8,128)S(1)}, f32[64,128]{1,0:T(8,128)S(1)}, u32[]{:S(2)}, u32[]{:S(2)}) collective-permute-start(f32[64,128]{1,0:T(8,128)S(1)} %sum.5.refs_0_), channel_id=1, source_target_pairs={{0,6},{1,7},{2,4},{3,5},{4,2},{5,3},{6,0},{7,1},{8,14},{9,15},{10,... | collective-permute-start | bytes 98312 | tf_op jit(solution)/shard_map/ppermute | solution.py:351
  39.6 3.2 %collective-permute-start.8 = (f32[64,128]{1,0:T(8,128)S(1)}, f32[64,128]{1,0:T(8,128)S(1)}, u32[]{:S(2)}, u32[]{:S(2)}) collective-permute-start(f32[64,128]{1,0:T(8,128)S(1)} %sum.5.refs_0_), channel_id=1, source_target_pairs={{0,2},{1,3},{2,0},{3,1},{4,6},{5,7},{6,4},{7,5},{8,10},{9,11},{10,... | collective-permute-start | bytes 98312 | tf_op jit(solution)/shard_map/ppermute | solution.py:351
  57.0 5.5 %collective-permute-start.11 = (f32[64,128]{1,0:T(8,128)S(1)}, f32[64,128]{1,0:T(8,128)S(1)}, u32[]{:S(2)}, u32[]{:S(2)}) collective-permute-start(f32[64,128]{1,0:T(8,128)S(1)} %sum.7.mine_ref), channel_id=1, source_target_pairs={{0,1},{1,0},{2,3},{3,2},{4,5},{5,4},{6,7},{7,6},{8,9},{9,8},{10,11... | collective-permute-start | bytes 98312 | tf_op jit(solution)/shard_map/ppermute | solution.py:351
  64.8 5.3 %collective-permute-start.13 = (f32[32,512]{1,0:T(8,128)S(1)}, f32[32,512]{1,0:T(8,128)S(1)}, u32[]{:S(2)}, u32[]{:S(2)}) collective-permute-start(f32[32,512]{1,0:T(8,128)S(1)} %get-tuple-element.40.down_ref), channel_id=1, source_target_pairs={{8,0},{16,8},{24,16},{32,24},{40,32},{48,40},{56,48},{64,56},{72,6... | collective-permute-start | bytes 196616 | tf_op jit(solution)/shard_map/ppermute | solution.py:541
  65.9 6.4 %collective-permute-start.12 = (f32[32,512]{1,0:T(8,128)S(1)}, f32[32,512]{1,0:T(8,128)S(1)}, u32[]{:S(2)}, u32[]{:S(2)}) collective-permute-start(f32[32,512]{1,0:T(8,128)S(1)} %get-tuple-element.41.up_ref), channel_id=1, source_target_pairs={{0,8},{8,16},{16,24},{24,32},{32,40},{40,48},{48,56},{56,64},{64,7... | collective-permute-start | bytes 196616 | tf_op jit(solution)/shard_map/ppermute | solution.py:542

commit v11 on v10

--- a/solution.py
+++ b/solution.py
@@ -265,26 +265,26 @@
     return jnp.concatenate([top, bottom], axis=0)
 
 
-def cross_terms(gram, heads, rests, early, late):
-    cross = jnp.zeros((SNAPS, SNAPS), F32)
-    scales = [wire_scale(wire) for wire in (early, late)]
-    for f in range(FIELDS):
-        part = slice(f * PART, (f + 1) * PART)
-        steps = [wire_steps(wire, part) * scale for wire, scale in zip((early, late), scales)]
-        head, rest = halves(jnp.concatenate(steps, axis=0))
-        rows = slice(f * SNAPS, (f + 1) * SNAPS)
-        own = heads[rows, :]
-        pair = dot_nt(jnp.concatenate([own, rests[rows, :]], axis=0), head)
-        cross += pair[:SNAPS] + pair[SNAPS:] + dot_nt(own, rest)
-    return gram + cross + cross.T
-
-
-def below_kernel(gram_ref, heads, rests, early, late, out_ref):
-    out_ref[...] = cross_terms(gram_ref[...], heads.at[1], rests.at[1], early, late)
-
-
-def above_kernel(gram_ref, heads, rests, early, late, mine_ref, other_ref):
-    packed = pack(cross_terms(gram_ref[...], heads.at[CX], rests.at[CX], early, late))
+def cross_terms(heads, rests, below, above):
+    cross = jnp.zeros((SNAPS, PART), F32)
+    for k, wire in ((1, below), (CX, above)):
+        scale = wire_scale(wire)
+        for f in range(FIELDS):
+            head, rest = halves(wire_steps(wire, slice(f * PART, (f + 1) * PART)) * scale)
+            rows = slice(f * SNAPS, (f + 1) * SNAPS)
+            own = heads[k, rows, :]
+            pair = dot_nt(jnp.concatenate([own, rests[k, rows, :]], axis=0), head)
+            cross += pair[:SNAPS] + pair[SNAPS:] + dot_nt(own, rest)
+    return cross
+
+
+def early_kernel(heads, rests, below, above, cross_ref):
+    cross_ref[...] = cross_terms(heads, rests, below, above)
+
+
+def late_kernel(gram_ref, early_ref, heads, rests, below, above, mine_ref, other_ref):
+    cross = jnp.concatenate([early_ref[...], cross_terms(heads, rests, below, above)], axis=1)
+    packed = pack(gram_ref[...] + cross + cross.T)
     first = on_first_core()
     mine_ref[...] = jnp.where(first, packed[: SPLIT // 2], packed[SPLIT // 2 :])
     other_ref[...] = jnp.where(first, packed[SPLIT // 2 :], packed[: SPLIT // 2])
@@ -292,22 +292,22 @@
 
 def packed_gram(gram, heads, rests, below, above):
     common = dict(compiler_params=params(16), cost_estimate=pl.CostEstimate(flops=400_000_000, bytes_accessed=3_000_000, transcendentals=0))
-    gram = pl.pallas_call(
-        below_kernel,
-        in_specs=[VMEM] * 5,
+    early = pl.pallas_call(
+        early_kernel,
+        in_specs=[VMEM] * 4,
         out_specs=VMEM,
-        out_shape=jax.ShapeDtypeStruct((SNAPS, SNAPS), F32),
-        name="below",
+        out_shape=jax.ShapeDtypeStruct((SNAPS, PART), F32),
+        name="early",
         **common,
-    )(gram, heads, rests, *below)
-    return pl.pallas_call(
-        above_kernel,
-        in_specs=[VMEM] * 5,
+    )(heads, rests, below[0], above[0])
+    return pl.pallas_call(
+        late_kernel,
+        in_specs=[VMEM] * 6,
         out_specs=[VMEM] * 2,
         out_shape=[jax.ShapeDtypeStruct((SPLIT // 2, SPLIT), F32)] * 2,
-        name="above",
+        name="late",
         **common,
-    )(gram, heads, rests, *above)
+    )(gram, early, heads, rests, below[1], above[1])
 
 
 def on_first_core():

time: 75.3 us -> 75.3 us (level)
  Pallas kernels: 22 us -> 23 us
    pallas_call x2, Pallas kernels: 1.66 us -> 2.61 us  [the longest x1 1.42 us: packed_gram(): pl.pallas_call(late_kernel, in_specs=[VMEM] * 6, out_specs=[VMEM] * 2, ou...]
  transfers between devices with their start and end apart: 14 -> 14, of which waited for: 8 -> 6; matrix products, arithmetic and copies ran while one was open for 0% -> 0% of each run, Pallas kernels for 18% -> 19%
where the time goes in v11:
time: 75.3 us; the launch traced here: 75.1 us
  starting transfers between devices  28 us (37%)
  Pallas kernels  23 us (31%)
  blocking collectives  14.1 us (19%)
  waiting for transfers between devices  8.94 us (12%)
    all_to_all x1, blocking collectives, add_over_devices(): lax.all_to_all(copies, axes, 0, 0, axis_index_groups=lines, tiled=True)  14.1 us
    ppermute x8, starting transfers between devices, move(): lax.ppermute(x, axes, [(number[place], number[target(*place)]) for place...  12.9 us
    ppermute x2, starting transfers between devices, on_device(): above.append(lax.ppermute(low, 'gx', to_lower))  11 us
    pallas_call x1, Pallas kernels, local_sums(): pl.pallas_call(local_kernel, in_specs=[SMEM, HBM] + [VMEM] * 5, out_specs...  6.81 us
    ppermute x8, waiting for transfers between devices, move(): lax.ppermute(x, axes, [(number[place], number[target(*place)]) for place...  6.69 us
    pallas_call x2, Pallas kernels, face_sums(): pl.pallas_call(functools.partial(faces_kernel, part), in_specs=[HBM, VMEM...  5.11 us
    pallas_call x1, Pallas kernels, inner_fields(): pl.pallas_call(inner_kernel, in_specs=[VMEM] * 11, out_specs=[HBM] + [VME...  3.55 us
    ppermute x2, starting transfers between devices, on_device(): below.append(lax.ppermute(high, 'gx', to_upper))  2.63 us
  transfers between devices with their start and end apart: 14, of which 6 were waited for; matrix products, arithmetic and copies ran while one was open for 0% of the time, Pallas kernels for 19%

profile of v11, /device:TPU:1, one launch (start us, length us, event | category | flops | bytes accessed | tf_op | source)
XLA Modules:
  0.0 75.1 jit_solution(1392246065712831405)
XLA Ops:
  0.0 0.7 pad_add_fusion.ids_ref.ids
  0.7 2.4 %faces.2 = (s16[336,512]{1,0:T(8,128)(2,1)S(1)}, s16[336,512]{1,0:T(8,128)(2,1)S(1)}, f32[2,4,320,128]{3,2,1,0:T(8,128)S(1)}) custom-call(bf16[160,4,4096]{2,1,0:T(4,128)(2,1)} %values_hbm.5, s32[40,128]{1,0:T(8,128)S(1)} %pad_add_fusion.ids_ref.ids), custom_call_target="tpu_custom_call" | custom-call | flops 1400000000 | bytes 4000000 | tf_op jit(solution)/shard_map/faces/pallas_call | solution.py:158
  3.2 0.0 copy-start
  3.2 2.5 %collective-permute-start = (s16[336,512]{1,0:T(8,128)(2,1)S(1)}, s16[336,512]{1,0:T(8,128)(2,1)S(1)}, u32[]{:S(2)}, u32[]{:S(2)}) collective-permute-start(s16[336,512]{1,0:T(8,128)(2,1)S(1)} %get-tuple-element.33), channel_id=1, source_target_pairs={{0,8},{8,16},{16,24},{24,32},{32,40},{40,48},{48,56},{56,64},{64,7... | collective-permute-start | bytes 1032200 | tf_op jit(solution)/shard_map/ppermute | solution.py:536
  5.7 6.2 %collective-permute-start.1 = (s16[336,512]{1,0:T(8,128)(2,1)S(1)}, s16[336,512]{1,0:T(8,128)(2,1)S(1)}, u32[]{:S(2)}, u32[]{:S(2)}) collective-permute-start(s16[336,512]{1,0:T(8,128)(2,1)S(1)} %get-tuple-element.34), channel_id=1, source_target_pairs={{8,0},{16,8},{24,16},{32,24},{40,32},{48,40},{56,48},{64,56},{72,6... | collective-permute-start | bytes 1032200 | tf_op jit(solution)/shard_map/ppermute | solution.py:535
  12.0 2.7 %faces.3 = (s16[336,512]{1,0:T(8,128)(2,1)S(1)}, s16[336,512]{1,0:T(8,128)(2,1)S(1)}, f32[2,4,320,128]{3,2,1,0:T(8,128)S(1)}, bf16[4,160,4,512]{3,2,1,0:T(4,128)(2,1)S(1)}, bf16[2,512,512]{2,1,0:T(8,128)(2,1)S(1)}) custom-call(bf16[160,4,4096]{2,1,0:T(4,128)(2,1)} %values_hbm.5, s32[40,128]{1,0:T(8,128)S(1)} %pad_add_fusion.ids_ref.ids), custom_call_target="tpu_custom_call" | custom-call | flops 1400000000 | bytes 4000000 | tf_op jit(solution)/shard_map/faces/pallas_call | solution.py:158
  14.6 0.1 collective-permute-start.2
  14.7 4.8 %collective-permute-start.3 = (s16[336,512]{1,0:T(8,128)(2,1)S(1)}, s16[336,512]{1,0:T(8,128)(2,1)S(1)}, u32[]{:S(2)}, u32[]{:S(2)}) collective-permute-start(s16[336,512]{1,0:T(8,128)(2,1)S(1)} %get-tuple-element.36), channel_id=1, source_target_pairs={{8,0},{16,8},{24,16},{32,24},{40,32},{48,40},{56,48},{64,56},{72,6... | collective-permute-start | bytes 1032200 | tf_op jit(solution)/shard_map/ppermute | solution.py:535
  19.5 6.8 %local.1 = (bf16[6,640,512]{2,1,0:T(8,128)(2,1)S(1)}, bf16[6,640,512]{2,1,0:T(8,128)(2,1)S(1)}, bf16[8,512,512]{2,1,0:T(8,128)(2,1)S(1)}, f32[160,160]{1,0:T(8,128)S(1)}) custom-call(s32[8]{0:T(128)S(1)} %copy-done, bf16[160,4,4096]{2,1,0:T(4,128)(2,1)} %values_hbm.5, s32[40,128]{1,0:T(8,128)S(1)} %pad_add_fusion.ids_ref.ids, ...), custom_call_target="tpu_custom_call" | custom-call | flops 6000000000 | bytes 14000000 | tf_op jit(solution)/shard_map/local/pallas_call | solution.py:217
  26.3 0.0 collective-permute-done.1.above.above_early
  26.4 1.2 %early.1.early_ref = f32[160,80]{1,0:T(8,128)S(1)} custom-call(bf16[6,640,512]{2,1,0:T(8,128)(2,1)S(1)} %get-tuple-element.31.heads, bf16[6,640,512]{2,1,0:T(8,128)(2,1)S(1)} %get-tuple-element.32.rests, s16[336,512]{1,0:T(8,128)(2,1)S(1)} %collective-permute-done.below.below_early, s16[336,512]{1,0:T(8,128)(2,1)S(1)} %collective-permute-done.1.above.above_early), custom_call_target="tpu_custom_call" | custom-call | flops 400000000 | bytes 3000000 | tf_op jit(solution)/shard_map/early/pallas_call | solution.py:295
  27.6 0.0 collective-permute-done.2.below.below_late
  27.6 1.4 %late.1 = (f32[64,128]{1,0:T(8,128)S(1)}, f32[64,128]{1,0:T(8,128)S(1)}) custom-call(f32[160,160]{1,0:T(8,128)S(1)} %get-tuple-element.30.gram_ref, f32[160,80]{1,0:T(8,128)S(1)} %early.1.early_ref, bf16[6,640,512]{2,1,0:T(8,128)(2,1)S(1)} %get-tuple-element.31.heads, bf16[6,640,512]{2,1,0:T(8,128)(2,1)S(1)} %get-tuple-element.32.rests, ...), custom_call_target="tpu_custom_call" | custom-call | flops 400000000 | bytes 3000000 | tf_op jit(solution)/shard_map/late/pallas_call | solution.py:303
  29.0 1.6 %collective-permute-start.4 = (f32[64,128]{1,0:T(8,128)S(1)}, f32[64,128]{1,0:T(8,128)S(1)}, u32[]{:S(2)}, u32[]{:S(2)}) collective-permute-start(f32[64,128]{1,0:T(8,128)S(1)} %get-tuple-element.38), channel_id=1, source_target_pairs={{0,1},{1,0},{2,3},{3,2},{4,5},{5,4},{6,7},{7,6},{8,9},{9,8},{10,11... | collective-permute-start | bytes 98312 | tf_op jit(solution)/shard_map/ppermute | solution.py:351
  30.6 0.9 %collective-permute-done.4.refs_1_ = f32[64,128]{1,0:T(8,128)S(1)} collective-permute-done((f32[64,128]{1,0:T(8,128)S(1)}, f32[64,128]{1,0:T(8,128)S(1)}, u32[]{:S(2)}, u32[]{:S(2)}) %collective-permute-start.4) | collective-permute-done | bytes 32800 | tf_op jit(solution)/shard_map/ppermute | solution.py:351
  31.5 0.5 collective-permute-start.6
  32.0 2.1 %collective-permute-start.5 = (f32[64,128]{1,0:T(8,128)S(1)}, f32[64,128]{1,0:T(8,128)S(1)}, u32[]{:S(2)}, u32[]{:S(2)}) collective-permute-start(f32[64,128]{1,0:T(8,128)S(1)} %sum.4.refs_0_), channel_id=1, source_target_pairs={{0,64},{1,65},{2,66},{3,67},{4,68},{5,69},{6,70},{7,71},{8,72},{9,... | collective-permute-start | bytes 98312 | tf_op jit(solution)/shard_map/ppermute | solution.py:351
  34.1 1.7 %collective-permute-done.7.refs_3_ = f32[64,128]{1,0:T(8,128)S(1)} collective-permute-done((f32[64,128]{1,0:T(8,128)S(1)}, f32[64,128]{1,0:T(8,128)S(1)}, u32[]{:S(2)}, u32[]{:S(2)}) %collective-permute-start.7) | collective-permute-done | bytes 32800 | tf_op jit(solution)/shard_map/ppermute | solution.py:351
  35.8 0.0 collective-permute-done.6.refs_2_
  35.9 3.0 %collective-permute-start.10 = (f32[64,128]{1,0:T(8,128)S(1)}, f32[64,128]{1,0:T(8,128)S(1)}, u32[]{:S(2)}, u32[]{:S(2)}) collective-permute-start(f32[64,128]{1,0:T(8,128)S(1)} %sum.5.refs_0_), channel_id=1, source_target_pairs={{0,4},{1,5},{2,6},{3,7},{4,0},{5,1},{6,2},{7,3},{8,12},{9,13},{10,... | collective-permute-start | bytes 98312 | tf_op jit(solution)/shard_map/ppermute | solution.py:351
  38.9 0.8 %collective-permute-start.9 = (f32[64,128]{1,0:T(8,128)S(1)}, f32[64,128]{1,0:T(8,128)S(1)}, u32[]{:S(2)}, u32[]{:S(2)}) collective-permute-start(f32[64,128]{1,0:T(8,128)S(1)} %sum.5.refs_0_), channel_id=1, source_target_pairs={{0,6},{1,7},{2,4},{3,5},{4,2},{5,3},{6,0},{7,1},{8,14},{9,15},{10,... | collective-permute-start | bytes 98312 | tf_op jit(solution)/shard_map/ppermute | solution.py:351
  39.7 0.6 collective-permute-done.10.refs_3_
  40.3 2.6 %collective-permute-done.9.refs_2_ = f32[64,128]{1,0:T(8,128)S(1)} collective-permute-done((f32[64,128]{1,0:T(8,128)S(1)}, f32[64,128]{1,0:T(8,128)S(1)}, u32[]{:S(2)}, u32[]{:S(2)}) %collective-permute-start.9) | collective-permute-done | bytes 32800 | tf_op jit(solution)/shard_map/ppermute | solution.py:351
  42.9 14.1 %all_to_all.5.parts = f32[8,64,128]{2,1,0:T(8,128)S(1)} all-to-all(f32[8,64,128]{2,1,0:T(8,128)S(1)} %sum.6), channel_id=1, replica_groups={{0,8,16,24,32,40,48,56},{1,9,17,25,33,41,49,57},{2,10,18,26,34,42,50,58..., dimensions={0} | all-to-all | bytes 524288 | tf_op jit(solution)/shard_map/all_to_all | solution.py:362
  57.0 4.8 %collective-permute-start.11 = (f32[64,128]{1,0:T(8,128)S(1)}, f32[64,128]{1,0:T(8,128)S(1)}, u32[]{:S(2)}, u32[]{:S(2)}) collective-permute-start(f32[64,128]{1,0:T(8,128)S(1)} %sum.7.mine_ref), channel_id=1, source_target_pairs={{0,1},{1,0},{2,3},{3,2},{4,5},{5,4},{6,7},{7,6},{8,9},{9,8},{10,11... | collective-permute-start | bytes 98312 | tf_op jit(solution)/shard_map/ppermute | solution.py:351
  61.9 0.9 %collective-permute-done.11.other_ref = f32[64,128]{1,0:T(8,128)S(1)} collective-permute-done((f32[64,128]{1,0:T(8,128)S(1)}, f32[64,128]{1,0:T(8,128)S(1)}, u32[]{:S(2)}, u32[]{:S(2)}) %collective-permute-start.11) | collective-permute-done | bytes 32800 | tf_op jit(solution)/shard_map/ppermute | solution.py:351
  62.7 2.3 %basis.1 = (f32[8,160]{1,0:T(8,128)S(1)}, f32[32,512]{1,0:T(8,128)S(1)}, f32[32,512]{1,0:T(8,128)S(1)}) custom-call(f32[64,128]{1,0:T(8,128)S(1)} %sum.7.mine_ref, f32[64,128]{1,0:T(8,128)S(1)} %collective-permute-done.11.other_ref, bf16[6,640,512]{2,1,0:T(8,128)(2,1)S(1)} %get-tuple-element.31.heads, bf16[6,640,512]{2,1,0:T(8,128)(2,1)S(1)} %get-tuple-element.32.rests), custom_call_target="tpu_custom_call" | custom-call | tf_op jit(solution)/shard_map/basis/pallas_call | solution.py:424
  65.0 0.9 %collective-permute-start.13 = (f32[32,512]{1,0:T(8,128)S(1)}, f32[32,512]{1,0:T(8,128)S(1)}, u32[]{:S(2)}, u32[]{:S(2)}) collective-permute-start(f32[32,512]{1,0:T(8,128)S(1)} %get-tuple-element.40.down_ref), channel_id=1, source_target_pairs={{8,0},{16,8},{24,16},{32,24},{40,32},{48,40},{56,48},{64,56},{72,6... | collective-permute-start | bytes 196616 | tf_op jit(solution)/shard_map/ppermute | solution.py:541
  65.9 0.6 collective-permute-start.12
  66.5 3.6 %inner.1 = (bf16[160,4,4096]{2,1,0:T(4,128)(2,1)}, bf16[6,64,512]{2,1,0:T(8,128)(2,1)S(1)}, f32[2,32,512]{2,1,0:T(8,128)S(1)}, bf16[640,128]{1,0:T(8,128)(2,1)S(1)}) custom-call(f32[8,160]{1,0:T(8,128)S(1)} %get-tuple-element.39.basis_ref, f32[32,512]{1,0:T(8,128)S(1)} %get-tuple-element.40.down_ref, f32[32,512]{1,0:T(8,128)S(1)} %get-tuple-element.41.up_ref, ...), custom_call_target="tpu_custom_call" | custom-call | flops 4000000000 | bytes 14000000 | tf_op jit(solution)/shard_map/inner/pallas_call | solution.py:478
  70.1 2.2 %collective-permute-done.12.below = f32[32,512]{1,0:T(8,128)S(1)} collective-permute-done((f32[32,512]{1,0:T(8,128)S(1)}, f32[32,512]{1,0:T(8,128)S(1)}, u32[]{:S(2)}, u32[]{:S(2)}) %collective-permute-start.12) | collective-permute-done | bytes 65568 | tf_op jit(solution)/shard_map/ppermute | solution.py:542
  72.4 2.5 %outer.1 = bf16[160,4,4096]{2,1,0:T(4,128)(2,1)} custom-call(bf16[160,4,4096]{2,1,0:T(4,128)(2,1)} %get-tuple-element.43.filled_hbm, bf16[6,64,512]{2,1,0:T(8,128)(2,1)S(1)} %get-tuple-element.44.whole_ref, f32[2,32,512]{2,1,0:T(8,128)S(1)} %get-tuple-element.45.ends_ref, ...), custom_call_target="tpu_custom_call", output_to_operand_aliasing={{}: (0, {})} | custom-call | tf_op jit(solution)/shard_map/outer/pallas_call | solution.py:511
  (12 shorter events, 0.1 us)
Async XLA Ops:
  3.2 16.3 %copy-start = (s32[8]{0:T(128)S(1)}, s32[8]{0:T(128)}, u32[]{:S(2)}) copy-start(s32[8]{0:T(128)} %column_ref.1) | copy-start | bytes 100
  3.2 23.1 %collective-permute-start = (s16[336,512]{1,0:T(8,128)(2,1)S(1)}, s16[336,512]{1,0:T(8,128)(2,1)S(1)}, u32[]{:S(2)}, u32[]{:S(2)}) collective-permute-start(s16[336,512]{1,0:T(8,128)(2,1)S(1)} %get-tuple-element.33), channel_id=1, source_target_pairs={{0,8},{8,16},{16,24},{24,32},{32,40},{40,48},{48,56},{56,64},{64,7... | collective-permute-start | bytes 1032200 | tf_op jit(solution)/shard_map/ppermute | solution.py:536
  5.7 20.6 %collective-permute-start.1 = (s16[336,512]{1,0:T(8,128)(2,1)S(1)}, s16[336,512]{1,0:T(8,128)(2,1)S(1)}, u32[]{:S(2)}, u32[]{:S(2)}) collective-permute-start(s16[336,512]{1,0:T(8,128)(2,1)S(1)} %get-tuple-element.34), channel_id=1, source_target_pairs={{8,0},{16,8},{24,16},{32,24},{40,32},{48,40},{56,48},{64,56},{72,6... | collective-permute-start | bytes 1032200 | tf_op jit(solution)/shard_map/ppermute | solution.py:535
  14.6 12.9 %collective-permute-start.2 = (s16[336,512]{1,0:T(8,128)(2,1)S(1)}, s16[336,512]{1,0:T(8,128)(2,1)S(1)}, u32[]{:S(2)}, u32[]{:S(2)}) collective-permute-start(s16[336,512]{1,0:T(8,128)(2,1)S(1)} %get-tuple-element.35), channel_id=1, source_target_pairs={{0,8},{8,16},{16,24},{24,32},{32,40},{40,48},{48,56},{56,64},{64,7... | collective-permute-start | bytes 1032200 | tf_op jit(solution)/shard_map/ppermute | solution.py:536
  14.7 12.8 %collective-permute-start.3 = (s16[336,512]{1,0:T(8,128)(2,1)S(1)}, s16[336,512]{1,0:T(8,128)(2,1)S(1)}, u32[]{:S(2)}, u32[]{:S(2)}) collective-permute-start(s16[336,512]{1,0:T(8,128)(2,1)S(1)} %get-tuple-element.36), channel_id=1, source_target_pairs={{8,0},{16,8},{24,16},{32,24},{40,32},{48,40},{56,48},{64,56},{72,6... | collective-permute-start | bytes 1032200 | tf_op jit(solution)/shard_map/ppermute | solution.py:535
  29.0 2.5 %collective-permute-start.4 = (f32[64,128]{1,0:T(8,128)S(1)}, f32[64,128]{1,0:T(8,128)S(1)}, u32[]{:S(2)}, u32[]{:S(2)}) collective-permute-start(f32[64,128]{1,0:T(8,128)S(1)} %get-tuple-element.38), channel_id=1, source_target_pairs={{0,1},{1,0},{2,3},{3,2},{4,5},{5,4},{6,7},{7,6},{8,9},{9,8},{10,11... | collective-permute-start | bytes 98312 | tf_op jit(solution)/shard_map/ppermute | solution.py:351
  31.5 4.4 %collective-permute-start.7 = (f32[64,128]{1,0:T(8,128)S(1)}, f32[64,128]{1,0:T(8,128)S(1)}, u32[]{:S(2)}, u32[]{:S(2)}) collective-permute-start(f32[64,128]{1,0:T(8,128)S(1)} %sum.4.refs_0_), channel_id=1, source_target_pairs={{0,128},{1,129},{2,130},{3,131},{4,132},{5,133},{6,134},{7,135},{8... | collective-permute-start | bytes 98312 | tf_op jit(solution)/shard_map/ppermute | solution.py:351
  31.5 4.4 %collective-permute-start.6 = (f32[64,128]{1,0:T(8,128)S(1)}, f32[64,128]{1,0:T(8,128)S(1)}, u32[]{:S(2)}, u32[]{:S(2)}) collective-permute-start(f32[64,128]{1,0:T(8,128)S(1)} %sum.4.refs_0_), channel_id=1, source_target_pairs={{0,192},{1,193},{2,194},{3,195},{4,196},{5,197},{6,198},{7,199},{8... | collective-permute-start | bytes 98312 | tf_op jit(solution)/shard_map/ppermute | solution.py:351
  32.0 3.9 %collective-permute-start.5 = (f32[64,128]{1,0:T(8,128)S(1)}, f32[64,128]{1,0:T(8,128)S(1)}, u32[]{:S(2)}, u32[]{:S(2)}) collective-permute-start(f32[64,128]{1,0:T(8,128)S(1)} %sum.4.refs_0_), channel_id=1, source_target_pairs={{0,64},{1,65},{2,66},{3,67},{4,68},{5,69},{6,70},{7,71},{8,72},{9,... | collective-permute-start | bytes 98312 | tf_op jit(solution)/shard_map/ppermute | solution.py:351
  35.9 4.4 %collective-permute-start.10 = (f32[64,128]{1,0:T(8,128)S(1)}, f32[64,128]{1,0:T(8,128)S(1)}, u32[]{:S(2)}, u32[]{:S(2)}) collective-permute-start(f32[64,128]{1,0:T(8,128)S(1)} %sum.5.refs_0_), channel_id=1, source_target_pairs={{0,4},{1,5},{2,6},{3,7},{4,0},{5,1},{6,2},{7,3},{8,12},{9,13},{10,... | collective-permute-start | bytes 98312 | tf_op jit(solution)/shard_map/ppermute | solution.py:351
  38.9 4.0 %collective-permute-start.9 = (f32[64,128]{1,0:T(8,128)S(1)}, f32[64,128]{1,0:T(8,128)S(1)}, u32[]{:S(2)}, u32[]{:S(2)}) collective-permute-start(f32[64,128]{1,0:T(8,128)S(1)} %sum.5.refs_0_), channel_id=1, source_target_pairs={{0,6},{1,7},{2,4},{3,5},{4,2},{5,3},{6,0},{7,1},{8,14},{9,15},{10,... | collective-permute-start | bytes 98312 | tf_op jit(solution)/shard_map/ppermute | solution.py:351
  39.7 3.2 %collective-permute-start.8 = (f32[64,128]{1,0:T(8,128)S(1)}, f32[64,128]{1,0:T(8,128)S(1)}, u32[]{:S(2)}, u32[]{:S(2)}) collective-permute-start(f32[64,128]{1,0:T(8,128)S(1)} %sum.5.refs_0_), channel_id=1, source_target_pairs={{0,2},{1,3},{2,0},{3,1},{4,6},{5,7},{6,4},{7,5},{8,10},{9,11},{10,... | collective-permute-start | bytes 98312 | tf_op jit(solution)/shard_map/ppermute | solution.py:351
  57.0 5.7 %collective-permute-start.11 = (f32[64,128]{1,0:T(8,128)S(1)}, f32[64,128]{1,0:T(8,128)S(1)}, u32[]{:S(2)}, u32[]{:S(2)}) collective-permute-start(f32[64,128]{1,0:T(8,128)S(1)} %sum.7.mine_ref), channel_id=1, source_target_pairs={{0,1},{1,0},{2,3},{3,2},{4,5},{5,4},{6,7},{7,6},{8,9},{9,8},{10,11... | collective-permute-start | bytes 98312 | tf_op jit(solution)/shard_map/ppermute | solution.py:351
  65.0 5.1 %collective-permute-start.13 = (f32[32,512]{1,0:T(8,128)S(1)}, f32[32,512]{1,0:T(8,128)S(1)}, u32[]{:S(2)}, u32[]{:S(2)}) collective-permute-start(f32[32,512]{1,0:T(8,128)S(1)} %get-tuple-element.40.down_ref), channel_id=1, source_target_pairs={{8,0},{16,8},{24,16},{32,24},{40,32},{48,40},{56,48},{64,56},{72,6... | collective-permute-start | bytes 196616 | tf_op jit(solution)/shard_map/ppermute | solution.py:541
  65.9 6.4 %collective-permute-start.12 = (f32[32,512]{1,0:T(8,128)S(1)}, f32[32,512]{1,0:T(8,128)S(1)}, u32[]{:S(2)}, u32[]{:S(2)}) collective-permute-start(f32[32,512]{1,0:T(8,128)S(1)} %get-tuple-element.41.up_ref), channel_id=1, source_target_pairs={{0,8},{8,16},{16,24},{24,32},{32,40},{40,48},{48,56},{56,64},{64,7... | collective-permute-start | bytes 196616 | tf_op jit(solution)/shard_map/ppermute | solution.py:542

commit v12 on v10

--- a/solution.py
+++ b/solution.py
@@ -432,8 +432,10 @@
 
 
 def column_of(ids, brick, whole):
-    mine = whole[0]
-    for k in range(1, EXT):
+    first = {0: 0, 1: 0, BRICKS - 1: EXT - 1}.get(brick, 1)
+    last = {0: 0, BRICKS - 2: EXT - 1, BRICKS - 1: EXT - 1}.get(brick, CX)
+    mine = whole[first]
+    for k in range(first + 1, last + 1):
         mine = jnp.where(column_id(ids, brick) == k, whole[k], mine)
     return mine
 

time: 75.3 us -> 75.2 us (level)
  no operation moved by 1% of the time
where the time goes in v12:
time: 75.2 us; the launch traced here: 75 us
  starting transfers between devices  28.4 us (38%)
  Pallas kernels  22 us (29%)
  blocking collectives  14.2 us (19%)
  waiting for transfers between devices  9.44 us (13%)
    all_to_all x1, blocking collectives, add_over_devices(): lax.all_to_all(copies, axes, 0, 0, axis_index_groups=lines, tiled=True)  14.2 us
    ppermute x8, starting transfers between devices, move(): lax.ppermute(x, axes, [(number[place], number[target(*place)]) for place...  13 us
    ppermute x2, starting transfers between devices, on_device(): above.append(lax.ppermute(low, 'gx', to_lower))  11 us
    ppermute x8, waiting for transfers between devices, move(): lax.ppermute(x, axes, [(number[place], number[target(*place)]) for place...  6.86 us
    pallas_call x1, Pallas kernels, local_sums(): pl.pallas_call(local_kernel, in_specs=[SMEM, HBM] + [VMEM] * 5, out_specs...  6.8 us
    pallas_call x2, Pallas kernels, face_sums(): pl.pallas_call(functools.partial(faces_kernel, part), in_specs=[HBM, VMEM...  5.11 us
    pallas_call x1, Pallas kernels, inner_fields(): pl.pallas_call(inner_kernel, in_specs=[VMEM] * 11, out_specs=[HBM] + [VME...  3.55 us
    ppermute x2, starting transfers between devices, on_device(): below.append(lax.ppermute(high, 'gx', to_upper))  2.63 us
  transfers between devices with their start and end apart: 14, of which 8 were waited for; matrix products, arithmetic and copies ran while one was open for 0% of the time, Pallas kernels for 18%

profile of v12, /device:TPU:1, one launch (start us, length us, event | category | flops | bytes accessed | tf_op | source)
XLA Modules:
  0.0 75.0 jit_solution(7415589757932622930)
XLA Ops:
  0.0 0.7 pad_add_fusion.ids_ref.ids
  0.7 2.4 %faces.2 = (s16[336,512]{1,0:T(8,128)(2,1)S(1)}, s16[336,512]{1,0:T(8,128)(2,1)S(1)}, f32[2,4,320,128]{3,2,1,0:T(8,128)S(1)}) custom-call(bf16[160,4,4096]{2,1,0:T(4,128)(2,1)} %values_hbm.5, s32[40,128]{1,0:T(8,128)S(1)} %pad_add_fusion.ids_ref.ids), custom_call_target="tpu_custom_call" | custom-call | flops 1400000000 | bytes 4000000 | tf_op jit(solution)/shard_map/faces/pallas_call | solution.py:158
  3.2 0.0 copy-start
  3.2 2.5 %collective-permute-start = (s16[336,512]{1,0:T(8,128)(2,1)S(1)}, s16[336,512]{1,0:T(8,128)(2,1)S(1)}, u32[]{:S(2)}, u32[]{:S(2)}) collective-permute-start(s16[336,512]{1,0:T(8,128)(2,1)S(1)} %get-tuple-element.33), channel_id=1, source_target_pairs={{0,8},{8,16},{16,24},{24,32},{32,40},{40,48},{48,56},{56,64},{64,7... | collective-permute-start | bytes 1032200 | tf_op jit(solution)/shard_map/ppermute | solution.py:538
  5.7 6.2 %collective-permute-start.2 = (s16[336,512]{1,0:T(8,128)(2,1)S(1)}, s16[336,512]{1,0:T(8,128)(2,1)S(1)}, u32[]{:S(2)}, u32[]{:S(2)}) collective-permute-start(s16[336,512]{1,0:T(8,128)(2,1)S(1)} %get-tuple-element.35), channel_id=1, source_target_pairs={{8,0},{16,8},{24,16},{32,24},{40,32},{48,40},{56,48},{64,56},{72,6... | collective-permute-start | bytes 1032200 | tf_op jit(solution)/shard_map/ppermute | solution.py:537
  12.0 2.7 %faces.3 = (s16[336,512]{1,0:T(8,128)(2,1)S(1)}, s16[336,512]{1,0:T(8,128)(2,1)S(1)}, f32[2,4,320,128]{3,2,1,0:T(8,128)S(1)}, bf16[4,160,4,512]{3,2,1,0:T(4,128)(2,1)S(1)}, bf16[2,512,512]{2,1,0:T(8,128)(2,1)S(1)}) custom-call(bf16[160,4,4096]{2,1,0:T(4,128)(2,1)} %values_hbm.5, s32[40,128]{1,0:T(8,128)S(1)} %pad_add_fusion.ids_ref.ids), custom_call_target="tpu_custom_call" | custom-call | flops 1400000000 | bytes 4000000 | tf_op jit(solution)/shard_map/faces/pallas_call | solution.py:158
  14.6 0.1 collective-permute-start.1
  14.7 4.8 %collective-permute-start.3 = (s16[336,512]{1,0:T(8,128)(2,1)S(1)}, s16[336,512]{1,0:T(8,128)(2,1)S(1)}, u32[]{:S(2)}, u32[]{:S(2)}) collective-permute-start(s16[336,512]{1,0:T(8,128)(2,1)S(1)} %get-tuple-element.36), channel_id=1, source_target_pairs={{8,0},{16,8},{24,16},{32,24},{40,32},{48,40},{56,48},{64,56},{72,6... | collective-permute-start | bytes 1032200 | tf_op jit(solution)/shard_map/ppermute | solution.py:537
  19.5 6.8 %local.1 = (bf16[6,640,512]{2,1,0:T(8,128)(2,1)S(1)}, bf16[6,640,512]{2,1,0:T(8,128)(2,1)S(1)}, bf16[8,512,512]{2,1,0:T(8,128)(2,1)S(1)}, f32[160,160]{1,0:T(8,128)S(1)}) custom-call(s32[8]{0:T(128)S(1)} %copy-done, bf16[160,4,4096]{2,1,0:T(4,128)(2,1)} %values_hbm.5, s32[40,128]{1,0:T(8,128)S(1)} %pad_add_fusion.ids_ref.ids, ...), custom_call_target="tpu_custom_call" | custom-call | flops 6000000000 | bytes 14000000 | tf_op jit(solution)/shard_map/local/pallas_call | solution.py:217
  26.3 0.3 collective-permute-done.1.late.below_late
  26.7 0.8 %below.1.gram_ref = f32[160,160]{1,0:T(8,128)S(1)} custom-call(f32[160,160]{1,0:T(8,128)S(1)} %get-tuple-element.30.gram_ref, bf16[6,640,512]{2,1,0:T(8,128)(2,1)S(1)} %get-tuple-element.31.heads, bf16[6,640,512]{2,1,0:T(8,128)(2,1)S(1)} %get-tuple-element.32.rests, s16[336,512]{1,0:T(8,128)(2,1)S(1)} %collective-permute-done.early.below_early, ...), custom_call_target="tpu_custom_call" | custom-call | flops 400000000 | bytes 3000000 | tf_op jit(solution)/shard_map/below/pallas_call | solution.py:295
  27.5 0.9 %above.1 = (f32[64,128]{1,0:T(8,128)S(1)}, f32[64,128]{1,0:T(8,128)S(1)}) custom-call(f32[160,160]{1,0:T(8,128)S(1)} %below.1.gram_ref, bf16[6,640,512]{2,1,0:T(8,128)(2,1)S(1)} %get-tuple-element.31.heads, bf16[6,640,512]{2,1,0:T(8,128)(2,1)S(1)} %get-tuple-element.32.rests, s16[336,512]{1,0:T(8,128)(2,1)S(1)} %collective-permute-done.2.early.above_early, ...), custom_call_target="tpu_custom_call" | custom-call | flops 400000000 | bytes 3000000 | tf_op jit(solution)/shard_map/above/pallas_call | solution.py:303
  28.3 2.0 %collective-permute-start.4 = (f32[64,128]{1,0:T(8,128)S(1)}, f32[64,128]{1,0:T(8,128)S(1)}, u32[]{:S(2)}, u32[]{:S(2)}) collective-permute-start(f32[64,128]{1,0:T(8,128)S(1)} %get-tuple-element.38), channel_id=1, source_target_pairs={{0,1},{1,0},{2,3},{3,2},{4,5},{5,4},{6,7},{7,6},{8,9},{9,8},{10,11... | collective-permute-start | bytes 98312 | tf_op jit(solution)/shard_map/ppermute | solution.py:351
  30.3 0.9 %collective-permute-done.4.refs_1_ = f32[64,128]{1,0:T(8,128)S(1)} collective-permute-done((f32[64,128]{1,0:T(8,128)S(1)}, f32[64,128]{1,0:T(8,128)S(1)}, u32[]{:S(2)}, u32[]{:S(2)}) %collective-permute-start.4) | collective-permute-done | bytes 32800 | tf_op jit(solution)/shard_map/ppermute | solution.py:351
  31.2 0.3 collective-permute-start.7
  31.4 0.9 %collective-permute-start.6 = (f32[64,128]{1,0:T(8,128)S(1)}, f32[64,128]{1,0:T(8,128)S(1)}, u32[]{:S(2)}, u32[]{:S(2)}) collective-permute-start(f32[64,128]{1,0:T(8,128)S(1)} %sum.4.refs_0_), channel_id=1, source_target_pairs={{0,192},{1,193},{2,194},{3,195},{4,196},{5,197},{6,198},{7,199},{8... | collective-permute-start | bytes 98312 | tf_op jit(solution)/shard_map/ppermute | solution.py:351
  32.3 1.5 %collective-permute-start.5 = (f32[64,128]{1,0:T(8,128)S(1)}, f32[64,128]{1,0:T(8,128)S(1)}, u32[]{:S(2)}, u32[]{:S(2)}) collective-permute-start(f32[64,128]{1,0:T(8,128)S(1)} %sum.4.refs_0_), channel_id=1, source_target_pairs={{0,64},{1,65},{2,66},{3,67},{4,68},{5,69},{6,70},{7,71},{8,72},{9,... | collective-permute-start | bytes 98312 | tf_op jit(solution)/shard_map/ppermute | solution.py:351
  33.8 1.7 %collective-permute-done.7.refs_3_ = f32[64,128]{1,0:T(8,128)S(1)} collective-permute-done((f32[64,128]{1,0:T(8,128)S(1)}, f32[64,128]{1,0:T(8,128)S(1)}, u32[]{:S(2)}, u32[]{:S(2)}) %collective-permute-start.7) | collective-permute-done | bytes 32800 | tf_op jit(solution)/shard_map/ppermute | solution.py:351
  35.6 0.2 collective-permute-done.6.refs_2_
  35.8 3.0 %collective-permute-start.10 = (f32[64,128]{1,0:T(8,128)S(1)}, f32[64,128]{1,0:T(8,128)S(1)}, u32[]{:S(2)}, u32[]{:S(2)}) collective-permute-start(f32[64,128]{1,0:T(8,128)S(1)} %sum.5.refs_0_), channel_id=1, source_target_pairs={{0,4},{1,5},{2,6},{3,7},{4,0},{5,1},{6,2},{7,3},{8,12},{9,13},{10,... | collective-permute-start | bytes 98312 | tf_op jit(solution)/shard_map/ppermute | solution.py:351
  38.8 0.8 %collective-permute-start.9 = (f32[64,128]{1,0:T(8,128)S(1)}, f32[64,128]{1,0:T(8,128)S(1)}, u32[]{:S(2)}, u32[]{:S(2)}) collective-permute-start(f32[64,128]{1,0:T(8,128)S(1)} %sum.5.refs_0_), channel_id=1, source_target_pairs={{0,6},{1,7},{2,4},{3,5},{4,2},{5,3},{6,0},{7,1},{8,14},{9,15},{10,... | collective-permute-start | bytes 98312 | tf_op jit(solution)/shard_map/ppermute | solution.py:351
  39.6 0.6 collective-permute-done.10.refs_3_
  40.1 2.6 %collective-permute-done.9.refs_2_ = f32[64,128]{1,0:T(8,128)S(1)} collective-permute-done((f32[64,128]{1,0:T(8,128)S(1)}, f32[64,128]{1,0:T(8,128)S(1)}, u32[]{:S(2)}, u32[]{:S(2)}) %collective-permute-start.9) | collective-permute-done | bytes 32800 | tf_op jit(solution)/shard_map/ppermute | solution.py:351
  42.8 14.2 %all_to_all.5.parts = f32[8,64,128]{2,1,0:T(8,128)S(1)} all-to-all(f32[8,64,128]{2,1,0:T(8,128)S(1)} %sum.6), channel_id=1, replica_groups={{0,8,16,24,32,40,48,56},{1,9,17,25,33,41,49,57},{2,10,18,26,34,42,50,58..., dimensions={0} | all-to-all | bytes 524288 | tf_op jit(solution)/shard_map/all_to_all | solution.py:362
  57.0 4.6 %collective-permute-start.11 = (f32[64,128]{1,0:T(8,128)S(1)}, f32[64,128]{1,0:T(8,128)S(1)}, u32[]{:S(2)}, u32[]{:S(2)}) collective-permute-start(f32[64,128]{1,0:T(8,128)S(1)} %sum.7.mine_ref), channel_id=1, source_target_pairs={{0,1},{1,0},{2,3},{3,2},{4,5},{5,4},{6,7},{7,6},{8,9},{9,8},{10,11... | collective-permute-start | bytes 98312 | tf_op jit(solution)/shard_map/ppermute | solution.py:351
  61.6 0.9 %collective-permute-done.11.other_ref = f32[64,128]{1,0:T(8,128)S(1)} collective-permute-done((f32[64,128]{1,0:T(8,128)S(1)}, f32[64,128]{1,0:T(8,128)S(1)}, u32[]{:S(2)}, u32[]{:S(2)}) %collective-permute-start.11) | collective-permute-done | bytes 32800 | tf_op jit(solution)/shard_map/ppermute | solution.py:351
  62.5 2.3 %basis.1 = (f32[8,160]{1,0:T(8,128)S(1)}, f32[32,512]{1,0:T(8,128)S(1)}, f32[32,512]{1,0:T(8,128)S(1)}) custom-call(f32[64,128]{1,0:T(8,128)S(1)} %sum.7.mine_ref, f32[64,128]{1,0:T(8,128)S(1)} %collective-permute-done.11.other_ref, bf16[6,640,512]{2,1,0:T(8,128)(2,1)S(1)} %get-tuple-element.31.heads, bf16[6,640,512]{2,1,0:T(8,128)(2,1)S(1)} %get-tuple-element.32.rests), custom_call_target="tpu_custom_call" | custom-call | tf_op jit(solution)/shard_map/basis/pallas_call | solution.py:424
  64.8 1.1 %collective-permute-start.13 = (f32[32,512]{1,0:T(8,128)S(1)}, f32[32,512]{1,0:T(8,128)S(1)}, u32[]{:S(2)}, u32[]{:S(2)}) collective-permute-start(f32[32,512]{1,0:T(8,128)S(1)} %get-tuple-element.40.down_ref), channel_id=1, source_target_pairs={{8,0},{16,8},{24,16},{32,24},{40,32},{48,40},{56,48},{64,56},{72,6... | collective-permute-start | bytes 196616 | tf_op jit(solution)/shard_map/ppermute | solution.py:543
  65.9 0.6 collective-permute-start.12
  66.6 3.5 %inner.1 = (bf16[160,4,4096]{2,1,0:T(4,128)(2,1)}, bf16[6,64,512]{2,1,0:T(8,128)(2,1)S(1)}, f32[2,32,512]{2,1,0:T(8,128)S(1)}, bf16[640,128]{1,0:T(8,128)(2,1)S(1)}) custom-call(f32[8,160]{1,0:T(8,128)S(1)} %get-tuple-element.39.basis_ref, f32[32,512]{1,0:T(8,128)S(1)} %get-tuple-element.40.down_ref, f32[32,512]{1,0:T(8,128)S(1)} %get-tuple-element.41.up_ref, ...), custom_call_target="tpu_custom_call" | custom-call | flops 4000000000 | bytes 14000000 | tf_op jit(solution)/shard_map/inner/pallas_call | solution.py:480
  70.1 2.2 %collective-permute-done.12.below = f32[32,512]{1,0:T(8,128)S(1)} collective-permute-done((f32[32,512]{1,0:T(8,128)S(1)}, f32[32,512]{1,0:T(8,128)S(1)}, u32[]{:S(2)}, u32[]{:S(2)}) %collective-permute-start.12) | collective-permute-done | bytes 65568 | tf_op jit(solution)/shard_map/ppermute | solution.py:544
  72.4 2.5 %outer.1 = bf16[160,4,4096]{2,1,0:T(4,128)(2,1)} custom-call(bf16[160,4,4096]{2,1,0:T(4,128)(2,1)} %get-tuple-element.43.filled_hbm, bf16[6,64,512]{2,1,0:T(8,128)(2,1)S(1)} %get-tuple-element.44.whole_ref, f32[2,32,512]{2,1,0:T(8,128)S(1)} %get-tuple-element.45.ends_ref, ...), custom_call_target="tpu_custom_call", output_to_operand_aliasing={{}: (0, {})} | custom-call | tf_op jit(solution)/shard_map/outer/pallas_call | solution.py:513
  (12 shorter events, 0.1 us)
Async XLA Ops:
  3.2 16.3 %copy-start = (s32[8]{0:T(128)S(1)}, s32[8]{0:T(128)}, u32[]{:S(2)}) copy-start(s32[8]{0:T(128)} %column_ref.1) | copy-start | bytes 100
  3.2 23.1 %collective-permute-start = (s16[336,512]{1,0:T(8,128)(2,1)S(1)}, s16[336,512]{1,0:T(8,128)(2,1)S(1)}, u32[]{:S(2)}, u32[]{:S(2)}) collective-permute-start(s16[336,512]{1,0:T(8,128)(2,1)S(1)} %get-tuple-element.33), channel_id=1, source_target_pairs={{0,8},{8,16},{16,24},{24,32},{32,40},{40,48},{48,56},{56,64},{64,7... | collective-permute-start | bytes 1032200 | tf_op jit(solution)/shard_map/ppermute | solution.py:538
  5.7 21.7 %collective-permute-start.2 = (s16[336,512]{1,0:T(8,128)(2,1)S(1)}, s16[336,512]{1,0:T(8,128)(2,1)S(1)}, u32[]{:S(2)}, u32[]{:S(2)}) collective-permute-start(s16[336,512]{1,0:T(8,128)(2,1)S(1)} %get-tuple-element.35), channel_id=1, source_target_pairs={{8,0},{16,8},{24,16},{32,24},{40,32},{48,40},{56,48},{64,56},{72,6... | collective-permute-start | bytes 1032200 | tf_op jit(solution)/shard_map/ppermute | solution.py:537
  14.6 12.0 %collective-permute-start.1 = (s16[336,512]{1,0:T(8,128)(2,1)S(1)}, s16[336,512]{1,0:T(8,128)(2,1)S(1)}, u32[]{:S(2)}, u32[]{:S(2)}) collective-permute-start(s16[336,512]{1,0:T(8,128)(2,1)S(1)} %get-tuple-element.34), channel_id=1, source_target_pairs={{0,8},{8,16},{16,24},{24,32},{32,40},{40,48},{48,56},{56,64},{64,7... | collective-permute-start | bytes 1032200 | tf_op jit(solution)/shard_map/ppermute | solution.py:538
  14.7 12.7 %collective-permute-start.3 = (s16[336,512]{1,0:T(8,128)(2,1)S(1)}, s16[336,512]{1,0:T(8,128)(2,1)S(1)}, u32[]{:S(2)}, u32[]{:S(2)}) collective-permute-start(s16[336,512]{1,0:T(8,128)(2,1)S(1)} %get-tuple-element.36), channel_id=1, source_target_pairs={{8,0},{16,8},{24,16},{32,24},{40,32},{48,40},{56,48},{64,56},{72,6... | collective-permute-start | bytes 1032200 | tf_op jit(solution)/shard_map/ppermute | solution.py:537
  28.3 2.8 %collective-permute-start.4 = (f32[64,128]{1,0:T(8,128)S(1)}, f32[64,128]{1,0:T(8,128)S(1)}, u32[]{:S(2)}, u32[]{:S(2)}) collective-permute-start(f32[64,128]{1,0:T(8,128)S(1)} %get-tuple-element.38), channel_id=1, source_target_pairs={{0,1},{1,0},{2,3},{3,2},{4,5},{5,4},{6,7},{7,6},{8,9},{9,8},{10,11... | collective-permute-start | bytes 98312 | tf_op jit(solution)/shard_map/ppermute | solution.py:351
  31.2 4.4 %collective-permute-start.7 = (f32[64,128]{1,0:T(8,128)S(1)}, f32[64,128]{1,0:T(8,128)S(1)}, u32[]{:S(2)}, u32[]{:S(2)}) collective-permute-start(f32[64,128]{1,0:T(8,128)S(1)} %sum.4.refs_0_), channel_id=1, source_target_pairs={{0,128},{1,129},{2,130},{3,131},{4,132},{5,133},{6,134},{7,135},{8... | collective-permute-start | bytes 98312 | tf_op jit(solution)/shard_map/ppermute | solution.py:351
  31.4 4.3 %collective-permute-start.6 = (f32[64,128]{1,0:T(8,128)S(1)}, f32[64,128]{1,0:T(8,128)S(1)}, u32[]{:S(2)}, u32[]{:S(2)}) collective-permute-start(f32[64,128]{1,0:T(8,128)S(1)} %sum.4.refs_0_), channel_id=1, source_target_pairs={{0,192},{1,193},{2,194},{3,195},{4,196},{5,197},{6,198},{7,199},{8... | collective-permute-start | bytes 98312 | tf_op jit(solution)/shard_map/ppermute | solution.py:351
  32.3 3.5 %collective-permute-start.5 = (f32[64,128]{1,0:T(8,128)S(1)}, f32[64,128]{1,0:T(8,128)S(1)}, u32[]{:S(2)}, u32[]{:S(2)}) collective-permute-start(f32[64,128]{1,0:T(8,128)S(1)} %sum.4.refs_0_), channel_id=1, source_target_pairs={{0,64},{1,65},{2,66},{3,67},{4,68},{5,69},{6,70},{7,71},{8,72},{9,... | collective-permute-start | bytes 98312 | tf_op jit(solution)/shard_map/ppermute | solution.py:351
  35.8 4.4 %collective-permute-start.10 = (f32[64,128]{1,0:T(8,128)S(1)}, f32[64,128]{1,0:T(8,128)S(1)}, u32[]{:S(2)}, u32[]{:S(2)}) collective-permute-start(f32[64,128]{1,0:T(8,128)S(1)} %sum.5.refs_0_), channel_id=1, source_target_pairs={{0,4},{1,5},{2,6},{3,7},{4,0},{5,1},{6,2},{7,3},{8,12},{9,13},{10,... | collective-permute-start | bytes 98312 | tf_op jit(solution)/shard_map/ppermute | solution.py:351
  38.8 4.0 %collective-permute-start.9 = (f32[64,128]{1,0:T(8,128)S(1)}, f32[64,128]{1,0:T(8,128)S(1)}, u32[]{:S(2)}, u32[]{:S(2)}) collective-permute-start(f32[64,128]{1,0:T(8,128)S(1)} %sum.5.refs_0_), channel_id=1, source_target_pairs={{0,6},{1,7},{2,4},{3,5},{4,2},{5,3},{6,0},{7,1},{8,14},{9,15},{10,... | collective-permute-start | bytes 98312 | tf_op jit(solution)/shard_map/ppermute | solution.py:351
  39.6 3.2 %collective-permute-start.8 = (f32[64,128]{1,0:T(8,128)S(1)}, f32[64,128]{1,0:T(8,128)S(1)}, u32[]{:S(2)}, u32[]{:S(2)}) collective-permute-start(f32[64,128]{1,0:T(8,128)S(1)} %sum.5.refs_0_), channel_id=1, source_target_pairs={{0,2},{1,3},{2,0},{3,1},{4,6},{5,7},{6,4},{7,5},{8,10},{9,11},{10,... | collective-permute-start | bytes 98312 | tf_op jit(solution)/shard_map/ppermute | solution.py:351
  57.0 5.5 %collective-permute-start.11 = (f32[64,128]{1,0:T(8,128)S(1)}, f32[64,128]{1,0:T(8,128)S(1)}, u32[]{:S(2)}, u32[]{:S(2)}) collective-permute-start(f32[64,128]{1,0:T(8,128)S(1)} %sum.7.mine_ref), channel_id=1, source_target_pairs={{0,1},{1,0},{2,3},{3,2},{4,5},{5,4},{6,7},{7,6},{8,9},{9,8},{10,11... | collective-permute-start | bytes 98312 | tf_op jit(solution)/shard_map/ppermute | solution.py:351
  64.8 5.3 %collective-permute-start.13 = (f32[32,512]{1,0:T(8,128)S(1)}, f32[32,512]{1,0:T(8,128)S(1)}, u32[]{:S(2)}, u32[]{:S(2)}) collective-permute-start(f32[32,512]{1,0:T(8,128)S(1)} %get-tuple-element.40.down_ref), channel_id=1, source_target_pairs={{8,0},{16,8},{24,16},{32,24},{40,32},{48,40},{56,48},{64,56},{72,6... | collective-permute-start | bytes 196616 | tf_op jit(solution)/shard_map/ppermute | solution.py:543
  65.9 6.4 %collective-permute-start.12 = (f32[32,512]{1,0:T(8,128)S(1)}, f32[32,512]{1,0:T(8,128)S(1)}, u32[]{:S(2)}, u32[]{:S(2)}) collective-permute-start(f32[32,512]{1,0:T(8,128)S(1)} %get-tuple-element.41.up_ref), channel_id=1, source_target_pairs={{0,8},{8,16},{16,24},{24,32},{32,40},{40,48},{48,56},{56,64},{64,7... | collective-permute-start | bytes 196616 | tf_op jit(solution)/shard_map/ppermute | solution.py:544
